TPU v7x, 256 devices: a whole 4x4x8 slice. The times are simulated.
256 devices in a mesh: ctx: 32 (over y, x, core), tp: 8 (over z).
Axes of the slice: x: 4, y: 4, z: 8, core: 2. Of those that a mesh axis runs over, the one named last changes fastest.
Arguments:
- concepts: bfloat16 [4096, 1024], P('ctx'), may hold values from -34 to 34
- noised: bfloat16 [4096, 1024], P('ctx'), may hold values from -6 to 6
- step_ids: int32 [4096], P('ctx'), may hold values from 1 to 99
- doc_lengths: int32 [4], replicated, may hold values from 1 to 3712, 4096 in all
- context: bfloat16 [4096, 4096], P('ctx'), may hold values from -96 to 96
- time_vec: float32 [4096], P('tp'), may hold values from -6 to 6
- w_pre: bfloat16 [1024, 4096], P(None, 'tp'), may hold values from -0.1875 to 0.1875
- w_query: bfloat16 [4096, 2048], P(None, 'tp'), may hold values from -2 to 2
- w_key: bfloat16 [4096, 2048], P(None, 'tp'), may hold values from -1 to 1
- w_value: bfloat16 [4096, 2048], P(None, 'tp'), may hold values from -0.09375 to 0.09375
- w_out: bfloat16 [2048, 4096], P('tp'), may hold values from -0.125 to 0.125
- w_post: bfloat16 [4096, 1024], P('tp'), may hold values from -0.09375 to 0.09375
Outputs:
- d_context: bfloat16 [4096, 4096], P('ctx', 'tp')
- loss: float32 [], replicated
Inputs may be any that keep to these rules, and one draw needn't show every extreme that they name: `doc_lengths`: they sum to 4096; the longest is exactly 3712.
All inputs are finite; a program needn't handle non-finite values.
Results may differ from a plain program's by a relative error of at most 0.04.
Values may be sent and summed in bfloat16 or wider, within the bound.
No kernel may reach another device: no remote copies, remote signals or barrier semaphores. Data moves between devices by JAX's collectives and lax.ppermute only.
A program may use at most 128 MiB of HBM per device.

v0:
```python
import math

import jax
import jax.numpy as jnp
from jax import lax
from jax.sharding import PartitionSpec as P

HDIM = 128
TSTEPS = 100


MASKED = -1e30
EPSILON = 1e-06


def from_behind(block, axis, distance):
    devices = range(lax.axis_size(axis))
    route = [(i - distance, i) for i in devices if i - distance in devices]
    return lax.ppermute(block, axis, route)


def document_tables(doc_lengths):
    doc_ends = jnp.cumsum(doc_lengths)
    doc_starts = doc_ends - doc_lengths
    return (doc_starts, doc_ends)


def document_index(positions, doc_ends):
    return jnp.sum((positions[:, None] >= doc_ends[None, :]).astype(jnp.int32), axis=1)


def pick_entry(table, which):
    return jnp.sum(jnp.where(jnp.arange(table.shape[0], dtype=jnp.int32) == which, table, 0))


def noise_plan(step_ids):
    angle = 0.5 * math.pi / TSTEPS * step_ids.astype(jnp.float32)
    return (jnp.cos(angle), jnp.sin(angle))


def local(
    concepts,
    noised,
    step_ids,
    doc_lengths,
    context,
    time_vec,
    w_pre,
    w_query,
    w_key,
    w_value,
    w_out,
    w_post,
):
    row_count = concepts.shape[0]
    seq_total = row_count * lax.axis_size("ctx")
    first_row = lax.axis_index("ctx") * row_count
    positions = first_row + jnp.arange(row_count, dtype=jnp.int32)
    doc_starts, doc_ends = document_tables(doc_lengths)
    doc_ids = document_index(positions, doc_ends)
    head_width = w_query.shape[1]
    local_heads = head_width // HDIM
    score_scale = 1.0 / math.sqrt(HDIM)
    block_rows = min(512, seq_total)
    query_floor = pick_entry(doc_starts, doc_ids[0])

    def block_mask(query_pos, query_docs, key_pos):
        key_docs = document_index(key_pos, doc_ends)
        return (key_docs[None, :] == query_docs[:, None]) & (key_pos[None, :] <= query_pos[:, None])

    def tile_grads(query_tile, grad_tile, total_tile, dot_tile, key_tile, value_tile, allowed):
        scores = (
            jnp.einsum("qhd,khd->hqk", query_tile, key_tile, preferred_element_type=jnp.float32)
            * score_scale
        )
        probs = jnp.where(
            allowed[None],
            jnp.exp(jnp.where(allowed[None], scores, MASKED) - total_tile[:, :, None]),
            0.0,
        )
        value_grad = jnp.einsum(
            "hqk,qhd->khd",
            probs.astype(jnp.bfloat16),
            grad_tile,
            preferred_element_type=jnp.float32,
        )
        prob_grad = jnp.einsum(
            "qhd,khd->hqk", grad_tile, value_tile, preferred_element_type=jnp.float32
        )
        score_grad = (probs * (prob_grad - dot_tile[:, :, None]) * score_scale).astype(jnp.bfloat16)
        key_grad = jnp.einsum(
            "hqk,qhd->khd", score_grad, query_tile, preferred_element_type=jnp.float32
        )
        return (key_grad, value_grad)

    keep_level, noise_level = noise_plan(step_ids)
    projected = (
        jnp.dot(noised, w_pre, preferred_element_type=jnp.float32)
        + noise_level[:, None] * time_vec[None, :]
    )
    input_part = projected.astype(jnp.bfloat16)
    input_full = lax.all_gather(input_part, "tp", axis=1, tiled=True)
    width = input_full.shape[1]
    input_wide = input_full.astype(jnp.float32)
    normed = (
        input_wide * lax.rsqrt(jnp.mean(input_wide * input_wide, axis=1, keepdims=True) + EPSILON)
    ).astype(jnp.bfloat16)
    queries = jnp.dot(normed, w_query, preferred_element_type=jnp.float32).astype(jnp.bfloat16)
    key_rows = jnp.dot(context, w_key, preferred_element_type=jnp.float32).astype(jnp.bfloat16)
    value_rows = jnp.dot(context, w_value, preferred_element_type=jnp.float32).astype(jnp.bfloat16)
    all_keys, all_values = (
        lax.all_gather(key_rows, "ctx", axis=0, tiled=True),
        lax.all_gather(value_rows, "ctx", axis=0, tiled=True),
    )
    query_heads = queries.reshape(row_count, local_heads, HDIM)

    def forward_block(block, carry):
        row_max, row_total, weighted = carry
        key_start = block * block_rows
        key_block = lax.dynamic_slice_in_dim(all_keys, key_start, block_rows, 0).reshape(
            block_rows, local_heads, HDIM
        )
        value_block = lax.dynamic_slice_in_dim(all_values, key_start, block_rows, 0).reshape(
            block_rows, local_heads, HDIM
        )
        allowed = block_mask(
            positions, doc_ids, key_start + jnp.arange(block_rows, dtype=jnp.int32)
        )[None]
        scores = (
            jnp.einsum("qhd,khd->hqk", query_heads, key_block, preferred_element_type=jnp.float32)
            * score_scale
        )
        scores = jnp.where(allowed, scores, MASKED)
        new_max = jnp.maximum(row_max, jnp.max(scores, axis=2))
        probs = jnp.where(allowed, jnp.exp(scores - new_max[:, :, None]), 0.0)
        fading = jnp.exp(row_max - new_max)
        row_total = row_total * fading + jnp.sum(probs, axis=2)
        weighted = weighted * fading[:, :, None] + jnp.einsum(
            "hqk,khd->hqd",
            probs.astype(jnp.bfloat16),
            value_block,
            preferred_element_type=jnp.float32,
        )
        return (new_max, row_total, weighted)

    start_block = query_floor // block_rows
    stop_block = (first_row + row_count - 1) // block_rows + 1
    initial = (
        jnp.full((local_heads, row_count), MASKED, jnp.float32),
        jnp.zeros((local_heads, row_count), jnp.float32),
        jnp.zeros((local_heads, row_count, HDIM), jnp.float32),
    )
    row_max, row_total, weighted = lax.fori_loop(start_block, stop_block, forward_block, initial)
    log_totals = row_max + jnp.log(row_total)
    attended = (
        (weighted / row_total[:, :, None])
        .transpose(1, 0, 2)
        .reshape(row_count, head_width)
        .astype(jnp.bfloat16)
    )
    head_terms = jnp.dot(attended, w_out, preferred_element_type=jnp.float32)
    mixed = input_part.astype(jnp.float32) + lax.psum_scatter(
        head_terms.astype(jnp.bfloat16), "tp", scatter_dimension=1, tiled=True
    ).astype(jnp.float32)
    squares = lax.psum(jnp.sum(mixed * mixed, axis=1), "tp")
    inverse = lax.rsqrt(squares / width + EPSILON)
    unit = mixed * inverse[:, None]
    prediction = lax.psum(
        jnp.dot(unit.astype(jnp.bfloat16), w_post, preferred_element_type=jnp.float32).astype(
            jnp.bfloat16
        ),
        "tp",
    ).astype(jnp.float32)
    following = from_behind(concepts[:1], "ctx", -1)
    targets = jnp.concatenate((concepts[1:], following), axis=0).astype(jnp.float32)
    valid = jnp.logical_not(jnp.any(doc_ends[None, :] == positions[:, None] + 1, axis=1))
    weights = jnp.where(valid, 1.0 + keep_level * keep_level, 0.0)
    missed = prediction - targets
    weighted_missed = weights[:, None] * missed
    loss = lax.psum(jnp.sum(weighted_missed * missed), "ctx") / (seq_total * concepts.shape[1])
    pred_grad = weighted_missed.astype(jnp.bfloat16)
    unit_grad = jnp.dot(pred_grad, w_post.T, preferred_element_type=jnp.float32)
    along = lax.psum(jnp.sum(unit_grad * unit, axis=1), "tp") / width
    mixed_grad = ((unit_grad - unit * along[:, None]) * inverse[:, None]).astype(jnp.bfloat16)
    mixed_full = lax.all_gather(mixed_grad, "tp", axis=1, tiled=True)
    attended_grad = jnp.dot(mixed_full, w_out.T, preferred_element_type=jnp.float32).astype(
        jnp.bfloat16
    )
    grad_heads = attended_grad.reshape(row_count, local_heads, HDIM)
    output_dot = jnp.sum(
        grad_heads.astype(jnp.float32)
        * attended.reshape(row_count, local_heads, HDIM).astype(jnp.float32),
        axis=2,
    ).T
    start = jnp.int32(0)
    count = row_count * lax.axis_size("ctx")
    key_pos = jnp.arange(count, dtype=jnp.int32)

    def compute(unused):
        key_tile = all_keys.reshape(count, local_heads, HDIM)
        value_tile = all_values.reshape(count, local_heads, HDIM)
        key_grad, value_grad = tile_grads(
            query_heads,
            grad_heads,
            log_totals,
            output_dot,
            key_tile,
            value_tile,
            block_mask(positions, doc_ids, key_pos),
        )
        return jnp.concatenate(
            (key_grad.reshape(count, head_width), value_grad.reshape(count, head_width)), axis=1
        )

    def skipped(unused):
        return jnp.zeros((count, 2 * head_width), jnp.float32)

    reached = (start <= positions[-1]) & (start + count > query_floor)
    both_grads = lax.psum_scatter(
        lax.cond(reached, compute, skipped, 0).astype(jnp.bfloat16),
        "ctx",
        scatter_dimension=0,
        tiled=True,
    ).astype(jnp.float32)
    key_merged = both_grads[:, :head_width].astype(jnp.bfloat16)
    value_merged = both_grads[:, head_width:].astype(jnp.bfloat16)
    context_terms = jnp.dot(key_merged, w_key.T, preferred_element_type=jnp.float32) + jnp.dot(
        value_merged, w_value.T, preferred_element_type=jnp.float32
    )
    d_context = lax.psum_scatter(
        context_terms.astype(jnp.bfloat16), "tp", scatter_dimension=1, tiled=True
    )
    return (d_context, loss)


def solution(mesh):
    return jax.shard_map(
        local,
        mesh=mesh,
        in_specs=(
            P("ctx", None),
            P("ctx", None),
            P("ctx"),
            P(),
            P("ctx", None),
            P("tp"),
            P(None, "tp"),
            P(None, "tp"),
            P(None, "tp"),
            P(None, "tp"),
            P("tp", None),
            P("tp", None),
        ),
        out_specs=(P("ctx", "tp"), P()),
        check_vma=False,
    )
```

profile of v0, /device:TPU:1, one launch (start us, length us, event | category | flops | bytes accessed | tf_op | source)
XLA Modules:
  0.0 559.5 jit_solution(4484492253566131755)
XLA Ops:
  7.2 1.0 reduce-window.8
  8.2 0.1 compare_reduce_fusion
  8.3 1.3 add_select_fusion
  9.6 2.3 fusion.31
  11.9 0.0 all-gather.9.cloned.1.call-start
  12.0 3.0 convolution_convert_fusion.3
  15.0 0.0 all-gather.5.cloned.1.call-start
  15.1 2.7 convolution_convert_fusion.5
  17.7 0.0 reduce-scatter.6.cloned.1.call-start
  17.8 0.1 convert_reduce_fusion.2
  17.9 0.7 fusion.44
  21.1 28.4 %all-gather.7.cloned.1.call-done = bf16[128,4096]{1,0:T(8,128)(2,1)} async-done(((bf16[128,512]{1,0:T(8,128)(2,1)}), bf16[128,4096]{1,0:T(8,128)(2,1)}) %all-gather.7.cloned.1.call-update) | async-done | bytes 1048592 | tf_op jit(solution)/shard_map/all_gather | solution.py:102
  49.5 1.5 fusion.29
  51.0 2.4 convolution_convert_fusion.4
  53.5 0.6 copy-done.9
  54.1 50.8 %all-gather.9.cloned.1.call-done = bf16[4096,256]{1,0:T(8,128)(2,1)} async-done(((bf16[128,256]{1,0:T(8,128)(2,1)}), bf16[4096,256]{1,0:T(8,128)(2,1)}) %all-gather.9.cloned.1.call-update) | async-done | bytes 2097168 | tf_op jit(solution)/shard_map/all_gather | solution.py:113
  104.9 50.7 %all-gather.5.cloned.1.call-done = bf16[4096,256]{1,0:T(8,128)(2,1)} async-done(((bf16[128,256]{1,0:T(8,128)(2,1)}), bf16[4096,256]{1,0:T(8,128)(2,1)}) %all-gather.5.cloned.1.call-update) | async-done | bytes 2097168 | tf_op jit(solution)/shard_map/all_gather | solution.py:112
  155.6 2.6 while.15
  155.7 0.1 convert_reduce_fusion.4
  155.7 0.2 compare_and_fusion.3
  156.0 1.1 constant_dynamic-slice_fusion.3
  157.0 0.1 copy.88
  157.2 0.1 copy.89
  157.3 0.3 fusion.83
  157.6 0.1 fusion.84
  157.8 0.4 convolution_add_fusion.4
  158.2 0.1 copy.57
  158.4 1.5 convolution_convert_fusion
  159.8 0.0 all-reduce.2.cloned.1.call-start
  159.9 50.8 %reduce-scatter.6.cloned.1.call-done = bf16[128,512]{1,0:T(8,128)(2,1)} async-done(((bf16[128,4096]{1,0:T(8,128)(2,1)}), bf16[128,512]{1,0:T(8,128)(2,1)}) %reduce-scatter.6.cloned.1.call-update) | async-done | bytes 131088 | tf_op jit(solution)/shard_map/reduce_scatter | solution.py:162
  210.7 1.6 multiply_reduce_fusion.1
  212.3 12.3 %psum.28 = f32[128]{0:T(128)} all-reduce(f32[128]{0:T(128)} %multiply_reduce_fusion.1), channel_id=1, replica_groups=mesh['ctx'=32,'tp'=8] {'tp'}, use_global_device_ids=true, to_apply=%region_12.13 | all-reduce | flops 128 | bytes 1024 | tf_op jit(solution)/shard_map/psum | solution.py:165
  224.6 0.7 add_rsqrt_fusion
  225.3 0.5 copy-done.11
  225.8 2.0 convolution_convert_fusion.1
  227.8 0.7 slice.23
  228.6 10.9 %collective-permute-start = (bf16[1,1024]{1,0:T(2,128)(2,1)S(1)}, bf16[1,1024]{1,0:T(2,128)(2,1)}, u32[]{:S(2)}, u32[]{:S(2)}) collective-permute-start(bf16[1,1024]{1,0:T(2,128)(2,1)S(1)} %slice.23), channel_id=1, source_target_pairs={{8,0},{16,8},{24,16},{32,24},{40,32},{48,40},{56,48},{64,56},{72,6... | collective-permute-start | bytes 6152 | tf_op jit(solution)/shard_map/ppermute | solution.py:19
  239.5 1.7 slice.22
  241.2 0.8 collective-permute-done
  242.0 62.1 %all-reduce.2.cloned.1.call-done = bf16[128,1024]{1,0:T(8,128)(2,1)} async-done(((bf16[128,1024]{1,0:T(8,128)(2,1)}), bf16[128,1024]{1,0:T(8,128)(2,1)}) %all-reduce.2.cloned.1.call-update) | async-done | bytes 262160 | tf_op jit(solution)/shard_map/psum | solution.py:168
  304.1 2.8 multiply_reduce_fusion
  306.9 12.6 %psum.30 = f32[128]{0:T(128)S(1)} all-reduce(f32[128]{0:T(128)} %get-tuple-element.253), channel_id=1, replica_groups=mesh['ctx'=32,'tp'=8] {'tp'}, use_global_device_ids=true, to_apply=%region_15.16 | all-reduce | flops 128 | bytes 1024 | tf_op jit(solution)/shard_map/psum | solution.py:183
  319.5 1.7 multiply_convert_fusion.2
  321.3 1.2 slice.20
  323.8 0.9 reshape.204
  324.7 37.5 %all-gather.11.cloned.1.call-done = bf16[128,4096]{1,0:T(8,128)(2,1)} async-done(((bf16[128,512]{1,0:T(8,128)(2,1)}), bf16[128,4096]{1,0:T(8,128)(2,1)}) %all-gather.11.cloned.1.call-update) | async-done | bytes 1048592 | tf_op jit(solution)/shard_map/all_gather | solution.py:185
  362.2 2.1 convolution_convert_fusion.2
  364.3 0.1 copy.58
  364.5 17.4 %conditional.1 = (bf16[4096,512]{0,1:T(8,128)(2,1)}) conditional(s32[]{:T(128)} %convert_element_type.100, () %tuple.18, (s32[4096]{0:T(1024)S(1)}, s32[4]{0:T(128)S(1)}, s32[128]{0:T(128)S(1)}, s32[4096]{0:T(1024)S(1)}, s32[128]{0:T(128)S(1)}, /*index=5*/bf16[4096,256]{1,0:T(8,128)(2,1)}, bf16[128,2,128]{2,1,0:T(2,128)(2,1)S(1)}, ...), branch_computations={%region_17.18_spmd, %region_18.20_spmd} | conditional | flops 1093185792 | bytes 39393332 | solution.py:220
  364.5 0.1 convert_reduce_fusion
  364.7 0.1 copy.60
  364.8 0.1 copy.59
  364.9 0.5 compare_and_fusion
  365.4 5.2 fusion.7
  370.6 5.7 %fusion.16 = bf16[2,4096,128]{1,2,0:T(8,128)(2,1)} fusion(bf16[128,2,128]{0,2,1:T(8,128)(2,1)S(1)} %copy.59, f32[2,128,4096]{2,1,0:T(8,128)} %fusion.7, bf16[128,2,128]{0,2,1:T(8,128)(2,1)S(1)} %copy.60, f32[2,128]{1,0:T(2,128)S(1)} %get-tuple-element.96, bf16[4096,256]{1,0:T(8,128)(2,1)} %get-tuple-element.95), kind=kOutput, calls=%fused_computation.18 | convolution fusion | flops 541065216 | bytes 8520704 | tf_op jit(solution)/shard_map/cond/branch_1_fun/hqk,qhd->khd/dot_general | solution.py:91
  376.4 3.0 fusion.13
  379.4 2.5 pad_maximum_fusion
  381.9 6.5 %copy.66 = bf16[4096,512]{1,0:T(8,128)(2,1)} copy(bf16[4096,512]{0,1:T(8,128)(2,1)} %get-tuple-element.380) | data formatting | bytes 8388608
  388.4 0.0 reduce-scatter.8.cloned.1.call-start
  388.5 91.5 %reduce-scatter.10.cloned.1.call-done = bf16[128,512]{1,0:T(8,128)(2,1)} async-done(((bf16[4096,512]{1,0:T(8,128)(2,1)}), bf16[128,512]{1,0:T(8,128)(2,1)}) %reduce-scatter.10.cloned.1.call-update) | async-done | bytes 131088
  479.9 2.6 fusion.42
  482.6 1.8 fusion.28
  484.4 1.5 fusion.34
  485.9 65.0 %psum.31 = f32[]{:T(128)} all-reduce(f32[]{:T(128)} %fusion.34), channel_id=1, replica_groups=mesh['ctx'=32,'tp'=8] {'ctx'}, use_global_device_ids=true, to_apply=%region_23.24 | all-reduce | flops 1 | bytes 8 | tf_op jit(solution)/shard_map/psum | solution.py:180
  (60 shorter events, 0.5 us)
Async XLA Ops:
  7.2 151.2 %copy-start = (bf16[256,4096]{1,0:T(8,128)(2,1)S(1)}, bf16[256,4096]{1,0:T(8,128)(2,1)}, u32[]{:S(2)}) copy-start(bf16[256,4096]{1,0:T(8,128)(2,1)} %param.26) | copy-start | bytes 6291460
  7.2 42.3 %all-gather.7.cloned.1.call-start = ((), (), s32[]{:S(2)}) async-start(), calls=%async_computation.4 | async-start | bytes 1179648 | tf_op jit(solution)/shard_map/all_gather | solution.py:102
  9.6 5.5 copy-start.3
  11.9 92.9 %all-gather.9.cloned.1.call-start = ((), (), s32[]{:S(2)}) async-start(), calls=%async_computation.5 | async-start | bytes 2162688 | tf_op jit(solution)/shard_map/all_gather | solution.py:113
  15.0 2.9 copy-start.13
  15.0 140.6 %all-gather.5.cloned.1.call-start = ((), (), s32[]{:S(2)}) async-start(), calls=%async_computation.3 | async-start | bytes 2162688 | tf_op jit(solution)/shard_map/all_gather | solution.py:112
  17.7 193.0 %reduce-scatter.6.cloned.1.call-start = ((), (), s32[]{:S(2)}) async-start(), calls=%async_computation.6 | async-start | bytes 1179648 | tf_op jit(solution)/shard_map/reduce_scatter | solution.py:162
  17.8 35.6 %copy-start.14 = (s32[128]{0:T(128)}, s32[128]{0:T(128)S(1)}, u32[]{:S(2)}) copy-start(s32[128]{0:T(128)S(1)} %iota_add_fusion.2) | copy-start | bytes 1540
  53.5 0.6 copy-start.9
  158.3 52.4 %copy-start.4 = (bf16[128,512]{1,0:T(8,128)(2,1)S(1)}, bf16[128,512]{1,0:T(8,128)(2,1)}, u32[]{:S(2)}) copy-start(bf16[128,512]{1,0:T(8,128)(2,1)} %fusion.31) | copy-start | bytes 393220
  158.3 67.4 %copy-start.6 = (bf16[512,1024]{1,0:T(8,128)(2,1)S(1)}, bf16[512,1024]{1,0:T(8,128)(2,1)}, u32[]{:S(2)}) copy-start(bf16[512,1024]{1,0:T(8,128)(2,1)} %param.27) | copy-start | bytes 3145732
  159.8 144.3 %all-reduce.2.cloned.1.call-start = ((), (), s32[]{:S(2)}) async-start(), calls=%async_computation.7 | async-start | bytes 524288 | tf_op jit(solution)/shard_map/psum | solution.py:168
  210.7 93.4 %copy-start.5 = (bf16[128,512]{1,0:T(8,128)(2,1)S(1)}, bf16[128,512]{1,0:T(8,128)(2,1)}, u32[]{:S(2)}) copy-start(bf16[128,512]{1,0:T(8,128)(2,1)} %reduce-scatter.6.cloned.1.call-done) | copy-start | bytes 393220
  225.3 0.5 copy-start.11
  227.8 134.4 %all-gather.11.cloned.1.call-start = ((), (), s32[]{:S(2)}) async-start(), calls=%async_computation.8 | async-start | bytes 1179648 | tf_op jit(solution)/shard_map/all_gather | solution.py:185
  228.6 13.4 %collective-permute-start = (bf16[1,1024]{1,0:T(2,128)(2,1)S(1)}, bf16[1,1024]{1,0:T(2,128)(2,1)}, u32[]{:S(2)}, u32[]{:S(2)}) collective-permute-start(bf16[1,1024]{1,0:T(2,128)(2,1)S(1)} %slice.23), channel_id=1, source_target_pairs={{8,0},{16,8},{24,16},{32,24},{40,32},{48,40},{56,48},{64,56},{72,6... | collective-permute-start | bytes 6152 | tf_op jit(solution)/shard_map/ppermute | solution.py:19
  321.3 43.2 %copy-start.15 = (s32[128]{0:T(128)S(1)}, s32[128]{0:T(128)}, u32[]{:S(2)}) copy-start(s32[128]{0:T(128)} %copy-done.14) | copy-start | bytes 1540
  321.3 158.6 %reduce-scatter.10.cloned.1.call-start = ((), (), s32[]{:S(2)}) async-start(), calls=%async_computation.10 | async-start | bytes 4325376
  376.3 3.0 copy-start.1
  388.4 163.1 %reduce-scatter.8.cloned.1.call-start = ((), (), s32[]{:S(2)}) async-start(), calls=%async_computation.9 | async-start | bytes 1179648 | tf_op jit(solution)/shard_map/reduce_scatter | solution.py:230
  479.9 2.6 copy-start.2
  479.9 2.6 copy-start.10
  482.5 1.9 copy-start.7
  482.5 1.9 copy-start.8
  482.5 1.9 copy-start.12
Sparse Core Ops, SparseCore 0:
  12.1 37.3 all-gather.6
  52.0 52.7 all-gather.8
  107.4 48.1 all-gather.4
  160.0 50.7 reduce-scatter.5
  227.9 76.1 all-reduce.1
  321.4 40.7 all-gather.10
  388.5 91.3 reduce-scatter.9
  484.5 35.4 reduce-scatter.7
where the time goes:
time: 561 us; the launch traced here: 560 us
  waiting for transfers between devices  373 us (66%)
  blocking collectives  89.8 us (16%)
  matrix products  37.7 us (7%)
  between operations  20 us (4%)
  local copies, waits for them, and re-layouts  14 us (2%)
  other arithmetic  13.8 us (2%)
  starting transfers between devices  11.2 us (2%)
    unnamed x9, waiting for transfers between devices  91.6 us
    psum x1, blocking collectives, local(): lax.psum(jnp.sum(weighted_missed * missed), 'ctx')  65 us
    psum x1, waiting for transfers between devices, local(): lax.psum(jnp.dot(unit.astype(jnp.bfloat16), w_post, preferred_element_typ...  62.1 us
    reduce_scatter x1, waiting for transfers between devices, local(): lax.psum_scatter(head_terms.astype(jnp.bfloat16), 'tp', scatter_dimension...  50.8 us
    all_gather x1, waiting for transfers between devices, local(): lax.all_gather(value_rows, 'ctx', axis=0, tiled=True)  50.8 us
    all_gather x1, waiting for transfers between devices, local(): lax.all_gather(key_rows, 'ctx', axis=0, tiled=True)  50.7 us
    all_gather x1, waiting for transfers between devices, local(): mixed_full = lax.all_gather(mixed_grad, 'tp', axis=1, tiled=True)  37.5 us
    all_gather x1, waiting for transfers between devices, local(): input_full = lax.all_gather(input_part, 'tp', axis=1, tiled=True)  28.4 us
  transfers between devices with their start and end apart: 9, of which 8 were waited for; matrix products, arithmetic and copies ran while one was open for 3% of the time, Pallas kernels for 0%

commit v1 on v0

v1 whole, which is shorter than its diff:
```python
import math

import jax
import jax.numpy as jnp
from jax import lax
from jax.experimental import pallas as pl
from jax.experimental.pallas import tpu as pltpu
from jax.sharding import Mesh
from jax.sharding import PartitionSpec as P

HDIM = 128
TSTEPS = 100
MASKED = -1e30
EPSILON = 1e-06
ROWS = ("y", "x", "core")
CHIPS = ("y", "x")
SCALE = 1.0 / math.sqrt(HDIM)
PAIR = 256
GROUP = 4
F32 = jnp.float32
BF16 = jnp.bfloat16


def dot(a, b, contract=((1,), (0,))):
    return lax.dot_general(a, b, (contract, ((), ())), preferred_element_type=F32)


def spread(block, axis):
    count = lax.axis_size(axis)
    stacked = jnp.broadcast_to(block[None], (count,) + block.shape)
    return lax.all_to_all(stacked, axis, 0, 0, tiled=True)


def swap(block):
    return lax.ppermute(block, "core", [(0, 1), (1, 0)])


def to_head(left, right, core):
    first = core == 0
    mine = jnp.where(first, left, right)
    got = swap(jnp.where(first, right, left))
    return jnp.concatenate((jnp.where(first, mine, got), jnp.where(first, got, mine)), axis=0)


def to_rows(block, core):
    first = core == 0
    half = block.shape[0] // 2
    top, bottom = block[:half], block[half:]
    mine = jnp.where(first, top, bottom)
    got = swap(jnp.where(first, bottom, top))
    return jnp.concatenate((jnp.where(first, mine, got), jnp.where(first, got, mine)), axis=1)


def pieces(values):
    high = lax.reduce_precision(values, 8, 7)
    rest = values - high
    middle = lax.reduce_precision(rest, 8, 7)
    low = rest - middle
    return high.astype(BF16), middle.astype(BF16), low.astype(BF16)


def start_of(ends_ref, positions):
    start = jnp.zeros_like(positions)
    for d in range(ends_ref.shape[0]):
        start = jnp.where(positions >= ends_ref[d], ends_ref[d], start)
    return start


def forward_kernel(ends_ref, chip_ref, q_ref, kv_ref, out_ref, total_ref):
    base = chip_ref[0] * PAIR
    width = GROUP * PAIR
    query_pos = base + lax.broadcasted_iota(jnp.int32, (1, PAIR), 1)
    query_start = start_of(ends_ref, query_pos)
    floor = start_of(ends_ref, base)
    q = q_ref[...]

    def body(step, carry):
        row_max, row_total, weighted = carry
        kv = kv_ref[pl.ds(step * GROUP, GROUP)].reshape(width, 2 * HDIM)
        scores = dot(kv[:, :HDIM], q, ((1,), (1,))) * SCALE
        key_pos = step * width + lax.broadcasted_iota(jnp.int32, (width, PAIR), 0)
        scores = jnp.where((key_pos >= query_start) & (key_pos <= query_pos), scores, MASKED)
        new_max = jnp.maximum(row_max, jnp.max(scores, axis=0, keepdims=True))
        probs = jnp.exp(scores - new_max)
        fading = jnp.exp(row_max - new_max)
        row_total = row_total * fading + jnp.sum(probs, axis=0, keepdims=True)
        weighted = weighted * fading + dot(kv[:, HDIM:], probs.astype(BF16), ((0,), (0,)))
        return new_max, row_total, weighted

    row_max, row_total, weighted = lax.fori_loop(
        floor // width,
        (base + PAIR - 1) // width + 1,
        body,
        (
            jnp.full((1, PAIR), MASKED, F32),
            jnp.zeros((1, PAIR), F32),
            jnp.zeros((HDIM, PAIR), F32),
        ),
    )
    out_ref[...] = (weighted / row_total).T.astype(BF16)
    total_ref[...] = row_max + jnp.log(row_total)


def backward_kernel(ends_ref, chip_ref, kv_ref, q_ref, sent_ref, out_ref):
    base = chip_ref[0] * PAIR
    width = GROUP * PAIR
    keys, values = kv_ref[:, :HDIM], kv_ref[:, HDIM:]
    last = base + PAIR - 1
    reach = q_ref.shape[0] * PAIR
    for d in reversed(range(ends_ref.shape[0])):
        reach = jnp.where(last < ends_ref[d], ends_ref[d], reach)
    key_pos = base + lax.broadcasted_iota(jnp.int32, (PAIR, width), 0)

    def body(step, carry):
        key_grad, value_grad = carry
        chips = pl.ds(step * GROUP, GROUP)
        q = q_ref[chips].reshape(width, HDIM)
        grad = sent_ref[chips, :PAIR, :].reshape(width, HDIM)
        stats = sent_ref[chips, PAIR:, :].astype(F32)

        def row(at):
            parts = [
                stats[g, at + r : at + r + 1]
                + stats[g, at + 2 + r : at + 3 + r]
                + stats[g, at + 4 + r : at + 5 + r]
                for g in range(GROUP)
                for r in range(2)
            ]
            return jnp.concatenate(parts, axis=1)

        query_pos = step * width + lax.broadcasted_iota(jnp.int32, (1, width), 1)
        query_start = start_of(ends_ref, query_pos)
        allowed = (key_pos >= query_start) & (key_pos <= query_pos)
        scores = dot(keys, q, ((1,), (1,))) * SCALE
        probs = jnp.where(allowed, jnp.exp(scores - row(0)), 0.0)
        value_grad = value_grad + dot(probs.astype(BF16), grad)
        prob_grad = dot(values, grad, ((1,), (1,)))
        score_grad = (probs * (prob_grad - row(6)) * SCALE).astype(BF16)
        key_grad = key_grad + dot(score_grad, q)
        return key_grad, value_grad

    zero = jnp.zeros((PAIR, HDIM), F32)
    key_grad, value_grad = lax.fori_loop(
        base // width, (reach + width - 1) // width, body, (zero, zero)
    )
    out_ref[:, :HDIM] = key_grad.astype(BF16)
    out_ref[:, HDIM:] = value_grad.astype(BF16)


def context_kernel(grad_ref, key_ref, value_ref, out_ref):
    key_grad = jnp.concatenate((grad_ref[:, :HDIM], grad_ref[:, 2 * HDIM : 3 * HDIM]), axis=1)
    value_grad = jnp.concatenate((grad_ref[:, HDIM : 2 * HDIM], grad_ref[:, 3 * HDIM :]), axis=1)
    total = dot(key_grad, key_ref[...], ((1,), (1,))) + dot(value_grad, value_ref[...], ((1,), (1,)))
    out_ref[0] = total.astype(BF16)


SMEM = pl.BlockSpec(memory_space=pltpu.SMEM)
VMEM = pl.BlockSpec(memory_space=pltpu.VMEM)
PARAMS = pltpu.CompilerParams(vmem_limit_bytes=40 * 1024 * 1024)


def local(
    concepts,
    noised,
    step_ids,
    doc_lengths,
    context,
    time_vec,
    w_pre,
    w_query,
    w_key,
    w_value,
    w_out,
    w_post,
):
    rows, features = concepts.shape
    parts = lax.axis_size("tp")
    chips = lax.axis_size(CHIPS)
    core = lax.axis_index("core")
    part = lax.axis_index("tp")
    seq_total = rows * lax.axis_size(ROWS)
    share = w_post.shape[0]
    width = share * parts
    own = rows // parts
    chip = lax.axis_index(CHIPS).astype(jnp.int32)
    chip_id = chip.reshape(1)
    doc_ends = jnp.cumsum(doc_lengths).astype(jnp.int32)
    positions = lax.axis_index(ROWS) * rows + jnp.arange(rows, dtype=jnp.int32)
    angle = 0.5 * math.pi / TSTEPS * step_ids.astype(F32)
    keep_level, noise_level = jnp.cos(angle), jnp.sin(angle)

    with jax.named_scope("inputs"):
        input_part = (dot(noised, w_pre) + noise_level[:, None] * time_vec[None, :]).astype(BF16)
        input_full = lax.all_gather(input_part, "tp", axis=1, tiled=True)
    with jax.named_scope("keys_values"):
        key_rows = dot(context, w_key).astype(BF16)
        value_rows = dot(context, w_value).astype(BF16)
        own_kv = to_head(
            jnp.concatenate((key_rows[:, :HDIM], value_rows[:, :HDIM]), axis=1),
            jnp.concatenate((key_rows[:, HDIM:], value_rows[:, HDIM:]), axis=1),
            core,
        )
        all_kv = spread(own_kv, CHIPS)
    with jax.named_scope("targets"):
        count = lax.axis_size(ROWS)
        following = lax.ppermute(concepts[:1], ROWS, [(i + 1, i) for i in range(count - 1)])
        targets = jnp.concatenate((concepts[1:], following), axis=0)
        targets = lax.dynamic_slice_in_dim(targets, part * own, own, 0).astype(F32)
        valid = jnp.logical_not(jnp.any(doc_ends[None, :] == positions[:, None] + 1, axis=1))
        weights = jnp.where(valid, 1.0 + keep_level * keep_level, 0.0)
        weights = lax.dynamic_slice_in_dim(weights, part * own, own, 0)
    with jax.named_scope("queries"):
        input_wide = input_full.astype(F32)
        scale = lax.rsqrt(jnp.mean(input_wide * input_wide, axis=1, keepdims=True) + EPSILON)
        normed = (input_wide * scale).astype(BF16)
        queries = dot(normed, w_query).astype(BF16)
        query_head = to_head(queries[:, :HDIM], queries[:, HDIM:], core)
        all_queries = lax.all_gather(query_head, CHIPS, axis=0, tiled=False)
    with jax.named_scope("attention"):
        attended_head, log_total = pl.pallas_call(
            forward_kernel,
            out_shape=(
                jax.ShapeDtypeStruct((PAIR, HDIM), BF16),
                jax.ShapeDtypeStruct((1, PAIR), F32),
            ),
            in_specs=[SMEM, SMEM, VMEM, VMEM],
            out_specs=(VMEM, VMEM),
            compiler_params=PARAMS,
        )(doc_ends, chip_id, query_head, all_kv)
        attended = to_rows(attended_head, core)
    with jax.named_scope("mixed"):
        head_terms = jnp.einsum(
            "rk,ktf->trf", attended, w_out.reshape(-1, parts, share), preferred_element_type=F32
        ).astype(BF16)
        arrived = lax.all_to_all(head_terms, "tp", 0, 0, tiled=True)
        mixed = input_part.astype(F32) + jnp.sum(arrived.astype(F32), axis=0)
    with jax.named_scope("prediction"):
        squares = jnp.sum(mixed * mixed, axis=1)
        raw = dot(mixed.astype(BF16), w_post).astype(BF16)
        side = jnp.stack(pieces(squares), axis=1)
        side = jnp.pad(side, ((0, 0), (0, HDIM - 3)))
        sent = jnp.concatenate((raw, side), axis=1).reshape(parts, own, features + HDIM)
        arrived = jnp.sum(lax.all_to_all(sent, "tp", 0, 0, tiled=True).astype(F32), axis=0)
        squares = jnp.sum(arrived[:, features : features + 3], axis=1)
        inverse = lax.rsqrt(squares / width + EPSILON)
        prediction = arrived[:, :features] * inverse[:, None]
    with jax.named_scope("loss"):
        missed = prediction - targets
        weighted_missed = weights[:, None] * missed
        row_loss = jnp.sum(weighted_missed * missed, axis=1)
        pred_grad = weighted_missed.astype(BF16)
        along = jnp.sum(pred_grad.astype(F32) * prediction, axis=1) / width
        side = jnp.stack(pieces(inverse) + pieces(along) + pieces(row_loss), axis=1)
        side = jnp.pad(side, ((0, 0), (0, HDIM - 9)))
        arrived = spread(jnp.concatenate((pred_grad, side), axis=1), "tp")
        arrived = arrived.reshape(rows, features + HDIM)
        side = arrived[:, features : features + 9].astype(F32)
        inverse, along, row_loss = (jnp.sum(side[:, i : i + 3], axis=1) for i in (0, 3, 6))
        loss_part = jnp.sum(row_loss)
    with jax.named_scope("mixed_grad"):
        unit_grad = dot(arrived[:, :features], w_post, ((1,), (1,)))
        unit = mixed * inverse[:, None]
        mixed_grad = ((unit_grad - unit * along[:, None]) * inverse[:, None]).astype(BF16)
        mixed_full = spread(mixed_grad, "tp")
        attended_grad = jnp.einsum(
            "trf,ktf->rk", mixed_full, w_out.reshape(-1, parts, share), preferred_element_type=F32
        ).astype(BF16)
    with jax.named_scope("sent_grads"):
        grad_head = to_head(attended_grad[:, :HDIM], attended_grad[:, HDIM:], core)
        output_dot = jnp.sum(grad_head.astype(F32) * attended_head.astype(F32), axis=1)
        stats = [p.reshape(2, HDIM) for p in pieces(log_total)]
        stats += [p.reshape(2, HDIM) for p in pieces(output_dot)]
        last = jnp.pad(jnp.stack(pieces(loss_part)), (0, HDIM - 3)).reshape(1, HDIM)
        stats = jnp.concatenate(stats + [jnp.pad(last, ((0, 3), (0, 0)))], axis=0)
        all_grads = spread(jnp.concatenate((grad_head, stats), axis=0), CHIPS)
        loss_sum = jnp.sum(all_grads[:, PAIR + 12, :3].astype(F32))
        loss = (loss_sum + swap(loss_sum)) / (seq_total * features)
    with jax.named_scope("attention_grad"):
        kv_grad = pl.pallas_call(
            backward_kernel,
            out_shape=jax.ShapeDtypeStruct((PAIR, 2 * HDIM), BF16),
            in_specs=[SMEM, SMEM, VMEM, VMEM, VMEM],
            out_specs=VMEM,
            compiler_params=PARAMS,
        )(doc_ends, chip_id, own_kv, all_queries, all_grads)
        kv_grad = to_rows(kv_grad, core)
    with jax.named_scope("d_context"):
        terms = pl.pallas_call(
            context_kernel,
            grid=(parts,),
            out_shape=jax.ShapeDtypeStruct((parts, rows, share), BF16),
            in_specs=[
                pl.BlockSpec((rows, 4 * HDIM), lambda t: (0, 0)),
                pl.BlockSpec((share, 2 * HDIM), lambda t: (t, 0)),
                pl.BlockSpec((share, 2 * HDIM), lambda t: (t, 0)),
            ],
            out_specs=pl.BlockSpec((1, rows, share), lambda t: (t, 0, 0)),
            compiler_params=PARAMS,
        )(kv_grad, w_key, w_value)
        arrived = lax.all_to_all(terms, "tp", 0, 0, tiled=True)
        d_context = jnp.sum(arrived.astype(F32), axis=0).astype(BF16)
    return d_context, loss


def solution(mesh):
    cores = 2
    count, parts = mesh.devices.shape
    side = math.isqrt(count // cores)
    split = Mesh(mesh.devices.reshape(side, side, cores, parts), ("y", "x", "core", "tp"))
    by_rows = P(ROWS, None)
    by_columns = P(None, "tp")
    return jax.shard_map(
        local,
        mesh=split,
        in_specs=(
            by_rows,
            by_rows,
            P(ROWS),
            P(),
            by_rows,
            P("tp"),
            by_columns,
            by_columns,
            by_columns,
            by_columns,
            P("tp", None),
            P("tp", None),
        ),
        out_specs=(P(ROWS, "tp"), P()),
        check_vma=False,
    )
```

time: 561 us -> 257 us (0.46)
  waiting for transfers between devices: 373 us -> 105 us
  blocking collectives: 89.8 us -> 48.8 us
  starting transfers between devices: 11.2 us -> 41.9 us
  matrix products: 37.7 us -> 13.3 us
  Pallas kernels: 0 us -> 6.7 us
    all_gather x3 -> x1, waiting for transfers between devices: 139 us -> 23 us  [local(): all_queries = lax.all_gather(query_head, CHIPS, axis=0, tiled=False)]
    unnamed x9 -> x2, waiting for transfers between devices: 91.6 us -> 0.71 us
    psum x3 -> x0, blocking collectives: 89.8 us -> none  [the longest x1 65 us: local(): lax.psum(jnp.sum(weighted_missed * missed), 'ctx')]
    psum x1 -> x0, waiting for transfers between devices: 62.1 us -> none  [local(): lax.psum(jnp.dot(unit.astype(jnp.bfloat16), w_post, preferred_element_typ...]
    all_to_all x0 -> x5, waiting for transfers between devices: none -> 53 us  [the longest x1 26 us: local(): arrived = lax.all_to_all(terms, 'tp', 0, 0, tiled=True)]
    reduce_scatter x2 -> x0, waiting for transfers between devices: 50.9 us -> none  [the longest x1 50.8 us: local(): lax.psum_scatter(head_terms.astype(jnp.bfloat16), 'tp', scatter_dimension...]
    all_to_all x0 -> x2, blocking collectives: none -> 48.8 us  [the longest x1 36.1 us: local(): arrived = lax.all_to_all(head_terms, 'tp', 0, 0, tiled=True)]
    dot_general x15 -> x8, matrix products: 37.7 us -> 13.3 us  [the longest x6 10.5 us: dot(): lax.dot_general(a, b, (contract, ((), ())), preferred_element_type=F32)]
  transfers between devices with their start and end apart: 9 -> 14, of which waited for: 8 -> 12; matrix products, arithmetic and copies ran while one was open for 3% -> 6% of each run, Pallas kernels for 0% -> 0%
where the time goes in v1:
time: 257 us; the launch traced here: 255 us
  waiting for transfers between devices  105 us (41%)
  blocking collectives  48.8 us (19%)
  starting transfers between devices  41.9 us (16%)
  between operations  21.8 us (8%)
  matrix products  13.3 us (5%)
  other arithmetic  8.43 us (3%)
  local copies, waits for them, and re-layouts  8.39 us (3%)
  Pallas kernels  6.7 us (3%)
    all_to_all x1, blocking collectives, local(): arrived = lax.all_to_all(head_terms, 'tp', 0, 0, tiled=True)  36.1 us
    all_to_all x1, waiting for transfers between devices, local(): arrived = lax.all_to_all(terms, 'tp', 0, 0, tiled=True)  26 us
    all_gather x1, waiting for transfers between devices, local(): input_full = lax.all_gather(input_part, 'tp', axis=1, tiled=True)  23.2 us
    all_gather x1, waiting for transfers between devices, local(): all_queries = lax.all_gather(query_head, CHIPS, axis=0, tiled=False)  23 us
    all_to_all x3, waiting for transfers between devices, spread(): return lax.all_to_all(stacked, axis, 0, 0, tiled=True)  20.4 us
    all_to_all x3, starting transfers between devices, spread(): return lax.all_to_all(stacked, axis, 0, 0, tiled=True)  15.6 us
    ppermute x6, starting transfers between devices, swap(): return lax.ppermute(block, 'core', [(0, 1), (1, 0)])  15 us
    all_to_all x1, blocking collectives, spread(): return lax.all_to_all(stacked, axis, 0, 0, tiled=True)  12.6 us
  transfers between devices with their start and end apart: 14, of which 12 were waited for; matrix products, arithmetic and copies ran while one was open for 6% of the time, Pallas kernels for 0%

profile of v1, /device:TPU:1, one launch (start us, length us, event | category | flops | bytes accessed | tf_op | source)
XLA Modules:
  0.0 254.7 jit_solution(15992424798152756390)
XLA Ops:
  7.2 1.0 reduce-window.8
  8.2 0.1 compare_reduce_fusion
  8.3 0.7 add_select_fusion
  9.0 2.3 fusion.15
  11.4 2.4 convolution_convert_fusion.2
  13.7 2.1 convolution_convert_fusion.3
  15.9 3.3 %collective-permute-start = (bf16[128,256]{1,0:T(8,128)(2,1)S(1)}, bf16[128,256]{1,0:T(8,128)(2,1)S(1)}, u32[]{:S(2)}, u32[]{:S(2)}) collective-permute-start(bf16[128,256]{1,0:T(8,128)(2,1)S(1)} %broadcast_select_fusion.6), channel_id=1, source_target_pairs={{0,8},{8,0},{1,9},{9,1},{2,10},{10,2},{3,11},{11,3},{4,12},{12,4},... | collective-permute-start | bytes 196616 | tf_op jit(solution)/shard_map/keys_values/ppermute | solution.py:35
  19.2 0.9 collective-permute-done
  20.2 1.5 broadcast_in_dim.13
  21.7 5.1 %all-to-all-start = ((bf16[16,256,256]{2,1,0:T(8,128)(2,1)}), bf16[16,256,256]{2,1,0:T(8,128)(2,1)}, u32[]{:S(2)}, u32[]{:S(2)}) async-start(bf16[16,256,256]{2,1,0:T(8,128)(2,1)} %broadcast_in_dim.13), calls=%async_computation | async-start | bytes 4194304 | tf_op jit(solution)/shard_map/keys_values/all_to_all | solution.py:31
  26.7 23.2 %all-gather.4.cloned.1.call-done = bf16[128,4096]{1,0:T(8,128)(2,1)} async-done(((bf16[128,512]{1,0:T(8,128)(2,1)}), bf16[128,4096]{1,0:T(8,128)(2,1)}) %all-gather.4.cloned.1.call-update) | async-done | bytes 1048592 | tf_op jit(solution)/shard_map/inputs/all_gather | solution.py:194
  49.9 1.5 fusion
  51.4 1.7 convolution_convert_fusion.1
  53.2 4.7 %collective-permute-start.1 = (bf16[128,128]{1,0:T(8,128)(2,1)S(1)}, bf16[128,128]{1,0:T(8,128)(2,1)S(1)}, u32[]{:S(2)}, u32[]{:S(2)}) collective-permute-start(bf16[128,128]{1,0:T(8,128)(2,1)S(1)} %broadcast_select_fusion.18), channel_id=1, source_target_pairs={{0,8},{8,0},{1,9},{9,1},{2,10},{10,2},{3,11},{11,3},{4,12},{12,4},... | collective-permute-start | bytes 98312 | tf_op jit(solution)/shard_map/queries/ppermute | solution.py:35
  57.9 0.9 collective-permute-done.1
  58.8 0.1 all-to-all-done.kv_ref
  58.9 2.7 %attention.1 = (bf16[256,128]{1,0:T(8,128)(2,1)S(1)}, f32[1,256]{1,0:T(1,128)S(1)}) custom-call(s32[4]{0:T(128)S(1)} %bitcast.84, s32[1]{0:T(128)} %bitcast.2.chip_ref, bf16[256,128]{1,0:T(8,128)(2,1)S(1)} %pad_maximum_fusion.4.q_ref, bf16[16,256,256]{2,1,0:T(8,128)(2,1)} %all-to-all-done.kv_ref), custom_call_target="tpu_custom_call" | custom-call | tf_op jit(solution)/shard_map/attention/pallas_call | solution.py:220
  61.6 1.5 collective-permute-start.2
  63.2 0.9 collective-permute-done.2
  64.1 0.4 fusion.11
  64.5 36.1 %all_to_all.35 = bf16[8,128,512]{2,1,0:T(8,128)(2,1)S(1)} all-to-all(bf16[8,128,512]{2,1,0:T(8,128)(2,1)S(1)} %fusion.11), channel_id=1, replica_groups=mesh['y'=4,'x'=4,'core'=2,'tp'=8] {'tp'}, dimensions={0} | all-to-all | bytes 2097152 | tf_op jit(solution)/shard_map/mixed/all_to_all | solution.py:235
  100.7 0.2 convert_reduce_fusion
  100.9 0.1 multiply_reduce_fusion
  101.0 0.3 convolution_convert_fusion
  101.3 0.1 copy.36
  101.5 0.7 fusion.26
  102.2 3.4 %all-to-all-start.2 = ((bf16[8,16,1152]{2,1,0:T(8,128)(2,1)}), bf16[8,16,1152]{2,1,0:T(8,128)(2,1)S(1)}, u32[]{:S(2)}, u32[]{:S(2)}) async-start(bf16[8,16,1152]{2,1,0:T(8,128)(2,1)} %bitcast.7), calls=%async_computation.2 | async-start | bytes 589824 | tf_op jit(solution)/shard_map/prediction/all_to_all | solution.py:243
  105.7 3.6 %collective-permute-start.3 = (bf16[1,1024]{1,0:T(2,128)(2,1)S(1)}, bf16[1,1024]{1,0:T(2,128)(2,1)S(1)}, u32[]{:S(2)}, u32[]{:S(2)}) collective-permute-start(bf16[1,1024]{1,0:T(2,128)(2,1)S(1)} %slice.77), channel_id=1, source_target_pairs={{8,0},{16,8},{24,16},{32,24},{40,32},{48,40},{56,48},{64,56},{72,6... | collective-permute-start | bytes 6152 | tf_op jit(solution)/shard_map/targets/ppermute | solution.py:206
  109.2 0.1 slice.76
  109.3 0.1 dynamic_slice.6
  109.4 6.7 %all-to-all-done.2 = bf16[8,16,1152]{2,1,0:T(8,128)(2,1)S(1)} async-done(((bf16[8,16,1152]{2,1,0:T(8,128)(2,1)}), bf16[8,16,1152]{2,1,0:T(8,128)(2,1)S(1)}, u32[]{:S(2)}, u32[]{:S(2)}) %all-to-all-start.2) | async-done | bytes 294944 | tf_op jit(solution)/shard_map/prediction/all_to_all | solution.py:243
  116.2 0.1 slice_reduce_fusion
  116.3 0.2 fusion.30
  116.6 0.1 copy.41
  116.7 12.6 %all_to_all.36 = bf16[8,16,1152]{2,1,0:T(8,128)(2,1)S(1)} all-to-all(bf16[8,16,1152]{2,1,0:T(8,128)(2,1)S(1)} %broadcast_in_dim.14), channel_id=1, replica_groups=mesh['y'=4,'x'=4,'core'=2,'tp'=8] {'tp'}, dimensions={0} | all-to-all | bytes 589824 | tf_op jit(solution)/shard_map/loss/all_to_all | solution.py:31
  129.4 0.1 copy.40
  129.5 0.6 slice_reduce_fusion.1
  130.1 1.7 fusion.16
  131.8 1.1 broadcast_in_dim.15
  132.9 3.6 %all-to-all-start.4 = ((bf16[8,128,512]{2,1,0:T(8,128)(2,1)}), bf16[8,128,512]{2,1,0:T(8,128)(2,1)S(1)}, u32[]{:S(2)}, u32[]{:S(2)}) async-start(bf16[8,128,512]{2,1,0:T(8,128)(2,1)} %broadcast_in_dim.15), calls=%async_computation.4 | async-start | bytes 2097152 | tf_op jit(solution)/shard_map/mixed_grad/all_to_all | solution.py:31
  136.5 0.7 all-gather.6.cloned.1.call-update
  142.2 20.2 %all-to-all-done.4 = bf16[8,128,512]{2,1,0:T(8,128)(2,1)S(1)} async-done(((bf16[8,128,512]{2,1,0:T(8,128)(2,1)}), bf16[8,128,512]{2,1,0:T(8,128)(2,1)S(1)}, u32[]{:S(2)}, u32[]{:S(2)}) %all-to-all-start.4) | async-done | bytes 1048608 | tf_op jit(solution)/shard_map/mixed_grad/all_to_all | solution.py:31
  162.4 2.4 fusion.20
  164.8 3.8 %collective-permute-start.4 = (bf16[128,128]{1,0:T(8,128)(2,1)S(1)}, bf16[128,128]{1,0:T(8,128)(2,1)S(1)}, u32[]{:S(2)}, u32[]{:S(2)}) collective-permute-start(bf16[128,128]{1,0:T(8,128)(2,1)S(1)} %broadcast_select_fusion.10), channel_id=1, source_target_pairs={{0,8},{8,0},{1,9},{9,1},{2,10},{10,2},{3,11},{11,3},{4,12},{12,4},... | collective-permute-start | bytes 98312 | tf_op jit(solution)/shard_map/sent_grads/ppermute | solution.py:35
  168.6 0.1 fusion.45
  168.7 0.8 collective-permute-done.4
  169.5 0.1 multiply_reduce_fusion.1
  169.6 0.1 concatenate.43
  169.7 1.1 broadcast_in_dim.16
  170.9 6.9 %all-to-all-start.5 = ((bf16[16,272,128]{2,1,0:T(8,128)(2,1)}), bf16[16,272,128]{2,1,0:T(8,128)(2,1)S(1)}, u32[]{:S(2)}, u32[]{:S(2)}) async-start(bf16[16,272,128]{2,1,0:T(8,128)(2,1)} %broadcast_in_dim.16), calls=%async_computation.5 | async-start | bytes 2228224 | tf_op jit(solution)/shard_map/sent_grads/all_to_all | solution.py:31
  177.8 23.0 %all-gather.6.cloned.1.call-done = bf16[4096,128]{1,0:T(8,128)(2,1)} async-done(((bf16[256,128]{1,0:T(8,128)(2,1)}), bf16[4096,128]{1,0:T(8,128)(2,1)}) %all-gather.6.cloned.1.call-update) | async-done | bytes 1048592 | tf_op jit(solution)/shard_map/queries/all_gather | solution.py:218
  200.8 1.4 copy-done.4
  202.2 1.5 attention_grad.1
  203.8 1.2 collective-permute-start.5
  205.0 0.9 collective-permute-done.5
  206.0 1.6 copy-done.2
  207.6 2.5 d_context.1
  210.1 1.0 copy-done.3
  211.1 4.2 %all-to-all-start.6 = ((bf16[8,128,512]{2,1,0:T(8,128)(2,1)}), bf16[8,128,512]{2,1,0:T(8,128)(2,1)}, u32[]{:S(2)}, u32[]{:S(2)}) async-start(bf16[8,128,512]{2,1,0:T(8,128)(2,1)} %copy-done.3), calls=%async_computation.6 | async-start | bytes 2097152 | tf_op jit(solution)/shard_map/d_context/all_to_all | solution.py:300
  215.3 0.6 fusion.35
  216.0 0.4 collective-permute-start.6
  216.3 1.1 collective-permute-done.6
  218.7 26.0 %all-to-all-done.6 = bf16[8,128,512]{2,1,0:T(8,128)(2,1)} async-done(((bf16[8,128,512]{2,1,0:T(8,128)(2,1)}), bf16[8,128,512]{2,1,0:T(8,128)(2,1)}, u32[]{:S(2)}, u32[]{:S(2)}) %all-to-all-start.6) | async-done | bytes 1048608 | tf_op jit(solution)/shard_map/d_context/all_to_all | solution.py:300
  244.6 2.1 reduce_sum.144
  (56 shorter events, 0.6 us)
Async XLA Ops:
  7.2 44.3 %copy-start = (bf16[4096,256]{1,0:T(8,128)(2,1)S(1)}, bf16[4096,256]{1,0:T(8,128)(2,1)}, u32[]{:S(2)}) copy-start(bf16[4096,256]{1,0:T(8,128)(2,1)} %param.19) | copy-start | bytes 6291460
  7.2 42.7 %all-gather.4.cloned.1.call-start = ((), (), s32[]{:S(2)}) async-start(), calls=%async_computation.7 | async-start | bytes 1179648 | tf_op jit(solution)/shard_map/inputs/all_gather | solution.py:194
  9.0 4.7 %copy-start.6 = (bf16[128,4096]{1,0:T(8,128)(2,1)S(1)}, bf16[128,4096]{1,0:T(8,128)(2,1)}, u32[]{:S(2)}) copy-start(bf16[128,4096]{1,0:T(8,128)(2,1)} %param.16) | copy-start | bytes 3145732
  15.9 4.2 %collective-permute-start = (bf16[128,256]{1,0:T(8,128)(2,1)S(1)}, bf16[128,256]{1,0:T(8,128)(2,1)S(1)}, u32[]{:S(2)}, u32[]{:S(2)}) collective-permute-start(bf16[128,256]{1,0:T(8,128)(2,1)S(1)} %broadcast_select_fusion.6), channel_id=1, source_target_pairs={{0,8},{8,0},{1,9},{9,1},{2,10},{10,2},{3,11},{11,3},{4,12},{12,4},... | collective-permute-start | bytes 196616 | tf_op jit(solution)/shard_map/keys_values/ppermute | solution.py:35
  21.7 37.3 %all-to-all-start = ((bf16[16,256,256]{2,1,0:T(8,128)(2,1)}), bf16[16,256,256]{2,1,0:T(8,128)(2,1)}, u32[]{:S(2)}, u32[]{:S(2)}) async-start(bf16[16,256,256]{2,1,0:T(8,128)(2,1)} %broadcast_in_dim.13), calls=%async_computation | async-start | bytes 4194304 | tf_op jit(solution)/shard_map/keys_values/all_to_all | solution.py:31
  53.2 5.6 %collective-permute-start.1 = (bf16[128,128]{1,0:T(8,128)(2,1)S(1)}, bf16[128,128]{1,0:T(8,128)(2,1)S(1)}, u32[]{:S(2)}, u32[]{:S(2)}) collective-permute-start(bf16[128,128]{1,0:T(8,128)(2,1)S(1)} %broadcast_select_fusion.18), channel_id=1, source_target_pairs={{0,8},{8,0},{1,9},{9,1},{2,10},{10,2},{3,11},{11,3},{4,12},{12,4},... | collective-permute-start | bytes 98312 | tf_op jit(solution)/shard_map/queries/ppermute | solution.py:35
  58.8 5.7 %copy-start.5 = (bf16[256,128]{1,0:T(8,128)(2,1)}, bf16[256,128]{1,0:T(8,128)(2,1)S(1)}, u32[]{:S(2)}) copy-start(bf16[256,128]{1,0:T(8,128)(2,1)S(1)} %pad_maximum_fusion.4.q_ref) | copy-start | bytes 196612
  58.9 5.1 %copy-start.9 = (bf16[256,4096]{1,0:T(8,128)(2,1)S(1)}, bf16[256,4096]{1,0:T(8,128)(2,1)}, u32[]{:S(2)}) copy-start(bf16[256,4096]{1,0:T(8,128)(2,1)} %param.22) | copy-start | bytes 6291460
  61.6 2.4 collective-permute-start.2
  64.5 36.3 %copy-start.8 = (bf16[128,512]{1,0:T(8,128)(2,1)S(1)}, bf16[128,512]{1,0:T(8,128)(2,1)}, u32[]{:S(2)}) copy-start(bf16[128,512]{1,0:T(8,128)(2,1)} %fusion.15) | copy-start | bytes 393220
  64.5 36.4 %copy-start.7 = (bf16[512,1024]{1,0:T(8,128)(2,1)S(1)}, bf16[512,1024]{1,0:T(8,128)(2,1)}, u32[]{:S(2)}) copy-start(bf16[512,1024]{1,0:T(8,128)(2,1)} %param.23) | copy-start | bytes 3145732
  100.7 4.9 %copy-start.10 = (bf16[128,1024]{1,0:T(8,128)(2,1)S(1)}, bf16[128,1024]{1,0:T(8,128)(2,1)}, u32[]{:S(2)}) copy-start(bf16[128,1024]{1,0:T(8,128)(2,1)} %param.12) | copy-start | bytes 786436
  102.2 13.9 %all-to-all-start.2 = ((bf16[8,16,1152]{2,1,0:T(8,128)(2,1)}), bf16[8,16,1152]{2,1,0:T(8,128)(2,1)S(1)}, u32[]{:S(2)}, u32[]{:S(2)}) async-start(bf16[8,16,1152]{2,1,0:T(8,128)(2,1)} %bitcast.7), calls=%async_computation.2 | async-start | bytes 589824 | tf_op jit(solution)/shard_map/prediction/all_to_all | solution.py:243
  105.7 10.6 %collective-permute-start.3 = (bf16[1,1024]{1,0:T(2,128)(2,1)S(1)}, bf16[1,1024]{1,0:T(2,128)(2,1)S(1)}, u32[]{:S(2)}, u32[]{:S(2)}) collective-permute-start(bf16[1,1024]{1,0:T(2,128)(2,1)S(1)} %slice.77), channel_id=1, source_target_pairs={{8,0},{16,8},{24,16},{32,24},{40,32},{48,40},{56,48},{64,56},{72,6... | collective-permute-start | bytes 6152 | tf_op jit(solution)/shard_map/targets/ppermute | solution.py:206
  132.9 29.5 %all-to-all-start.4 = ((bf16[8,128,512]{2,1,0:T(8,128)(2,1)}), bf16[8,128,512]{2,1,0:T(8,128)(2,1)S(1)}, u32[]{:S(2)}, u32[]{:S(2)}) async-start(bf16[8,128,512]{2,1,0:T(8,128)(2,1)} %broadcast_in_dim.15), calls=%async_computation.4 | async-start | bytes 2097152 | tf_op jit(solution)/shard_map/mixed_grad/all_to_all | solution.py:31
  136.5 64.4 %all-gather.6.cloned.1.call-start = ((), (), s32[]{:S(2)}) async-start(), calls=%async_computation.8 | async-start | bytes 1114112 | tf_op jit(solution)/shard_map/queries/all_gather | solution.py:218
  164.8 4.7 %collective-permute-start.4 = (bf16[128,128]{1,0:T(8,128)(2,1)S(1)}, bf16[128,128]{1,0:T(8,128)(2,1)S(1)}, u32[]{:S(2)}, u32[]{:S(2)}) collective-permute-start(bf16[128,128]{1,0:T(8,128)(2,1)S(1)} %broadcast_select_fusion.10), channel_id=1, source_target_pairs={{0,8},{8,0},{1,9},{9,1},{2,10},{10,2},{3,11},{11,3},{4,12},{12,4},... | collective-permute-start | bytes 98312 | tf_op jit(solution)/shard_map/sent_grads/ppermute | solution.py:35
  170.9 30.0 %all-to-all-start.5 = ((bf16[16,272,128]{2,1,0:T(8,128)(2,1)}), bf16[16,272,128]{2,1,0:T(8,128)(2,1)S(1)}, u32[]{:S(2)}, u32[]{:S(2)}) async-start(bf16[16,272,128]{2,1,0:T(8,128)(2,1)} %broadcast_in_dim.16), calls=%async_computation.5 | async-start | bytes 2228224 | tf_op jit(solution)/shard_map/sent_grads/all_to_all | solution.py:31
  200.8 5.1 %copy-start.1 = (bf16[4096,256]{1,0:T(8,128)(2,1)S(1)}, bf16[4096,256]{1,0:T(8,128)(2,1)}, u32[]{:S(2)}) copy-start(bf16[4096,256]{1,0:T(8,128)(2,1)} %key_ref.1) | copy-start | bytes 6291460
  200.8 1.4 copy-start.4
  203.8 2.1 collective-permute-start.5
  206.0 1.6 copy-start.2
  210.1 1.0 copy-start.3
  211.1 33.5 %all-to-all-start.6 = ((bf16[8,128,512]{2,1,0:T(8,128)(2,1)}), bf16[8,128,512]{2,1,0:T(8,128)(2,1)}, u32[]{:S(2)}, u32[]{:S(2)}) async-start(bf16[8,128,512]{2,1,0:T(8,128)(2,1)} %copy-done.3), calls=%async_computation.6 | async-start | bytes 2097152 | tf_op jit(solution)/shard_map/d_context/all_to_all | solution.py:300
  216.0 1.4 collective-permute-start.6
Sparse Core Ops, SparseCore 0:
  11.5 38.3 all-gather.3
  139.7 61.0 all-gather.5

commit v2 on v1

--- a/solution.py
+++ b/solution.py
@@ -1,3 +1,4 @@
+import functools
 import math
 
 import jax
@@ -17,12 +18,20 @@
 SCALE = 1.0 / math.sqrt(HDIM)
 PAIR = 256
 GROUP = 4
+FOLD_POST = 32
+FOLD_OUT = 8
 F32 = jnp.float32
 BF16 = jnp.bfloat16
 
 
 def dot(a, b, contract=((1,), (0,))):
     return lax.dot_general(a, b, (contract, ((), ())), preferred_element_type=F32)
+
+
+def shifted(block, axis):
+    count = lax.axis_size(axis)
+    routes = [[(i, (i + s) % count) for i in range(count)] for s in range(1, count)]
+    return [block] + [lax.ppermute(block, axis, route) for route in routes]
 
 
 def spread(block, axis):
@@ -59,19 +68,47 @@
     return high.astype(BF16), middle.astype(BF16), low.astype(BF16)
 
 
-def start_of(ends_ref, positions):
+def ends_of(lengths_ref):
+    ends = [lengths_ref[0]]
+    for d in range(1, lengths_ref.shape[0]):
+        ends.append(ends[-1] + lengths_ref[d])
+    return ends
+
+
+def start_of(ends, positions):
     start = jnp.zeros_like(positions)
-    for d in range(ends_ref.shape[0]):
-        start = jnp.where(positions >= ends_ref[d], ends_ref[d], start)
+    for end in ends:
+        start = jnp.where(positions >= end, end, start)
     return start
 
 
-def forward_kernel(ends_ref, chip_ref, q_ref, kv_ref, out_ref, total_ref):
-    base = chip_ref[0] * PAIR
+def query_kernel(place_ref, *refs):
+    *blocks, w_query_ref, w_out_ref, query_ref, cross_ref = refs
+    parts = len(blocks)
+    rows, share = blocks[0].shape
+    query = jnp.zeros(query_ref.shape, F32)
+    cross = jnp.zeros(cross_ref.shape, F32)
+    squares = jnp.zeros((rows, 1), F32)
+    for distance, block_ref in enumerate(blocks):
+        owner = lax.rem(place_ref[0] + (parts - distance), parts)
+        at = pl.ds(pl.multiple_of(owner * share, share), share)
+        block = block_ref[...]
+        wide = block.astype(F32)
+        squares = squares + jnp.sum(wide * wide, axis=1, keepdims=True)
+        query = query + dot(block, w_query_ref[at, :])
+        cross = cross + dot(block, w_out_ref[:, at], ((1,), (1,)))
+    scale = lax.rsqrt(squares / (share * parts) + EPSILON)
+    query_ref[...] = (query * scale).astype(BF16)
+    cross_ref[...] = cross
+
+
+def forward_kernel(lengths_ref, place_ref, q_ref, kv_ref, out_ref, total_ref):
+    ends = ends_of(lengths_ref)
+    base = place_ref[1] * PAIR
     width = GROUP * PAIR
     query_pos = base + lax.broadcasted_iota(jnp.int32, (1, PAIR), 1)
-    query_start = start_of(ends_ref, query_pos)
-    floor = start_of(ends_ref, base)
+    query_start = start_of(ends, query_pos)
+    floor = start_of(ends, base)
     q = q_ref[...]
 
     def body(step, carry):
@@ -101,20 +138,116 @@
     total_ref[...] = row_max + jnp.log(row_total)
 
 
-def backward_kernel(ends_ref, chip_ref, kv_ref, q_ref, sent_ref, out_ref):
-    base = chip_ref[0] * PAIR
+def both_cores(place_ref, own_ref, other_ref, count):
+    own = own_ref[:, :count, :].reshape(-1, own_ref.shape[2])
+    other = other_ref[:, :count, :].reshape(-1, other_ref.shape[2])
+    first = place_ref[2] == 0
+    return jnp.where(first, own, other), jnp.where(first, other, own)
+
+
+def raw_kernel(place_ref, attended_ref, own_ref, other_ref, input_ref, out_ref):
+    parts, own, _ = out_ref.shape
+    attended = attended_ref[...]
+    low, high = both_cores(place_ref, own_ref, other_ref, FOLD_POST)
+    half = low.shape[0]
+    raw_low = (dot(attended, low, ((1,), (1,))) + input_ref[:, :half]).astype(BF16)
+    raw_high = (dot(attended, high, ((1,), (1,))) + input_ref[:, half:]).astype(BF16)
+    packed = jnp.concatenate([attended[own * k : own * (k + 1)] for k in range(parts)], axis=1)
+    for k in range(parts):
+        out_ref[k, :, :half] = raw_low[own * k : own * (k + 1)]
+        out_ref[k, :, half : 2 * half] = raw_high[own * k : own * (k + 1)]
+        out_ref[k, :, 2 * half :] = packed
+
+
+def norm_kernel(place_ref, arrived_ref, gram_ref, attended_ref, cross_ref, input_ref, back_ref, out_ref):
+    parts, own, _ = arrived_ref.shape
+    features = out_ref.shape[2] - HDIM
+    wide = attended_ref.shape[1]
+    total = arrived_ref[0, :, :features].astype(F32)
+    for k in range(1, parts):
+        total = total + arrived_ref[k, :, :features].astype(F32)
+    cross = cross_ref[...]
+    back = jnp.zeros_like(cross)
+    for k in range(parts):
+        theirs = jnp.concatenate(
+            [
+                arrived_ref[k, :, features + wide * j : features + wide * (j + 1)]
+                for j in range(parts)
+            ],
+            axis=0,
+        )
+        distance = lax.rem(place_ref[0] + (parts - k), parts)
+        back = back + dot(theirs, gram_ref[distance])
+    back_ref[...] = cross + back
+    attended = attended_ref[...].astype(F32)
+    features_in = input_ref[...].astype(F32)
+    squares = jnp.sum((attended * (2.0 * cross + back)).T, axis=0, keepdims=True) + jnp.sum(
+        (features_in * features_in).T, axis=0, keepdims=True
+    )
+    high = squares.astype(BF16)
+    rest = squares - high.astype(F32)
+    middle = rest.astype(BF16)
+    low = (rest - middle.astype(F32)).astype(BF16)
+    side = jnp.concatenate((high, middle, low, jnp.zeros((own - 3, HDIM), BF16)), axis=0)
+    summed = total.astype(BF16)
+    for k in range(parts):
+        out_ref[k, :, :features] = summed
+        out_ref[k, :, features:] = side
+
+
+def loss_kernel(
+    width,
+    place_ref,
+    arrived_ref,
+    target_ref,
+    weight_ref,
+    own_ref,
+    other_ref,
+    back_ref,
+    hold_ref,
+    grad_ref,
+    loss_ref,
+):
+    parts, own, _ = arrived_ref.shape
+    rows, features = target_ref.shape
+    side = arrived_ref[:, :, features:].astype(F32)
+    squares = jnp.sum(jnp.sum(side, axis=0), axis=0, keepdims=True)
+    squares = jnp.broadcast_to(squares, (rows, rows)).T[:, :1]
+    inverse = lax.rsqrt(jnp.maximum(squares / width, 0.0) + EPSILON)
+    prediction = arrived_ref[:, :, :features].reshape(rows, features).astype(F32) * inverse
+    missed = prediction - target_ref[...].astype(F32)
+    weighted_missed = weight_ref[...] * missed
+    loss = jnp.sum(weighted_missed * missed, axis=1, keepdims=True)
+    loss_ref[...] = jnp.sum(loss, axis=0, keepdims=True)
+    pred_grad = weighted_missed.astype(BF16)
+    along = jnp.sum(pred_grad.astype(F32) * prediction, axis=1, keepdims=True) / width
+    low, high = both_cores(place_ref, own_ref, other_ref, FOLD_POST)
+    half = low.shape[0]
+    direct = dot(pred_grad[:, :half], low) + dot(pred_grad[:, half:], high)
+    grad_ref[...] = (inverse * (direct - along * inverse * back_ref[...])).astype(BF16)
+
+
+def backward_kernel(lengths_ref, place_ref, kv_ref, q_ref, sent_ref, out_ref):
+    ends = ends_of(lengths_ref)
+    chip = place_ref[1]
+    base = chip * PAIR
     width = GROUP * PAIR
     keys, values = kv_ref[:, :HDIM], kv_ref[:, HDIM:]
     last = base + PAIR - 1
-    reach = q_ref.shape[0] * PAIR
-    for d in reversed(range(ends_ref.shape[0])):
-        reach = jnp.where(last < ends_ref[d], ends_ref[d], reach)
+    reach = jnp.int32(sent_ref.shape[0] * PAIR)
+    for end in reversed(ends):
+        reach = jnp.where(last < end, end, reach)
     key_pos = base + lax.broadcasted_iota(jnp.int32, (PAIR, width), 0)
+    here_y, here_x = chip // GROUP, lax.rem(chip, GROUP)
+    sides = sent_ref.shape[0] // GROUP
 
     def body(step, carry):
         key_grad, value_grad = carry
         chips = pl.ds(step * GROUP, GROUP)
-        q = q_ref[chips].reshape(width, HDIM)
+        away_y = lax.rem(here_y + (sides - step), sides)
+        q = jnp.concatenate(
+            [q_ref[away_y, lax.rem(here_x + (GROUP - k), GROUP)] for k in range(GROUP)], axis=0
+        )
         grad = sent_ref[chips, :PAIR, :].reshape(width, HDIM)
         stats = sent_ref[chips, PAIR:, :].astype(F32)
 
@@ -129,7 +262,7 @@
             return jnp.concatenate(parts, axis=1)
 
         query_pos = step * width + lax.broadcasted_iota(jnp.int32, (1, width), 1)
-        query_start = start_of(ends_ref, query_pos)
+        query_start = start_of(ends, query_pos)
         allowed = (key_pos >= query_start) & (key_pos <= query_pos)
         scores = dot(keys, q, ((1,), (1,))) * SCALE
         probs = jnp.where(allowed, jnp.exp(scores - row(0)), 0.0)
@@ -180,18 +313,24 @@
     part = lax.axis_index("tp")
     seq_total = rows * lax.axis_size(ROWS)
     share = w_post.shape[0]
-    width = share * parts
     own = rows // parts
     chip = lax.axis_index(CHIPS).astype(jnp.int32)
-    chip_id = chip.reshape(1)
-    doc_ends = jnp.cumsum(doc_lengths).astype(jnp.int32)
-    positions = lax.axis_index(ROWS) * rows + jnp.arange(rows, dtype=jnp.int32)
-    angle = 0.5 * math.pi / TSTEPS * step_ids.astype(F32)
-    keep_level, noise_level = jnp.cos(angle), jnp.sin(angle)
-
+    place = jnp.stack((part, chip, core)).astype(jnp.int32)
+    width = share * parts
+
+    with jax.named_scope("fold_send"):
+        slot = core * chips + chip
+        post_rows = lax.dynamic_slice_in_dim(w_post, slot * FOLD_POST, FOLD_POST, 1).T
+        out_rows = lax.dynamic_slice_in_dim(w_out, slot * FOLD_OUT, FOLD_OUT, 0)
+        fold_blocks = shifted(
+            jnp.concatenate((post_rows, out_rows.reshape(-1, share)), axis=0), "tp"
+        )
     with jax.named_scope("inputs"):
+        angle = 0.5 * math.pi / TSTEPS * step_ids.astype(F32)
+        keep_level, noise_level = jnp.cos(angle), jnp.sin(angle)
         input_part = (dot(noised, w_pre) + noise_level[:, None] * time_vec[None, :]).astype(BF16)
-        input_full = lax.all_gather(input_part, "tp", axis=1, tiled=True)
+        input_blocks = shifted(input_part, "tp")
+        input_post = dot(input_part, w_post)
     with jax.named_scope("keys_values"):
         key_rows = dot(context, w_key).astype(BF16)
         value_rows = dot(context, w_value).astype(BF16)
@@ -201,21 +340,45 @@
             core,
         )
         all_kv = spread(own_kv, CHIPS)
+    with jax.named_scope("fold"):
+        turned = [fold_blocks[-k % parts][:FOLD_POST] for k in range(parts)]
+        turned = lax.dynamic_slice_in_dim(jnp.stack(turned + turned), (parts - part) % parts, parts, 0)
+        post_full = turned.transpose(1, 0, 2).reshape(FOLD_POST, width)
+        out_full = [b[FOLD_POST:].reshape(FOLD_OUT, width) for b in fold_blocks]
+        stacked = jnp.concatenate([post_full] + out_full, axis=0)
+        folded = dot(stacked, w_out, ((1,), (1,))).astype(BF16)
+        own_fold = spread(folded, CHIPS)
+        other_fold = swap(own_fold)
+        gram = [f[:, FOLD_POST:].reshape(chips, parts, FOLD_OUT, -1) for f in (own_fold, other_fold)]
+        first = core == 0
+        gram = jnp.stack((jnp.where(first, gram[0], gram[1]), jnp.where(first, gram[1], gram[0])))
+        gram = gram.transpose(2, 0, 1, 3, 4).reshape(parts, 2 * chips * FOLD_OUT, -1)
     with jax.named_scope("targets"):
         count = lax.axis_size(ROWS)
         following = lax.ppermute(concepts[:1], ROWS, [(i + 1, i) for i in range(count - 1)])
         targets = jnp.concatenate((concepts[1:], following), axis=0)
-        targets = lax.dynamic_slice_in_dim(targets, part * own, own, 0).astype(F32)
-        valid = jnp.logical_not(jnp.any(doc_ends[None, :] == positions[:, None] + 1, axis=1))
-        weights = jnp.where(valid, 1.0 + keep_level * keep_level, 0.0)
-        weights = lax.dynamic_slice_in_dim(weights, part * own, own, 0)
+        positions = lax.axis_index(ROWS) * rows + jnp.arange(rows, dtype=jnp.int32)
+        document_end = jnp.zeros(rows, jnp.bool_)
+        end = jnp.int32(0)
+        for d in range(doc_lengths.shape[0]):
+            end = end + doc_lengths[d]
+            document_end = document_end | (end == positions + 1)
+        weights = jnp.where(document_end, 0.0, 1.0 + keep_level * keep_level)[:, None]
     with jax.named_scope("queries"):
-        input_wide = input_full.astype(F32)
-        scale = lax.rsqrt(jnp.mean(input_wide * input_wide, axis=1, keepdims=True) + EPSILON)
-        normed = (input_wide * scale).astype(BF16)
-        queries = dot(normed, w_query).astype(BF16)
+        head_width = w_query.shape[1]
+        queries, cross = pl.pallas_call(
+            query_kernel,
+            out_shape=(
+                jax.ShapeDtypeStruct((rows, head_width), BF16),
+                jax.ShapeDtypeStruct((rows, head_width), F32),
+            ),
+            in_specs=[SMEM] + [VMEM] * (parts + 2),
+            out_specs=(VMEM, VMEM),
+            compiler_params=PARAMS,
+        )(place, *input_blocks, w_query, w_out)
         query_head = to_head(queries[:, :HDIM], queries[:, HDIM:], core)
-        all_queries = lax.all_gather(query_head, CHIPS, axis=0, tiled=False)
+        along_x = jnp.stack(shifted(query_head, "x"))
+        all_queries = jnp.stack(shifted(along_x, "y"))
     with jax.named_scope("attention"):
         attended_head, log_total = pl.pallas_call(
             forward_kernel,
@@ -226,51 +389,46 @@
             in_specs=[SMEM, SMEM, VMEM, VMEM],
             out_specs=(VMEM, VMEM),
             compiler_params=PARAMS,
-        )(doc_ends, chip_id, query_head, all_kv)
+        )(doc_lengths, place, query_head, all_kv)
         attended = to_rows(attended_head, core)
-    with jax.named_scope("mixed"):
-        head_terms = jnp.einsum(
-            "rk,ktf->trf", attended, w_out.reshape(-1, parts, share), preferred_element_type=F32
-        ).astype(BF16)
-        arrived = lax.all_to_all(head_terms, "tp", 0, 0, tiled=True)
-        mixed = input_part.astype(F32) + jnp.sum(arrived.astype(F32), axis=0)
-    with jax.named_scope("prediction"):
-        squares = jnp.sum(mixed * mixed, axis=1)
-        raw = dot(mixed.astype(BF16), w_post).astype(BF16)
-        side = jnp.stack(pieces(squares), axis=1)
-        side = jnp.pad(side, ((0, 0), (0, HDIM - 3)))
-        sent = jnp.concatenate((raw, side), axis=1).reshape(parts, own, features + HDIM)
-        arrived = jnp.sum(lax.all_to_all(sent, "tp", 0, 0, tiled=True).astype(F32), axis=0)
-        squares = jnp.sum(arrived[:, features : features + 3], axis=1)
-        inverse = lax.rsqrt(squares / width + EPSILON)
-        prediction = arrived[:, :features] * inverse[:, None]
+    with jax.named_scope("raw"):
+        sent = pl.pallas_call(
+            raw_kernel,
+            out_shape=jax.ShapeDtypeStruct((parts, own, features + head_width * parts), BF16),
+            in_specs=[SMEM, VMEM, VMEM, VMEM, VMEM],
+            out_specs=VMEM,
+            compiler_params=PARAMS,
+        )(place, attended, own_fold, other_fold, input_post)
+        arrived = lax.all_to_all(sent, "tp", 0, 0, tiled=True)
+    with jax.named_scope("norm"):
+        back, sent = pl.pallas_call(
+            norm_kernel,
+            out_shape=(
+                jax.ShapeDtypeStruct((rows, head_width), F32),
+                jax.ShapeDtypeStruct((parts, own, features + HDIM), BF16),
+            ),
+            in_specs=[SMEM] + [VMEM] * 5,
+            out_specs=(VMEM, VMEM),
+            compiler_params=PARAMS,
+        )(place, arrived, gram, attended, cross, input_part)
+        arrived = lax.all_to_all(sent, "tp", 0, 0, tiled=True)
     with jax.named_scope("loss"):
-        missed = prediction - targets
-        weighted_missed = weights[:, None] * missed
-        row_loss = jnp.sum(weighted_missed * missed, axis=1)
-        pred_grad = weighted_missed.astype(BF16)
-        along = jnp.sum(pred_grad.astype(F32) * prediction, axis=1) / width
-        side = jnp.stack(pieces(inverse) + pieces(along) + pieces(row_loss), axis=1)
-        side = jnp.pad(side, ((0, 0), (0, HDIM - 9)))
-        arrived = spread(jnp.concatenate((pred_grad, side), axis=1), "tp")
-        arrived = arrived.reshape(rows, features + HDIM)
-        side = arrived[:, features : features + 9].astype(F32)
-        inverse, along, row_loss = (jnp.sum(side[:, i : i + 3], axis=1) for i in (0, 3, 6))
-        loss_part = jnp.sum(row_loss)
-    with jax.named_scope("mixed_grad"):
-        unit_grad = dot(arrived[:, :features], w_post, ((1,), (1,)))
-        unit = mixed * inverse[:, None]
-        mixed_grad = ((unit_grad - unit * along[:, None]) * inverse[:, None]).astype(BF16)
-        mixed_full = spread(mixed_grad, "tp")
-        attended_grad = jnp.einsum(
-            "trf,ktf->rk", mixed_full, w_out.reshape(-1, parts, share), preferred_element_type=F32
-        ).astype(BF16)
+        attended_grad, loss_part = pl.pallas_call(
+            functools.partial(loss_kernel, width),
+            out_shape=(
+                jax.ShapeDtypeStruct((rows, head_width), BF16),
+                jax.ShapeDtypeStruct((1, 1), F32),
+            ),
+            in_specs=[SMEM] + [VMEM] * 6 + [pl.BlockSpec(memory_space=pl.ANY)],
+            out_specs=(VMEM, VMEM),
+            compiler_params=PARAMS,
+        )(place, arrived, targets, weights, own_fold, other_fold, back, all_queries)
     with jax.named_scope("sent_grads"):
         grad_head = to_head(attended_grad[:, :HDIM], attended_grad[:, HDIM:], core)
         output_dot = jnp.sum(grad_head.astype(F32) * attended_head.astype(F32), axis=1)
         stats = [p.reshape(2, HDIM) for p in pieces(log_total)]
         stats += [p.reshape(2, HDIM) for p in pieces(output_dot)]
-        last = jnp.pad(jnp.stack(pieces(loss_part)), (0, HDIM - 3)).reshape(1, HDIM)
+        last = jnp.pad(jnp.stack(pieces(loss_part[0, 0])), (0, HDIM - 3)).reshape(1, HDIM)
         stats = jnp.concatenate(stats + [jnp.pad(last, ((0, 3), (0, 0)))], axis=0)
         all_grads = spread(jnp.concatenate((grad_head, stats), axis=0), CHIPS)
         loss_sum = jnp.sum(all_grads[:, PAIR + 12, :3].astype(F32))
@@ -282,7 +440,7 @@
             in_specs=[SMEM, SMEM, VMEM, VMEM, VMEM],
             out_specs=VMEM,
             compiler_params=PARAMS,
-        )(doc_ends, chip_id, own_kv, all_queries, all_grads)
+        )(doc_lengths, place, own_kv, all_queries, all_grads)
         kv_grad = to_rows(kv_grad, core)
     with jax.named_scope("d_context"):
         terms = pl.pallas_call(

time: 257 us -> 283 us (1.10)
  local copies, waits for them, and re-layouts: 8.39 us -> 52.1 us
  starting transfers between devices: 41.9 us -> 73.1 us
  blocking collectives: 48.8 us -> 21.5 us
  waiting for transfers between devices: 105 us -> 92.9 us
  between operations: 21.8 us -> 11.1 us
  Pallas kernels: 6.7 us -> 14.8 us
  matrix products: 13.3 us -> 5.33 us
    all_gather x2 -> x0, waiting for transfers between devices: 46.2 us -> none  [the longest x1 23.2 us: local(): input_full = lax.all_gather(input_part, 'tp', axis=1, tiled=True)]
    ppermute x0 -> x20, starting transfers between devices: none -> 36.9 us  [shifted(): return [block] + [lax.ppermute(block, axis, route) for route in routes]]
    all_to_all x1 -> x0, blocking collectives: 36.1 us -> none  [local(): arrived = lax.all_to_all(head_terms, 'tp', 0, 0, tiled=True)]
    ppermute x0 -> x20, waiting for transfers between devices: none -> 31.1 us  [shifted(): return [block] + [lax.ppermute(block, axis, route) for route in routes]]
    unnamed x24 -> x75, local copies, waits for them, and re-layouts: 4.19 us -> 30.4 us
    all_to_all x1 -> x2, waiting for transfers between devices: 6.73 us -> 19.7 us  [local(): arrived = lax.all_to_all(sent, 'tp', 0, 0, tiled=True)]
    all_to_all x3 -> x2, waiting for transfers between devices: 20.4 us -> 10.5 us  [spread(): return lax.all_to_all(stacked, axis, 0, 0, tiled=True)]
    all_to_all x1, blocking collectives: 12.6 us -> 21.5 us  [spread(): return lax.all_to_all(stacked, axis, 0, 0, tiled=True)]
  transfers between devices with their start and end apart: 14 -> 33, of which waited for: 12 -> 18; matrix products, arithmetic and copies ran while one was open for 6% -> 7% of each run, Pallas kernels for 0% -> 2%
where the time goes in v2:
time: 283 us; the launch traced here: 279 us
  waiting for transfers between devices  92.9 us (33%)
  starting transfers between devices  73.1 us (26%)
  local copies, waits for them, and re-layouts  52.1 us (18%)
  blocking collectives  21.5 us (8%)
  Pallas kernels  14.8 us (5%)
  between operations  11.1 us (4%)
  other arithmetic  8.55 us (3%)
  matrix products  5.33 us (2%)
    ppermute x20, starting transfers between devices, shifted(): return [block] + [lax.ppermute(block, axis, route) for route in routes]  36.9 us
    ppermute x20, waiting for transfers between devices, shifted(): return [block] + [lax.ppermute(block, axis, route) for route in routes]  31.1 us
    unnamed x75, local copies, waits for them, and re-layouts  30.4 us
    all_to_all x1, waiting for transfers between devices, local(): arrived = lax.all_to_all(terms, 'tp', 0, 0, tiled=True)  24.9 us
    all_to_all x1, blocking collectives, spread(): return lax.all_to_all(stacked, axis, 0, 0, tiled=True)  21.5 us
    all_to_all x2, waiting for transfers between devices, local(): arrived = lax.all_to_all(sent, 'tp', 0, 0, tiled=True)  19.7 us
    all_to_all x2, starting transfers between devices, spread(): return lax.all_to_all(stacked, axis, 0, 0, tiled=True)  11 us
    all_to_all x2, waiting for transfers between devices, spread(): return lax.all_to_all(stacked, axis, 0, 0, tiled=True)  10.5 us
  transfers between devices with their start and end apart: 33, of which 18 were waited for; matrix products, arithmetic and copies ran while one was open for 7% of the time, Pallas kernels for 2%

profile of v2, /device:TPU:1, one launch (start us, length us, event | category | flops | bytes accessed | tf_op | source)
XLA Modules:
  0.0 279.4 jit_solution(11302246678007918115)
XLA Ops:
  0.7 1.2 copy-done
  3.6 6.4 %collective-permute-start.16 = (bf16[96,512]{1,0:T(8,128)(2,1)}, bf16[96,512]{1,0:T(8,128)(2,1)S(1)}, u32[]{:S(2)}, u32[]{:S(2)}) collective-permute-start(bf16[96,512]{1,0:T(8,128)(2,1)} %pad_maximum_fusion.5), channel_id=1, source_target_pairs={{0,7},{1,0},{2,1},{3,2},{4,3},{5,4},{6,5},{7,6},{8,15},{9,8},{10,9... | collective-permute-start | bytes 294920 | tf_op jit(solution)/shard_map/fold_send/ppermute | solution.py:34
  11.6 4.5 %collective-permute-start.19 = (bf16[96,512]{1,0:T(8,128)(2,1)}, bf16[96,512]{1,0:T(8,128)(2,1)}, u32[]{:S(2)}, u32[]{:S(2)}) collective-permute-start(bf16[96,512]{1,0:T(8,128)(2,1)} %pad_maximum_fusion.5), channel_id=1, source_target_pairs={{0,4},{1,5},{2,6},{3,7},{4,0},{5,1},{6,2},{7,3},{8,12},{9,13},{10,... | collective-permute-start | bytes 294920 | tf_op jit(solution)/shard_map/fold_send/ppermute | solution.py:34
  16.1 2.4 convolution_convert_fusion.1
  19.6 2.1 collective-permute-start.21
  22.3 1.5 collective-permute-start.22
  24.4 1.4 constant_dynamic-update-slice_fusion.12
  25.7 1.4 constant_dynamic-update-slice_fusion.11
  27.1 1.4 constant_dynamic-update-slice_fusion.10
  28.5 3.6 %collective-permute-done.21 = bf16[96,512]{1,0:T(8,128)(2,1)S(1)} collective-permute-done((bf16[96,512]{1,0:T(8,128)(2,1)}, bf16[96,512]{1,0:T(8,128)(2,1)S(1)}, u32[]{:S(2)}, u32[]{:S(2)}) %collective-permute-start.21) | collective-permute-done | bytes 98336 | tf_op jit(solution)/shard_map/fold_send/ppermute | solution.py:34
  32.7 2.2 collective-permute-done.22
  37.4 1.4 constant_dynamic-update-slice_fusion.4
  38.7 1.4 constant_dynamic-update-slice_fusion.3
  40.1 1.4 constant_dynamic-update-slice_fusion.2
  46.9 1.5 slice.154
  49.2 1.5 slice.155
  50.7 1.5 reshape.104
  52.2 1.5 slice.156
  53.7 1.5 reshape.105
  55.2 1.5 slice.157
  56.7 1.5 reshape.106
  60.7 1.5 constant_dynamic-update-slice_fusion.18
  62.2 1.5 constant_dynamic-update-slice_fusion.17
  63.6 1.5 constant_dynamic-update-slice_fusion.16
  65.1 1.9 convolution_convert_fusion.2
  68.0 6.4 %all-to-all-start.1 = ((bf16[16,96,256]{2,1,0:T(8,128)(2,1)}), bf16[16,96,256]{2,1,0:T(8,128)(2,1)S(1)}, u32[]{:S(2)}, u32[]{:S(2)}) async-start(bf16[16,96,256]{2,1,0:T(8,128)(2,1)} %broadcast_in_dim.13), calls=%async_computation.1 | async-start | bytes 1572864 | tf_op jit(solution)/shard_map/fold/all_to_all | solution.py:40
  74.5 1.4 collective-permute-start
  76.8 10.5 %all-to-all-done.1.own_ref = bf16[16,96,256]{2,1,0:T(8,128)(2,1)S(1)} async-done(((bf16[16,96,256]{2,1,0:T(8,128)(2,1)}), bf16[16,96,256]{2,1,0:T(8,128)(2,1)S(1)}, u32[]{:S(2)}, u32[]{:S(2)}) %all-to-all-start.1) | async-done | bytes 786464 | tf_op jit(solution)/shard_map/fold/all_to_all | solution.py:40
  87.3 1.6 broadcast_in_dim.12
  88.9 4.6 %all-to-all-start = ((bf16[16,256,256]{2,1,0:T(8,128)(2,1)}), bf16[16,256,256]{2,1,0:T(8,128)(2,1)}, u32[]{:S(2)}, u32[]{:S(2)}) async-start(bf16[16,256,256]{2,1,0:T(8,128)(2,1)} %broadcast_in_dim.12), calls=%async_computation | async-start | bytes 4194304 | tf_op jit(solution)/shard_map/keys_values/all_to_all | solution.py:40
  98.3 2.2 collective-permute-start.2
  100.5 5.6 %collective-permute-start.4 = (bf16[128,512]{1,0:T(8,128)(2,1)S(1)}, bf16[128,512]{1,0:T(8,128)(2,1)S(1)}, u32[]{:S(2)}, u32[]{:S(2)}) collective-permute-start(bf16[128,512]{1,0:T(8,128)(2,1)S(1)} %fusion.refs_0_.input_ref), channel_id=1, source_target_pairs={{0,4},{1,5},{2,6},{3,7},{4,0},{5,1},{6,2},{7,3},{8,12},{9,13},{10,... | collective-permute-start | bytes 393224 | tf_op jit(solution)/shard_map/inputs/ppermute | solution.py:34
  106.9 1.6 collective-permute-start.6
  108.5 1.2 collective-permute-start.7
  109.7 4.5 %collective-permute-done.3.refs_3_ = bf16[128,512]{1,0:T(8,128)(2,1)S(1)} collective-permute-done((bf16[128,512]{1,0:T(8,128)(2,1)S(1)}, bf16[128,512]{1,0:T(8,128)(2,1)S(1)}, u32[]{:S(2)}, u32[]{:S(2)}) %collective-permute-start.3) | collective-permute-done | bytes 131104 | tf_op jit(solution)/shard_map/inputs/ppermute | solution.py:34
  114.2 6.6 %collective-permute-done.4.refs_4_ = bf16[128,512]{1,0:T(8,128)(2,1)S(1)} collective-permute-done((bf16[128,512]{1,0:T(8,128)(2,1)S(1)}, bf16[128,512]{1,0:T(8,128)(2,1)S(1)}, u32[]{:S(2)}, u32[]{:S(2)}) %collective-permute-start.4) | collective-permute-done | bytes 131104 | tf_op jit(solution)/shard_map/inputs/ppermute | solution.py:34
  120.8 5.7 %collective-permute-done.6.refs_6_ = bf16[128,512]{1,0:T(8,128)(2,1)S(1)} collective-permute-done((bf16[128,512]{1,0:T(8,128)(2,1)S(1)}, bf16[128,512]{1,0:T(8,128)(2,1)S(1)}, u32[]{:S(2)}, u32[]{:S(2)}) %collective-permute-start.6) | collective-permute-done | bytes 131104 | tf_op jit(solution)/shard_map/inputs/ppermute | solution.py:34
  126.6 1.3 collective-permute-done.7.refs_7_
  127.8 1.6 copy-done.2
  129.4 1.6 copy-done.9
  131.0 1.7 queries.1
  132.7 2.5 collective-permute-start.8
  137.0 2.5 attention.1
  141.0 1.8 raw.1
  142.7 4.2 %all-to-all-start.2 = ((bf16[8,16,3072]{2,1,0:T(8,128)(2,1)}), bf16[8,16,3072]{2,1,0:T(8,128)(2,1)}, u32[]{:S(2)}, u32[]{:S(2)}) async-start(bf16[8,16,3072]{2,1,0:T(8,128)(2,1)} %raw.1), calls=%async_computation.2 | async-start | bytes 1572864 | tf_op jit(solution)/shard_map/raw/all_to_all | solution.py:402
  146.9 2.5 collective-permute-start.11
  150.9 19.7 %all-to-all-done.2.arrived_ref = bf16[8,16,3072]{2,1,0:T(8,128)(2,1)} async-done(((bf16[8,16,3072]{2,1,0:T(8,128)(2,1)}), bf16[8,16,3072]{2,1,0:T(8,128)(2,1)}, u32[]{:S(2)}, u32[]{:S(2)}) %all-to-all-start.2) | async-done | bytes 786464 | tf_op jit(solution)/shard_map/raw/all_to_all | solution.py:402
  170.6 1.6 norm.1
  173.6 3.4 %all-to-all-start.3 = ((bf16[8,16,1152]{2,1,0:T(8,128)(2,1)}), bf16[8,16,1152]{2,1,0:T(8,128)(2,1)S(1)}, u32[]{:S(2)}, u32[]{:S(2)}) async-start(bf16[8,16,1152]{2,1,0:T(8,128)(2,1)} %copy-done.11), calls=%async_computation.3 | async-start | bytes 589824 | tf_op jit(solution)/shard_map/norm/all_to_all | solution.py:414
  177.0 1.7 fusion.11
  178.7 4.8 %collective-permute-start.14 = (bf16[4,256,128]{2,1,0:T(8,128)(2,1)S(1)}, bf16[4,256,128]{2,1,0:T(8,128)(2,1)S(1)}, u32[]{:S(2)}, u32[]{:S(2)}) collective-permute-start(bf16[4,256,128]{2,1,0:T(8,128)(2,1)S(1)} %get-tuple-element.24), channel_id=1, source_target_pairs={{0,192},{64,0},{128,64},{192,128},{1,193},{65,1},{129,65},{193,129... | collective-permute-start | bytes 786440 | tf_op jit(solution)/shard_map/queries/ppermute | solution.py:34
  184.8 3.0 %collective-permute-start.24 = (bf16[1,1024]{1,0:T(2,128)(2,1)S(1)}, bf16[1,1024]{1,0:T(2,128)(2,1)S(1)}, u32[]{:S(2)}, u32[]{:S(2)}) collective-permute-start(bf16[1,1024]{1,0:T(2,128)(2,1)S(1)} %slice.130), channel_id=1, source_target_pairs={{8,0},{16,8},{24,16},{32,24},{40,32},{48,40},{56,48},{64,56},{72,6... | collective-permute-start | bytes 6152 | tf_op jit(solution)/shard_map/targets/ppermute | solution.py:358
  188.9 1.5 collective-permute-done.24
  191.2 3.2 %collective-permute-done.14 = bf16[4,256,128]{2,1,0:T(8,128)(2,1)S(1)} collective-permute-done((bf16[4,256,128]{2,1,0:T(8,128)(2,1)S(1)}, bf16[4,256,128]{2,1,0:T(8,128)(2,1)S(1)}, u32[]{:S(2)}, u32[]{:S(2)}) %collective-permute-start.14) | collective-permute-done | bytes 262176 | tf_op jit(solution)/shard_map/queries/ppermute | solution.py:34
  194.4 4.0 %collective-permute-done.12 = bf16[4,256,128]{2,1,0:T(8,128)(2,1)} collective-permute-done((bf16[4,256,128]{2,1,0:T(8,128)(2,1)S(1)}, bf16[4,256,128]{2,1,0:T(8,128)(2,1)}, u32[]{:S(2)}, u32[]{:S(2)}) %collective-permute-start.12) | collective-permute-done | bytes 262176 | tf_op jit(solution)/shard_map/queries/ppermute | solution.py:34
  198.4 1.3 pad_maximum_fusion.hold_ref.q_ref
  202.7 1.5 loss.1
  211.5 21.5 %all_to_all.30.sent_ref = bf16[16,272,128]{2,1,0:T(8,128)(2,1)S(1)} all-to-all(bf16[16,272,128]{2,1,0:T(8,128)(2,1)S(1)} %broadcast_in_dim.16), channel_id=1, replica_groups=mesh['y'=4,'x'=4,'core'=2,'tp'=8] {'y','x'}, dimensions={0} | all-to-all | bytes 2228224 | tf_op jit(solution)/shard_map/sent_grads/all_to_all | solution.py:40
  233.0 1.5 attention_grad.1
  234.6 1.9 collective-permute-start.26
  237.4 4.2 %d_context.1 = bf16[8,128,512]{2,1,0:T(8,128)(2,1)} custom-call(bf16[128,512]{1,0:T(8,128)(2,1)S(1)} %pad_maximum_fusion.4.grad_ref, bf16[4096,256]{1,0:T(8,128)(2,1)S(1)} %copy-done.3, bf16[4096,256]{1,0:T(8,128)(2,1)S(1)} %copy-done.5), custom_call_target="tpu_custom_call" | custom-call | tf_op jit(solution)/shard_map/d_context/pallas_call | solution.py:446
  241.6 6.6 %all-to-all-start.5 = ((bf16[8,128,512]{2,1,0:T(8,128)(2,1)}), bf16[8,128,512]{2,1,0:T(8,128)(2,1)S(1)}, u32[]{:S(2)}, u32[]{:S(2)}) async-start(bf16[8,128,512]{2,1,0:T(8,128)(2,1)} %d_context.1), calls=%async_computation.5 | async-start | bytes 2097152 | tf_op jit(solution)/shard_map/d_context/all_to_all | solution.py:458
  248.2 1.4 fusion.1
  252.5 24.9 %all-to-all-done.5 = bf16[8,128,512]{2,1,0:T(8,128)(2,1)S(1)} async-done(((bf16[8,128,512]{2,1,0:T(8,128)(2,1)}), bf16[8,128,512]{2,1,0:T(8,128)(2,1)S(1)}, u32[]{:S(2)}, u32[]{:S(2)}) %all-to-all-start.5) | async-done | bytes 1048608 | tf_op jit(solution)/shard_map/d_context/all_to_all | solution.py:458
  (149 shorter events, 40.5 us)
Async XLA Ops:
  0.6 1.2 copy-start
  0.6 17.8 %copy-start.4 = (bf16[4096,256]{1,0:T(8,128)(2,1)S(1)}, bf16[4096,256]{1,0:T(8,128)(2,1)}, u32[]{:S(2)}) copy-start(bf16[4096,256]{1,0:T(8,128)(2,1)} %value_ref.1) | copy-start | bytes 6291460
  3.0 15.6 %copy-start.15 = (bf16[128,4096]{1,0:T(8,128)(2,1)S(1)}, bf16[128,4096]{1,0:T(8,128)(2,1)}, u32[]{:S(2)}) copy-start(bf16[128,4096]{1,0:T(8,128)(2,1)} %param.16) | copy-start | bytes 3145732
  3.6 16.0 %collective-permute-start.16 = (bf16[96,512]{1,0:T(8,128)(2,1)}, bf16[96,512]{1,0:T(8,128)(2,1)S(1)}, u32[]{:S(2)}, u32[]{:S(2)}) collective-permute-start(bf16[96,512]{1,0:T(8,128)(2,1)} %pad_maximum_fusion.5), channel_id=1, source_target_pairs={{0,7},{1,0},{2,1},{3,2},{4,3},{5,4},{6,5},{7,6},{8,15},{9,8},{10,9... | collective-permute-start | bytes 294920 | tf_op jit(solution)/shard_map/fold_send/ppermute | solution.py:34
  10.0 12.3 %collective-permute-start.17 = (bf16[96,512]{1,0:T(8,128)(2,1)}, bf16[96,512]{1,0:T(8,128)(2,1)S(1)}, u32[]{:S(2)}, u32[]{:S(2)}) collective-permute-start(bf16[96,512]{1,0:T(8,128)(2,1)} %pad_maximum_fusion.5), channel_id=1, source_target_pairs={{0,6},{1,7},{2,0},{3,1},{4,2},{5,3},{6,4},{7,5},{8,14},{9,15},{10,... | collective-permute-start | bytes 294920 | tf_op jit(solution)/shard_map/fold_send/ppermute | solution.py:34
  11.2 13.2 %collective-permute-start.18 = (bf16[96,512]{1,0:T(8,128)(2,1)}, bf16[96,512]{1,0:T(8,128)(2,1)}, u32[]{:S(2)}, u32[]{:S(2)}) collective-permute-start(bf16[96,512]{1,0:T(8,128)(2,1)} %pad_maximum_fusion.5), channel_id=1, source_target_pairs={{0,5},{1,6},{2,7},{3,0},{4,1},{5,2},{6,3},{7,4},{8,13},{9,14},{10,... | collective-permute-start | bytes 294920 | tf_op jit(solution)/shard_map/fold_send/ppermute | solution.py:34
  11.6 14.1 %collective-permute-start.19 = (bf16[96,512]{1,0:T(8,128)(2,1)}, bf16[96,512]{1,0:T(8,128)(2,1)}, u32[]{:S(2)}, u32[]{:S(2)}) collective-permute-start(bf16[96,512]{1,0:T(8,128)(2,1)} %pad_maximum_fusion.5), channel_id=1, source_target_pairs={{0,4},{1,5},{2,6},{3,7},{4,0},{5,1},{6,2},{7,3},{8,12},{9,13},{10,... | collective-permute-start | bytes 294920 | tf_op jit(solution)/shard_map/fold_send/ppermute | solution.py:34
  16.1 11.0 %collective-permute-start.20 = (bf16[96,512]{1,0:T(8,128)(2,1)}, bf16[96,512]{1,0:T(8,128)(2,1)}, u32[]{:S(2)}, u32[]{:S(2)}) collective-permute-start(bf16[96,512]{1,0:T(8,128)(2,1)} %pad_maximum_fusion.5), channel_id=1, source_target_pairs={{0,3},{1,4},{2,5},{3,6},{4,7},{5,0},{6,1},{7,2},{8,11},{9,12},{10,... | collective-permute-start | bytes 294920 | tf_op jit(solution)/shard_map/fold_send/ppermute | solution.py:34
  19.0 25.5 %copy-start.1 = (bf16[256,4096]{1,0:T(8,128)(2,1)S(1)}, bf16[256,4096]{1,0:T(8,128)(2,1)}, u32[]{:S(2)}) copy-start(bf16[256,4096]{1,0:T(8,128)(2,1)} %refs_9_.1) | copy-start | bytes 6291460
  19.6 24.9 %copy-start.20 = (bf16[96,512]{1,0:T(8,128)(2,1)}, bf16[96,512]{1,0:T(8,128)(2,1)S(1)}, u32[]{:S(2)}) copy-start(bf16[96,512]{1,0:T(8,128)(2,1)S(1)} %collective-permute-done.16) | copy-start | bytes 294916
  19.6 12.5 %collective-permute-start.21 = (bf16[96,512]{1,0:T(8,128)(2,1)}, bf16[96,512]{1,0:T(8,128)(2,1)S(1)}, u32[]{:S(2)}, u32[]{:S(2)}) collective-permute-start(bf16[96,512]{1,0:T(8,128)(2,1)} %pad_maximum_fusion.5), channel_id=1, source_target_pairs={{0,2},{1,3},{2,4},{3,5},{4,6},{5,7},{6,0},{7,1},{8,10},{9,11},{10,... | collective-permute-start | bytes 294920 | tf_op jit(solution)/shard_map/fold_send/ppermute | solution.py:34
  22.3 22.8 %copy-start.21 = (bf16[96,512]{1,0:T(8,128)(2,1)}, bf16[96,512]{1,0:T(8,128)(2,1)S(1)}, u32[]{:S(2)}) copy-start(bf16[96,512]{1,0:T(8,128)(2,1)S(1)} %collective-permute-done.17) | copy-start | bytes 294916
  22.3 12.6 %collective-permute-start.22 = (bf16[96,512]{1,0:T(8,128)(2,1)}, bf16[96,512]{1,0:T(8,128)(2,1)S(1)}, u32[]{:S(2)}, u32[]{:S(2)}) collective-permute-start(bf16[96,512]{1,0:T(8,128)(2,1)} %pad_maximum_fusion.5), channel_id=1, source_target_pairs={{0,1},{1,2},{2,3},{3,4},{4,5},{5,6},{6,7},{7,0},{8,9},{9,10},{10,1... | collective-permute-start | bytes 294920 | tf_op jit(solution)/shard_map/fold_send/ppermute | solution.py:34
  32.1 10.0 %copy-start.22 = (bf16[96,512]{1,0:T(8,128)(2,1)}, bf16[96,512]{1,0:T(8,128)(2,1)S(1)}, u32[]{:S(2)}) copy-start(bf16[96,512]{1,0:T(8,128)(2,1)S(1)} %collective-permute-done.21) | copy-start | bytes 294916
  68.0 19.3 %all-to-all-start.1 = ((bf16[16,96,256]{2,1,0:T(8,128)(2,1)}), bf16[16,96,256]{2,1,0:T(8,128)(2,1)S(1)}, u32[]{:S(2)}, u32[]{:S(2)}) async-start(bf16[16,96,256]{2,1,0:T(8,128)(2,1)} %broadcast_in_dim.13), calls=%async_computation.1 | async-start | bytes 1572864 | tf_op jit(solution)/shard_map/fold/all_to_all | solution.py:40
  74.5 2.3 collective-permute-start
  88.9 4.6 %copy-start.14 = (s32[4]{0:T(128)S(1)}, s32[4]{0:T(128)}, u32[]{:S(2)}) copy-start(s32[4]{0:T(128)} %lengths_ref.3) | copy-start | bytes 52
  88.9 7.8 %copy-start.24 = (s32[128]{0:T(128)S(1)}, s32[128]{0:T(128)}, u32[]{:S(2)}) copy-start(s32[128]{0:T(128)} %param.14) | copy-start | bytes 1540
  88.9 8.5 %copy-start.16 = (bf16[1024,512]{1,0:T(8,128)(2,1)S(1)}, bf16[1024,512]{1,0:T(8,128)(2,1)}, u32[]{:S(2)}) copy-start(bf16[1024,512]{1,0:T(8,128)(2,1)} %param.18) | copy-start | bytes 3145732
  88.9 8.5 %copy-start.17 = (bf16[128,1024]{1,0:T(8,128)(2,1)S(1)}, bf16[128,1024]{1,0:T(8,128)(2,1)}, u32[]{:S(2)}) copy-start(bf16[128,1024]{1,0:T(8,128)(2,1)} %param.13) | copy-start | bytes 786436
  88.9 8.5 %copy-start.23 = (f32[512]{0:T(512)S(1)}, f32[512]{0:T(512)}, u32[]{:S(2)}) copy-start(f32[512]{0:T(512)} %param.17) | copy-start | bytes 6148
  88.9 48.1 %all-to-all-start = ((bf16[16,256,256]{2,1,0:T(8,128)(2,1)}), bf16[16,256,256]{2,1,0:T(8,128)(2,1)}, u32[]{:S(2)}, u32[]{:S(2)}) async-start(bf16[16,256,256]{2,1,0:T(8,128)(2,1)} %broadcast_in_dim.12), calls=%async_computation | async-start | bytes 4194304 | tf_op jit(solution)/shard_map/keys_values/all_to_all | solution.py:40
  97.7 9.1 %collective-permute-start.1 = (bf16[128,512]{1,0:T(8,128)(2,1)S(1)}, bf16[128,512]{1,0:T(8,128)(2,1)S(1)}, u32[]{:S(2)}, u32[]{:S(2)}) collective-permute-start(bf16[128,512]{1,0:T(8,128)(2,1)S(1)} %fusion.refs_0_.input_ref), channel_id=1, source_target_pairs={{0,1},{1,2},{2,3},{3,4},{4,5},{5,6},{6,7},{7,0},{8,9},{9,10},{10,1... | collective-permute-start | bytes 393224 | tf_op jit(solution)/shard_map/inputs/ppermute | solution.py:34
  98.3 10.2 %collective-permute-start.2 = (bf16[128,512]{1,0:T(8,128)(2,1)S(1)}, bf16[128,512]{1,0:T(8,128)(2,1)S(1)}, u32[]{:S(2)}, u32[]{:S(2)}) collective-permute-start(bf16[128,512]{1,0:T(8,128)(2,1)S(1)} %fusion.refs_0_.input_ref), channel_id=1, source_target_pairs={{0,2},{1,3},{2,4},{3,5},{4,6},{5,7},{6,0},{7,1},{8,10},{9,11},{10,... | collective-permute-start | bytes 393224 | tf_op jit(solution)/shard_map/inputs/ppermute | solution.py:34
  100.5 13.8 %collective-permute-start.3 = (bf16[128,512]{1,0:T(8,128)(2,1)S(1)}, bf16[128,512]{1,0:T(8,128)(2,1)S(1)}, u32[]{:S(2)}, u32[]{:S(2)}) collective-permute-start(bf16[128,512]{1,0:T(8,128)(2,1)S(1)} %fusion.refs_0_.input_ref), channel_id=1, source_target_pairs={{0,3},{1,4},{2,5},{3,6},{4,7},{5,0},{6,1},{7,2},{8,11},{9,12},{10,... | collective-permute-start | bytes 393224 | tf_op jit(solution)/shard_map/inputs/ppermute | solution.py:34
  100.5 20.3 %collective-permute-start.4 = (bf16[128,512]{1,0:T(8,128)(2,1)S(1)}, bf16[128,512]{1,0:T(8,128)(2,1)S(1)}, u32[]{:S(2)}, u32[]{:S(2)}) collective-permute-start(bf16[128,512]{1,0:T(8,128)(2,1)S(1)} %fusion.refs_0_.input_ref), channel_id=1, source_target_pairs={{0,4},{1,5},{2,6},{3,7},{4,0},{5,1},{6,2},{7,3},{8,12},{9,13},{10,... | collective-permute-start | bytes 393224 | tf_op jit(solution)/shard_map/inputs/ppermute | solution.py:34
  106.0 14.8 %collective-permute-start.5 = (bf16[128,512]{1,0:T(8,128)(2,1)S(1)}, bf16[128,512]{1,0:T(8,128)(2,1)S(1)}, u32[]{:S(2)}, u32[]{:S(2)}) collective-permute-start(bf16[128,512]{1,0:T(8,128)(2,1)S(1)} %fusion.refs_0_.input_ref), channel_id=1, source_target_pairs={{0,5},{1,6},{2,7},{3,0},{4,1},{5,2},{6,3},{7,4},{8,13},{9,14},{10,... | collective-permute-start | bytes 393224 | tf_op jit(solution)/shard_map/inputs/ppermute | solution.py:34
  106.9 19.7 %collective-permute-start.6 = (bf16[128,512]{1,0:T(8,128)(2,1)S(1)}, bf16[128,512]{1,0:T(8,128)(2,1)S(1)}, u32[]{:S(2)}, u32[]{:S(2)}) collective-permute-start(bf16[128,512]{1,0:T(8,128)(2,1)S(1)} %fusion.refs_0_.input_ref), channel_id=1, source_target_pairs={{0,6},{1,7},{2,0},{3,1},{4,2},{5,3},{6,4},{7,5},{8,14},{9,15},{10,... | collective-permute-start | bytes 393224 | tf_op jit(solution)/shard_map/inputs/ppermute | solution.py:34
  108.5 19.4 %collective-permute-start.7 = (bf16[128,512]{1,0:T(8,128)(2,1)S(1)}, bf16[128,512]{1,0:T(8,128)(2,1)S(1)}, u32[]{:S(2)}, u32[]{:S(2)}) collective-permute-start(bf16[128,512]{1,0:T(8,128)(2,1)S(1)} %fusion.refs_0_.input_ref), channel_id=1, source_target_pairs={{0,7},{1,0},{2,1},{3,2},{4,3},{5,4},{6,5},{7,6},{8,15},{9,8},{10,9... | collective-permute-start | bytes 393224 | tf_op jit(solution)/shard_map/inputs/ppermute | solution.py:34
  127.8 1.6 copy-start.2
  129.4 1.6 copy-start.9
  132.7 3.3 %collective-permute-start.8 = (bf16[128,128]{1,0:T(8,128)(2,1)S(1)}, bf16[128,128]{1,0:T(8,128)(2,1)S(1)}, u32[]{:S(2)}, u32[]{:S(2)}) collective-permute-start(bf16[128,128]{1,0:T(8,128)(2,1)S(1)} %broadcast_select_fusion.18), channel_id=1, source_target_pairs={{0,8},{8,0},{1,9},{9,1},{2,10},{10,2},{3,11},{11,3},{4,12},{12,4},... | collective-permute-start | bytes 98312 | tf_op jit(solution)/shard_map/queries/ppermute | solution.py:44
  136.7 4.3 %collective-permute-start.23 = (bf16[16,96,256]{2,1,0:T(8,128)(2,1)S(1)}, bf16[16,96,256]{2,1,0:T(8,128)(2,1)S(1)}, u32[]{:S(2)}, u32[]{:S(2)}) collective-permute-start(bf16[16,96,256]{2,1,0:T(8,128)(2,1)S(1)} %all-to-all-done.1.own_ref), channel_id=1, source_target_pairs={{0,8},{8,0},{1,9},{9,1},{2,10},{10,2},{3,11},{11,3},{4,12},{12,4},... | collective-permute-start | bytes 2359304 | tf_op jit(solution)/shard_map/fold/ppermute | solution.py:44
  139.6 1.3 collective-permute-start.15
  140.9 9.6 %copy-start.6 = (bf16[16,96,256]{2,1,0:T(8,128)(2,1)}, bf16[16,96,256]{2,1,0:T(8,128)(2,1)S(1)}, u32[]{:S(2)}) copy-start(bf16[16,96,256]{2,1,0:T(8,128)(2,1)S(1)} %collective-permute-done.23.other_ref) | copy-start | bytes 2359300
  142.7 27.9 %all-to-all-start.2 = ((bf16[8,16,3072]{2,1,0:T(8,128)(2,1)}), bf16[8,16,3072]{2,1,0:T(8,128)(2,1)}, u32[]{:S(2)}, u32[]{:S(2)}) async-start(bf16[8,16,3072]{2,1,0:T(8,128)(2,1)} %raw.1), calls=%async_computation.2 | async-start | bytes 1572864 | tf_op jit(solution)/shard_map/raw/all_to_all | solution.py:402
  146.9 30.0 %collective-permute-start.11 = (bf16[256,128]{1,0:T(8,128)(2,1)}, bf16[256,128]{1,0:T(8,128)(2,1)}, u32[]{:S(2)}, u32[]{:S(2)}) collective-permute-start(bf16[256,128]{1,0:T(8,128)(2,1)} %get-tuple-element.36.q_ref), channel_id=1, source_target_pairs={{0,48},{16,0},{32,16},{48,32},{1,49},{17,1},{33,17},{49,33},{2,50}... | collective-permute-start | bytes 196616 | tf_op jit(solution)/shard_map/queries/ppermute | solution.py:34
  149.4 27.6 %collective-permute-start.10 = (bf16[256,128]{1,0:T(8,128)(2,1)}, bf16[256,128]{1,0:T(8,128)(2,1)}, u32[]{:S(2)}, u32[]{:S(2)}) collective-permute-start(bf16[256,128]{1,0:T(8,128)(2,1)} %get-tuple-element.36.q_ref), channel_id=1, source_target_pairs={{0,32},{16,48},{32,0},{48,16},{1,33},{17,49},{33,1},{49,17},{2,34}... | collective-permute-start | bytes 196616 | tf_op jit(solution)/shard_map/queries/ppermute | solution.py:34
  150.0 27.0 %collective-permute-start.9 = (bf16[256,128]{1,0:T(8,128)(2,1)}, bf16[256,128]{1,0:T(8,128)(2,1)}, u32[]{:S(2)}, u32[]{:S(2)}) collective-permute-start(bf16[256,128]{1,0:T(8,128)(2,1)} %get-tuple-element.36.q_ref), channel_id=1, source_target_pairs={{0,16},{16,32},{32,48},{48,0},{1,17},{17,33},{33,49},{49,1},{2,18}... | collective-permute-start | bytes 196616 | tf_op jit(solution)/shard_map/queries/ppermute | solution.py:34
  172.2 0.7 copy-start.11
  172.9 0.7 copy-start.12
  173.6 26.2 %all-to-all-start.3 = ((bf16[8,16,1152]{2,1,0:T(8,128)(2,1)}), bf16[8,16,1152]{2,1,0:T(8,128)(2,1)S(1)}, u32[]{:S(2)}, u32[]{:S(2)}) async-start(bf16[8,16,1152]{2,1,0:T(8,128)(2,1)} %copy-done.11), calls=%async_computation.3 | async-start | bytes 589824 | tf_op jit(solution)/shard_map/norm/all_to_all | solution.py:414
  178.7 15.6 %collective-permute-start.14 = (bf16[4,256,128]{2,1,0:T(8,128)(2,1)S(1)}, bf16[4,256,128]{2,1,0:T(8,128)(2,1)S(1)}, u32[]{:S(2)}, u32[]{:S(2)}) collective-permute-start(bf16[4,256,128]{2,1,0:T(8,128)(2,1)S(1)} %get-tuple-element.24), channel_id=1, source_target_pairs={{0,192},{64,0},{128,64},{192,128},{1,193},{65,1},{129,65},{193,129... | collective-permute-start | bytes 786440 | tf_op jit(solution)/shard_map/queries/ppermute | solution.py:34
  183.5 10.8 %collective-permute-start.13 = (bf16[4,256,128]{2,1,0:T(8,128)(2,1)S(1)}, bf16[4,256,128]{2,1,0:T(8,128)(2,1)S(1)}, u32[]{:S(2)}, u32[]{:S(2)}) collective-permute-start(bf16[4,256,128]{2,1,0:T(8,128)(2,1)S(1)} %get-tuple-element.24), channel_id=1, source_target_pairs={{0,128},{64,192},{128,0},{192,64},{1,129},{65,193},{129,1},{193,65... | collective-permute-start | bytes 786440 | tf_op jit(solution)/shard_map/queries/ppermute | solution.py:34
  183.5 14.8 %collective-permute-start.12 = (bf16[4,256,128]{2,1,0:T(8,128)(2,1)S(1)}, bf16[4,256,128]{2,1,0:T(8,128)(2,1)}, u32[]{:S(2)}, u32[]{:S(2)}) collective-permute-start(bf16[4,256,128]{2,1,0:T(8,128)(2,1)S(1)} %get-tuple-element.24), channel_id=1, source_target_pairs={{0,64},{64,128},{128,192},{192,0},{1,65},{65,129},{129,193},{193,1... | collective-permute-start | bytes 786440 | tf_op jit(solution)/shard_map/queries/ppermute | solution.py:34
  184.8 5.6 %collective-permute-start.24 = (bf16[1,1024]{1,0:T(2,128)(2,1)S(1)}, bf16[1,1024]{1,0:T(2,128)(2,1)S(1)}, u32[]{:S(2)}, u32[]{:S(2)}) collective-permute-start(bf16[1,1024]{1,0:T(2,128)(2,1)S(1)} %slice.130), channel_id=1, source_target_pairs={{8,0},{16,8},{24,16},{32,24},{40,32},{48,40},{56,48},{64,56},{72,6... | collective-permute-start | bytes 6152 | tf_op jit(solution)/shard_map/targets/ppermute | solution.py:358
  194.4 4.0 %copy-start.18 = (bf16[4,256,128]{2,1,0:T(8,128)(2,1)}, bf16[4,256,128]{2,1,0:T(8,128)(2,1)S(1)}, u32[]{:S(2)}) copy-start(bf16[4,256,128]{2,1,0:T(8,128)(2,1)S(1)} %collective-permute-done.14) | copy-start | bytes 786436
  194.4 4.0 %copy-start.19 = (bf16[4,256,128]{2,1,0:T(8,128)(2,1)}, bf16[4,256,128]{2,1,0:T(8,128)(2,1)S(1)}, u32[]{:S(2)}) copy-start(bf16[4,256,128]{2,1,0:T(8,128)(2,1)S(1)} %collective-permute-done.13) | copy-start | bytes 786436
  199.7 1.1 copy-start.7
  200.9 0.9 copy-start.10
  201.8 0.9 copy-start.13
  209.2 2.0 collective-permute-start.25
  211.5 25.9 %copy-start.5 = (bf16[4096,256]{1,0:T(8,128)(2,1)S(1)}, bf16[4096,256]{1,0:T(8,128)(2,1)}, u32[]{:S(2)}) copy-start(bf16[4096,256]{1,0:T(8,128)(2,1)} %value_ref.1) | copy-start | bytes 6291460
  233.0 1.5 copy-start.8
  233.0 4.4 %copy-start.3 = (bf16[4096,256]{1,0:T(8,128)(2,1)S(1)}, bf16[4096,256]{1,0:T(8,128)(2,1)}, u32[]{:S(2)}) copy-start(bf16[4096,256]{1,0:T(8,128)(2,1)} %key_ref.1) | copy-start | bytes 6291460
  234.6 2.8 collective-permute-start.26
  241.6 35.8 %all-to-all-start.5 = ((bf16[8,128,512]{2,1,0:T(8,128)(2,1)}), bf16[8,128,512]{2,1,0:T(8,128)(2,1)S(1)}, u32[]{:S(2)}, u32[]{:S(2)}) async-start(bf16[8,128,512]{2,1,0:T(8,128)(2,1)} %d_context.1), calls=%async_computation.5 | async-start | bytes 2097152 | tf_op jit(solution)/shard_map/d_context/all_to_all | solution.py:458
  249.6 1.6 collective-permute-start.27

commit v3 on v2

v3 whole, which is shorter than its diff:
```python
import functools
import math

import jax
import jax.numpy as jnp
from jax import lax
from jax.experimental import pallas as pl
from jax.experimental.pallas import tpu as pltpu
from jax.sharding import Mesh
from jax.sharding import PartitionSpec as P

HDIM = 128
TSTEPS = 100
MASKED = -1e30
EPSILON = 1e-06
ROWS = ("y", "x", "core")
CHIPS = ("y", "x")
SCALE = 1.0 / math.sqrt(HDIM)
PAIR = 256
GROUP = 4
FOLD_POST = 32
FOLD_OUT = 8
STATS = 16
F32 = jnp.float32
BF16 = jnp.bfloat16


def dot(a, b, contract=((1,), (0,))):
    return lax.dot_general(a, b, (contract, ((), ())), preferred_element_type=F32)


def shifted(block, axis):
    count = lax.axis_size(axis)
    routes = [[(i, (i + s) % count) for i in range(count)] for s in range(1, count)]
    return [block] + [lax.ppermute(block, axis, route) for route in routes]


def returned(blocks, axis):
    count = lax.axis_size(axis)
    routes = [[(i, (i - s) % count) for i in range(count)] for s in range(count)]
    return [blocks[0]] + [lax.ppermute(blocks[s], axis, routes[s]) for s in range(1, count)]


def spread(block, axis):
    count = lax.axis_size(axis)
    stacked = jnp.broadcast_to(block[None], (count,) + block.shape)
    return lax.all_to_all(stacked, axis, 0, 0, tiled=True)


def swap(block):
    return lax.ppermute(block, "core", [(0, 1), (1, 0)])


def to_head(left, right, core):
    first = core == 0
    mine = jnp.where(first, left, right)
    got = swap(jnp.where(first, right, left))
    return jnp.concatenate((jnp.where(first, mine, got), jnp.where(first, got, mine)), axis=0)


def to_rows(block, core):
    first = core == 0
    half = block.shape[0] // 2
    top, bottom = block[:half], block[half:]
    mine = jnp.where(first, top, bottom)
    got = swap(jnp.where(first, bottom, top))
    return jnp.concatenate((jnp.where(first, mine, got), jnp.where(first, got, mine)), axis=1)


def pieces(values):
    high = values.astype(BF16)
    rest = values - high.astype(F32)
    middle = rest.astype(BF16)
    return high, middle, (rest - middle.astype(F32)).astype(BF16)


def stat_rows(*rows):
    out = []
    for row in rows:
        for piece in pieces(row):
            out += [piece[:, :HDIM].astype(F32), piece[:, HDIM:].astype(F32)]
    out.append(jnp.zeros((STATS - len(out), HDIM), F32))
    return jnp.concatenate(out, axis=0).astype(BF16)


def stat_row(block, at):
    total = block[at : at + 2] + block[at + 2 : at + 4] + block[at + 4 : at + 6]
    return jnp.concatenate((total[:1], total[1:]), axis=1)


def sine(x):
    y = x * x
    total = jnp.full_like(x, 1.0 / 6227020800.0)
    for c in (-1.0 / 39916800.0, 1.0 / 362880.0, -1.0 / 5040.0, 1.0 / 120.0, -1.0 / 6.0, 1.0):
        total = total * y + c
    return total * x


def column(row):
    return jnp.broadcast_to(row, (HDIM, HDIM)).T[:, :1]


def ends_of(lengths_ref):
    ends = [lengths_ref[0]]
    for d in range(1, lengths_ref.shape[0]):
        ends.append(ends[-1] + lengths_ref[d])
    return ends


def start_of(ends, positions):
    start = jnp.zeros_like(positions)
    for end in ends:
        start = jnp.where(positions >= end, end, start)
    return start


def send_kernel(
    place_ref, steps_ref, noised_ref, pre_ref, time_ref, post_ref, out_rows_ref, sent_ref, input_ref
):
    parts = sent_ref.shape[0]
    rows, share = input_ref.shape
    slot = place_ref[2] * place_ref[3] + place_ref[1]
    angle = (0.5 * math.pi / TSTEPS) * steps_ref[...].astype(F32)
    features = dot(noised_ref[...], pre_ref[...]) + column(sine(angle)) * time_ref[...]
    features = features.astype(BF16)
    input_ref[...] = features
    post = post_ref[...].astype(F32).T
    quarter = lax.rem(slot, HDIM // FOLD_POST)
    post_rows = post[:FOLD_POST]
    for k in range(1, HDIM // FOLD_POST):
        post_rows = jnp.where(quarter == k, post[FOLD_POST * k : FOLD_POST * (k + 1)], post_rows)
    out_rows = out_rows_ref[...].astype(F32)
    out_rows = jnp.where(lax.rem(slot, 2) == 0, out_rows[:FOLD_OUT], out_rows[FOLD_OUT:])
    out_rows = [out_rows[:, share * k : share * (k + 1)] for k in range(parts)]
    rest = jnp.concatenate([post_rows] + out_rows, axis=0).astype(BF16)
    for k in range(parts):
        sent_ref[k, :rows, :] = features
        sent_ref[k, rows:, :] = rest


def fold_kernel(gathered_ref, w_out_ref, out_ref):
    parts, _, share = gathered_ref.shape
    heads = w_out_ref.shape[0]
    rows = gathered_ref.shape[1] - FOLD_POST - FOLD_OUT * parts
    middle = rows + FOLD_POST
    direct = jnp.zeros((FOLD_POST, heads), F32)
    span = FOLD_OUT * parts
    rest = gathered_ref[:, middle:, :].reshape(parts * span, share)
    gram = [jnp.zeros((FOLD_OUT, heads), F32)] * parts
    for k in range(parts):
        weight = w_out_ref[:, share * k : share * (k + 1)]
        direct = direct + dot(gathered_ref[k, rows:middle, :], weight, ((1,), (1,)))
        product = dot(rest, weight, ((1,), (1,)))
        for b in range(parts):
            at = span * b + FOLD_OUT * k
            gram[b] = gram[b] + product[at : at + FOLD_OUT]
    folded = jnp.concatenate([direct] + gram, axis=0).astype(BF16)
    for k in range(out_ref.shape[0]):
        out_ref[k] = folded


def query_kernel(gathered_ref, w_query_ref, w_out_ref, query_ref, cross_ref):
    parts, _, share = gathered_ref.shape
    rows = query_ref.shape[0]
    query = jnp.zeros(query_ref.shape, F32)
    cross = jnp.zeros(cross_ref.shape, F32)
    squares = jnp.zeros((rows, 1), F32)
    for k in range(parts):
        at = slice(share * k, share * (k + 1))
        block = gathered_ref[k, :rows, :]
        wide = block.astype(F32)
        squares = squares + jnp.sum(wide * wide, axis=1, keepdims=True)
        query = query + dot(block, w_query_ref[at, :])
        cross = cross + dot(block, w_out_ref[:, at], ((1,), (1,)))
    scale = lax.rsqrt(squares / (share * parts) + EPSILON)
    query_ref[...] = (query * scale).astype(BF16)
    cross_ref[...] = cross


def line_positions(place_ref):
    row = place_ref[1] // GROUP
    here = lax.rem(place_ref[1], GROUP)
    chips = [row * GROUP + lax.rem(here + (GROUP - k), GROUP) for k in range(GROUP)]
    lanes = lax.broadcasted_iota(jnp.int32, (1, PAIR), 1)
    return jnp.concatenate([chip * PAIR + lanes for chip in chips], axis=1)


def key_steps(place_ref, ends):
    row = place_ref[1] // GROUP
    here = lax.rem(place_ref[1], GROUP)
    floor = start_of(ends, row * (GROUP * PAIR))
    past = jnp.maximum(floor - (here * PAIR + PAIR - 1), 0)
    lowest = (past + GROUP * PAIR - 1) // (GROUP * PAIR)
    return row - lowest + 1


def allowed_pairs(place_ref, step, query_start, query_pos):
    base = (place_ref[1] - step * GROUP) * PAIR
    key_pos = base + lax.broadcasted_iota(jnp.int32, (PAIR, query_pos.shape[1]), 0)
    return (key_pos >= query_start) & (key_pos <= query_pos)


def forward_kernel(lengths_ref, place_ref, q_ref, kv_ref, out_ref):
    ends = ends_of(lengths_ref)
    width = GROUP * PAIR
    query_pos = line_positions(place_ref)
    query_start = start_of(ends, query_pos)
    q = q_ref[...].reshape(width, HDIM)

    def body(step, carry):
        row_max, row_total, weighted = carry
        scores = dot(kv_ref[step, :, :HDIM], q, ((1,), (1,))) * SCALE
        scores = jnp.where(allowed_pairs(place_ref, step, query_start, query_pos), scores, MASKED)
        new_max = jnp.maximum(row_max, jnp.max(scores, axis=0, keepdims=True))
        probs = jnp.exp(scores - new_max)
        fading = jnp.exp(row_max - new_max)
        row_total = row_total * fading + jnp.sum(probs, axis=0, keepdims=True)
        weighted = weighted * fading + dot(kv_ref[step, :, HDIM:], probs.astype(BF16), ((0,), (0,)))
        return new_max, row_total, weighted

    row_max, row_total, weighted = lax.fori_loop(
        0,
        key_steps(place_ref, ends),
        body,
        (
            jnp.full((1, width), MASKED, F32),
            jnp.zeros((1, width), F32),
            jnp.zeros((HDIM, width), F32),
        ),
    )
    out = (weighted / row_total).T.astype(BF16)
    log_total = row_max + jnp.log(row_total)
    for k in range(GROUP):
        at = slice(PAIR * k, PAIR * (k + 1))
        out_ref[k, :PAIR, :] = out[at]
        out_ref[k, PAIR:, :] = stat_rows(log_total[:, at])


def merge_kernel(*refs):
    *part_refs, out_ref, total_ref = refs
    logs = [stat_row(ref[PAIR:, :].astype(F32), 0) for ref in part_refs]
    top = functools.reduce(jnp.maximum, logs)
    log_total = top + jnp.log(functools.reduce(jnp.add, [jnp.exp(x - top) for x in logs]))
    out = jnp.zeros((PAIR, HDIM), F32)
    for x, ref in zip(logs, part_refs):
        weight = jnp.broadcast_to(jnp.exp(x - log_total), (HDIM, PAIR)).T
        out = out + weight * ref[:PAIR, :].astype(F32)
    out_ref[...] = out.astype(BF16)
    total_ref[...] = log_total


def both_cores(place_ref, own_ref, other_ref, count):
    own = own_ref[:, :count, :].reshape(-1, own_ref.shape[2])
    other = other_ref[:, :count, :].reshape(-1, other_ref.shape[2])
    first = place_ref[2] == 0
    return jnp.where(first, own, other), jnp.where(first, other, own)


def raw_kernel(place_ref, attended_ref, own_ref, other_ref, input_ref, out_ref):
    parts, own, _ = out_ref.shape
    attended = attended_ref[...]
    low, high = both_cores(place_ref, own_ref, other_ref, FOLD_POST)
    half = low.shape[0]
    raw_low = (dot(attended, low, ((1,), (1,))) + input_ref[:, :half]).astype(BF16)
    raw_high = (dot(attended, high, ((1,), (1,))) + input_ref[:, half:]).astype(BF16)
    packed = jnp.concatenate([attended[own * k : own * (k + 1)] for k in range(parts)], axis=1)
    for k in range(parts):
        out_ref[k, :, :half] = raw_low[own * k : own * (k + 1)]
        out_ref[k, :, half : 2 * half] = raw_high[own * k : own * (k + 1)]
        out_ref[k, :, 2 * half :] = packed


def norm_kernel(
    arrived_ref, gram_ref, attended_ref, cross_ref, input_ref, back_ref, out_ref
):
    parts, own, _ = arrived_ref.shape
    features = out_ref.shape[2] - HDIM
    wide = attended_ref.shape[1]
    total = arrived_ref[0, :, :features].astype(F32)
    for k in range(1, parts):
        total = total + arrived_ref[k, :, :features].astype(F32)
    cross = cross_ref[...]
    back = jnp.zeros_like(cross)
    for k in range(parts):
        theirs = jnp.concatenate(
            [
                arrived_ref[k, :, features + wide * j : features + wide * (j + 1)]
                for j in range(parts)
            ],
            axis=0,
        )
        back = back + dot(theirs, gram_ref[k])
    back_ref[...] = cross + back
    attended = attended_ref[...].astype(F32)
    features_in = input_ref[...].astype(F32)
    squares = jnp.sum((attended * (2.0 * cross + back)).T, axis=0, keepdims=True) + jnp.sum(
        (features_in * features_in).T, axis=0, keepdims=True
    )
    side = jnp.concatenate(pieces(squares) + (jnp.zeros((own - 3, HDIM), BF16),), axis=0)
    summed = total.astype(BF16)
    for k in range(parts):
        out_ref[k, :, :features] = summed
        out_ref[k, :, features:] = side


def loss_kernel(
    width,
    lengths_ref,
    place_ref,
    steps_ref,
    arrived_ref,
    target_ref,
    own_ref,
    other_ref,
    back_ref,
    grad_ref,
    loss_ref,
):
    parts, own, _ = arrived_ref.shape
    rows, features = target_ref.shape
    position = (place_ref[1] * 2 + place_ref[2]) * rows
    position = position + lax.broadcasted_iota(jnp.int32, (1, rows), 1)
    angle = (0.5 * math.pi / TSTEPS) * steps_ref[...].astype(F32)
    keep_level = sine(0.5 * math.pi - angle)
    weight = 1.0 + keep_level * keep_level
    for end in ends_of(lengths_ref):
        weight = jnp.where(position + 1 == end, 0.0, weight)
    side = arrived_ref[:, :, features:].astype(F32)
    squares = jnp.sum(jnp.sum(side, axis=0), axis=0, keepdims=True)
    inverse = column(lax.rsqrt(jnp.maximum(squares / width, 0.0) + EPSILON))
    prediction = arrived_ref[:, :, :features].reshape(rows, features).astype(F32) * inverse
    missed = prediction - target_ref[...].astype(F32)
    weighted_missed = column(weight) * missed
    loss = jnp.sum(weighted_missed * missed, axis=1, keepdims=True)
    loss_ref[...] = jnp.broadcast_to(jnp.sum(loss, axis=0, keepdims=True), (1, HDIM))
    pred_grad = weighted_missed.astype(BF16)
    along = jnp.sum(pred_grad.astype(F32) * prediction, axis=1, keepdims=True) / width
    low, high = both_cores(place_ref, own_ref, other_ref, FOLD_POST)
    half = low.shape[0]
    direct = dot(pred_grad[:, :half], low) + dot(pred_grad[:, half:], high)
    grad_ref[...] = (inverse * (direct - along * inverse * back_ref[...])).astype(BF16)


def sent_kernel(grad_ref, attended_ref, total_ref, loss_ref, out_ref):
    grad = grad_ref[...]
    product = grad.astype(F32) * attended_ref[...].astype(F32)
    output_dot = jnp.sum(product.T, axis=0, keepdims=True)
    stats = stat_rows(total_ref[...], output_dot).astype(F32)
    loss_rows = [p.astype(F32) for p in pieces(loss_ref[...])]
    stats = jnp.concatenate([stats[:12]] + loss_rows + [stats[15:]], axis=0)
    out_ref[:PAIR, :] = grad
    out_ref[PAIR:, :] = stats.astype(BF16)


def backward_kernel(lengths_ref, place_ref, kv_ref, q_ref, *refs):
    *sent_refs, out_ref = refs
    ends = ends_of(lengths_ref)
    width = GROUP * PAIR
    query_pos = line_positions(place_ref)
    query_start = start_of(ends, query_pos)
    q = q_ref[...].reshape(width, HDIM)
    grad = jnp.concatenate([ref[:PAIR, :] for ref in sent_refs], axis=0)
    stats = [ref[PAIR:, :].astype(F32) for ref in sent_refs]
    log_total = jnp.concatenate([stat_row(x, 0) for x in stats], axis=1)
    output_dot = jnp.concatenate([stat_row(x, 6) for x in stats], axis=1)
    loss = functools.reduce(jnp.add, [x[12:13] + x[13:14] + x[14:15] for x in stats])
    tail = jnp.concatenate(
        [p.astype(F32) for p in pieces(loss)] + [jnp.zeros((STATS - 3, HDIM), F32)], axis=0
    )
    tail = jnp.concatenate((tail, tail), axis=1).astype(BF16)
    steps = key_steps(place_ref, ends)
    for step in range(out_ref.shape[0]):
        out_ref[step, PAIR:, :] = tail

        @pl.when(step < steps)
        def _():
            allowed = allowed_pairs(place_ref, step, query_start, query_pos)
            scores = dot(kv_ref[step, :, :HDIM], q, ((1,), (1,))) * SCALE
            probs = jnp.where(allowed, jnp.exp(scores - log_total), 0.0)
            out_ref[step, :PAIR, HDIM:] = dot(probs.astype(BF16), grad).astype(BF16)
            prob_grad = dot(kv_ref[step, :, HDIM:], grad, ((1,), (1,)))
            score_grad = (probs * (prob_grad - output_dot) * SCALE).astype(BF16)
            out_ref[step, :PAIR, :HDIM] = dot(score_grad, q).astype(BF16)

        @pl.when(step >= steps)
        def _():
            out_ref[step, :PAIR, :] = jnp.zeros((PAIR, 2 * HDIM), BF16)


def collect_kernel(*refs):
    *part_refs, out_ref, loss_ref = refs
    total = functools.reduce(jnp.add, [ref[...].astype(F32) for ref in part_refs])
    out_ref[...] = total[:PAIR].astype(BF16)
    rows = total[PAIR : PAIR + 3, :HDIM]
    loss_ref[...] = jnp.sum(rows, axis=0, keepdims=True)


def context_kernel(grad_ref, key_ref, value_ref, out_ref):
    key_grad = jnp.concatenate((grad_ref[:, :HDIM], grad_ref[:, 2 * HDIM : 3 * HDIM]), axis=1)
    value_grad = jnp.concatenate((grad_ref[:, HDIM : 2 * HDIM], grad_ref[:, 3 * HDIM :]), axis=1)
    total = dot(key_grad, key_ref[...], ((1,), (1,))) + dot(value_grad, value_ref[...], ((1,), (1,)))
    out_ref[0] = total.astype(BF16)


SMEM = pl.BlockSpec(memory_space=pltpu.SMEM)
VMEM = pl.BlockSpec(memory_space=pltpu.VMEM)
PARAMS = pltpu.CompilerParams(vmem_limit_bytes=20 * 1024 * 1024)


def local(
    concepts,
    noised,
    step_ids,
    doc_lengths,
    context,
    time_vec,
    w_pre,
    w_query,
    w_key,
    w_value,
    w_out,
    w_post,
):
    rows, features = concepts.shape
    parts = lax.axis_size("tp")
    chips = lax.axis_size(CHIPS)
    core = lax.axis_index("core")
    part = lax.axis_index("tp")
    seq_total = rows * lax.axis_size(ROWS)
    share = w_post.shape[0]
    own = rows // parts
    chip = lax.axis_index(CHIPS)
    place = jnp.stack((part, chip, core, chips)).astype(jnp.int32)
    width = share * parts
    head_width = w_out.shape[0]
    fold_rows = FOLD_POST + FOLD_OUT * parts
    steps = step_ids.reshape(1, rows)

    with jax.named_scope("inputs"):
        sent, input_part = pl.pallas_call(
            send_kernel,
            out_shape=(
                jax.ShapeDtypeStruct((parts, rows + fold_rows, share), BF16),
                jax.ShapeDtypeStruct((rows, share), BF16),
            ),
            grid_spec=pltpu.PrefetchScalarGridSpec(
                num_scalar_prefetch=1,
                grid=(1,),
                in_specs=[
                    pl.BlockSpec((1, rows), lambda i, p: (0, 0)),
                    pl.BlockSpec((rows, features), lambda i, p: (0, 0)),
                    pl.BlockSpec((features, share), lambda i, p: (0, 0)),
                    pl.BlockSpec((1, share), lambda i, p: (0, 0)),
                    pl.BlockSpec(
                        (share, HDIM),
                        lambda i, p: (0, (p[2] * p[3] + p[1]) // (HDIM // FOLD_POST)),
                    ),
                    pl.BlockSpec((2 * FOLD_OUT, width), lambda i, p: ((p[2] * p[3] + p[1]) // 2, 0)),
                ],
                out_specs=(
                    pl.BlockSpec((parts, rows + fold_rows, share), lambda i, p: (0, 0, 0)),
                    pl.BlockSpec((rows, share), lambda i, p: (0, 0)),
                ),
            ),
            compiler_params=PARAMS,
        )(place, steps, noised, w_pre, time_vec.reshape(1, share), w_post, w_out)
        gathered = lax.all_to_all(sent, "tp", 0, 0, tiled=True)
        input_post = dot(input_part, w_post)
    with jax.named_scope("keys_values"):
        key_rows = dot(context, w_key).astype(BF16)
        value_rows = dot(context, w_value).astype(BF16)
        own_kv = to_head(
            jnp.concatenate((key_rows[:, :HDIM], value_rows[:, :HDIM]), axis=1),
            jnp.concatenate((key_rows[:, HDIM:], value_rows[:, HDIM:]), axis=1),
            core,
        )
        all_kv = jnp.stack(shifted(own_kv, "y"))
    with jax.named_scope("fold"):
        folded = pl.pallas_call(
            fold_kernel,
            out_shape=jax.ShapeDtypeStruct((chips, fold_rows, head_width), BF16),
            in_specs=[VMEM, VMEM],
            out_specs=VMEM,
            compiler_params=PARAMS,
        )(gathered, w_out)
        own_fold = lax.all_to_all(folded, CHIPS, 0, 0, tiled=True)
        other_fold = swap(own_fold)
        gram = [f[:, FOLD_POST:].reshape(chips, parts, FOLD_OUT, -1) for f in (own_fold, other_fold)]
        first = core == 0
        gram = jnp.stack((jnp.where(first, gram[0], gram[1]), jnp.where(first, gram[1], gram[0])))
        gram = gram.transpose(2, 0, 1, 3, 4).reshape(parts, 2 * chips * FOLD_OUT, -1)
    with jax.named_scope("targets"):
        count = lax.axis_size(ROWS)
        following = lax.ppermute(concepts[:1], ROWS, [(i + 1, i) for i in range(count - 1)])
        targets = jnp.concatenate((concepts[1:], following), axis=0)
    with jax.named_scope("queries"):
        queries, cross = pl.pallas_call(
            query_kernel,
            out_shape=(
                jax.ShapeDtypeStruct((rows, head_width), BF16),
                jax.ShapeDtypeStruct((rows, head_width), F32),
            ),
            in_specs=[VMEM, VMEM, VMEM],
            out_specs=(VMEM, VMEM),
            compiler_params=PARAMS,
        )(gathered, w_query, w_out)
        query_head = to_head(queries[:, :HDIM], queries[:, HDIM:], core)
        line_queries = jnp.stack(shifted(query_head, "x"))
    with jax.named_scope("attention"):
        sent = pl.pallas_call(
            forward_kernel,
            out_shape=jax.ShapeDtypeStruct((GROUP, PAIR + STATS, HDIM), BF16),
            in_specs=[SMEM, SMEM, VMEM, VMEM],
            out_specs=VMEM,
            compiler_params=PARAMS,
        )(doc_lengths, place, line_queries, all_kv)
        attended_head, log_total = pl.pallas_call(
            merge_kernel,
            out_shape=(
                jax.ShapeDtypeStruct((PAIR, HDIM), BF16),
                jax.ShapeDtypeStruct((1, PAIR), F32),
            ),
            in_specs=[VMEM] * GROUP,
            out_specs=(VMEM, VMEM),
            compiler_params=PARAMS,
        )(*returned(sent, "x"))
        attended = to_rows(attended_head, core)
    with jax.named_scope("raw"):
        sent = pl.pallas_call(
            raw_kernel,
            out_shape=jax.ShapeDtypeStruct((parts, own, features + head_width * parts), BF16),
            in_specs=[SMEM, VMEM, VMEM, VMEM, VMEM],
            out_specs=VMEM,
            compiler_params=PARAMS,
        )(place, attended, own_fold, other_fold, input_post)
        arrived = lax.all_to_all(sent, "tp", 0, 0, tiled=True)
    with jax.named_scope("norm"):
        back, sent = pl.pallas_call(
            norm_kernel,
            out_shape=(
                jax.ShapeDtypeStruct((rows, head_width), F32),
                jax.ShapeDtypeStruct((parts, own, features + HDIM), BF16),
            ),
            in_specs=[VMEM] * 5,
            out_specs=(VMEM, VMEM),
            compiler_params=PARAMS,
        )(arrived, gram, attended, cross, input_part)
        arrived = lax.all_to_all(sent, "tp", 0, 0, tiled=True)
    with jax.named_scope("loss"):
        attended_grad, loss_part = pl.pallas_call(
            functools.partial(loss_kernel, width),
            out_shape=(
                jax.ShapeDtypeStruct((rows, head_width), BF16),
                jax.ShapeDtypeStruct((1, HDIM), F32),
            ),
            in_specs=[SMEM, SMEM] + [VMEM] * 6,
            out_specs=(VMEM, VMEM),
            compiler_params=PARAMS,
        )(doc_lengths, place, steps, arrived, targets, own_fold, other_fold, back)
    with jax.named_scope("sent_grads"):
        grad_head = to_head(attended_grad[:, :HDIM], attended_grad[:, HDIM:], core)
        sent = pl.pallas_call(
            sent_kernel,
            out_shape=jax.ShapeDtypeStruct((PAIR + STATS, HDIM), BF16),
            in_specs=[VMEM] * 4,
            out_specs=VMEM,
            compiler_params=PARAMS,
        )(grad_head, attended_head, log_total, loss_part)
        line_grads = shifted(sent, "x")
    with jax.named_scope("attention_grad"):
        sent = pl.pallas_call(
            backward_kernel,
            out_shape=jax.ShapeDtypeStruct((chips // GROUP, PAIR + STATS, 2 * HDIM), BF16),
            in_specs=[SMEM, SMEM] + [VMEM] * (2 + GROUP),
            out_specs=VMEM,
            compiler_params=PARAMS,
        )(doc_lengths, place, all_kv, line_queries, *line_grads)
        kv_grad, loss_part = pl.pallas_call(
            collect_kernel,
            out_shape=(
                jax.ShapeDtypeStruct((PAIR, 2 * HDIM), BF16),
                jax.ShapeDtypeStruct((1, HDIM), F32),
            ),
            in_specs=[VMEM] * (chips // GROUP),
            out_specs=(VMEM, VMEM),
            compiler_params=PARAMS,
        )(*returned(sent, "y"))
        kv_grad = to_rows(kv_grad, core)
        loss_part = loss_part[0, 0]
        loss = (loss_part + swap(loss_part)) / (seq_total * features)
    with jax.named_scope("d_context"):
        terms = pl.pallas_call(
            context_kernel,
            grid=(parts,),
            out_shape=jax.ShapeDtypeStruct((parts, rows, share), BF16),
            in_specs=[
                pl.BlockSpec((rows, 4 * HDIM), lambda t: (0, 0)),
                pl.BlockSpec((share, 2 * HDIM), lambda t: (t, 0)),
                pl.BlockSpec((share, 2 * HDIM), lambda t: (t, 0)),
            ],
            out_specs=pl.BlockSpec((1, rows, share), lambda t: (t, 0, 0)),
            compiler_params=PARAMS,
        )(kv_grad, w_key, w_value)
        arrived = lax.all_to_all(terms, "tp", 0, 0, tiled=True)
        d_context = jnp.sum(arrived.astype(F32), axis=0).astype(BF16)
    return d_context, loss


def solution(mesh):
    cores = 2
    count, parts = mesh.devices.shape
    side = math.isqrt(count // cores)
    split = Mesh(mesh.devices.reshape(side, side, cores, parts), ("y", "x", "core", "tp"))
    by_rows = P(ROWS, None)
    by_columns = P(None, "tp")
    return jax.shard_map(
        local,
        mesh=split,
        in_specs=(
            by_rows,
            by_rows,
            P(ROWS),
            P(),
            by_rows,
            P("tp"),
            by_columns,
            by_columns,
            by_columns,
            by_columns,
            P("tp", None),
            P("tp", None),
        ),
        out_specs=(P(ROWS, "tp"), P()),
        check_vma=False,
    )
```

time: 283 us -> 238 us (0.84)
  waiting for transfers between devices: 92.9 us -> 128 us
  local copies, waits for them, and re-layouts: 52.1 us -> 22.1 us
  blocking collectives: 21.5 us -> 0 us
  starting transfers between devices: 73.1 us -> 57.6 us
  between operations: 11.1 us -> 2.93 us
  other arithmetic: 8.55 us -> 3.79 us
  Pallas kernels: 14.8 us -> 18.6 us
  matrix products: 5.33 us -> 2.49 us
    all_to_all x2, waiting for transfers between devices: 10.5 us -> 42.1 us  [the longest x1 42 us: local(): gathered = lax.all_to_all(sent, 'tp', 0, 0, tiled=True)]
    ppermute x20 -> x9, starting transfers between devices: 36.9 us -> 12.8 us  [shifted(): return [block] + [lax.ppermute(block, axis, route) for route in routes]]
    all_to_all x1 -> x0, blocking collectives: 21.5 us -> none  [spread(): return lax.all_to_all(stacked, axis, 0, 0, tiled=True)]
    ppermute x20 -> x9, waiting for transfers between devices: 31.1 us -> 11.4 us  [shifted(): return [block] + [lax.ppermute(block, axis, route) for route in routes]]
    ppermute x0 -> x6, waiting for transfers between devices: none -> 13.2 us  [returned(): lax.ppermute(blocks[s], axis, routes[s])]
    unnamed x75 -> x54, local copies, waits for them, and re-layouts: 30.4 us -> 19.1 us
    ppermute x0 -> x6, starting transfers between devices: none -> 9.25 us  [returned(): lax.ppermute(blocks[s], axis, routes[s])]
    all_to_all x2, waiting for transfers between devices: 19.7 us -> 29 us  [local(): arrived = lax.all_to_all(sent, 'tp', 0, 0, tiled=True)]
  transfers between devices with their start and end apart: 33 -> 28, of which waited for: 18 -> 18; matrix products, arithmetic and copies ran while one was open for 7% -> 3% of each run, Pallas kernels for 2% -> 2%
where the time goes in v3:
time: 238 us; the launch traced here: 236 us
  waiting for transfers between devices  128 us (54%)
  starting transfers between devices  57.6 us (24%)
  local copies, waits for them, and re-layouts  22.1 us (9%)
  Pallas kernels  18.6 us (8%)
  other arithmetic  3.79 us (2%)
  between operations  2.93 us (1%)
  matrix products  2.49 us (1%)
    all_to_all x1, waiting for transfers between devices, local(): gathered = lax.all_to_all(sent, 'tp', 0, 0, tiled=True)  42 us
    all_to_all x2, waiting for transfers between devices, local(): arrived = lax.all_to_all(sent, 'tp', 0, 0, tiled=True)  29 us
    all_to_all x1, waiting for transfers between devices, local(): arrived = lax.all_to_all(terms, 'tp', 0, 0, tiled=True)  27.2 us
    unnamed x54, local copies, waits for them, and re-layouts  19.1 us
    ppermute x6, waiting for transfers between devices, returned(): lax.ppermute(blocks[s], axis, routes[s])  13.2 us
    ppermute x9, starting transfers between devices, shifted(): return [block] + [lax.ppermute(block, axis, route) for route in routes]  12.8 us
    ppermute x9, waiting for transfers between devices, shifted(): return [block] + [lax.ppermute(block, axis, route) for route in routes]  11.4 us
    ppermute x6, starting transfers between devices, returned(): lax.ppermute(blocks[s], axis, routes[s])  9.25 us
  transfers between devices with their start and end apart: 28, of which 18 were waited for; matrix products, arithmetic and copies ran while one was open for 3% of the time, Pallas kernels for 2%

profile of v3, /device:TPU:1, one launch (start us, length us, event | category | flops | bytes accessed | tf_op | source)
XLA Modules:
  0.0 235.6 jit_solution(15094406518982732395)
XLA Ops:
  0.7 1.7 copy-done.1
  2.4 1.2 copy-done.7
  3.6 1.2 copy-done.13
  4.8 0.9 copy-done.18
  7.1 0.9 inputs.1
  8.1 1.2 copy-done.12
  10.0 9.1 %all-to-all-start = ((bf16[8,224,512]{2,1,0:T(8,128)(2,1)}), bf16[8,224,512]{2,1,0:T(8,128)(2,1)}, u32[]{:S(2)}, u32[]{:S(2)}) async-start(bf16[8,224,512]{2,1,0:T(8,128)(2,1)} %copy-done.12), calls=%async_computation | async-start | bytes 3670016 | tf_op jit(solution)/shard_map/inputs/all_to_all | solution.py:467
  19.6 1.1 copy-done.3
  21.2 1.0 collective-permute-start
  22.3 0.9 collective-permute-done
  23.2 42.0 %all-to-all-done.gathered_ref = bf16[8,224,512]{2,1,0:T(8,128)(2,1)} async-done(((bf16[8,224,512]{2,1,0:T(8,128)(2,1)}), bf16[8,224,512]{2,1,0:T(8,128)(2,1)}, u32[]{:S(2)}, u32[]{:S(2)}) %all-to-all-start) | async-done | bytes 1835040 | tf_op jit(solution)/shard_map/inputs/all_to_all | solution.py:467
  65.3 1.6 copy-done.11
  66.9 2.6 %queries.1 = (bf16[128,256]{1,0:T(8,128)(2,1)S(1)}, f32[128,256]{1,0:T(8,128)S(1)}) custom-call(bf16[8,224,512]{2,1,0:T(8,128)(2,1)} %all-to-all-done.gathered_ref, bf16[4096,256]{1,0:T(8,128)(2,1)S(1)} %copy-done.11, bf16[256,4096]{1,0:T(8,128)(2,1)S(1)} %copy-done.2), custom_call_target="tpu_custom_call" | custom-call | tf_op jit(solution)/shard_map/queries/pallas_call | solution.py:497
  70.7 1.3 collective-permute-start.1
  72.0 2.6 %collective-permute-start.2 = (bf16[256,256]{1,0:T(8,128)(2,1)}, bf16[256,256]{1,0:T(8,128)(2,1)}, u32[]{:S(2)}, u32[]{:S(2)}) collective-permute-start(bf16[256,256]{1,0:T(8,128)(2,1)} %get-tuple-element.41), channel_id=1, source_target_pairs={{0,128},{64,192},{128,0},{192,64},{1,129},{65,193},{129,1},{193,65... | collective-permute-start | bytes 393224 | tf_op jit(solution)/shard_map/keys_values/ppermute | solution.py:35
  74.6 1.1 collective-permute-start.3
  75.7 3.4 %fold.1 = bf16[16,96,256]{2,1,0:T(8,128)(2,1)S(1)} custom-call(bf16[8,224,512]{2,1,0:T(8,128)(2,1)} %all-to-all-done.gathered_ref, bf16[256,4096]{1,0:T(8,128)(2,1)S(1)} %copy-done.2), custom_call_target="tpu_custom_call" | custom-call | tf_op jit(solution)/shard_map/fold/pallas_call | solution.py:479
  79.1 0.9 copy-done.9
  80.0 4.4 %all-to-all-start.1 = ((bf16[16,96,256]{2,1,0:T(8,128)(2,1)}), bf16[16,96,256]{2,1,0:T(8,128)(2,1)S(1)}, u32[]{:S(2)}, u32[]{:S(2)}) async-start(bf16[16,96,256]{2,1,0:T(8,128)(2,1)} %copy-done.9), calls=%async_computation.1 | async-start | bytes 1572864 | tf_op jit(solution)/shard_map/fold/all_to_all | solution.py:486
  84.4 1.4 collective-permute-start.5
  85.9 2.4 %collective-permute-start.6 = (bf16[256,128]{1,0:T(8,128)(2,1)S(1)}, bf16[256,128]{1,0:T(8,128)(2,1)S(1)}, u32[]{:S(2)}, u32[]{:S(2)}) collective-permute-start(bf16[256,128]{1,0:T(8,128)(2,1)S(1)} %get-tuple-element.49), channel_id=1, source_target_pairs={{0,32},{16,48},{32,0},{48,16},{1,33},{17,49},{33,1},{49,17},{2,34}... | collective-permute-start | bytes 196616 | tf_op jit(solution)/shard_map/queries/ppermute | solution.py:35
  88.3 1.2 collective-permute-start.7
  89.5 1.1 pad_maximum_fusion.kv_ref
  90.6 7.0 %collective-permute-done.5 = bf16[256,128]{1,0:T(8,128)(2,1)S(1)} collective-permute-done((bf16[256,128]{1,0:T(8,128)(2,1)S(1)}, bf16[256,128]{1,0:T(8,128)(2,1)S(1)}, u32[]{:S(2)}, u32[]{:S(2)}) %collective-permute-start.5) | collective-permute-done | bytes 65568 | tf_op jit(solution)/shard_map/queries/ppermute | solution.py:35
  98.2 1.6 attention.2
  100.0 2.7 %collective-permute-start.8 = (bf16[272,128]{1,0:T(8,128)(2,1)S(1)}, bf16[272,128]{1,0:T(8,128)(2,1)S(1)}, u32[]{:S(2)}, u32[]{:S(2)}) collective-permute-start(bf16[272,128]{1,0:T(8,128)(2,1)S(1)} %get-tuple-element.34), channel_id=1, source_target_pairs={{0,48},{16,0},{32,16},{48,32},{1,49},{17,1},{33,17},{49,33},{2,50}... | collective-permute-start | bytes 208904 | tf_op jit(solution)/shard_map/attention/ppermute | solution.py:41
  102.7 1.7 collective-permute-done.10.refs_3_
  104.7 2.8 %collective-permute-done.9.refs_2_ = bf16[272,128]{1,0:T(8,128)(2,1)S(1)} collective-permute-done((bf16[272,128]{1,0:T(8,128)(2,1)S(1)}, bf16[272,128]{1,0:T(8,128)(2,1)S(1)}, u32[]{:S(2)}, u32[]{:S(2)}) %collective-permute-start.9) | collective-permute-done | bytes 69664 | tf_op jit(solution)/shard_map/attention/ppermute | solution.py:41
  107.7 3.9 %collective-permute-start.12 = (bf16[16,96,256]{2,1,0:T(8,128)(2,1)S(1)}, bf16[16,96,256]{2,1,0:T(8,128)(2,1)S(1)}, u32[]{:S(2)}, u32[]{:S(2)}) collective-permute-start(bf16[16,96,256]{2,1,0:T(8,128)(2,1)S(1)} %all-to-all-done.1.own_ref), channel_id=1, source_target_pairs={{0,8},{8,0},{1,9},{9,1},{2,10},{10,2},{3,11},{11,3},{4,12},{12,4},... | collective-permute-start | bytes 2359304 | tf_op jit(solution)/shard_map/fold/ppermute | solution.py:51
  111.7 1.6 fusion.4.input_ref
  113.6 0.9 raw.1
  114.5 0.9 copy-done.10
  115.4 4.2 %all-to-all-start.2 = ((bf16[8,16,3072]{2,1,0:T(8,128)(2,1)}), bf16[8,16,3072]{2,1,0:T(8,128)(2,1)}, u32[]{:S(2)}, u32[]{:S(2)}) async-start(bf16[8,16,3072]{2,1,0:T(8,128)(2,1)} %copy-done.10), calls=%async_computation.2 | async-start | bytes 1572864 | tf_op jit(solution)/shard_map/raw/all_to_all | solution.py:536
  119.8 1.1 copy.14
  120.9 22.3 %all-to-all-done.2.arrived_ref = bf16[8,16,3072]{2,1,0:T(8,128)(2,1)} async-done(((bf16[8,16,3072]{2,1,0:T(8,128)(2,1)}), bf16[8,16,3072]{2,1,0:T(8,128)(2,1)}, u32[]{:S(2)}, u32[]{:S(2)}) %all-to-all-start.2) | async-done | bytes 786464 | tf_op jit(solution)/shard_map/raw/all_to_all | solution.py:536
  143.2 1.2 copy-done.8
  144.4 0.9 copy-done.16
  145.3 0.9 copy-done.20
  146.2 1.6 norm.1
  149.2 4.1 %all-to-all-start.3 = ((bf16[8,16,1152]{2,1,0:T(8,128)(2,1)}), bf16[8,16,1152]{2,1,0:T(8,128)(2,1)}, u32[]{:S(2)}, u32[]{:S(2)}) async-start(bf16[8,16,1152]{2,1,0:T(8,128)(2,1)} %copy-done.17), calls=%async_computation.3 | async-start | bytes 589824 | tf_op jit(solution)/shard_map/norm/all_to_all | solution.py:548
  153.3 0.7 slice.90
  154.0 2.4 %collective-permute-start.13 = (bf16[1,1024]{1,0:T(2,128)(2,1)S(1)}, bf16[1,1024]{1,0:T(2,128)(2,1)S(1)}, u32[]{:S(2)}, u32[]{:S(2)}) collective-permute-start(bf16[1,1024]{1,0:T(2,128)(2,1)S(1)} %slice.90), channel_id=1, source_target_pairs={{8,0},{16,8},{24,16},{32,24},{40,32},{48,40},{56,48},{64,56},{72,6... | collective-permute-start | bytes 6152 | tf_op jit(solution)/shard_map/targets/ppermute | solution.py:494
  156.4 1.0 slice.89
  157.4 1.5 collective-permute-done.13
  158.9 0.7 pad_maximum_fusion.2.target_ref
  159.7 6.7 %all-to-all-done.3.arrived_ref = bf16[8,16,1152]{2,1,0:T(8,128)(2,1)} async-done(((bf16[8,16,1152]{2,1,0:T(8,128)(2,1)}), bf16[8,16,1152]{2,1,0:T(8,128)(2,1)}, u32[]{:S(2)}, u32[]{:S(2)}) %all-to-all-start.3) | async-done | bytes 294944 | tf_op jit(solution)/shard_map/norm/all_to_all | solution.py:548
  166.3 0.9 copy-done.14
  167.3 0.9 copy-done.22
  168.2 1.5 loss.1
  170.2 0.9 collective-permute-done.14
  171.4 1.3 collective-permute-start.16
  172.7 1.3 collective-permute-start.17
  174.0 3.8 %collective-permute-done.15.refs_1_ = bf16[272,128]{1,0:T(8,128)(2,1)S(1)} collective-permute-done((bf16[272,128]{1,0:T(8,128)(2,1)S(1)}, bf16[272,128]{1,0:T(8,128)(2,1)S(1)}, u32[]{:S(2)}, u32[]{:S(2)}) %collective-permute-start.15) | collective-permute-done | bytes 69664 | tf_op jit(solution)/shard_map/sent_grads/ppermute | solution.py:35
  177.8 1.6 attention_grad.2
  179.4 5.8 %collective-permute-start.18 = (bf16[272,256]{1,0:T(8,128)(2,1)S(1)}, bf16[272,256]{1,0:T(8,128)(2,1)S(1)}, u32[]{:S(2)}, u32[]{:S(2)}) collective-permute-start(bf16[272,256]{1,0:T(8,128)(2,1)S(1)} %get-tuple-element.30), channel_id=1, source_target_pairs={{0,192},{64,0},{128,64},{192,128},{1,193},{65,1},{129,65},{193,129... | collective-permute-start | bytes 417800 | tf_op jit(solution)/shard_map/attention_grad/ppermute | solution.py:41
  185.9 5.2 %collective-permute-done.18.refs_1_ = bf16[272,256]{1,0:T(8,128)(2,1)S(1)} collective-permute-done((bf16[272,256]{1,0:T(8,128)(2,1)S(1)}, bf16[272,256]{1,0:T(8,128)(2,1)S(1)}, u32[]{:S(2)}, u32[]{:S(2)}) %collective-permute-start.18) | collective-permute-done | bytes 139296 | tf_op jit(solution)/shard_map/attention_grad/ppermute | solution.py:41
  191.2 3.2 %collective-permute-done.20.refs_3_ = bf16[272,256]{1,0:T(8,128)(2,1)S(1)} collective-permute-done((bf16[272,256]{1,0:T(8,128)(2,1)S(1)}, bf16[272,256]{1,0:T(8,128)(2,1)S(1)}, u32[]{:S(2)}, u32[]{:S(2)}) %collective-permute-start.20) | collective-permute-done | bytes 139296 | tf_op jit(solution)/shard_map/attention_grad/ppermute | solution.py:41
  194.5 1.2 collective-permute-start.21
  195.7 0.9 collective-permute-done.21
  196.7 4.2 %d_context.1 = bf16[8,128,512]{2,1,0:T(8,128)(2,1)} custom-call(bf16[128,512]{1,0:T(8,128)(2,1)S(1)} %pad_maximum_fusion.4.grad_ref, bf16[4096,256]{1,0:T(8,128)(2,1)S(1)} %copy-done.4, bf16[4096,256]{1,0:T(8,128)(2,1)S(1)} %copy-done.6), custom_call_target="tpu_custom_call" | custom-call | tf_op jit(solution)/shard_map/d_context/pallas_call | solution.py:592
  200.9 3.6 %all-to-all-start.4 = ((bf16[8,128,512]{2,1,0:T(8,128)(2,1)}), bf16[8,128,512]{2,1,0:T(8,128)(2,1)S(1)}, u32[]{:S(2)}, u32[]{:S(2)}) async-start(bf16[8,128,512]{2,1,0:T(8,128)(2,1)} %d_context.1), calls=%async_computation.4 | async-start | bytes 2097152 | tf_op jit(solution)/shard_map/d_context/all_to_all | solution.py:604
  204.9 0.8 collective-permute-done.22
  206.4 27.2 %all-to-all-done.4 = bf16[8,128,512]{2,1,0:T(8,128)(2,1)S(1)} async-done(((bf16[8,128,512]{2,1,0:T(8,128)(2,1)}), bf16[8,128,512]{2,1,0:T(8,128)(2,1)S(1)}, u32[]{:S(2)}, u32[]{:S(2)}) %all-to-all-start.4) | async-done | bytes 1048608 | tf_op jit(solution)/shard_map/d_context/all_to_all | solution.py:604
  233.7 0.8 reduce_sum.12
  (89 shorter events, 9.7 us)
Async XLA Ops:
  0.6 18.5 %copy-start = (bf16[128,4096]{1,0:T(8,128)(2,1)S(1)}, bf16[128,4096]{1,0:T(8,128)(2,1)}, u32[]{:S(2)}) copy-start(bf16[128,4096]{1,0:T(8,128)(2,1)} %param.16) | copy-start | bytes 3145732
  0.7 1.7 copy-start.1
  2.4 1.2 copy-start.7
  3.6 1.2 copy-start.13
  4.8 0.9 copy-start.18
  5.8 0.7 copy-start.24
  6.5 0.7 copy-start.25
  8.1 1.3 copy-start.12
  9.3 0.6 copy-start.15
  10.0 9.2 %copy-start.5 = (bf16[4096,256]{1,0:T(8,128)(2,1)S(1)}, bf16[4096,256]{1,0:T(8,128)(2,1)}, u32[]{:S(2)}) copy-start(bf16[4096,256]{1,0:T(8,128)(2,1)} %value_ref.1) | copy-start | bytes 6291460
  10.0 55.3 %all-to-all-start = ((bf16[8,224,512]{2,1,0:T(8,128)(2,1)}), bf16[8,224,512]{2,1,0:T(8,128)(2,1)}, u32[]{:S(2)}, u32[]{:S(2)}) async-start(bf16[8,224,512]{2,1,0:T(8,128)(2,1)} %copy-done.12), calls=%async_computation | async-start | bytes 3670016 | tf_op jit(solution)/shard_map/inputs/all_to_all | solution.py:467
  19.1 1.6 copy-start.3
  20.7 44.5 %copy-start.2 = (bf16[256,4096]{1,0:T(8,128)(2,1)S(1)}, bf16[256,4096]{1,0:T(8,128)(2,1)}, u32[]{:S(2)}) copy-start(bf16[256,4096]{1,0:T(8,128)(2,1)} %w_out_ref.3) | copy-start | bytes 6291460
  21.2 1.9 collective-permute-start
  65.3 1.6 copy-start.11
  69.4 5.2 %copy-start.19 = (f32[128,256]{1,0:T(8,128)}, f32[128,256]{1,0:T(8,128)S(1)}, u32[]{:S(2)}) copy-start(f32[128,256]{1,0:T(8,128)S(1)} %get-tuple-element.18.cross_ref) | copy-start | bytes 393220
  69.5 14.9 %collective-permute-start.4 = (bf16[128,128]{1,0:T(8,128)(2,1)S(1)}, bf16[128,128]{1,0:T(8,128)(2,1)S(1)}, u32[]{:S(2)}, u32[]{:S(2)}) collective-permute-start(bf16[128,128]{1,0:T(8,128)(2,1)S(1)} %broadcast_select_fusion.18), channel_id=1, source_target_pairs={{0,8},{8,0},{1,9},{9,1},{2,10},{10,2},{3,11},{11,3},{4,12},{12,4},... | collective-permute-start | bytes 98312 | tf_op jit(solution)/shard_map/queries/ppermute | solution.py:51
  70.7 17.6 %collective-permute-start.1 = (bf16[256,256]{1,0:T(8,128)(2,1)}, bf16[256,256]{1,0:T(8,128)(2,1)}, u32[]{:S(2)}, u32[]{:S(2)}) collective-permute-start(bf16[256,256]{1,0:T(8,128)(2,1)} %get-tuple-element.41), channel_id=1, source_target_pairs={{0,64},{64,128},{128,192},{192,0},{1,65},{65,129},{129,193},{193,1... | collective-permute-start | bytes 393224 | tf_op jit(solution)/shard_map/keys_values/ppermute | solution.py:35
  72.0 17.5 %collective-permute-start.2 = (bf16[256,256]{1,0:T(8,128)(2,1)}, bf16[256,256]{1,0:T(8,128)(2,1)}, u32[]{:S(2)}, u32[]{:S(2)}) collective-permute-start(bf16[256,256]{1,0:T(8,128)(2,1)} %get-tuple-element.41), channel_id=1, source_target_pairs={{0,128},{64,192},{128,0},{192,64},{1,129},{65,193},{129,1},{193,65... | collective-permute-start | bytes 393224 | tf_op jit(solution)/shard_map/keys_values/ppermute | solution.py:35
  74.6 14.8 %collective-permute-start.3 = (bf16[256,256]{1,0:T(8,128)(2,1)}, bf16[256,256]{1,0:T(8,128)(2,1)}, u32[]{:S(2)}, u32[]{:S(2)}) collective-permute-start(bf16[256,256]{1,0:T(8,128)(2,1)} %get-tuple-element.41), channel_id=1, source_target_pairs={{0,192},{64,0},{128,64},{192,128},{1,193},{65,1},{129,65},{193,129... | collective-permute-start | bytes 393224 | tf_op jit(solution)/shard_map/keys_values/ppermute | solution.py:35
  79.1 0.9 copy-start.9
  80.0 18.2 %copy-start.23 = (s32[4]{0:T(128)S(1)}, s32[4]{0:T(128)}, u32[]{:S(2)}) copy-start(s32[4]{0:T(128)} %lengths_ref.5) | copy-start | bytes 52
  80.0 27.7 %all-to-all-start.1 = ((bf16[16,96,256]{2,1,0:T(8,128)(2,1)}), bf16[16,96,256]{2,1,0:T(8,128)(2,1)S(1)}, u32[]{:S(2)}, u32[]{:S(2)}) async-start(bf16[16,96,256]{2,1,0:T(8,128)(2,1)} %copy-done.9), calls=%async_computation.1 | async-start | bytes 1572864 | tf_op jit(solution)/shard_map/fold/all_to_all | solution.py:486
  84.4 13.1 %collective-permute-start.5 = (bf16[256,128]{1,0:T(8,128)(2,1)S(1)}, bf16[256,128]{1,0:T(8,128)(2,1)S(1)}, u32[]{:S(2)}, u32[]{:S(2)}) collective-permute-start(bf16[256,128]{1,0:T(8,128)(2,1)S(1)} %get-tuple-element.49), channel_id=1, source_target_pairs={{0,16},{16,32},{32,48},{48,0},{1,17},{17,33},{33,49},{49,1},{2,18}... | collective-permute-start | bytes 196616 | tf_op jit(solution)/shard_map/queries/ppermute | solution.py:35
  85.9 12.3 %collective-permute-start.6 = (bf16[256,128]{1,0:T(8,128)(2,1)S(1)}, bf16[256,128]{1,0:T(8,128)(2,1)S(1)}, u32[]{:S(2)}, u32[]{:S(2)}) collective-permute-start(bf16[256,128]{1,0:T(8,128)(2,1)S(1)} %get-tuple-element.49), channel_id=1, source_target_pairs={{0,32},{16,48},{32,0},{48,16},{1,33},{17,49},{33,1},{49,17},{2,34}... | collective-permute-start | bytes 196616 | tf_op jit(solution)/shard_map/queries/ppermute | solution.py:35
  88.3 9.9 %collective-permute-start.7 = (bf16[256,128]{1,0:T(8,128)(2,1)S(1)}, bf16[256,128]{1,0:T(8,128)(2,1)S(1)}, u32[]{:S(2)}, u32[]{:S(2)}) collective-permute-start(bf16[256,128]{1,0:T(8,128)(2,1)S(1)} %get-tuple-element.49), channel_id=1, source_target_pairs={{0,48},{16,0},{32,16},{48,32},{1,49},{17,1},{33,17},{49,33},{2,50}... | collective-permute-start | bytes 196616 | tf_op jit(solution)/shard_map/queries/ppermute | solution.py:35
  99.9 4.4 %collective-permute-start.10 = (bf16[272,128]{1,0:T(8,128)(2,1)S(1)}, bf16[272,128]{1,0:T(8,128)(2,1)S(1)}, u32[]{:S(2)}, u32[]{:S(2)}) collective-permute-start(bf16[272,128]{1,0:T(8,128)(2,1)S(1)} %get-tuple-element.32), channel_id=1, source_target_pairs={{0,16},{16,32},{32,48},{48,0},{1,17},{17,33},{33,49},{49,1},{2,18}... | collective-permute-start | bytes 208904 | tf_op jit(solution)/shard_map/attention/ppermute | solution.py:41
  100.0 4.7 %collective-permute-start.8 = (bf16[272,128]{1,0:T(8,128)(2,1)S(1)}, bf16[272,128]{1,0:T(8,128)(2,1)S(1)}, u32[]{:S(2)}, u32[]{:S(2)}) collective-permute-start(bf16[272,128]{1,0:T(8,128)(2,1)S(1)} %get-tuple-element.34), channel_id=1, source_target_pairs={{0,48},{16,0},{32,16},{48,32},{1,49},{17,1},{33,17},{49,33},{2,50}... | collective-permute-start | bytes 208904 | tf_op jit(solution)/shard_map/attention/ppermute | solution.py:41
  102.7 4.8 %collective-permute-start.9 = (bf16[272,128]{1,0:T(8,128)(2,1)S(1)}, bf16[272,128]{1,0:T(8,128)(2,1)S(1)}, u32[]{:S(2)}, u32[]{:S(2)}) collective-permute-start(bf16[272,128]{1,0:T(8,128)(2,1)S(1)} %get-tuple-element.33), channel_id=1, source_target_pairs={{0,32},{16,48},{32,0},{48,16},{1,33},{17,49},{33,1},{49,17},{2,34}... | collective-permute-start | bytes 208904 | tf_op jit(solution)/shard_map/attention/ppermute | solution.py:41
  107.7 5.9 %collective-permute-start.12 = (bf16[16,96,256]{2,1,0:T(8,128)(2,1)S(1)}, bf16[16,96,256]{2,1,0:T(8,128)(2,1)S(1)}, u32[]{:S(2)}, u32[]{:S(2)}) collective-permute-start(bf16[16,96,256]{2,1,0:T(8,128)(2,1)S(1)} %all-to-all-done.1.own_ref), channel_id=1, source_target_pairs={{0,8},{8,0},{1,9},{9,1},{2,10},{10,2},{3,11},{11,3},{4,12},{12,4},... | collective-permute-start | bytes 2359304 | tf_op jit(solution)/shard_map/fold/ppermute | solution.py:51
  111.6 2.0 collective-permute-start.11
  114.5 0.9 copy-start.10
  115.4 27.8 %all-to-all-start.2 = ((bf16[8,16,3072]{2,1,0:T(8,128)(2,1)}), bf16[8,16,3072]{2,1,0:T(8,128)(2,1)}, u32[]{:S(2)}, u32[]{:S(2)}) async-start(bf16[8,16,3072]{2,1,0:T(8,128)(2,1)} %copy-done.10), calls=%async_computation.2 | async-start | bytes 1572864 | tf_op jit(solution)/shard_map/raw/all_to_all | solution.py:536
  120.9 45.4 %copy-start.26 = (s32[128]{0:T(128)S(1)}, s32[128]{0:T(128)}, u32[]{:S(2)}) copy-start(s32[128]{0:T(128)} %param.14) | copy-start | bytes 1540
  143.2 1.2 copy-start.8
  144.4 0.9 copy-start.16
  145.3 0.9 copy-start.20
  147.8 0.7 copy-start.17
  148.6 0.7 copy-start.21
  149.2 17.1 %all-to-all-start.3 = ((bf16[8,16,1152]{2,1,0:T(8,128)(2,1)}), bf16[8,16,1152]{2,1,0:T(8,128)(2,1)}, u32[]{:S(2)}, u32[]{:S(2)}) async-start(bf16[8,16,1152]{2,1,0:T(8,128)(2,1)} %copy-done.17), calls=%async_computation.3 | async-start | bytes 589824 | tf_op jit(solution)/shard_map/norm/all_to_all | solution.py:548
  154.0 4.9 %collective-permute-start.13 = (bf16[1,1024]{1,0:T(2,128)(2,1)S(1)}, bf16[1,1024]{1,0:T(2,128)(2,1)S(1)}, u32[]{:S(2)}, u32[]{:S(2)}) collective-permute-start(bf16[1,1024]{1,0:T(2,128)(2,1)S(1)} %slice.90), channel_id=1, source_target_pairs={{8,0},{16,8},{24,16},{32,24},{40,32},{48,40},{56,48},{64,56},{72,6... | collective-permute-start | bytes 6152 | tf_op jit(solution)/shard_map/targets/ppermute | solution.py:494
  166.3 1.0 copy-start.14
  167.3 0.9 copy-start.22
  169.7 1.4 collective-permute-start.14
  171.1 25.5 %copy-start.6 = (bf16[4096,256]{1,0:T(8,128)(2,1)S(1)}, bf16[4096,256]{1,0:T(8,128)(2,1)}, u32[]{:S(2)}) copy-start(bf16[4096,256]{1,0:T(8,128)(2,1)} %value_ref.1) | copy-start | bytes 6291460
  171.3 25.4 %copy-start.4 = (bf16[4096,256]{1,0:T(8,128)(2,1)S(1)}, bf16[4096,256]{1,0:T(8,128)(2,1)}, u32[]{:S(2)}) copy-start(bf16[4096,256]{1,0:T(8,128)(2,1)} %key_ref.1) | copy-start | bytes 6291460
  171.3 6.5 %collective-permute-start.15 = (bf16[272,128]{1,0:T(8,128)(2,1)S(1)}, bf16[272,128]{1,0:T(8,128)(2,1)S(1)}, u32[]{:S(2)}, u32[]{:S(2)}) collective-permute-start(bf16[272,128]{1,0:T(8,128)(2,1)S(1)} %sent_grads.1.refs_0_), channel_id=1, source_target_pairs={{0,16},{16,32},{32,48},{48,0},{1,17},{17,33},{33,49},{49,1},{2,18}... | collective-permute-start | bytes 208904 | tf_op jit(solution)/shard_map/sent_grads/ppermute | solution.py:35
  171.4 6.4 %collective-permute-start.16 = (bf16[272,128]{1,0:T(8,128)(2,1)S(1)}, bf16[272,128]{1,0:T(8,128)(2,1)S(1)}, u32[]{:S(2)}, u32[]{:S(2)}) collective-permute-start(bf16[272,128]{1,0:T(8,128)(2,1)S(1)} %sent_grads.1.refs_0_), channel_id=1, source_target_pairs={{0,32},{16,48},{32,0},{48,16},{1,33},{17,49},{33,1},{49,17},{2,34}... | collective-permute-start | bytes 208904 | tf_op jit(solution)/shard_map/sent_grads/ppermute | solution.py:35
  172.7 5.1 %collective-permute-start.17 = (bf16[272,128]{1,0:T(8,128)(2,1)S(1)}, bf16[272,128]{1,0:T(8,128)(2,1)S(1)}, u32[]{:S(2)}, u32[]{:S(2)}) collective-permute-start(bf16[272,128]{1,0:T(8,128)(2,1)S(1)} %sent_grads.1.refs_0_), channel_id=1, source_target_pairs={{0,48},{16,0},{32,16},{48,32},{1,49},{17,1},{33,17},{49,33},{2,50}... | collective-permute-start | bytes 208904 | tf_op jit(solution)/shard_map/sent_grads/ppermute | solution.py:35
  179.4 11.7 %collective-permute-start.18 = (bf16[272,256]{1,0:T(8,128)(2,1)S(1)}, bf16[272,256]{1,0:T(8,128)(2,1)S(1)}, u32[]{:S(2)}, u32[]{:S(2)}) collective-permute-start(bf16[272,256]{1,0:T(8,128)(2,1)S(1)} %get-tuple-element.30), channel_id=1, source_target_pairs={{0,192},{64,0},{128,64},{192,128},{1,193},{65,1},{129,65},{193,129... | collective-permute-start | bytes 417800 | tf_op jit(solution)/shard_map/attention_grad/ppermute | solution.py:41
  185.2 5.9 %collective-permute-start.19 = (bf16[272,256]{1,0:T(8,128)(2,1)S(1)}, bf16[272,256]{1,0:T(8,128)(2,1)S(1)}, u32[]{:S(2)}, u32[]{:S(2)}) collective-permute-start(bf16[272,256]{1,0:T(8,128)(2,1)S(1)} %get-tuple-element.29), channel_id=1, source_target_pairs={{0,128},{64,192},{128,0},{192,64},{1,129},{65,193},{129,1},{193,65... | collective-permute-start | bytes 417800 | tf_op jit(solution)/shard_map/attention_grad/ppermute | solution.py:41
  185.2 9.1 %collective-permute-start.20 = (bf16[272,256]{1,0:T(8,128)(2,1)S(1)}, bf16[272,256]{1,0:T(8,128)(2,1)S(1)}, u32[]{:S(2)}, u32[]{:S(2)}) collective-permute-start(bf16[272,256]{1,0:T(8,128)(2,1)S(1)} %get-tuple-element.28), channel_id=1, source_target_pairs={{0,64},{64,128},{128,192},{192,0},{1,65},{65,129},{129,193},{193,1... | collective-permute-start | bytes 417800 | tf_op jit(solution)/shard_map/attention_grad/ppermute | solution.py:41
  194.5 2.1 collective-permute-start.21
  200.9 32.8 %all-to-all-start.4 = ((bf16[8,128,512]{2,1,0:T(8,128)(2,1)}), bf16[8,128,512]{2,1,0:T(8,128)(2,1)S(1)}, u32[]{:S(2)}, u32[]{:S(2)}) async-start(bf16[8,128,512]{2,1,0:T(8,128)(2,1)} %d_context.1), calls=%async_computation.4 | async-start | bytes 2097152 | tf_op jit(solution)/shard_map/d_context/all_to_all | solution.py:604
  204.4 1.3 collective-permute-start.22

commit v4 on v3

--- a/solution.py
+++ b/solution.py
@@ -41,20 +41,36 @@
     return [blocks[0]] + [lax.ppermute(blocks[s], axis, routes[s]) for s in range(1, count)]
 
 
-def spread(block, axis):
+def around(block, axis):
     count = lax.axis_size(axis)
-    stacked = jnp.broadcast_to(block[None], (count,) + block.shape)
-    return lax.all_to_all(stacked, axis, 0, 0, tiled=True)
+    up = [(i, (i + 1) % count) for i in range(count)]
+    down = [(i, (i - 1) % count) for i in range(count)]
+    behind, ahead = [block], [block]
+    for _ in range(count // 2 - 1):
+        behind.append(lax.ppermute(behind[-1], axis, up))
+        ahead.append(lax.ppermute(ahead[-1], axis, down))
+    half = block.shape[0] // 2
+    far = [lax.ppermute(behind[-1][:half], axis, up), lax.ppermute(ahead[-1][half:], axis, down)]
+    return behind + far + ahead[:0:-1]
+
+
+def gathered_blocks(refs):
+    half = (len(refs) - 1) // 2
+    far = jnp.concatenate((refs[half][...], refs[half + 1][...]), axis=0)
+    return [r[...] for r in refs[:half]] + [far] + [r[...] for r in refs[half + 2 :]]
+
+
+def owner_of(place_ref, distance, parts):
+    return lax.rem(place_ref[0] + (parts - distance), parts)
 
 
 def swap(block):
     return lax.ppermute(block, "core", [(0, 1), (1, 0)])
 
 
-def to_head(left, right, core):
+def to_head(mine, theirs, core):
     first = core == 0
-    mine = jnp.where(first, left, right)
-    got = swap(jnp.where(first, right, left))
+    got = swap(theirs)
     return jnp.concatenate((jnp.where(first, mine, got), jnp.where(first, got, mine)), axis=0)
 
 
@@ -114,43 +130,115 @@
     return start
 
 
+def fetch(pairs, sems):
+    copies = [pltpu.make_async_copy(f, t, sems.at[i]) for i, (f, t) in enumerate(pairs)]
+    for copy in copies:
+        copy.start()
+    return copies
+
+
 def send_kernel(
-    place_ref, steps_ref, noised_ref, pre_ref, time_ref, post_ref, out_rows_ref, sent_ref, input_ref
+    place_ref,
+    steps_ref,
+    time_ref,
+    noised_ref,
+    pre_ref,
+    post_ref,
+    out_ref,
+    sent_ref,
+    noised,
+    pre,
+    post_part,
+    out_part,
+    sems,
 ):
-    parts = sent_ref.shape[0]
-    rows, share = input_ref.shape
+    rows, features = noised.shape
+    share = pre.shape[1]
     slot = place_ref[2] * place_ref[3] + place_ref[1]
+    lanes = pl.ds(pl.multiple_of(slot // (HDIM // FOLD_POST) * HDIM, HDIM), HDIM)
+    lines = pl.ds(pl.multiple_of(slot // 2 * (2 * FOLD_OUT), 2 * FOLD_OUT), 2 * FOLD_OUT)
+    half = features // 2
+    copies = fetch(
+        (
+            (noised_ref, noised),
+            (pre_ref.at[:half], pre.at[:half]),
+            (pre_ref.at[half:], pre.at[half:]),
+            (post_ref.at[:, lanes], post_part),
+            (out_ref.at[lines], out_part),
+        ),
+        sems,
+    )
     angle = (0.5 * math.pi / TSTEPS) * steps_ref[...].astype(F32)
-    features = dot(noised_ref[...], pre_ref[...]) + column(sine(angle)) * time_ref[...]
-    features = features.astype(BF16)
-    input_ref[...] = features
-    post = post_ref[...].astype(F32).T
+    noise = column(sine(angle)) * time_ref[...]
+    copies[3].wait()
+    post = post_part[...].astype(F32).T
     quarter = lax.rem(slot, HDIM // FOLD_POST)
     post_rows = post[:FOLD_POST]
     for k in range(1, HDIM // FOLD_POST):
         post_rows = jnp.where(quarter == k, post[FOLD_POST * k : FOLD_POST * (k + 1)], post_rows)
-    out_rows = out_rows_ref[...].astype(F32)
+    copies[4].wait()
+    out_rows = out_part[...].astype(F32)
     out_rows = jnp.where(lax.rem(slot, 2) == 0, out_rows[:FOLD_OUT], out_rows[FOLD_OUT:])
+    parts = out_rows.shape[1] // share
     out_rows = [out_rows[:, share * k : share * (k + 1)] for k in range(parts)]
-    rest = jnp.concatenate([post_rows] + out_rows, axis=0).astype(BF16)
+    sent_ref[rows:, :] = jnp.concatenate([post_rows] + out_rows, axis=0).astype(BF16)
+    for k in range(3):
+        copies[k].wait()
+    sent_ref[:rows, :] = (dot(noised[...], pre[...]) + noise).astype(BF16)
+
+
+def project_kernel(
+    place_ref, context_ref, key_ref, value_ref, mine_ref, theirs_ref, context, weight, sems
+):
+    parts = 4
+    share = context.shape[1] // parts
+    pairs = []
     for k in range(parts):
-        sent_ref[k, :rows, :] = features
-        sent_ref[k, rows:, :] = rest
-
-
-def fold_kernel(gathered_ref, w_out_ref, out_ref):
-    parts, _, share = gathered_ref.shape
-    heads = w_out_ref.shape[0]
-    rows = gathered_ref.shape[1] - FOLD_POST - FOLD_OUT * parts
-    middle = rows + FOLD_POST
+        at = pl.ds(share * k, share)
+        pairs.append((context_ref.at[:, at], context.at[:, at]))
+        pairs.append((key_ref.at[at], weight.at[0, at]))
+        pairs.append((value_ref.at[at], weight.at[1, at]))
+    copies = fetch(pairs, sems)
+    keys = jnp.zeros((context.shape[0], 2 * HDIM), F32)
+    values = keys
+    for k in range(parts):
+        at = slice(share * k, share * (k + 1))
+        for copy in copies[3 * k : 3 * k + 3]:
+            copy.wait()
+        keys = keys + dot(context[:, at], weight[0, at])
+        values = values + dot(context[:, at], weight[1, at])
+    left = jnp.concatenate((keys[:, :HDIM], values[:, :HDIM]), axis=1)
+    right = jnp.concatenate((keys[:, HDIM:], values[:, HDIM:]), axis=1)
+    first = place_ref[2] == 0
+    mine_ref[...] = jnp.where(first, left, right).astype(BF16)
+    theirs_ref[...] = jnp.where(first, right, left).astype(BF16)
+
+
+def fold_kernel(place_ref, w_out_ref, *refs):
+    *block_refs, out_ref, weight, sems = refs
+    heads, width = weight.shape
+    blocks = gathered_blocks(block_refs)
+    parts = len(blocks)
+    share = blocks[0].shape[1]
+    half = heads // 2
+    copies = fetch(
+        [(w_out_ref.at[pl.ds(half * k, half)], weight.at[pl.ds(half * k, half)]) for k in range(2)],
+        sems,
+    )
+    span = FOLD_OUT * parts
+    rest = blocks[0].shape[0] - span
+    top = rest - FOLD_POST
+    for copy in copies:
+        copy.wait()
     direct = jnp.zeros((FOLD_POST, heads), F32)
-    span = FOLD_OUT * parts
-    rest = gathered_ref[:, middle:, :].reshape(parts * span, share)
+    for distance, block in enumerate(blocks):
+        owner = owner_of(place_ref, distance, parts)
+        at = pl.ds(pl.multiple_of(owner * share, share), share)
+        direct = direct + dot(block[top:rest], weight[:, at], ((1,), (1,)))
+    rows = jnp.concatenate([block[rest:] for block in blocks], axis=0)
     gram = [jnp.zeros((FOLD_OUT, heads), F32)] * parts
     for k in range(parts):
-        weight = w_out_ref[:, share * k : share * (k + 1)]
-        direct = direct + dot(gathered_ref[k, rows:middle, :], weight, ((1,), (1,)))
-        product = dot(rest, weight, ((1,), (1,)))
+        product = dot(rows, weight[:, share * k : share * (k + 1)], ((1,), (1,)))
         for b in range(parts):
             at = span * b + FOLD_OUT * k
             gram[b] = gram[b] + product[at : at + FOLD_OUT]
@@ -159,22 +247,45 @@
         out_ref[k] = folded
 
 
-def query_kernel(gathered_ref, w_query_ref, w_out_ref, query_ref, cross_ref):
-    parts, _, share = gathered_ref.shape
-    rows = query_ref.shape[0]
-    query = jnp.zeros(query_ref.shape, F32)
-    cross = jnp.zeros(cross_ref.shape, F32)
+def query_kernel(place_ref, w_query_ref, hold_ref, wait_ref, *refs):
+    *block_refs, mine_ref, theirs_ref, weight, sems = refs
+    rows = mine_ref.shape[0]
+    parts, share, _ = weight.shape
+    copies = []
+    for distance in range(parts):
+        owner = owner_of(place_ref, distance, parts)
+        at = pl.ds(pl.multiple_of(owner * share, share), share)
+        copies.append(
+            pltpu.make_async_copy(w_query_ref.at[at], weight.at[distance], sems.at[distance])
+        )
+        copies[-1].start()
+    blocks = gathered_blocks(block_refs)
+    query = jnp.zeros((rows, weight.shape[2]), F32)
     squares = jnp.zeros((rows, 1), F32)
-    for k in range(parts):
-        at = slice(share * k, share * (k + 1))
-        block = gathered_ref[k, :rows, :]
-        wide = block.astype(F32)
+    for distance, block in enumerate(blocks):
+        wide = block[:rows].astype(F32)
         squares = squares + jnp.sum(wide * wide, axis=1, keepdims=True)
-        query = query + dot(block, w_query_ref[at, :])
-        cross = cross + dot(block, w_out_ref[:, at], ((1,), (1,)))
-    scale = lax.rsqrt(squares / (share * parts) + EPSILON)
-    query_ref[...] = (query * scale).astype(BF16)
-    cross_ref[...] = cross
+    for distance, block in enumerate(blocks):
+        copies[distance].wait()
+        query = query + dot(block[:rows], weight[distance])
+    query = (query * lax.rsqrt(squares / (share * parts) + EPSILON)).astype(BF16)
+    first = place_ref[2] == 0
+    mine_ref[...] = jnp.where(first, query[:, :HDIM], query[:, HDIM:])
+    theirs_ref[...] = jnp.where(first, query[:, HDIM:], query[:, :HDIM])
+
+
+def cross_kernel(place_ref, w_out_ref, *refs):
+    *block_refs, out_ref = refs
+    blocks = gathered_blocks(block_refs)
+    parts = len(blocks)
+    share = blocks[0].shape[1]
+    rows, heads = out_ref.shape
+    cross = jnp.zeros((rows, heads), F32)
+    for distance, block in enumerate(blocks):
+        owner = owner_of(place_ref, distance, parts)
+        at = pl.ds(pl.multiple_of(owner * share, share), share)
+        cross = cross + dot(block[:rows], w_out_ref[:, at], ((1,), (1,)))
+    out_ref[...] = cross
 
 
 def line_positions(place_ref):
@@ -271,7 +382,7 @@
 
 
 def norm_kernel(
-    arrived_ref, gram_ref, attended_ref, cross_ref, input_ref, back_ref, out_ref
+    place_ref, arrived_ref, gram_ref, attended_ref, cross_ref, input_ref, back_ref, out_ref
 ):
     parts, own, _ = arrived_ref.shape
     features = out_ref.shape[2] - HDIM
@@ -289,7 +400,7 @@
             ],
             axis=0,
         )
-        back = back + dot(theirs, gram_ref[k])
+        back = back + dot(theirs, gram_ref[owner_of(place_ref, k, parts)])
     back_ref[...] = cross + back
     attended = attended_ref[...].astype(F32)
     features_in = input_ref[...].astype(F32)
@@ -313,7 +424,8 @@
     own_ref,
     other_ref,
     back_ref,
-    grad_ref,
+    mine_ref,
+    theirs_ref,
     loss_ref,
 ):
     parts, own, _ = arrived_ref.shape
@@ -338,7 +450,10 @@
     low, high = both_cores(place_ref, own_ref, other_ref, FOLD_POST)
     half = low.shape[0]
     direct = dot(pred_grad[:, :half], low) + dot(pred_grad[:, half:], high)
-    grad_ref[...] = (inverse * (direct - along * inverse * back_ref[...])).astype(BF16)
+    grad = (inverse * (direct - along * inverse * back_ref[...])).astype(BF16)
+    first = place_ref[2] == 0
+    mine_ref[...] = jnp.where(first, grad[:, :HDIM], grad[:, HDIM:])
+    theirs_ref[...] = jnp.where(first, grad[:, HDIM:], grad[:, :HDIM])
 
 
 def sent_kernel(grad_ref, attended_ref, total_ref, loss_ref, out_ref):
@@ -403,8 +518,10 @@
 
 
 SMEM = pl.BlockSpec(memory_space=pltpu.SMEM)
+HBM = pl.BlockSpec(memory_space=pltpu.HBM)
+ANY = pl.BlockSpec(memory_space=pl.ANY)
 VMEM = pl.BlockSpec(memory_space=pltpu.VMEM)
-PARAMS = pltpu.CompilerParams(vmem_limit_bytes=20 * 1024 * 1024)
+PARAMS = pltpu.CompilerParams(vmem_limit_bytes=32 * 1024 * 1024)
 
 
 def local(
@@ -437,52 +554,48 @@
     steps = step_ids.reshape(1, rows)
 
     with jax.named_scope("inputs"):
-        sent, input_part = pl.pallas_call(
+        sent = pl.pallas_call(
             send_kernel,
-            out_shape=(
-                jax.ShapeDtypeStruct((parts, rows + fold_rows, share), BF16),
-                jax.ShapeDtypeStruct((rows, share), BF16),
-            ),
-            grid_spec=pltpu.PrefetchScalarGridSpec(
-                num_scalar_prefetch=1,
-                grid=(1,),
-                in_specs=[
-                    pl.BlockSpec((1, rows), lambda i, p: (0, 0)),
-                    pl.BlockSpec((rows, features), lambda i, p: (0, 0)),
-                    pl.BlockSpec((features, share), lambda i, p: (0, 0)),
-                    pl.BlockSpec((1, share), lambda i, p: (0, 0)),
-                    pl.BlockSpec(
-                        (share, HDIM),
-                        lambda i, p: (0, (p[2] * p[3] + p[1]) // (HDIM // FOLD_POST)),
-                    ),
-                    pl.BlockSpec((2 * FOLD_OUT, width), lambda i, p: ((p[2] * p[3] + p[1]) // 2, 0)),
-                ],
-                out_specs=(
-                    pl.BlockSpec((parts, rows + fold_rows, share), lambda i, p: (0, 0, 0)),
-                    pl.BlockSpec((rows, share), lambda i, p: (0, 0)),
-                ),
-            ),
-            compiler_params=PARAMS,
-        )(place, steps, noised, w_pre, time_vec.reshape(1, share), w_post, w_out)
-        gathered = lax.all_to_all(sent, "tp", 0, 0, tiled=True)
+            out_shape=jax.ShapeDtypeStruct((rows + fold_rows, share), BF16),
+            in_specs=[SMEM, VMEM, VMEM, HBM, HBM, HBM, HBM],
+            out_specs=VMEM,
+            scratch_shapes=[
+                pltpu.VMEM((rows, features), BF16),
+                pltpu.VMEM((features, share), BF16),
+                pltpu.VMEM((share, HDIM), BF16),
+                pltpu.VMEM((2 * FOLD_OUT, width), BF16),
+                pltpu.SemaphoreType.DMA((5,)),
+            ],
+            compiler_params=PARAMS,
+        )(place, steps, time_vec.reshape(1, share), noised, w_pre, w_post, w_out)
+        blocks = around(sent, "tp")
+        input_part = sent[:rows]
         input_post = dot(input_part, w_post)
     with jax.named_scope("keys_values"):
-        key_rows = dot(context, w_key).astype(BF16)
-        value_rows = dot(context, w_value).astype(BF16)
-        own_kv = to_head(
-            jnp.concatenate((key_rows[:, :HDIM], value_rows[:, :HDIM]), axis=1),
-            jnp.concatenate((key_rows[:, HDIM:], value_rows[:, HDIM:]), axis=1),
-            core,
-        )
+        kv_shape = jax.ShapeDtypeStruct((rows, 2 * HDIM), BF16)
+        mine, theirs = pl.pallas_call(
+            project_kernel,
+            out_shape=(kv_shape, kv_shape),
+            in_specs=[SMEM, HBM, HBM, HBM],
+            out_specs=(VMEM, VMEM),
+            scratch_shapes=[
+                pltpu.VMEM(context.shape, BF16),
+                pltpu.VMEM((2,) + w_key.shape, BF16),
+                pltpu.SemaphoreType.DMA((12,)),
+            ],
+            compiler_params=PARAMS,
+        )(place, context, w_key, w_value)
+        own_kv = to_head(mine, theirs, core)
         all_kv = jnp.stack(shifted(own_kv, "y"))
     with jax.named_scope("fold"):
         folded = pl.pallas_call(
             fold_kernel,
             out_shape=jax.ShapeDtypeStruct((chips, fold_rows, head_width), BF16),
-            in_specs=[VMEM, VMEM],
+            in_specs=[SMEM, HBM] + [VMEM] * len(blocks),
             out_specs=VMEM,
-            compiler_params=PARAMS,
-        )(gathered, w_out)
+            scratch_shapes=[pltpu.VMEM(w_out.shape, BF16), pltpu.SemaphoreType.DMA((2,))],
+            compiler_params=PARAMS,
+        )(place, w_out, *blocks)
         own_fold = lax.all_to_all(folded, CHIPS, 0, 0, tiled=True)
         other_fold = swap(own_fold)
         gram = [f[:, FOLD_POST:].reshape(chips, parts, FOLD_OUT, -1) for f in (own_fold, other_fold)]
@@ -494,17 +607,26 @@
         following = lax.ppermute(concepts[:1], ROWS, [(i + 1, i) for i in range(count - 1)])
         targets = jnp.concatenate((concepts[1:], following), axis=0)
     with jax.named_scope("queries"):
-        queries, cross = pl.pallas_call(
+        query_shape = jax.ShapeDtypeStruct((rows, HDIM), BF16)
+        mine, theirs = pl.pallas_call(
             query_kernel,
-            out_shape=(
-                jax.ShapeDtypeStruct((rows, head_width), BF16),
-                jax.ShapeDtypeStruct((rows, head_width), F32),
-            ),
-            in_specs=[VMEM, VMEM, VMEM],
+            out_shape=(query_shape, query_shape),
+            in_specs=[SMEM, HBM, ANY, ANY] + [VMEM] * len(blocks),
             out_specs=(VMEM, VMEM),
-            compiler_params=PARAMS,
-        )(gathered, w_query, w_out)
-        query_head = to_head(queries[:, :HDIM], queries[:, HDIM:], core)
+            scratch_shapes=[
+                pltpu.VMEM((parts, share, head_width), BF16),
+                pltpu.SemaphoreType.DMA((parts,)),
+            ],
+            compiler_params=PARAMS,
+        )(place, w_query, folded, all_kv, *blocks)
+        query_head = to_head(mine, theirs, core)
+        cross = pl.pallas_call(
+            cross_kernel,
+            out_shape=jax.ShapeDtypeStruct((rows, head_width), F32),
+            in_specs=[SMEM] + [VMEM] * (1 + len(blocks)),
+            out_specs=VMEM,
+            compiler_params=PARAMS,
+        )(place, w_out, *blocks)
         line_queries = jnp.stack(shifted(query_head, "x"))
     with jax.named_scope("attention"):
         sent = pl.pallas_call(
@@ -541,24 +663,25 @@
                 jax.ShapeDtypeStruct((rows, head_width), F32),
                 jax.ShapeDtypeStruct((parts, own, features + HDIM), BF16),
             ),
-            in_specs=[VMEM] * 5,
+            in_specs=[SMEM] + [VMEM] * 5,
             out_specs=(VMEM, VMEM),
             compiler_params=PARAMS,
-        )(arrived, gram, attended, cross, input_part)
+        )(place, arrived, gram, attended, cross, input_part)
         arrived = lax.all_to_all(sent, "tp", 0, 0, tiled=True)
     with jax.named_scope("loss"):
-        attended_grad, loss_part = pl.pallas_call(
+        mine, theirs, loss_part = pl.pallas_call(
             functools.partial(loss_kernel, width),
             out_shape=(
-                jax.ShapeDtypeStruct((rows, head_width), BF16),
+                query_shape,
+                query_shape,
                 jax.ShapeDtypeStruct((1, HDIM), F32),
             ),
             in_specs=[SMEM, SMEM] + [VMEM] * 6,
-            out_specs=(VMEM, VMEM),
+            out_specs=(VMEM, VMEM, VMEM),
             compiler_params=PARAMS,
         )(doc_lengths, place, steps, arrived, targets, own_fold, other_fold, back)
     with jax.named_scope("sent_grads"):
-        grad_head = to_head(attended_grad[:, :HDIM], attended_grad[:, HDIM:], core)
+        grad_head = to_head(mine, theirs, core)
         sent = pl.pallas_call(
             sent_kernel,
             out_shape=jax.ShapeDtypeStruct((PAIR + STATS, HDIM), BF16),

time: 238 us -> 212 us (0.89)
  waiting for transfers between devices: 128 us -> 78.6 us
  starting transfers between devices: 57.6 us -> 73.5 us
  local copies, waits for them, and re-layouts: 22.1 us -> 29.3 us
  Pallas kernels: 18.6 us -> 21.5 us
    all_to_all x1 -> x0, waiting for transfers between devices: 42 us -> none  [local(): gathered = lax.all_to_all(sent, 'tp', 0, 0, tiled=True)]
    ppermute x0 -> x8, starting transfers between devices: none -> 16.3 us  [the longest x3 13.3 us: around(): ahead.append(lax.ppermute(ahead[-1], axis, down))]
    all_to_all x2, waiting for transfers between devices: 29 us -> 17 us  [local(): arrived = lax.all_to_all(sent, 'tp', 0, 0, tiled=True)]
    all_to_all x1 -> x0, starting transfers between devices: 9.15 us -> none  [local(): gathered = lax.all_to_all(sent, 'tp', 0, 0, tiled=True)]
    ppermute x0 -> x8, waiting for transfers between devices: none -> 7.27 us  [the longest x3 3.34 us: around(): ahead.append(lax.ppermute(ahead[-1], axis, down))]
    unnamed x54 -> x102, local copies, waits for them, and re-layouts: 19.1 us -> 25.8 us
    ppermute x6, waiting for transfers between devices: 13.2 us -> 8.08 us  [returned(): lax.ppermute(blocks[s], axis, routes[s])]
    ppermute x7, starting transfers between devices: 7.87 us -> 12.3 us  [swap(): return lax.ppermute(block, 'core', [(0, 1), (1, 0)])]
  transfers between devices with their start and end apart: 28 -> 35, of which waited for: 18 -> 22; matrix products, arithmetic and copies ran while one was open for 3% -> 4% of each run, Pallas kernels for 2% -> 2%
where the time goes in v4:
time: 212 us; the launch traced here: 211 us
  waiting for transfers between devices  78.6 us (37%)
  starting transfers between devices  73.5 us (35%)
  local copies, waits for them, and re-layouts  29.3 us (14%)
  Pallas kernels  21.5 us (10%)
  other arithmetic  3.65 us (2%)
  between operations  3.1 us (1%)
    all_to_all x1, waiting for transfers between devices, local(): arrived = lax.all_to_all(terms, 'tp', 0, 0, tiled=True)  27.2 us
    unnamed x102, local copies, waits for them, and re-layouts  25.8 us
    all_to_all x2, waiting for transfers between devices, local(): arrived = lax.all_to_all(sent, 'tp', 0, 0, tiled=True)  17 us
    ppermute x9, waiting for transfers between devices, shifted(): return [block] + [lax.ppermute(block, axis, route) for route in routes]  15 us
    ppermute x9, starting transfers between devices, shifted(): return [block] + [lax.ppermute(block, axis, route) for route in routes]  14.4 us
    ppermute x3, starting transfers between devices, around(): ahead.append(lax.ppermute(ahead[-1], axis, down))  13.3 us
    ppermute x6, starting transfers between devices, returned(): lax.ppermute(blocks[s], axis, routes[s])  12.3 us
    ppermute x7, starting transfers between devices, swap(): return lax.ppermute(block, 'core', [(0, 1), (1, 0)])  12.3 us
  transfers between devices with their start and end apart: 35, of which 22 were waited for; matrix products, arithmetic and copies ran while one was open for 4% of the time, Pallas kernels for 2%

profile of v4, /device:TPU:1, one launch (start us, length us, event | category | flops | bytes accessed | tf_op | source)
XLA Modules:
  0.0 211.2 jit_solution(17408411744118439484)
XLA Ops:
  0.7 1.6 copy-done
  2.3 1.2 copy-done.12
  3.5 1.2 copy-done.31
  4.8 0.9 copy-done.43
  7.1 1.5 inputs.1.refs_0_
  8.6 6.5 %collective-permute-start.8 = (bf16[224,512]{1,0:T(8,128)(2,1)S(1)}, bf16[224,512]{1,0:T(8,128)(2,1)S(1)}, u32[]{:S(2)}, u32[]{:S(2)}) collective-permute-start(bf16[224,512]{1,0:T(8,128)(2,1)S(1)} %inputs.1.refs_0_), channel_id=1, source_target_pairs={{0,7},{1,0},{2,1},{3,2},{4,3},{5,4},{6,5},{7,6},{8,15},{9,8},{10,9... | collective-permute-start | bytes 688136 | tf_op jit(solution)/shard_map/inputs/ppermute | solution.py:51
  15.1 1.2 copy-done.32
  16.3 1.9 keys_values.1
  18.3 1.0 collective-permute-start
  19.3 3.4 %collective-permute-start.9 = (bf16[224,512]{1,0:T(8,128)(2,1)S(1)}, bf16[224,512]{1,0:T(8,128)(2,1)S(1)}, u32[]{:S(2)}, u32[]{:S(2)}) collective-permute-start(bf16[224,512]{1,0:T(8,128)(2,1)S(1)} %collective-permute-done.8.refs_8_), channel_id=1, source_target_pairs={{0,7},{1,0},{2,1},{3,2},{4,3},{5,4},{6,5},{7,6},{8,15},{9,8},{10,9... | collective-permute-start | bytes 688136 | tf_op jit(solution)/shard_map/inputs/ppermute | solution.py:51
  22.8 3.3 %collective-permute-done.9.refs_7_ = bf16[224,512]{1,0:T(8,128)(2,1)S(1)} collective-permute-done((bf16[224,512]{1,0:T(8,128)(2,1)S(1)}, bf16[224,512]{1,0:T(8,128)(2,1)S(1)}, u32[]{:S(2)}, u32[]{:S(2)}) %collective-permute-start.9) | collective-permute-done | bytes 229408 | tf_op jit(solution)/shard_map/inputs/ppermute | solution.py:51
  26.1 3.4 %collective-permute-start.10 = (bf16[224,512]{1,0:T(8,128)(2,1)S(1)}, bf16[224,512]{1,0:T(8,128)(2,1)S(1)}, u32[]{:S(2)}, u32[]{:S(2)}) collective-permute-start(bf16[224,512]{1,0:T(8,128)(2,1)S(1)} %collective-permute-done.9.refs_7_), channel_id=1, source_target_pairs={{0,7},{1,0},{2,1},{3,2},{4,3},{5,4},{6,5},{7,6},{8,15},{9,8},{10,9... | collective-permute-start | bytes 688136 | tf_op jit(solution)/shard_map/inputs/ppermute | solution.py:51
  29.6 3.0 %collective-permute-start.2 = (bf16[256,256]{1,0:T(8,128)(2,1)S(1)}, bf16[256,256]{1,0:T(8,128)(2,1)S(1)}, u32[]{:S(2)}, u32[]{:S(2)}) collective-permute-start(bf16[256,256]{1,0:T(8,128)(2,1)S(1)} %get-tuple-element.41), channel_id=1, source_target_pairs={{0,128},{64,192},{128,0},{192,64},{1,129},{65,193},{129,1},{193,65... | collective-permute-start | bytes 393224 | tf_op jit(solution)/shard_map/keys_values/ppermute | solution.py:35
  32.9 2.3 %collective-permute-start.3 = (bf16[256,256]{1,0:T(8,128)(2,1)S(1)}, bf16[256,256]{1,0:T(8,128)(2,1)S(1)}, u32[]{:S(2)}, u32[]{:S(2)}) collective-permute-start(bf16[256,256]{1,0:T(8,128)(2,1)S(1)} %get-tuple-element.41), channel_id=1, source_target_pairs={{0,192},{64,0},{128,64},{192,128},{1,193},{65,1},{129,65},{193,129... | collective-permute-start | bytes 393224 | tf_op jit(solution)/shard_map/keys_values/ppermute | solution.py:35
  35.2 2.7 %collective-permute-start.11 = (bf16[112,512]{1,0:T(8,128)(2,1)S(1)}, bf16[112,512]{1,0:T(8,128)(2,1)S(1)}, u32[]{:S(2)}, u32[]{:S(2)}) collective-permute-start(bf16[112,512]{1,0:T(8,128)(2,1)S(1)} %slice.81), channel_id=1, source_target_pairs={{0,7},{1,0},{2,1},{3,2},{4,3},{5,4},{6,5},{7,6},{8,15},{9,8},{10,9... | collective-permute-start | bytes 344072 | tf_op jit(solution)/shard_map/inputs/ppermute | solution.py:53
  39.8 3.3 %collective-permute-done.7.refs_4_ = bf16[112,512]{1,0:T(8,128)(2,1)S(1)} collective-permute-done((bf16[112,512]{1,0:T(8,128)(2,1)S(1)}, bf16[112,512]{1,0:T(8,128)(2,1)S(1)}, u32[]{:S(2)}, u32[]{:S(2)}) %collective-permute-start.7) | collective-permute-done | bytes 114720 | tf_op jit(solution)/shard_map/inputs/ppermute | solution.py:53
  43.1 2.6 %fold.1.hold_ref = bf16[16,96,256]{2,1,0:T(8,128)(2,1)S(1)} custom-call(s32[4]{0:T(128)S(1)} %pad_add_fusion.place_ref, bf16[256,4096]{1,0:T(8,128)(2,1)S(1)} %copy-done.1, bf16[224,512]{1,0:T(8,128)(2,1)S(1)} %inputs.1.refs_0_, bf16[224,512]{1,0:T(8,128)(2,1)S(1)} %collective-permute-done.4.refs_1_, bf16[224,512]{1,0:T(8,128)(2,1)S(1)} %collective-permute-done.5.refs_2_, ...), custom_call_target="tpu_custom_call" | custom-call | tf_op jit(solution)/shard_map/fold/pallas_call | solution.py:591
  45.8 2.7 %queries.2 = (bf16[128,128]{1,0:T(8,128)(2,1)S(1)}, bf16[128,128]{1,0:T(8,128)(2,1)}) custom-call(s32[4]{0:T(128)S(1)} %pad_add_fusion.place_ref, bf16[4096,256]{1,0:T(8,128)(2,1)S(1)} %copy-done.20, bf16[16,96,256]{2,1,0:T(8,128)(2,1)S(1)} %fold.1.hold_ref, bf16[4,256,256]{2,1,0:T(8,128)(2,1)S(1)} %pad_maximum_fusion.wait_ref.kv_ref, ...), custom_call_target="tpu_custom_call" | custom-call | tf_op jit(solution)/shard_map/queries/pallas_call | solution.py:611
  49.2 5.3 %collective-permute-start.12 = (bf16[128,128]{1,0:T(8,128)(2,1)}, bf16[128,128]{1,0:T(8,128)(2,1)}, u32[]{:S(2)}, u32[]{:S(2)}) collective-permute-start(bf16[128,128]{1,0:T(8,128)(2,1)} %get-tuple-element.18), channel_id=1, source_target_pairs={{0,8},{8,0},{1,9},{9,1},{2,10},{10,2},{3,11},{11,3},{4,12},{12,4},... | collective-permute-start | bytes 98312 | tf_op jit(solution)/shard_map/queries/ppermute | solution.py:68
  54.5 4.2 %all-to-all-start = ((bf16[16,96,256]{2,1,0:T(8,128)(2,1)}), bf16[16,96,256]{2,1,0:T(8,128)(2,1)S(1)}, u32[]{:S(2)}, u32[]{:S(2)}) async-start(bf16[16,96,256]{2,1,0:T(8,128)(2,1)} %copy-done.6), calls=%async_computation | async-start | bytes 1572864 | tf_op jit(solution)/shard_map/fold/all_to_all | solution.py:599
  59.5 3.0 %collective-permute-start.14 = (bf16[256,128]{1,0:T(8,128)(2,1)S(1)}, bf16[256,128]{1,0:T(8,128)(2,1)S(1)}, u32[]{:S(2)}, u32[]{:S(2)}) collective-permute-start(bf16[256,128]{1,0:T(8,128)(2,1)S(1)} %get-tuple-element.49), channel_id=1, source_target_pairs={{0,32},{16,48},{32,0},{48,16},{1,33},{17,49},{33,1},{49,17},{2,34}... | collective-permute-start | bytes 196616 | tf_op jit(solution)/shard_map/queries/ppermute | solution.py:35
  62.7 2.4 %collective-permute-start.15 = (bf16[256,128]{1,0:T(8,128)(2,1)S(1)}, bf16[256,128]{1,0:T(8,128)(2,1)S(1)}, u32[]{:S(2)}, u32[]{:S(2)}) collective-permute-start(bf16[256,128]{1,0:T(8,128)(2,1)S(1)} %get-tuple-element.49), channel_id=1, source_target_pairs={{0,48},{16,0},{32,16},{48,32},{1,49},{17,1},{33,17},{49,33},{2,50}... | collective-permute-start | bytes 196616 | tf_op jit(solution)/shard_map/queries/ppermute | solution.py:35
  65.1 6.7 %collective-permute-done.14 = bf16[256,128]{1,0:T(8,128)(2,1)S(1)} collective-permute-done((bf16[256,128]{1,0:T(8,128)(2,1)S(1)}, bf16[256,128]{1,0:T(8,128)(2,1)S(1)}, u32[]{:S(2)}, u32[]{:S(2)}) %collective-permute-start.14) | collective-permute-done | bytes 65568 | tf_op jit(solution)/shard_map/queries/ppermute | solution.py:35
  71.8 1.6 collective-permute-done.13
  73.5 1.6 attention.2
  75.9 1.5 collective-permute-start.17
  77.4 2.0 collective-permute-start.16
  79.4 1.3 collective-permute-done.18.refs_3_
  82.8 2.1 collective-permute-start.20
  85.6 1.6 fusion.input_ref
  91.3 4.4 %all-to-all-start.1 = ((bf16[8,16,3072]{2,1,0:T(8,128)(2,1)}), bf16[8,16,3072]{2,1,0:T(8,128)(2,1)}, u32[]{:S(2)}, u32[]{:S(2)}) async-start(bf16[8,16,3072]{2,1,0:T(8,128)(2,1)} %copy-done.13), calls=%async_computation.1 | async-start | bytes 1572864 | tf_op jit(solution)/shard_map/raw/all_to_all | solution.py:658
  95.8 1.6 slice.86.input_ref
  97.3 0.9 copy-done.8
  98.3 0.9 copy-done.15
  99.2 0.9 copy-done.17
  100.2 0.9 copy-done.22
  101.1 0.9 copy-done.24
  102.0 0.9 copy-done.26
  103.0 0.9 copy-done.28
  104.8 1.4 queries.3.cross_ref
  107.0 10.5 %all-to-all-done.1.arrived_ref = bf16[8,16,3072]{2,1,0:T(8,128)(2,1)} async-done(((bf16[8,16,3072]{2,1,0:T(8,128)(2,1)}), bf16[8,16,3072]{2,1,0:T(8,128)(2,1)}, u32[]{:S(2)}, u32[]{:S(2)}) %all-to-all-start.1) | async-done | bytes 786464 | tf_op jit(solution)/shard_map/raw/all_to_all | solution.py:658
  118.3 1.6 norm.1
  121.3 3.6 %all-to-all-start.2 = ((bf16[8,16,1152]{2,1,0:T(8,128)(2,1)}), bf16[8,16,1152]{2,1,0:T(8,128)(2,1)S(1)}, u32[]{:S(2)}, u32[]{:S(2)}) async-start(bf16[8,16,1152]{2,1,0:T(8,128)(2,1)} %copy-done.42), calls=%async_computation.2 | async-start | bytes 589824 | tf_op jit(solution)/shard_map/norm/all_to_all | solution.py:670
  125.6 2.5 %collective-permute-start.21 = (bf16[1,1024]{1,0:T(2,128)(2,1)S(1)}, bf16[1,1024]{1,0:T(2,128)(2,1)S(1)}, u32[]{:S(2)}, u32[]{:S(2)}) collective-permute-start(bf16[1,1024]{1,0:T(2,128)(2,1)S(1)} %slice.72), channel_id=1, source_target_pairs={{8,0},{16,8},{24,16},{32,24},{40,32},{48,40},{56,48},{64,56},{72,6... | collective-permute-start | bytes 6152 | tf_op jit(solution)/shard_map/targets/ppermute | solution.py:607
  128.1 1.0 slice.71
  129.1 1.4 collective-permute-done.21
  130.5 6.6 %all-to-all-done.2.arrived_ref = bf16[8,16,1152]{2,1,0:T(8,128)(2,1)S(1)} async-done(((bf16[8,16,1152]{2,1,0:T(8,128)(2,1)}), bf16[8,16,1152]{2,1,0:T(8,128)(2,1)S(1)}, u32[]{:S(2)}, u32[]{:S(2)}) %all-to-all-start.2) | async-done | bytes 294944 | tf_op jit(solution)/shard_map/norm/all_to_all | solution.py:670
  137.8 1.1 copy-done.11
  138.9 1.0 copy-done.30
  140.8 1.0 loss.1
  141.8 1.3 collective-permute-start.22
  144.2 2.5 %collective-permute-start.25 = (bf16[272,128]{1,0:T(8,128)(2,1)S(1)}, bf16[272,128]{1,0:T(8,128)(2,1)S(1)}, u32[]{:S(2)}, u32[]{:S(2)}) collective-permute-start(bf16[272,128]{1,0:T(8,128)(2,1)S(1)} %sent_grads.1.refs_0_), channel_id=1, source_target_pairs={{0,48},{16,0},{32,16},{48,32},{1,49},{17,1},{33,17},{49,33},{2,50}... | collective-permute-start | bytes 208904 | tf_op jit(solution)/shard_map/sent_grads/ppermute | solution.py:35
  147.3 2.2 %collective-permute-done.25.refs_3_ = bf16[272,128]{1,0:T(8,128)(2,1)S(1)} collective-permute-done((bf16[272,128]{1,0:T(8,128)(2,1)S(1)}, bf16[272,128]{1,0:T(8,128)(2,1)S(1)}, u32[]{:S(2)}, u32[]{:S(2)}) %collective-permute-start.25) | collective-permute-done | bytes 69664 | tf_op jit(solution)/shard_map/sent_grads/ppermute | solution.py:35
  149.5 1.8 collective-permute-done.24.refs_2_
  151.4 1.9 collective-permute-done.23.refs_1_
  153.3 1.6 attention_grad.2
  154.9 2.9 %collective-permute-start.28 = (bf16[272,256]{1,0:T(8,128)(2,1)S(1)}, bf16[272,256]{1,0:T(8,128)(2,1)S(1)}, u32[]{:S(2)}, u32[]{:S(2)}) collective-permute-start(bf16[272,256]{1,0:T(8,128)(2,1)S(1)} %get-tuple-element.30), channel_id=1, source_target_pairs={{0,64},{64,128},{128,192},{192,0},{1,65},{65,129},{129,193},{193,1... | collective-permute-start | bytes 417800 | tf_op jit(solution)/shard_map/attention_grad/ppermute | solution.py:41
  157.8 5.8 %collective-permute-start.27 = (bf16[272,256]{1,0:T(8,128)(2,1)S(1)}, bf16[272,256]{1,0:T(8,128)(2,1)S(1)}, u32[]{:S(2)}, u32[]{:S(2)}) collective-permute-start(bf16[272,256]{1,0:T(8,128)(2,1)S(1)} %get-tuple-element.31), channel_id=1, source_target_pairs={{0,128},{64,192},{128,0},{192,64},{1,129},{65,193},{129,1},{193,65... | collective-permute-start | bytes 417800 | tf_op jit(solution)/shard_map/attention_grad/ppermute | solution.py:41
  163.5 1.9 collective-permute-done.28.refs_3_
  165.4 3.5 %collective-permute-done.27.refs_2_ = bf16[272,256]{1,0:T(8,128)(2,1)S(1)} collective-permute-done((bf16[272,256]{1,0:T(8,128)(2,1)S(1)}, bf16[272,256]{1,0:T(8,128)(2,1)S(1)}, u32[]{:S(2)}, u32[]{:S(2)}) %collective-permute-start.27) | collective-permute-done | bytes 139296 | tf_op jit(solution)/shard_map/attention_grad/ppermute | solution.py:41
  169.3 2.1 collective-permute-start.29
  172.3 4.2 %d_context.1 = bf16[8,128,512]{2,1,0:T(8,128)(2,1)} custom-call(bf16[128,512]{1,0:T(8,128)(2,1)S(1)} %pad_maximum_fusion.4.grad_ref, bf16[4096,256]{1,0:T(8,128)(2,1)S(1)} %copy-done.3, bf16[4096,256]{1,0:T(8,128)(2,1)S(1)} %copy-done.5), custom_call_target="tpu_custom_call" | custom-call | tf_op jit(solution)/shard_map/d_context/pallas_call | solution.py:715
  176.5 3.6 %all-to-all-start.3 = ((bf16[8,128,512]{2,1,0:T(8,128)(2,1)}), bf16[8,128,512]{2,1,0:T(8,128)(2,1)S(1)}, u32[]{:S(2)}, u32[]{:S(2)}) async-start(bf16[8,128,512]{2,1,0:T(8,128)(2,1)} %d_context.1), calls=%async_computation.3 | async-start | bytes 2097152 | tf_op jit(solution)/shard_map/d_context/all_to_all | solution.py:727
  182.0 27.2 %all-to-all-done.3 = bf16[8,128,512]{2,1,0:T(8,128)(2,1)S(1)} async-done(((bf16[8,128,512]{2,1,0:T(8,128)(2,1)}), bf16[8,128,512]{2,1,0:T(8,128)(2,1)S(1)}, u32[]{:S(2)}, u32[]{:S(2)}) %all-to-all-start.3) | async-done | bytes 1048608 | tf_op jit(solution)/shard_map/d_context/all_to_all | solution.py:727
  (150 shorter events, 24.4 us)
Async XLA Ops:
  0.7 1.6 copy-start
  2.3 1.2 copy-start.12
  3.5 1.2 copy-start.31
  4.8 0.9 copy-start.43
  7.0 8.0 %copy-start.2 = (bf16[4096,256]{1,0:T(8,128)(2,1)S(1)}, bf16[4096,256]{1,0:T(8,128)(2,1)}, u32[]{:S(2)}) copy-start(bf16[4096,256]{1,0:T(8,128)(2,1)} %key_ref.3) | copy-start | bytes 6291460
  7.0 8.0 %copy-start.4 = (bf16[4096,256]{1,0:T(8,128)(2,1)S(1)}, bf16[4096,256]{1,0:T(8,128)(2,1)}, u32[]{:S(2)}) copy-start(bf16[4096,256]{1,0:T(8,128)(2,1)} %value_ref.3) | copy-start | bytes 6291460
  8.6 37.2 %copy-start.7 = (bf16[224,512]{1,0:T(8,128)(2,1)}, bf16[224,512]{1,0:T(8,128)(2,1)S(1)}, u32[]{:S(2)}) copy-start(bf16[224,512]{1,0:T(8,128)(2,1)S(1)} %inputs.1.refs_0_) | copy-start | bytes 688132
  8.6 10.8 %collective-permute-start.8 = (bf16[224,512]{1,0:T(8,128)(2,1)S(1)}, bf16[224,512]{1,0:T(8,128)(2,1)S(1)}, u32[]{:S(2)}, u32[]{:S(2)}) collective-permute-start(bf16[224,512]{1,0:T(8,128)(2,1)S(1)} %inputs.1.refs_0_), channel_id=1, source_target_pairs={{0,7},{1,0},{2,1},{3,2},{4,3},{5,4},{6,5},{7,6},{8,15},{9,8},{10,9... | collective-permute-start | bytes 688136 | tf_op jit(solution)/shard_map/inputs/ppermute | solution.py:51
  15.1 7.7 %collective-permute-start.4 = (bf16[224,512]{1,0:T(8,128)(2,1)S(1)}, bf16[224,512]{1,0:T(8,128)(2,1)S(1)}, u32[]{:S(2)}, u32[]{:S(2)}) collective-permute-start(bf16[224,512]{1,0:T(8,128)(2,1)S(1)} %inputs.1.refs_0_), channel_id=1, source_target_pairs={{0,1},{1,2},{2,3},{3,4},{4,5},{5,6},{6,7},{7,0},{8,9},{9,10},{10,1... | collective-permute-start | bytes 688136 | tf_op jit(solution)/shard_map/inputs/ppermute | solution.py:50
  15.1 1.2 copy-start.32
  18.3 24.9 %copy-start.1 = (bf16[256,4096]{1,0:T(8,128)(2,1)S(1)}, bf16[256,4096]{1,0:T(8,128)(2,1)}, u32[]{:S(2)}) copy-start(bf16[256,4096]{1,0:T(8,128)(2,1)} %w_out_ref.3) | copy-start | bytes 6291460
  18.3 4.5 %collective-permute-start = (bf16[128,256]{1,0:T(8,128)(2,1)S(1)}, bf16[128,256]{1,0:T(8,128)(2,1)S(1)}, u32[]{:S(2)}, u32[]{:S(2)}) collective-permute-start(bf16[128,256]{1,0:T(8,128)(2,1)S(1)} %get-tuple-element.16), channel_id=1, source_target_pairs={{0,8},{8,0},{1,9},{9,1},{2,10},{10,2},{3,11},{11,3},{4,12},{12,4},... | collective-permute-start | bytes 196616 | tf_op jit(solution)/shard_map/keys_values/ppermute | solution.py:68
  19.3 26.4 %copy-start.21 = (bf16[224,512]{1,0:T(8,128)(2,1)}, bf16[224,512]{1,0:T(8,128)(2,1)S(1)}, u32[]{:S(2)}) copy-start(bf16[224,512]{1,0:T(8,128)(2,1)S(1)} %collective-permute-done.8.refs_8_) | copy-start | bytes 688132
  19.3 6.8 %collective-permute-start.9 = (bf16[224,512]{1,0:T(8,128)(2,1)S(1)}, bf16[224,512]{1,0:T(8,128)(2,1)S(1)}, u32[]{:S(2)}, u32[]{:S(2)}) collective-permute-start(bf16[224,512]{1,0:T(8,128)(2,1)S(1)} %collective-permute-done.8.refs_8_), channel_id=1, source_target_pairs={{0,7},{1,0},{2,1},{3,2},{4,3},{5,4},{6,5},{7,6},{8,15},{9,8},{10,9... | collective-permute-start | bytes 688136 | tf_op jit(solution)/shard_map/inputs/ppermute | solution.py:51
  22.8 23.0 %copy-start.23 = (bf16[224,512]{1,0:T(8,128)(2,1)}, bf16[224,512]{1,0:T(8,128)(2,1)S(1)}, u32[]{:S(2)}) copy-start(bf16[224,512]{1,0:T(8,128)(2,1)S(1)} %collective-permute-done.4.refs_1_) | copy-start | bytes 688132
  22.8 6.8 %collective-permute-start.5 = (bf16[224,512]{1,0:T(8,128)(2,1)S(1)}, bf16[224,512]{1,0:T(8,128)(2,1)S(1)}, u32[]{:S(2)}, u32[]{:S(2)}) collective-permute-start(bf16[224,512]{1,0:T(8,128)(2,1)S(1)} %collective-permute-done.4.refs_1_), channel_id=1, source_target_pairs={{0,1},{1,2},{2,3},{3,4},{4,5},{5,6},{6,7},{7,0},{8,9},{9,10},{10,1... | collective-permute-start | bytes 688136 | tf_op jit(solution)/shard_map/inputs/ppermute | solution.py:50
  26.1 19.7 %copy-start.25 = (bf16[224,512]{1,0:T(8,128)(2,1)}, bf16[224,512]{1,0:T(8,128)(2,1)S(1)}, u32[]{:S(2)}) copy-start(bf16[224,512]{1,0:T(8,128)(2,1)S(1)} %collective-permute-done.9.refs_7_) | copy-start | bytes 688132
  26.1 9.1 %collective-permute-start.10 = (bf16[224,512]{1,0:T(8,128)(2,1)S(1)}, bf16[224,512]{1,0:T(8,128)(2,1)S(1)}, u32[]{:S(2)}, u32[]{:S(2)}) collective-permute-start(bf16[224,512]{1,0:T(8,128)(2,1)S(1)} %collective-permute-done.9.refs_7_), channel_id=1, source_target_pairs={{0,7},{1,0},{2,1},{3,2},{4,3},{5,4},{6,5},{7,6},{8,15},{9,8},{10,9... | collective-permute-start | bytes 688136 | tf_op jit(solution)/shard_map/inputs/ppermute | solution.py:51
  29.5 16.3 %copy-start.27 = (bf16[224,512]{1,0:T(8,128)(2,1)}, bf16[224,512]{1,0:T(8,128)(2,1)S(1)}, u32[]{:S(2)}) copy-start(bf16[224,512]{1,0:T(8,128)(2,1)S(1)} %collective-permute-done.5.refs_2_) | copy-start | bytes 688132
  29.5 8.5 %collective-permute-start.6 = (bf16[224,512]{1,0:T(8,128)(2,1)S(1)}, bf16[224,512]{1,0:T(8,128)(2,1)S(1)}, u32[]{:S(2)}, u32[]{:S(2)}) collective-permute-start(bf16[224,512]{1,0:T(8,128)(2,1)S(1)} %collective-permute-done.5.refs_2_), channel_id=1, source_target_pairs={{0,1},{1,2},{2,3},{3,4},{4,5},{5,6},{6,7},{7,0},{8,9},{9,10},{10,1... | collective-permute-start | bytes 688136 | tf_op jit(solution)/shard_map/inputs/ppermute | solution.py:50
  29.6 8.7 %collective-permute-start.2 = (bf16[256,256]{1,0:T(8,128)(2,1)S(1)}, bf16[256,256]{1,0:T(8,128)(2,1)S(1)}, u32[]{:S(2)}, u32[]{:S(2)}) collective-permute-start(bf16[256,256]{1,0:T(8,128)(2,1)S(1)} %get-tuple-element.41), channel_id=1, source_target_pairs={{0,128},{64,192},{128,0},{192,64},{1,129},{65,193},{129,1},{193,65... | collective-permute-start | bytes 393224 | tf_op jit(solution)/shard_map/keys_values/ppermute | solution.py:35
  32.5 6.6 %collective-permute-start.1 = (bf16[256,256]{1,0:T(8,128)(2,1)S(1)}, bf16[256,256]{1,0:T(8,128)(2,1)S(1)}, u32[]{:S(2)}, u32[]{:S(2)}) collective-permute-start(bf16[256,256]{1,0:T(8,128)(2,1)S(1)} %get-tuple-element.41), channel_id=1, source_target_pairs={{0,64},{64,128},{128,192},{192,0},{1,65},{65,129},{129,193},{193,1... | collective-permute-start | bytes 393224 | tf_op jit(solution)/shard_map/keys_values/ppermute | solution.py:35
  32.9 6.2 %collective-permute-start.3 = (bf16[256,256]{1,0:T(8,128)(2,1)S(1)}, bf16[256,256]{1,0:T(8,128)(2,1)S(1)}, u32[]{:S(2)}, u32[]{:S(2)}) collective-permute-start(bf16[256,256]{1,0:T(8,128)(2,1)S(1)} %get-tuple-element.41), channel_id=1, source_target_pairs={{0,192},{64,0},{128,64},{192,128},{1,193},{65,1},{129,65},{193,129... | collective-permute-start | bytes 393224 | tf_op jit(solution)/shard_map/keys_values/ppermute | solution.py:35
  35.2 10.6 %copy-start.14 = (bf16[224,512]{1,0:T(8,128)(2,1)}, bf16[224,512]{1,0:T(8,128)(2,1)S(1)}, u32[]{:S(2)}) copy-start(bf16[224,512]{1,0:T(8,128)(2,1)S(1)} %collective-permute-done.10.refs_6_) | copy-start | bytes 688132
  35.2 4.5 %collective-permute-start.11 = (bf16[112,512]{1,0:T(8,128)(2,1)S(1)}, bf16[112,512]{1,0:T(8,128)(2,1)S(1)}, u32[]{:S(2)}, u32[]{:S(2)}) collective-permute-start(bf16[112,512]{1,0:T(8,128)(2,1)S(1)} %slice.81), channel_id=1, source_target_pairs={{0,7},{1,0},{2,1},{3,2},{4,3},{5,4},{6,5},{7,6},{8,15},{9,8},{10,9... | collective-permute-start | bytes 344072 | tf_op jit(solution)/shard_map/inputs/ppermute | solution.py:53
  38.0 7.8 %copy-start.16 = (bf16[224,512]{1,0:T(8,128)(2,1)}, bf16[224,512]{1,0:T(8,128)(2,1)S(1)}, u32[]{:S(2)}) copy-start(bf16[224,512]{1,0:T(8,128)(2,1)S(1)} %collective-permute-done.6.refs_3_) | copy-start | bytes 688132
  38.0 5.1 %collective-permute-start.7 = (bf16[112,512]{1,0:T(8,128)(2,1)S(1)}, bf16[112,512]{1,0:T(8,128)(2,1)S(1)}, u32[]{:S(2)}, u32[]{:S(2)}) collective-permute-start(bf16[112,512]{1,0:T(8,128)(2,1)S(1)} %slice.80), channel_id=1, source_target_pairs={{0,1},{1,2},{2,3},{3,4},{4,5},{5,6},{6,7},{7,0},{8,9},{9,10},{10,1... | collective-permute-start | bytes 344072 | tf_op jit(solution)/shard_map/inputs/ppermute | solution.py:53
  39.2 6.6 %copy-start.20 = (bf16[4096,256]{1,0:T(8,128)(2,1)S(1)}, bf16[4096,256]{1,0:T(8,128)(2,1)}, u32[]{:S(2)}) copy-start(bf16[4096,256]{1,0:T(8,128)(2,1)} %w_query_ref.1) | copy-start | bytes 6291460
  43.1 2.7 %copy-start.33 = (bf16[112,512]{1,0:T(8,128)(2,1)}, bf16[112,512]{1,0:T(8,128)(2,1)S(1)}, u32[]{:S(2)}) copy-start(bf16[112,512]{1,0:T(8,128)(2,1)S(1)} %collective-permute-done.7.refs_4_) | copy-start | bytes 344068
  45.8 2.7 %copy-start.6 = (bf16[16,96,256]{2,1,0:T(8,128)(2,1)}, bf16[16,96,256]{2,1,0:T(8,128)(2,1)S(1)}, u32[]{:S(2)}) copy-start(bf16[16,96,256]{2,1,0:T(8,128)(2,1)S(1)} %fold.1.hold_ref) | copy-start | bytes 2359300
  49.2 24.3 %copy-start.47 = (s32[4]{0:T(128)S(1)}, s32[4]{0:T(128)}, u32[]{:S(2)}) copy-start(s32[4]{0:T(128)} %lengths_ref.5) | copy-start | bytes 52
  49.2 9.5 %collective-permute-start.12 = (bf16[128,128]{1,0:T(8,128)(2,1)}, bf16[128,128]{1,0:T(8,128)(2,1)}, u32[]{:S(2)}, u32[]{:S(2)}) collective-permute-start(bf16[128,128]{1,0:T(8,128)(2,1)} %get-tuple-element.18), channel_id=1, source_target_pairs={{0,8},{8,0},{1,9},{9,1},{2,10},{10,2},{3,11},{11,3},{4,12},{12,4},... | collective-permute-start | bytes 98312 | tf_op jit(solution)/shard_map/queries/ppermute | solution.py:68
  54.5 28.3 %all-to-all-start = ((bf16[16,96,256]{2,1,0:T(8,128)(2,1)}), bf16[16,96,256]{2,1,0:T(8,128)(2,1)S(1)}, u32[]{:S(2)}, u32[]{:S(2)}) async-start(bf16[16,96,256]{2,1,0:T(8,128)(2,1)} %copy-done.6), calls=%async_computation | async-start | bytes 1572864 | tf_op jit(solution)/shard_map/fold/all_to_all | solution.py:599
  59.5 12.3 %collective-permute-start.14 = (bf16[256,128]{1,0:T(8,128)(2,1)S(1)}, bf16[256,128]{1,0:T(8,128)(2,1)S(1)}, u32[]{:S(2)}, u32[]{:S(2)}) collective-permute-start(bf16[256,128]{1,0:T(8,128)(2,1)S(1)} %get-tuple-element.49), channel_id=1, source_target_pairs={{0,32},{16,48},{32,0},{48,16},{1,33},{17,49},{33,1},{49,17},{2,34}... | collective-permute-start | bytes 196616 | tf_op jit(solution)/shard_map/queries/ppermute | solution.py:35
  62.5 10.9 %collective-permute-start.13 = (bf16[256,128]{1,0:T(8,128)(2,1)S(1)}, bf16[256,128]{1,0:T(8,128)(2,1)S(1)}, u32[]{:S(2)}, u32[]{:S(2)}) collective-permute-start(bf16[256,128]{1,0:T(8,128)(2,1)S(1)} %get-tuple-element.49), channel_id=1, source_target_pairs={{0,16},{16,32},{32,48},{48,0},{1,17},{17,33},{33,49},{49,1},{2,18}... | collective-permute-start | bytes 196616 | tf_op jit(solution)/shard_map/queries/ppermute | solution.py:35
  62.7 10.7 %collective-permute-start.15 = (bf16[256,128]{1,0:T(8,128)(2,1)S(1)}, bf16[256,128]{1,0:T(8,128)(2,1)S(1)}, u32[]{:S(2)}, u32[]{:S(2)}) collective-permute-start(bf16[256,128]{1,0:T(8,128)(2,1)S(1)} %get-tuple-element.49), channel_id=1, source_target_pairs={{0,48},{16,0},{32,16},{48,32},{1,49},{17,1},{33,17},{49,33},{2,50}... | collective-permute-start | bytes 196616 | tf_op jit(solution)/shard_map/queries/ppermute | solution.py:35
  75.8 4.9 %collective-permute-start.18 = (bf16[272,128]{1,0:T(8,128)(2,1)S(1)}, bf16[272,128]{1,0:T(8,128)(2,1)S(1)}, u32[]{:S(2)}, u32[]{:S(2)}) collective-permute-start(bf16[272,128]{1,0:T(8,128)(2,1)S(1)} %get-tuple-element.34), channel_id=1, source_target_pairs={{0,16},{16,32},{32,48},{48,0},{1,17},{17,33},{33,49},{49,1},{2,18}... | collective-permute-start | bytes 208904 | tf_op jit(solution)/shard_map/attention/ppermute | solution.py:41
  75.9 5.4 %collective-permute-start.17 = (bf16[272,128]{1,0:T(8,128)(2,1)S(1)}, bf16[272,128]{1,0:T(8,128)(2,1)S(1)}, u32[]{:S(2)}, u32[]{:S(2)}) collective-permute-start(bf16[272,128]{1,0:T(8,128)(2,1)S(1)} %get-tuple-element.35), channel_id=1, source_target_pairs={{0,32},{16,48},{32,0},{48,16},{1,33},{17,49},{33,1},{49,17},{2,34}... | collective-permute-start | bytes 208904 | tf_op jit(solution)/shard_map/attention/ppermute | solution.py:41
  77.4 4.4 %collective-permute-start.16 = (bf16[272,128]{1,0:T(8,128)(2,1)S(1)}, bf16[272,128]{1,0:T(8,128)(2,1)S(1)}, u32[]{:S(2)}, u32[]{:S(2)}) collective-permute-start(bf16[272,128]{1,0:T(8,128)(2,1)S(1)} %get-tuple-element.36), channel_id=1, source_target_pairs={{0,48},{16,0},{32,16},{48,32},{1,49},{17,1},{33,17},{49,33},{2,50}... | collective-permute-start | bytes 208904 | tf_op jit(solution)/shard_map/attention/ppermute | solution.py:41
  82.8 5.3 %collective-permute-start.20 = (bf16[16,96,256]{2,1,0:T(8,128)(2,1)S(1)}, bf16[16,96,256]{2,1,0:T(8,128)(2,1)S(1)}, u32[]{:S(2)}, u32[]{:S(2)}) collective-permute-start(bf16[16,96,256]{2,1,0:T(8,128)(2,1)S(1)} %all-to-all-done.own_ref), channel_id=1, source_target_pairs={{0,8},{8,0},{1,9},{9,1},{2,10},{10,2},{3,11},{11,3},{4,12},{12,4},... | collective-permute-start | bytes 2359304 | tf_op jit(solution)/shard_map/fold/ppermute | solution.py:68
  85.6 1.6 collective-permute-start.19
  91.3 26.1 %all-to-all-start.1 = ((bf16[8,16,3072]{2,1,0:T(8,128)(2,1)}), bf16[8,16,3072]{2,1,0:T(8,128)(2,1)}, u32[]{:S(2)}, u32[]{:S(2)}) async-start(bf16[8,16,3072]{2,1,0:T(8,128)(2,1)} %copy-done.13), calls=%async_computation.1 | async-start | bytes 1572864 | tf_op jit(solution)/shard_map/raw/all_to_all | solution.py:658
  104.8 1.4 copy-start.10
  106.3 11.1 %copy-start.36 = (bf16[128,256]{1,0:T(8,128)(2,1)S(1)}, bf16[128,256]{1,0:T(8,128)(2,1)}, u32[]{:S(2)}) copy-start(bf16[128,256]{1,0:T(8,128)(2,1)} %copy-done.35) | copy-start | bytes 196612
  106.3 11.1 %copy-start.41 = (bf16[128,512]{1,0:T(8,128)(2,1)S(1)}, bf16[128,512]{1,0:T(8,128)(2,1)}, u32[]{:S(2)}) copy-start(bf16[128,512]{1,0:T(8,128)(2,1)} %slice.86.input_ref) | copy-start | bytes 393220
  106.9 30.8 %copy-start.50 = (s32[128]{0:T(128)S(1)}, s32[128]{0:T(128)}, u32[]{:S(2)}) copy-start(s32[128]{0:T(128)} %param.14) | copy-start | bytes 1540
  121.3 22.8 %copy-start.38 = (bf16[256,128]{1,0:T(8,128)(2,1)S(1)}, bf16[256,128]{1,0:T(8,128)(2,1)}, u32[]{:S(2)}) copy-start(bf16[256,128]{1,0:T(8,128)(2,1)} %copy-done.37) | copy-start | bytes 196612
  121.3 32.0 %copy-start.19 = (bf16[4,256,128]{2,1,0:T(8,128)(2,1)S(1)}, bf16[4,256,128]{2,1,0:T(8,128)(2,1)}, u32[]{:S(2)}) copy-start(bf16[4,256,128]{2,1,0:T(8,128)(2,1)} %copy-done.18) | copy-start | bytes 786436
  121.3 15.8 %all-to-all-start.2 = ((bf16[8,16,1152]{2,1,0:T(8,128)(2,1)}), bf16[8,16,1152]{2,1,0:T(8,128)(2,1)S(1)}, u32[]{:S(2)}, u32[]{:S(2)}) async-start(bf16[8,16,1152]{2,1,0:T(8,128)(2,1)} %copy-done.42), calls=%async_computation.2 | async-start | bytes 589824 | tf_op jit(solution)/shard_map/norm/all_to_all | solution.py:670
  125.6 4.9 %collective-permute-start.21 = (bf16[1,1024]{1,0:T(2,128)(2,1)S(1)}, bf16[1,1024]{1,0:T(2,128)(2,1)S(1)}, u32[]{:S(2)}, u32[]{:S(2)}) collective-permute-start(bf16[1,1024]{1,0:T(2,128)(2,1)S(1)} %slice.72), channel_id=1, source_target_pairs={{8,0},{16,8},{24,16},{32,24},{40,32},{48,40},{56,48},{64,56},{72,6... | collective-permute-start | bytes 6152 | tf_op jit(solution)/shard_map/targets/ppermute | solution.py:607
  137.8 1.1 copy-start.11
  138.9 1.0 copy-start.30
  141.8 2.2 %collective-permute-start.22 = (bf16[128,128]{1,0:T(8,128)(2,1)S(1)}, bf16[128,128]{1,0:T(8,128)(2,1)S(1)}, u32[]{:S(2)}, u32[]{:S(2)}) collective-permute-start(bf16[128,128]{1,0:T(8,128)(2,1)S(1)} %get-tuple-element.23), channel_id=1, source_target_pairs={{0,8},{8,0},{1,9},{9,1},{2,10},{10,2},{3,11},{11,3},{4,12},{12,4},... | collective-permute-start | bytes 98312 | tf_op jit(solution)/shard_map/sent_grads/ppermute | solution.py:68
  144.0 28.2 %copy-start.5 = (bf16[4096,256]{1,0:T(8,128)(2,1)S(1)}, bf16[4096,256]{1,0:T(8,128)(2,1)}, u32[]{:S(2)}) copy-start(bf16[4096,256]{1,0:T(8,128)(2,1)} %value_ref.3) | copy-start | bytes 6291460
  144.2 28.1 %copy-start.3 = (bf16[4096,256]{1,0:T(8,128)(2,1)S(1)}, bf16[4096,256]{1,0:T(8,128)(2,1)}, u32[]{:S(2)}) copy-start(bf16[4096,256]{1,0:T(8,128)(2,1)} %key_ref.3) | copy-start | bytes 6291460
  144.2 5.3 %collective-permute-start.25 = (bf16[272,128]{1,0:T(8,128)(2,1)S(1)}, bf16[272,128]{1,0:T(8,128)(2,1)S(1)}, u32[]{:S(2)}, u32[]{:S(2)}) collective-permute-start(bf16[272,128]{1,0:T(8,128)(2,1)S(1)} %sent_grads.1.refs_0_), channel_id=1, source_target_pairs={{0,48},{16,0},{32,16},{48,32},{1,49},{17,1},{33,17},{49,33},{2,50}... | collective-permute-start | bytes 208904 | tf_op jit(solution)/shard_map/sent_grads/ppermute | solution.py:35
  146.6 4.7 %collective-permute-start.24 = (bf16[272,128]{1,0:T(8,128)(2,1)S(1)}, bf16[272,128]{1,0:T(8,128)(2,1)S(1)}, u32[]{:S(2)}, u32[]{:S(2)}) collective-permute-start(bf16[272,128]{1,0:T(8,128)(2,1)S(1)} %sent_grads.1.refs_0_), channel_id=1, source_target_pairs={{0,32},{16,48},{32,0},{48,16},{1,33},{17,49},{33,1},{49,17},{2,34}... | collective-permute-start | bytes 208904 | tf_op jit(solution)/shard_map/sent_grads/ppermute | solution.py:35
  147.0 6.2 %collective-permute-start.23 = (bf16[272,128]{1,0:T(8,128)(2,1)S(1)}, bf16[272,128]{1,0:T(8,128)(2,1)S(1)}, u32[]{:S(2)}, u32[]{:S(2)}) collective-permute-start(bf16[272,128]{1,0:T(8,128)(2,1)S(1)} %sent_grads.1.refs_0_), channel_id=1, source_target_pairs={{0,16},{16,32},{32,48},{48,0},{1,17},{17,33},{33,49},{49,1},{2,18}... | collective-permute-start | bytes 208904 | tf_op jit(solution)/shard_map/sent_grads/ppermute | solution.py:35
  154.9 10.5 %collective-permute-start.28 = (bf16[272,256]{1,0:T(8,128)(2,1)S(1)}, bf16[272,256]{1,0:T(8,128)(2,1)S(1)}, u32[]{:S(2)}, u32[]{:S(2)}) collective-permute-start(bf16[272,256]{1,0:T(8,128)(2,1)S(1)} %get-tuple-element.30), channel_id=1, source_target_pairs={{0,64},{64,128},{128,192},{192,0},{1,65},{65,129},{129,193},{193,1... | collective-permute-start | bytes 417800 | tf_op jit(solution)/shard_map/attention_grad/ppermute | solution.py:41
  157.8 11.2 %collective-permute-start.27 = (bf16[272,256]{1,0:T(8,128)(2,1)S(1)}, bf16[272,256]{1,0:T(8,128)(2,1)S(1)}, u32[]{:S(2)}, u32[]{:S(2)}) collective-permute-start(bf16[272,256]{1,0:T(8,128)(2,1)S(1)} %get-tuple-element.31), channel_id=1, source_target_pairs={{0,128},{64,192},{128,0},{192,64},{1,129},{65,193},{129,1},{193,65... | collective-permute-start | bytes 417800 | tf_op jit(solution)/shard_map/attention_grad/ppermute | solution.py:41
  163.5 5.6 %collective-permute-start.26 = (bf16[272,256]{1,0:T(8,128)(2,1)S(1)}, bf16[272,256]{1,0:T(8,128)(2,1)S(1)}, u32[]{:S(2)}, u32[]{:S(2)}) collective-permute-start(bf16[272,256]{1,0:T(8,128)(2,1)S(1)} %get-tuple-element.32), channel_id=1, source_target_pairs={{0,192},{64,0},{128,64},{192,128},{1,193},{65,1},{129,65},{193,129... | collective-permute-start | bytes 417800 | tf_op jit(solution)/shard_map/attention_grad/ppermute | solution.py:41
  169.3 3.0 %collective-permute-start.29 = (bf16[128,256]{1,0:T(8,128)(2,1)S(1)}, bf16[128,256]{1,0:T(8,128)(2,1)S(1)}, u32[]{:S(2)}, u32[]{:S(2)}) collective-permute-start(bf16[128,256]{1,0:T(8,128)(2,1)S(1)} %broadcast_select_fusion.2), channel_id=1, source_target_pairs={{0,8},{8,0},{1,9},{9,1},{2,10},{10,2},{3,11},{11,3},{4,12},{12,4},... | collective-permute-start | bytes 196616 | tf_op jit(solution)/shard_map/attention_grad/ppermute | solution.py:68
  176.5 32.8 %all-to-all-start.3 = ((bf16[8,128,512]{2,1,0:T(8,128)(2,1)}), bf16[8,128,512]{2,1,0:T(8,128)(2,1)S(1)}, u32[]{:S(2)}, u32[]{:S(2)}) async-start(bf16[8,128,512]{2,1,0:T(8,128)(2,1)} %d_context.1), calls=%async_computation.3 | async-start | bytes 2097152 | tf_op jit(solution)/shard_map/d_context/all_to_all | solution.py:727
  180.0 1.3 collective-permute-start.30
  (22 other events, 17.6 us)

commit v5 on v4

--- a/solution.py
+++ b/solution.py
@@ -214,78 +214,48 @@
     theirs_ref[...] = jnp.where(first, right, left).astype(BF16)
 
 
-def fold_kernel(place_ref, w_out_ref, *refs):
-    *block_refs, out_ref, weight, sems = refs
-    heads, width = weight.shape
+def gathered_kernel(place_ref, w_query_ref, w_out_ref, post_ref, hold_ref, *refs):
+    block_refs, refs = refs[:-6], refs[-6:]
+    mine_ref, theirs_ref, cross_ref, post_out_ref, input_ref, folded_ref = refs
+    rows = mine_ref.shape[0]
+    heads, width = w_out_ref.shape
     blocks = gathered_blocks(block_refs)
+    squares = jnp.zeros((rows, 1), F32)
+    for block in blocks:
+        wide = block[:rows].astype(F32)
+        squares = squares + jnp.sum(wide * wide, axis=1, keepdims=True)
+    query = jnp.zeros((rows, heads), F32)
     parts = len(blocks)
     share = blocks[0].shape[1]
-    half = heads // 2
-    copies = fetch(
-        [(w_out_ref.at[pl.ds(half * k, half)], weight.at[pl.ds(half * k, half)]) for k in range(2)],
-        sems,
-    )
-    span = FOLD_OUT * parts
-    rest = blocks[0].shape[0] - span
-    top = rest - FOLD_POST
-    for copy in copies:
-        copy.wait()
-    direct = jnp.zeros((FOLD_POST, heads), F32)
     for distance, block in enumerate(blocks):
         owner = owner_of(place_ref, distance, parts)
         at = pl.ds(pl.multiple_of(owner * share, share), share)
-        direct = direct + dot(block[top:rest], weight[:, at], ((1,), (1,)))
-    rows = jnp.concatenate([block[rest:] for block in blocks], axis=0)
+        query = query + dot(block[:rows], w_query_ref[at, :])
+    query = (query * lax.rsqrt(squares / width + EPSILON)).astype(BF16)
+    first = place_ref[2] == 0
+    mine_ref[...] = jnp.where(first, query[:, :HDIM], query[:, HDIM:])
+    theirs_ref[...] = jnp.where(first, query[:, HDIM:], query[:, :HDIM])
+
+    top = rows + FOLD_POST
+    both = jnp.zeros((top, heads), F32)
+    for distance, block in enumerate(blocks):
+        owner = owner_of(place_ref, distance, parts)
+        at = pl.ds(pl.multiple_of(owner * share, share), share)
+        both = both + dot(block[:top], w_out_ref[:, at], ((1,), (1,)))
+    cross_ref[...] = both[:rows]
+    span = FOLD_OUT * parts
+    slices = jnp.concatenate([block[top:] for block in blocks], axis=0)
     gram = [jnp.zeros((FOLD_OUT, heads), F32)] * parts
     for k in range(parts):
-        product = dot(rows, weight[:, share * k : share * (k + 1)], ((1,), (1,)))
+        product = dot(slices, w_out_ref[:, share * k : share * (k + 1)], ((1,), (1,)))
         for b in range(parts):
             at = span * b + FOLD_OUT * k
             gram[b] = gram[b] + product[at : at + FOLD_OUT]
-    folded = jnp.concatenate([direct] + gram, axis=0).astype(BF16)
-    for k in range(out_ref.shape[0]):
-        out_ref[k] = folded
-
-
-def query_kernel(place_ref, w_query_ref, hold_ref, wait_ref, *refs):
-    *block_refs, mine_ref, theirs_ref, weight, sems = refs
-    rows = mine_ref.shape[0]
-    parts, share, _ = weight.shape
-    copies = []
-    for distance in range(parts):
-        owner = owner_of(place_ref, distance, parts)
-        at = pl.ds(pl.multiple_of(owner * share, share), share)
-        copies.append(
-            pltpu.make_async_copy(w_query_ref.at[at], weight.at[distance], sems.at[distance])
-        )
-        copies[-1].start()
-    blocks = gathered_blocks(block_refs)
-    query = jnp.zeros((rows, weight.shape[2]), F32)
-    squares = jnp.zeros((rows, 1), F32)
-    for distance, block in enumerate(blocks):
-        wide = block[:rows].astype(F32)
-        squares = squares + jnp.sum(wide * wide, axis=1, keepdims=True)
-    for distance, block in enumerate(blocks):
-        copies[distance].wait()
-        query = query + dot(block[:rows], weight[distance])
-    query = (query * lax.rsqrt(squares / (share * parts) + EPSILON)).astype(BF16)
-    first = place_ref[2] == 0
-    mine_ref[...] = jnp.where(first, query[:, :HDIM], query[:, HDIM:])
-    theirs_ref[...] = jnp.where(first, query[:, HDIM:], query[:, :HDIM])
-
-
-def cross_kernel(place_ref, w_out_ref, *refs):
-    *block_refs, out_ref = refs
-    blocks = gathered_blocks(block_refs)
-    parts = len(blocks)
-    share = blocks[0].shape[1]
-    rows, heads = out_ref.shape
-    cross = jnp.zeros((rows, heads), F32)
-    for distance, block in enumerate(blocks):
-        owner = owner_of(place_ref, distance, parts)
-        at = pl.ds(pl.multiple_of(owner * share, share), share)
-        cross = cross + dot(block[:rows], w_out_ref[:, at], ((1,), (1,)))
-    out_ref[...] = cross
+    folded = jnp.concatenate([both[rows:]] + gram, axis=0).astype(BF16)
+    for k in range(folded_ref.shape[0]):
+        folded_ref[k] = folded
+    post_out_ref[...] = dot(blocks[0][:rows], post_ref[...])
+    input_ref[...] = blocks[0][:rows]
 
 
 def line_positions(place_ref):
@@ -367,7 +337,7 @@
     return jnp.where(first, own, other), jnp.where(first, other, own)
 
 
-def raw_kernel(place_ref, attended_ref, own_ref, other_ref, input_ref, out_ref):
+def raw_kernel(place_ref, attended_ref, own_ref, other_ref, input_ref, hold_ref, out_ref):
     parts, own, _ = out_ref.shape
     attended = attended_ref[...]
     low, high = both_cores(place_ref, own_ref, other_ref, FOLD_POST)
@@ -382,17 +352,33 @@
 
 
 def norm_kernel(
-    place_ref, arrived_ref, gram_ref, attended_ref, cross_ref, input_ref, back_ref, out_ref
+    place_ref,
+    arrived_ref,
+    own_ref,
+    other_ref,
+    attended_ref,
+    cross_ref,
+    input_ref,
+    back_ref,
+    out_ref,
 ):
     parts, own, _ = arrived_ref.shape
     features = out_ref.shape[2] - HDIM
+    rows, share = input_ref.shape
     wide = attended_ref.shape[1]
     total = arrived_ref[0, :, :features].astype(F32)
     for k in range(1, parts):
         total = total + arrived_ref[k, :, :features].astype(F32)
     cross = cross_ref[...]
     back = jnp.zeros_like(cross)
-    for k in range(parts):
+    first = place_ref[2] == 0
+    chips = own_ref.shape[0]
+    grams = []
+    for ref in (own_ref, other_ref):
+        gram = ref[:, FOLD_POST:, :].astype(F32)
+        grams.append(gram.reshape(chips, parts, FOLD_OUT, wide))
+    for distance in range(parts):
+        k = owner_of(place_ref, distance, parts)
         theirs = jnp.concatenate(
             [
                 arrived_ref[k, :, features + wide * j : features + wide * (j + 1)]
@@ -400,7 +386,10 @@
             ],
             axis=0,
         )
-        back = back + dot(theirs, gram_ref[owner_of(place_ref, k, parts)])
+        half = chips * FOLD_OUT
+        own_gram, other_gram = (g[:, distance].reshape(half, wide).astype(BF16) for g in grams)
+        back = back + dot(theirs[:, :half], jnp.where(first, own_gram, other_gram))
+        back = back + dot(theirs[:, half:], jnp.where(first, other_gram, own_gram))
     back_ref[...] = cross + back
     attended = attended_ref[...].astype(F32)
     features_in = input_ref[...].astype(F32)
@@ -485,36 +474,47 @@
     tail = jnp.concatenate((tail, tail), axis=1).astype(BF16)
     steps = key_steps(place_ref, ends)
     for step in range(out_ref.shape[0]):
-        out_ref[step, PAIR:, :] = tail
+        row = lax.rem(place_ref[1] // GROUP + (out_ref.shape[0] - step), out_ref.shape[0])
+        out_ref[row, PAIR:, :] = tail
 
         @pl.when(step < steps)
         def _():
             allowed = allowed_pairs(place_ref, step, query_start, query_pos)
             scores = dot(kv_ref[step, :, :HDIM], q, ((1,), (1,))) * SCALE
             probs = jnp.where(allowed, jnp.exp(scores - log_total), 0.0)
-            out_ref[step, :PAIR, HDIM:] = dot(probs.astype(BF16), grad).astype(BF16)
+            out_ref[row, :PAIR, HDIM:] = dot(probs.astype(BF16), grad).astype(BF16)
             prob_grad = dot(kv_ref[step, :, HDIM:], grad, ((1,), (1,)))
             score_grad = (probs * (prob_grad - output_dot) * SCALE).astype(BF16)
-            out_ref[step, :PAIR, :HDIM] = dot(score_grad, q).astype(BF16)
+            out_ref[row, :PAIR, :HDIM] = dot(score_grad, q).astype(BF16)
 
         @pl.when(step >= steps)
         def _():
-            out_ref[step, :PAIR, :] = jnp.zeros((PAIR, 2 * HDIM), BF16)
+            out_ref[row, :PAIR, :] = jnp.zeros((PAIR, 2 * HDIM), BF16)
 
 
 def collect_kernel(*refs):
-    *part_refs, out_ref, loss_ref = refs
-    total = functools.reduce(jnp.add, [ref[...].astype(F32) for ref in part_refs])
+    arrived_ref, out_ref, loss_ref = refs
+    parts = [arrived_ref[k].astype(F32) for k in range(arrived_ref.shape[0])]
+    total = functools.reduce(jnp.add, parts)
     out_ref[...] = total[:PAIR].astype(BF16)
     rows = total[PAIR : PAIR + 3, :HDIM]
     loss_ref[...] = jnp.sum(rows, axis=0, keepdims=True)
 
 
-def context_kernel(grad_ref, key_ref, value_ref, out_ref):
-    key_grad = jnp.concatenate((grad_ref[:, :HDIM], grad_ref[:, 2 * HDIM : 3 * HDIM]), axis=1)
-    value_grad = jnp.concatenate((grad_ref[:, HDIM : 2 * HDIM], grad_ref[:, 3 * HDIM :]), axis=1)
-    total = dot(key_grad, key_ref[...], ((1,), (1,))) + dot(value_grad, value_ref[...], ((1,), (1,)))
-    out_ref[0] = total.astype(BF16)
+def context_kernel(grad_ref, hold_ref, key_ref, value_ref, out_ref):
+    grad = grad_ref[...].astype(F32).T.astype(BF16)
+    key_grad = jnp.concatenate((grad[:HDIM], grad[2 * HDIM : 3 * HDIM]), axis=0)
+    value_grad = jnp.concatenate((grad[HDIM : 2 * HDIM], grad[3 * HDIM :]), axis=0)
+    parts, share, _ = out_ref.shape
+    for k in range(parts):
+        at = slice(share * k, share * (k + 1))
+        total = dot(key_ref[at], key_grad) + dot(value_ref[at], value_grad)
+        out_ref[k] = total.astype(BF16)
+
+
+def total_kernel(arrived_ref, out_ref):
+    parts = [arrived_ref[k].astype(F32) for k in range(arrived_ref.shape[0])]
+    out_ref[...] = functools.reduce(jnp.add, parts).T.astype(BF16)
 
 
 SMEM = pl.BlockSpec(memory_space=pltpu.SMEM)
@@ -522,6 +522,7 @@
 ANY = pl.BlockSpec(memory_space=pl.ANY)
 VMEM = pl.BlockSpec(memory_space=pltpu.VMEM)
 PARAMS = pltpu.CompilerParams(vmem_limit_bytes=32 * 1024 * 1024)
+WHOLE = pltpu.CompilerParams(vmem_limit_bytes=60 * 1024 * 1024)
 
 
 def local(
@@ -566,11 +567,9 @@
                 pltpu.VMEM((2 * FOLD_OUT, width), BF16),
                 pltpu.SemaphoreType.DMA((5,)),
             ],
-            compiler_params=PARAMS,
+            compiler_params=WHOLE,
         )(place, steps, time_vec.reshape(1, share), noised, w_pre, w_post, w_out)
         blocks = around(sent, "tp")
-        input_part = sent[:rows]
-        input_post = dot(input_part, w_post)
     with jax.named_scope("keys_values"):
         kv_shape = jax.ShapeDtypeStruct((rows, 2 * HDIM), BF16)
         mine, theirs = pl.pallas_call(
@@ -587,47 +586,30 @@
         )(place, context, w_key, w_value)
         own_kv = to_head(mine, theirs, core)
         all_kv = jnp.stack(shifted(own_kv, "y"))
-    with jax.named_scope("fold"):
-        folded = pl.pallas_call(
-            fold_kernel,
-            out_shape=jax.ShapeDtypeStruct((chips, fold_rows, head_width), BF16),
-            in_specs=[SMEM, HBM] + [VMEM] * len(blocks),
-            out_specs=VMEM,
-            scratch_shapes=[pltpu.VMEM(w_out.shape, BF16), pltpu.SemaphoreType.DMA((2,))],
-            compiler_params=PARAMS,
-        )(place, w_out, *blocks)
-        own_fold = lax.all_to_all(folded, CHIPS, 0, 0, tiled=True)
-        other_fold = swap(own_fold)
-        gram = [f[:, FOLD_POST:].reshape(chips, parts, FOLD_OUT, -1) for f in (own_fold, other_fold)]
-        first = core == 0
-        gram = jnp.stack((jnp.where(first, gram[0], gram[1]), jnp.where(first, gram[1], gram[0])))
-        gram = gram.transpose(2, 0, 1, 3, 4).reshape(parts, 2 * chips * FOLD_OUT, -1)
     with jax.named_scope("targets"):
         count = lax.axis_size(ROWS)
         following = lax.ppermute(concepts[:1], ROWS, [(i + 1, i) for i in range(count - 1)])
         targets = jnp.concatenate((concepts[1:], following), axis=0)
-    with jax.named_scope("queries"):
+    with jax.named_scope("gathered"):
         query_shape = jax.ShapeDtypeStruct((rows, HDIM), BF16)
-        mine, theirs = pl.pallas_call(
-            query_kernel,
-            out_shape=(query_shape, query_shape),
-            in_specs=[SMEM, HBM, ANY, ANY] + [VMEM] * len(blocks),
-            out_specs=(VMEM, VMEM),
-            scratch_shapes=[
-                pltpu.VMEM((parts, share, head_width), BF16),
-                pltpu.SemaphoreType.DMA((parts,)),
-            ],
-            compiler_params=PARAMS,
-        )(place, w_query, folded, all_kv, *blocks)
+        mine, theirs, cross, input_post, input_part, folded = pl.pallas_call(
+            gathered_kernel,
+            out_shape=(
+                query_shape,
+                query_shape,
+                jax.ShapeDtypeStruct((rows, head_width), F32),
+                jax.ShapeDtypeStruct((rows, features), F32),
+                jax.ShapeDtypeStruct((rows, share), BF16),
+                jax.ShapeDtypeStruct((chips, fold_rows, head_width), BF16),
+            ),
+            in_specs=[SMEM, VMEM, VMEM, VMEM, ANY] + [VMEM] * len(blocks),
+            out_specs=(VMEM,) * 6,
+            compiler_params=PARAMS,
+        )(place, w_query, w_out, w_post, all_kv, *blocks)
         query_head = to_head(mine, theirs, core)
-        cross = pl.pallas_call(
-            cross_kernel,
-            out_shape=jax.ShapeDtypeStruct((rows, head_width), F32),
-            in_specs=[SMEM] + [VMEM] * (1 + len(blocks)),
-            out_specs=VMEM,
-            compiler_params=PARAMS,
-        )(place, w_out, *blocks)
         line_queries = jnp.stack(shifted(query_head, "x"))
+        own_fold = lax.all_to_all(folded, CHIPS, 0, 0, tiled=True)
+        other_fold = swap(own_fold)
     with jax.named_scope("attention"):
         sent = pl.pallas_call(
             forward_kernel,
@@ -651,10 +633,10 @@
         sent = pl.pallas_call(
             raw_kernel,
             out_shape=jax.ShapeDtypeStruct((parts, own, features + head_width * parts), BF16),
-            in_specs=[SMEM, VMEM, VMEM, VMEM, VMEM],
+            in_specs=[SMEM, VMEM, VMEM, VMEM, VMEM, ANY],
             out_specs=VMEM,
             compiler_params=PARAMS,
-        )(place, attended, own_fold, other_fold, input_post)
+        )(place, attended, own_fold, other_fold, input_post, targets)
         arrived = lax.all_to_all(sent, "tp", 0, 0, tiled=True)
     with jax.named_scope("norm"):
         back, sent = pl.pallas_call(
@@ -663,10 +645,10 @@
                 jax.ShapeDtypeStruct((rows, head_width), F32),
                 jax.ShapeDtypeStruct((parts, own, features + HDIM), BF16),
             ),
-            in_specs=[SMEM] + [VMEM] * 5,
+            in_specs=[SMEM] + [VMEM] * 6,
             out_specs=(VMEM, VMEM),
             compiler_params=PARAMS,
-        )(place, arrived, gram, attended, cross, input_part)
+        )(place, arrived, own_fold, other_fold, attended, cross, input_part)
         arrived = lax.all_to_all(sent, "tp", 0, 0, tiled=True)
     with jax.named_scope("loss"):
         mine, theirs, loss_part = pl.pallas_call(
@@ -704,28 +686,28 @@
                 jax.ShapeDtypeStruct((PAIR, 2 * HDIM), BF16),
                 jax.ShapeDtypeStruct((1, HDIM), F32),
             ),
-            in_specs=[VMEM] * (chips // GROUP),
+            in_specs=[VMEM],
             out_specs=(VMEM, VMEM),
             compiler_params=PARAMS,
-        )(*returned(sent, "y"))
+        )(lax.all_to_all(sent, "y", 0, 0, tiled=True))
         kv_grad = to_rows(kv_grad, core)
         loss_part = loss_part[0, 0]
         loss = (loss_part + swap(loss_part)) / (seq_total * features)
     with jax.named_scope("d_context"):
         terms = pl.pallas_call(
             context_kernel,
-            grid=(parts,),
-            out_shape=jax.ShapeDtypeStruct((parts, rows, share), BF16),
-            in_specs=[
-                pl.BlockSpec((rows, 4 * HDIM), lambda t: (0, 0)),
-                pl.BlockSpec((share, 2 * HDIM), lambda t: (t, 0)),
-                pl.BlockSpec((share, 2 * HDIM), lambda t: (t, 0)),
-            ],
-            out_specs=pl.BlockSpec((1, rows, share), lambda t: (t, 0, 0)),
-            compiler_params=PARAMS,
-        )(kv_grad, w_key, w_value)
-        arrived = lax.all_to_all(terms, "tp", 0, 0, tiled=True)
-        d_context = jnp.sum(arrived.astype(F32), axis=0).astype(BF16)
+            out_shape=jax.ShapeDtypeStruct((parts, share, rows), BF16),
+            in_specs=[VMEM, ANY, VMEM, VMEM],
+            out_specs=VMEM,
+            compiler_params=PARAMS,
+        )(kv_grad, loss.reshape(1, 1), w_key, w_value)
+        d_context = pl.pallas_call(
+            total_kernel,
+            out_shape=jax.ShapeDtypeStruct((rows, share), BF16),
+            in_specs=[VMEM],
+            out_specs=VMEM,
+            compiler_params=PARAMS,
+        )(lax.all_to_all(terms, "tp", 0, 0, tiled=True))
     return d_context, loss
 
 

time: 212 us -> 197 us (0.929)
  blocking collectives: 0 us -> 86.9 us
  waiting for transfers between devices: 78.6 us -> 20.1 us
  starting transfers between devices: 73.5 us -> 55.6 us
  local copies, waits for them, and re-layouts: 29.3 us -> 11.9 us
  Pallas kernels: 21.5 us -> 17.3 us
  other arithmetic: 3.65 us -> 0.85 us
    all_to_all x0 -> x4, blocking collectives: none -> 86.9 us  [the longest x2 40.8 us: local(): arrived = lax.all_to_all(sent, 'tp', 0, 0, tiled=True)]
    all_to_all x3 -> x0, waiting for transfers between devices: 44.2 us -> none  [the longest x1 27.2 us: local(): arrived = lax.all_to_all(terms, 'tp', 0, 0, tiled=True)]
    unnamed x102 -> x40, local copies, waits for them, and re-layouts: 25.8 us -> 10.1 us
    all_to_all x3 -> x0, starting transfers between devices: 11.5 us -> none  [the longest x2 7.98 us: local(): arrived = lax.all_to_all(sent, 'tp', 0, 0, tiled=True)]
    ppermute x6 -> x3, starting transfers between devices: 12.3 us -> 3.36 us  [returned(): lax.ppermute(blocks[s], axis, routes[s])]
    ppermute x6 -> x3, waiting for transfers between devices: 8.08 us -> 0.01 us  [returned(): lax.ppermute(blocks[s], axis, routes[s])]
    ppermute x9, waiting for transfers between devices: 15 us -> 8.78 us  [shifted(): return [block] + [lax.ppermute(block, axis, route) for route in routes]]
    pallas_call x4 -> x3, Pallas kernels: 10.8 us -> 5.16 us  [the longest x1 2.96 us: local(): pl.pallas_call(gathered_kernel, out_shape=(query_shape, query_shape, jax....]
  transfers between devices with their start and end apart: 35 -> 29, of which waited for: 22 -> 13; matrix products, arithmetic and copies ran while one was open for 4% -> 1% of each run, Pallas kernels for 2% -> 2%
where the time goes in v5:
time: 197 us; the launch traced here: 195 us
  blocking collectives  86.9 us (44%)
  starting transfers between devices  55.6 us (28%)
  waiting for transfers between devices  20.1 us (10%)
  Pallas kernels  17.3 us (9%)
  local copies, waits for them, and re-layouts  11.9 us (6%)
  between operations  2.9 us (1%)
    all_to_all x2, blocking collectives, local(): arrived = lax.all_to_all(sent, 'tp', 0, 0, tiled=True)  40.8 us
    all_to_all x1, blocking collectives, local(): lax.all_to_all(terms, 'tp', 0, 0, tiled=True)  31.6 us
    ppermute x9, starting transfers between devices, shifted(): return [block] + [lax.ppermute(block, axis, route) for route in routes]  15.6 us
    all_to_all x1, blocking collectives, local(): lax.all_to_all(sent, 'y', 0, 0, tiled=True)  14.4 us
    ppermute x3, starting transfers between devices, around(): ahead.append(lax.ppermute(ahead[-1], axis, down))  13.2 us
    ppermute x7, starting transfers between devices, swap(): return lax.ppermute(block, 'core', [(0, 1), (1, 0)])  13 us
    unnamed x40, local copies, waits for them, and re-layouts  10.1 us
    ppermute x9, waiting for transfers between devices, shifted(): return [block] + [lax.ppermute(block, axis, route) for route in routes]  8.78 us
  transfers between devices with their start and end apart: 29, of which 13 were waited for; matrix products, arithmetic and copies ran while one was open for 1% of the time, Pallas kernels for 2%

profile of v5, /device:TPU:1, one launch (start us, length us, event | category | flops | bytes accessed | tf_op | source)
XLA Modules:
  0.0 195.4 jit_solution(2977778081683891731)
XLA Ops:
  0.6 0.6 pad_add_fusion.place_ref
  1.2 3.5 %inputs.1.refs_0_ = bf16[224,512]{1,0:T(8,128)(2,1)} custom-call(s32[4]{0:T(128)} %pad_add_fusion.place_ref, s32[1,128]{1,0:T(1,128)} %bitcast.26, f32[1,512]{1,0:T(1,128)} %bitcast.36, bf16[128,1024]{1,0:T(8,128)(2,1)} %noised_ref.1, bf16[1024,512]{1,0:T(8,128)(2,1)} %pre_ref.1, bf16[512,1024]{1,0:T(8,128)(2,1)} %post_ref.3, bf16[256,4096]{1,0:T(8,128)(2,1)} %w_out_ref.1), custom_call_target="tpu_custom_call" | custom-call | tf_op jit(solution)/shard_map/inputs/pallas_call | solution.py:558
  4.7 6.5 %collective-permute-start.8 = (bf16[224,512]{1,0:T(8,128)(2,1)}, bf16[224,512]{1,0:T(8,128)(2,1)S(1)}, u32[]{:S(2)}, u32[]{:S(2)}) collective-permute-start(bf16[224,512]{1,0:T(8,128)(2,1)} %inputs.1.refs_0_), channel_id=1, source_target_pairs={{0,7},{1,0},{2,1},{3,2},{4,3},{5,4},{6,5},{7,6},{8,15},{9,8},{10,9... | collective-permute-start | bytes 688136 | tf_op jit(solution)/shard_map/inputs/ppermute | solution.py:51
  11.2 1.6 copy-done.3
  12.8 1.9 keys_values.1
  14.7 1.0 collective-permute-start
  15.8 3.3 %collective-permute-start.9 = (bf16[224,512]{1,0:T(8,128)(2,1)S(1)}, bf16[224,512]{1,0:T(8,128)(2,1)S(1)}, u32[]{:S(2)}, u32[]{:S(2)}) collective-permute-start(bf16[224,512]{1,0:T(8,128)(2,1)S(1)} %collective-permute-done.8.refs_8_), channel_id=1, source_target_pairs={{0,7},{1,0},{2,1},{3,2},{4,3},{5,4},{6,5},{7,6},{8,15},{9,8},{10,9... | collective-permute-start | bytes 688136 | tf_op jit(solution)/shard_map/inputs/ppermute | solution.py:51
  19.1 3.3 %collective-permute-done.9.refs_7_ = bf16[224,512]{1,0:T(8,128)(2,1)S(1)} collective-permute-done((bf16[224,512]{1,0:T(8,128)(2,1)S(1)}, bf16[224,512]{1,0:T(8,128)(2,1)S(1)}, u32[]{:S(2)}, u32[]{:S(2)}) %collective-permute-start.9) | collective-permute-done | bytes 229408 | tf_op jit(solution)/shard_map/inputs/ppermute | solution.py:51
  22.4 3.4 %collective-permute-start.10 = (bf16[224,512]{1,0:T(8,128)(2,1)S(1)}, bf16[224,512]{1,0:T(8,128)(2,1)S(1)}, u32[]{:S(2)}, u32[]{:S(2)}) collective-permute-start(bf16[224,512]{1,0:T(8,128)(2,1)S(1)} %collective-permute-done.9.refs_7_), channel_id=1, source_target_pairs={{0,7},{1,0},{2,1},{3,2},{4,3},{5,4},{6,5},{7,6},{8,15},{9,8},{10,9... | collective-permute-start | bytes 688136 | tf_op jit(solution)/shard_map/inputs/ppermute | solution.py:51
  25.9 3.0 %collective-permute-start.2 = (bf16[256,256]{1,0:T(8,128)(2,1)S(1)}, bf16[256,256]{1,0:T(8,128)(2,1)S(1)}, u32[]{:S(2)}, u32[]{:S(2)}) collective-permute-start(bf16[256,256]{1,0:T(8,128)(2,1)S(1)} %get-tuple-element.43), channel_id=1, source_target_pairs={{0,128},{64,192},{128,0},{192,64},{1,129},{65,193},{129,1},{193,65... | collective-permute-start | bytes 393224 | tf_op jit(solution)/shard_map/keys_values/ppermute | solution.py:35
  28.9 0.4 collective-permute-start.1
  29.3 2.3 %collective-permute-start.3 = (bf16[256,256]{1,0:T(8,128)(2,1)S(1)}, bf16[256,256]{1,0:T(8,128)(2,1)S(1)}, u32[]{:S(2)}, u32[]{:S(2)}) collective-permute-start(bf16[256,256]{1,0:T(8,128)(2,1)S(1)} %get-tuple-element.43), channel_id=1, source_target_pairs={{0,192},{64,0},{128,64},{192,128},{1,193},{65,1},{129,65},{193,129... | collective-permute-start | bytes 393224 | tf_op jit(solution)/shard_map/keys_values/ppermute | solution.py:35
  31.6 2.7 %collective-permute-start.11 = (bf16[112,512]{1,0:T(8,128)(2,1)S(1)}, bf16[112,512]{1,0:T(8,128)(2,1)S(1)}, u32[]{:S(2)}, u32[]{:S(2)}) collective-permute-start(bf16[112,512]{1,0:T(8,128)(2,1)S(1)} %slice.53), channel_id=1, source_target_pairs={{0,7},{1,0},{2,1},{3,2},{4,3},{5,4},{6,5},{7,6},{8,15},{9,8},{10,9... | collective-permute-start | bytes 344072 | tf_op jit(solution)/shard_map/inputs/ppermute | solution.py:53
  34.3 0.3 collective-permute-start.7
  34.6 0.8 collective-permute-done.1
  35.5 0.6 collective-permute-done.11.refs_5_
  36.1 3.3 %collective-permute-done.7.refs_4_ = bf16[112,512]{1,0:T(8,128)(2,1)S(1)} collective-permute-done((bf16[112,512]{1,0:T(8,128)(2,1)S(1)}, bf16[112,512]{1,0:T(8,128)(2,1)S(1)}, u32[]{:S(2)}, u32[]{:S(2)}) %collective-permute-start.7) | collective-permute-done | bytes 114720 | tf_op jit(solution)/shard_map/inputs/ppermute | solution.py:53
  39.5 1.2 copy-done.5
  40.7 1.6 copy-done.6
  42.3 0.9 copy-done.11
  43.2 0.9 copy-done.13
  44.1 3.0 %gathered.1 = (bf16[128,128]{1,0:T(8,128)(2,1)S(1)}, bf16[128,128]{1,0:T(8,128)(2,1)S(1)}, f32[128,256]{1,0:T(8,128)S(1)}, f32[128,1024]{1,0:T(8,128)S(1)}, bf16...) custom-call(s32[4]{0:T(128)S(1)} %copy-done.16, bf16[4096,256]{1,0:T(8,128)(2,1)S(1)} %copy-done.6, ...), custom_call_target="tpu_custom_call" | custom-call | tf_op jit(solution)/shard_map/gathered/pallas_call | solution.py:595
  47.1 0.9 copy-done.9
  48.0 0.7 copy-done.14
  48.7 0.6 copy-done.19
  49.3 4.7 %all-to-all-start = ((bf16[16,96,256]{2,1,0:T(8,128)(2,1)}), bf16[16,96,256]{2,1,0:T(8,128)(2,1)S(1)}, u32[]{:S(2)}, u32[]{:S(2)}) async-start(bf16[16,96,256]{2,1,0:T(8,128)(2,1)} %copy-done.9), calls=%async_computation | async-start | bytes 1572864 | tf_op jit(solution)/shard_map/gathered/all_to_all | solution.py:611
  54.0 5.3 %collective-permute-start.12 = (bf16[128,128]{1,0:T(8,128)(2,1)}, bf16[128,128]{1,0:T(8,128)(2,1)S(1)}, u32[]{:S(2)}, u32[]{:S(2)}) collective-permute-start(bf16[128,128]{1,0:T(8,128)(2,1)} %copy-done.19), channel_id=1, source_target_pairs={{0,8},{8,0},{1,9},{9,1},{2,10},{10,2},{3,11},{11,3},{4,12},{12,4},... | collective-permute-start | bytes 98312 | tf_op jit(solution)/shard_map/gathered/ppermute | solution.py:68
  59.3 1.1 collective-permute-done.12
  60.4 3.2 %collective-permute-start.14 = (bf16[256,128]{1,0:T(8,128)(2,1)S(1)}, bf16[256,128]{1,0:T(8,128)(2,1)S(1)}, u32[]{:S(2)}, u32[]{:S(2)}) collective-permute-start(bf16[256,128]{1,0:T(8,128)(2,1)S(1)} %get-tuple-element.51), channel_id=1, source_target_pairs={{0,32},{16,48},{32,0},{48,16},{1,33},{17,49},{33,1},{49,17},{2,34}... | collective-permute-start | bytes 196616 | tf_op jit(solution)/shard_map/gathered/ppermute | solution.py:35
  63.5 0.3 collective-permute-start.13
  63.8 2.4 %collective-permute-start.15 = (bf16[256,128]{1,0:T(8,128)(2,1)S(1)}, bf16[256,128]{1,0:T(8,128)(2,1)S(1)}, u32[]{:S(2)}, u32[]{:S(2)}) collective-permute-start(bf16[256,128]{1,0:T(8,128)(2,1)S(1)} %get-tuple-element.51), channel_id=1, source_target_pairs={{0,48},{16,0},{32,16},{48,32},{1,49},{17,1},{33,17},{49,33},{2,50}... | collective-permute-start | bytes 196616 | tf_op jit(solution)/shard_map/gathered/ppermute | solution.py:35
  66.2 2.7 %collective-permute-done.13 = bf16[256,128]{1,0:T(8,128)(2,1)S(1)} collective-permute-done((bf16[256,128]{1,0:T(8,128)(2,1)S(1)}, bf16[256,128]{1,0:T(8,128)(2,1)S(1)}, u32[]{:S(2)}, u32[]{:S(2)}) %collective-permute-start.13) | collective-permute-done | bytes 65568 | tf_op jit(solution)/shard_map/gathered/ppermute | solution.py:35
  69.0 1.6 attention.2
  70.6 2.3 %collective-permute-start.20 = (bf16[16,96,256]{2,1,0:T(8,128)(2,1)S(1)}, bf16[16,96,256]{2,1,0:T(8,128)(2,1)S(1)}, u32[]{:S(2)}, u32[]{:S(2)}) collective-permute-start(bf16[16,96,256]{2,1,0:T(8,128)(2,1)S(1)} %all-to-all-done.own_ref), channel_id=1, source_target_pairs={{0,8},{8,0},{1,9},{9,1},{2,10},{10,2},{3,11},{11,3},{4,12},{12,4},... | collective-permute-start | bytes 2359304 | tf_op jit(solution)/shard_map/gathered/ppermute | solution.py:68
  73.0 3.0 %collective-permute-start.17 = (bf16[272,128]{1,0:T(8,128)(2,1)S(1)}, bf16[272,128]{1,0:T(8,128)(2,1)S(1)}, u32[]{:S(2)}, u32[]{:S(2)}) collective-permute-start(bf16[272,128]{1,0:T(8,128)(2,1)S(1)} %get-tuple-element.37), channel_id=1, source_target_pairs={{0,32},{16,48},{32,0},{48,16},{1,33},{17,49},{33,1},{49,17},{2,34}... | collective-permute-start | bytes 208904 | tf_op jit(solution)/shard_map/attention/ppermute | solution.py:41
  76.0 0.2 collective-permute-start.16
  76.3 0.7 slice.48
  77.0 2.8 %collective-permute-start.21 = (bf16[1,1024]{1,0:T(2,128)(2,1)S(1)}, bf16[1,1024]{1,0:T(2,128)(2,1)S(1)}, u32[]{:S(2)}, u32[]{:S(2)}) collective-permute-start(bf16[1,1024]{1,0:T(2,128)(2,1)S(1)} %slice.48), channel_id=1, source_target_pairs={{8,0},{16,8},{24,16},{32,24},{40,32},{48,40},{56,48},{64,56},{72,6... | collective-permute-start | bytes 6152 | tf_op jit(solution)/shard_map/targets/ppermute | solution.py:591
  79.8 1.0 slice.47
  80.8 0.2 attention.3
  81.1 0.2 collective-permute-start.19
  81.3 0.9 collective-permute-done.21
  82.2 0.2 collective-permute-done.19
  82.4 0.9 raw.1
  83.3 26.1 %all_to_all.25.arrived_ref = bf16[8,16,3072]{2,1,0:T(8,128)(2,1)S(1)} all-to-all(bf16[8,16,3072]{2,1,0:T(8,128)(2,1)S(1)} %raw.1), channel_id=1, replica_groups=mesh['y'=4,'x'=4,'core'=2,'tp'=8] {'tp'}, dimensions={0} | all-to-all | bytes 1572864 | tf_op jit(solution)/shard_map/raw/all_to_all | solution.py:640
  109.5 1.1 norm.1
  110.6 14.7 %all_to_all.26.arrived_ref = bf16[8,16,1152]{2,1,0:T(8,128)(2,1)S(1)} all-to-all(bf16[8,16,1152]{2,1,0:T(8,128)(2,1)S(1)} %get-tuple-element.28), channel_id=1, replica_groups=mesh['y'=4,'x'=4,'core'=2,'tp'=8] {'tp'}, dimensions={0} | all-to-all | bytes 589824 | tf_op jit(solution)/shard_map/norm/all_to_all | solution.py:652
  125.3 1.0 loss.1
  126.4 1.3 collective-permute-start.22
  127.6 0.9 collective-permute-done.22
  128.5 0.1 sent_grads.1.refs_0_
  128.7 3.4 %collective-permute-start.25 = (bf16[272,128]{1,0:T(8,128)(2,1)S(1)}, bf16[272,128]{1,0:T(8,128)(2,1)S(1)}, u32[]{:S(2)}, u32[]{:S(2)}) collective-permute-start(bf16[272,128]{1,0:T(8,128)(2,1)S(1)} %sent_grads.1.refs_0_), channel_id=1, source_target_pairs={{0,48},{16,0},{32,16},{48,32},{1,49},{17,1},{33,17},{49,33},{2,50}... | collective-permute-start | bytes 208904 | tf_op jit(solution)/shard_map/sent_grads/ppermute | solution.py:35
  132.1 0.7 collective-permute-start.23
  132.8 2.2 %collective-permute-done.25.refs_3_ = bf16[272,128]{1,0:T(8,128)(2,1)S(1)} collective-permute-done((bf16[272,128]{1,0:T(8,128)(2,1)S(1)}, bf16[272,128]{1,0:T(8,128)(2,1)S(1)}, u32[]{:S(2)}, u32[]{:S(2)}) %collective-permute-start.25) | collective-permute-done | bytes 69664 | tf_op jit(solution)/shard_map/sent_grads/ppermute | solution.py:35
  135.0 1.9 collective-permute-done.24.refs_2_
  136.9 1.2 collective-permute-done.23.refs_1_
  138.0 1.6 attention_grad.2
  139.6 14.4 %all_to_all.27.refs_0_ = bf16[4,272,256]{2,1,0:T(8,128)(2,1)S(1)} all-to-all(bf16[4,272,256]{2,1,0:T(8,128)(2,1)S(1)} %attention_grad.2), channel_id=1, replica_groups=mesh['y'=4,'x'=4,'core'=2,'tp'=8] {'y'}, dimensions={0} | all-to-all | bytes 1114112 | tf_op jit(solution)/shard_map/attention_grad/all_to_all | solution.py:692
  154.2 2.8 %collective-permute-start.26 = (bf16[128,256]{1,0:T(8,128)(2,1)S(1)}, bf16[128,256]{1,0:T(8,128)(2,1)S(1)}, u32[]{:S(2)}, u32[]{:S(2)}) collective-permute-start(bf16[128,256]{1,0:T(8,128)(2,1)S(1)} %broadcast_select_fusion.2), channel_id=1, source_target_pairs={{0,8},{8,0},{1,9},{9,1},{2,10},{10,2},{3,11},{11,3},{4,12},{12,4},... | collective-permute-start | bytes 196616 | tf_op jit(solution)/shard_map/attention_grad/ppermute | solution.py:68
  157.1 1.0 collective-permute-done.27
  158.9 1.6 copy-done.4
  160.5 1.3 d_context.2
  161.8 31.6 %all_to_all.28.arrived_ref = bf16[8,512,128]{2,1,0:T(8,128)(2,1)S(1)} all-to-all(bf16[8,512,128]{2,1,0:T(8,128)(2,1)S(1)} %d_context.2), channel_id=1, replica_groups=mesh['y'=4,'x'=4,'core'=2,'tp'=8] {'tp'}, dimensions={0} | all-to-all | bytes 2097152 | tf_op jit(solution)/shard_map/d_context/all_to_all | solution.py:710
  193.4 0.9 d_context.3
  (72 shorter events, 0.7 us)
Async XLA Ops:
  1.2 10.0 %copy-start.1 = (bf16[4096,256]{1,0:T(8,128)(2,1)S(1)}, bf16[4096,256]{1,0:T(8,128)(2,1)}, u32[]{:S(2)}) copy-start(bf16[4096,256]{1,0:T(8,128)(2,1)} %key_ref.3) | copy-start | bytes 6291460
  1.2 10.0 %copy-start.7 = (bf16[128,4096]{1,0:T(8,128)(2,1)S(1)}, bf16[128,4096]{1,0:T(8,128)(2,1)}, u32[]{:S(2)}) copy-start(bf16[128,4096]{1,0:T(8,128)(2,1)} %context_ref.1) | copy-start | bytes 3145732
  1.2 10.0 %copy-start.16 = (s32[4]{0:T(128)S(1)}, s32[4]{0:T(128)}, u32[]{:S(2)}) copy-start(s32[4]{0:T(128)} %pad_add_fusion.place_ref) | copy-start | bytes 52
  4.7 11.1 %collective-permute-start.8 = (bf16[224,512]{1,0:T(8,128)(2,1)}, bf16[224,512]{1,0:T(8,128)(2,1)S(1)}, u32[]{:S(2)}, u32[]{:S(2)}) collective-permute-start(bf16[224,512]{1,0:T(8,128)(2,1)} %inputs.1.refs_0_), channel_id=1, source_target_pairs={{0,7},{1,0},{2,1},{3,2},{4,3},{5,4},{6,5},{7,6},{8,15},{9,8},{10,9... | collective-permute-start | bytes 688136 | tf_op jit(solution)/shard_map/inputs/ppermute | solution.py:51
  11.2 7.9 %collective-permute-start.4 = (bf16[224,512]{1,0:T(8,128)(2,1)}, bf16[224,512]{1,0:T(8,128)(2,1)S(1)}, u32[]{:S(2)}, u32[]{:S(2)}) collective-permute-start(bf16[224,512]{1,0:T(8,128)(2,1)} %inputs.1.refs_0_), channel_id=1, source_target_pairs={{0,1},{1,2},{2,3},{3,4},{4,5},{5,6},{6,7},{7,0},{8,9},{9,10},{10,1... | collective-permute-start | bytes 688136 | tf_op jit(solution)/shard_map/inputs/ppermute | solution.py:50
  11.2 1.6 copy-start.3
  12.8 26.7 %copy-start.8 = (bf16[224,512]{1,0:T(8,128)(2,1)S(1)}, bf16[224,512]{1,0:T(8,128)(2,1)}, u32[]{:S(2)}) copy-start(bf16[224,512]{1,0:T(8,128)(2,1)} %inputs.1.refs_0_) | copy-start | bytes 688132
  14.7 24.7 %copy-start = (bf16[256,4096]{1,0:T(8,128)(2,1)S(1)}, bf16[256,4096]{1,0:T(8,128)(2,1)}, u32[]{:S(2)}) copy-start(bf16[256,4096]{1,0:T(8,128)(2,1)} %w_out_ref.1) | copy-start | bytes 6291460
  14.7 4.3 %collective-permute-start = (bf16[128,256]{1,0:T(8,128)(2,1)S(1)}, bf16[128,256]{1,0:T(8,128)(2,1)S(1)}, u32[]{:S(2)}, u32[]{:S(2)}) collective-permute-start(bf16[128,256]{1,0:T(8,128)(2,1)S(1)} %get-tuple-element.20), channel_id=1, source_target_pairs={{0,8},{8,0},{1,9},{9,1},{2,10},{10,2},{3,11},{11,3},{4,12},{12,4},... | collective-permute-start | bytes 196616 | tf_op jit(solution)/shard_map/keys_values/ppermute | solution.py:68
  15.8 20.3 %copy-start.10 = (bf16[224,512]{1,0:T(8,128)(2,1)}, bf16[224,512]{1,0:T(8,128)(2,1)S(1)}, u32[]{:S(2)}) copy-start(bf16[224,512]{1,0:T(8,128)(2,1)S(1)} %collective-permute-done.8.refs_8_) | copy-start | bytes 688132
  15.8 6.6 %collective-permute-start.9 = (bf16[224,512]{1,0:T(8,128)(2,1)S(1)}, bf16[224,512]{1,0:T(8,128)(2,1)S(1)}, u32[]{:S(2)}, u32[]{:S(2)}) collective-permute-start(bf16[224,512]{1,0:T(8,128)(2,1)S(1)} %collective-permute-done.8.refs_8_), channel_id=1, source_target_pairs={{0,7},{1,0},{2,1},{3,2},{4,3},{5,4},{6,5},{7,6},{8,15},{9,8},{10,9... | collective-permute-start | bytes 688136 | tf_op jit(solution)/shard_map/inputs/ppermute | solution.py:51
  19.1 17.0 %copy-start.12 = (bf16[224,512]{1,0:T(8,128)(2,1)}, bf16[224,512]{1,0:T(8,128)(2,1)S(1)}, u32[]{:S(2)}) copy-start(bf16[224,512]{1,0:T(8,128)(2,1)S(1)} %collective-permute-done.4.refs_1_) | copy-start | bytes 688132
  19.1 6.8 %collective-permute-start.5 = (bf16[224,512]{1,0:T(8,128)(2,1)S(1)}, bf16[224,512]{1,0:T(8,128)(2,1)S(1)}, u32[]{:S(2)}, u32[]{:S(2)}) collective-permute-start(bf16[224,512]{1,0:T(8,128)(2,1)S(1)} %collective-permute-done.4.refs_1_), channel_id=1, source_target_pairs={{0,1},{1,2},{2,3},{3,4},{4,5},{5,6},{6,7},{7,0},{8,9},{9,10},{10,1... | collective-permute-start | bytes 688136 | tf_op jit(solution)/shard_map/inputs/ppermute | solution.py:50
  22.4 9.1 %collective-permute-start.10 = (bf16[224,512]{1,0:T(8,128)(2,1)S(1)}, bf16[224,512]{1,0:T(8,128)(2,1)S(1)}, u32[]{:S(2)}, u32[]{:S(2)}) collective-permute-start(bf16[224,512]{1,0:T(8,128)(2,1)S(1)} %collective-permute-done.9.refs_7_), channel_id=1, source_target_pairs={{0,7},{1,0},{2,1},{3,2},{4,3},{5,4},{6,5},{7,6},{8,15},{9,8},{10,9... | collective-permute-start | bytes 688136 | tf_op jit(solution)/shard_map/inputs/ppermute | solution.py:51
  25.8 8.5 %collective-permute-start.6 = (bf16[224,512]{1,0:T(8,128)(2,1)S(1)}, bf16[224,512]{1,0:T(8,128)(2,1)S(1)}, u32[]{:S(2)}, u32[]{:S(2)}) collective-permute-start(bf16[224,512]{1,0:T(8,128)(2,1)S(1)} %collective-permute-done.5.refs_2_), channel_id=1, source_target_pairs={{0,1},{1,2},{2,3},{3,4},{4,5},{5,6},{6,7},{7,0},{8,9},{9,10},{10,1... | collective-permute-start | bytes 688136 | tf_op jit(solution)/shard_map/inputs/ppermute | solution.py:50
  25.9 8.8 %collective-permute-start.2 = (bf16[256,256]{1,0:T(8,128)(2,1)S(1)}, bf16[256,256]{1,0:T(8,128)(2,1)S(1)}, u32[]{:S(2)}, u32[]{:S(2)}) collective-permute-start(bf16[256,256]{1,0:T(8,128)(2,1)S(1)} %get-tuple-element.43), channel_id=1, source_target_pairs={{0,128},{64,192},{128,0},{192,64},{1,129},{65,193},{129,1},{193,65... | collective-permute-start | bytes 393224 | tf_op jit(solution)/shard_map/keys_values/ppermute | solution.py:35
  28.9 6.5 %collective-permute-start.1 = (bf16[256,256]{1,0:T(8,128)(2,1)S(1)}, bf16[256,256]{1,0:T(8,128)(2,1)S(1)}, u32[]{:S(2)}, u32[]{:S(2)}) collective-permute-start(bf16[256,256]{1,0:T(8,128)(2,1)S(1)} %get-tuple-element.43), channel_id=1, source_target_pairs={{0,64},{64,128},{128,192},{192,0},{1,65},{65,129},{129,193},{193,1... | collective-permute-start | bytes 393224 | tf_op jit(solution)/shard_map/keys_values/ppermute | solution.py:35
  29.3 6.1 %collective-permute-start.3 = (bf16[256,256]{1,0:T(8,128)(2,1)S(1)}, bf16[256,256]{1,0:T(8,128)(2,1)S(1)}, u32[]{:S(2)}, u32[]{:S(2)}) collective-permute-start(bf16[256,256]{1,0:T(8,128)(2,1)S(1)} %get-tuple-element.43), channel_id=1, source_target_pairs={{0,192},{64,0},{128,64},{192,128},{1,193},{65,1},{129,65},{193,129... | collective-permute-start | bytes 393224 | tf_op jit(solution)/shard_map/keys_values/ppermute | solution.py:35
  31.6 4.5 %collective-permute-start.11 = (bf16[112,512]{1,0:T(8,128)(2,1)S(1)}, bf16[112,512]{1,0:T(8,128)(2,1)S(1)}, u32[]{:S(2)}, u32[]{:S(2)}) collective-permute-start(bf16[112,512]{1,0:T(8,128)(2,1)S(1)} %slice.53), channel_id=1, source_target_pairs={{0,7},{1,0},{2,1},{3,2},{4,3},{5,4},{6,5},{7,6},{8,15},{9,8},{10,9... | collective-permute-start | bytes 344072 | tf_op jit(solution)/shard_map/inputs/ppermute | solution.py:53
  34.3 5.1 %collective-permute-start.7 = (bf16[112,512]{1,0:T(8,128)(2,1)S(1)}, bf16[112,512]{1,0:T(8,128)(2,1)S(1)}, u32[]{:S(2)}, u32[]{:S(2)}) collective-permute-start(bf16[112,512]{1,0:T(8,128)(2,1)S(1)} %slice.52), channel_id=1, source_target_pairs={{0,1},{1,2},{2,3},{3,4},{4,5},{5,6},{6,7},{7,0},{8,9},{9,10},{10,1... | collective-permute-start | bytes 344072 | tf_op jit(solution)/shard_map/inputs/ppermute | solution.py:53
  39.5 1.2 copy-start.5
  40.7 1.6 copy-start.6
  42.3 0.9 copy-start.11
  43.2 0.9 copy-start.13
  47.1 0.9 copy-start.9
  48.0 0.7 copy-start.14
  48.7 0.6 copy-start.19
  49.3 19.7 %copy-start.17 = (s32[4]{0:T(128)S(1)}, s32[4]{0:T(128)}, u32[]{:S(2)}) copy-start(s32[4]{0:T(128)} %lengths_ref.5) | copy-start | bytes 52
  49.3 21.3 %all-to-all-start = ((bf16[16,96,256]{2,1,0:T(8,128)(2,1)}), bf16[16,96,256]{2,1,0:T(8,128)(2,1)S(1)}, u32[]{:S(2)}, u32[]{:S(2)}) async-start(bf16[16,96,256]{2,1,0:T(8,128)(2,1)} %copy-done.9), calls=%async_computation | async-start | bytes 1572864 | tf_op jit(solution)/shard_map/gathered/all_to_all | solution.py:611
  54.0 6.4 %collective-permute-start.12 = (bf16[128,128]{1,0:T(8,128)(2,1)}, bf16[128,128]{1,0:T(8,128)(2,1)S(1)}, u32[]{:S(2)}, u32[]{:S(2)}) collective-permute-start(bf16[128,128]{1,0:T(8,128)(2,1)} %copy-done.19), channel_id=1, source_target_pairs={{0,8},{8,0},{1,9},{9,1},{2,10},{10,2},{3,11},{11,3},{4,12},{12,4},... | collective-permute-start | bytes 98312 | tf_op jit(solution)/shard_map/gathered/ppermute | solution.py:68
  60.4 5.8 %collective-permute-start.14 = (bf16[256,128]{1,0:T(8,128)(2,1)S(1)}, bf16[256,128]{1,0:T(8,128)(2,1)S(1)}, u32[]{:S(2)}, u32[]{:S(2)}) collective-permute-start(bf16[256,128]{1,0:T(8,128)(2,1)S(1)} %get-tuple-element.51), channel_id=1, source_target_pairs={{0,32},{16,48},{32,0},{48,16},{1,33},{17,49},{33,1},{49,17},{2,34}... | collective-permute-start | bytes 196616 | tf_op jit(solution)/shard_map/gathered/ppermute | solution.py:35
  63.5 5.4 %collective-permute-start.13 = (bf16[256,128]{1,0:T(8,128)(2,1)S(1)}, bf16[256,128]{1,0:T(8,128)(2,1)S(1)}, u32[]{:S(2)}, u32[]{:S(2)}) collective-permute-start(bf16[256,128]{1,0:T(8,128)(2,1)S(1)} %get-tuple-element.51), channel_id=1, source_target_pairs={{0,16},{16,32},{32,48},{48,0},{1,17},{17,33},{33,49},{49,1},{2,18}... | collective-permute-start | bytes 196616 | tf_op jit(solution)/shard_map/gathered/ppermute | solution.py:35
  63.8 5.1 %collective-permute-start.15 = (bf16[256,128]{1,0:T(8,128)(2,1)S(1)}, bf16[256,128]{1,0:T(8,128)(2,1)S(1)}, u32[]{:S(2)}, u32[]{:S(2)}) collective-permute-start(bf16[256,128]{1,0:T(8,128)(2,1)S(1)} %get-tuple-element.51), channel_id=1, source_target_pairs={{0,48},{16,0},{32,16},{48,32},{1,49},{17,1},{33,17},{49,33},{2,50}... | collective-permute-start | bytes 196616 | tf_op jit(solution)/shard_map/gathered/ppermute | solution.py:35
  70.6 11.8 %collective-permute-start.20 = (bf16[16,96,256]{2,1,0:T(8,128)(2,1)S(1)}, bf16[16,96,256]{2,1,0:T(8,128)(2,1)S(1)}, u32[]{:S(2)}, u32[]{:S(2)}) collective-permute-start(bf16[16,96,256]{2,1,0:T(8,128)(2,1)S(1)} %all-to-all-done.own_ref), channel_id=1, source_target_pairs={{0,8},{8,0},{1,9},{9,1},{2,10},{10,2},{3,11},{11,3},{4,12},{12,4},... | collective-permute-start | bytes 2359304 | tf_op jit(solution)/shard_map/gathered/ppermute | solution.py:68
  72.9 7.9 %collective-permute-start.18 = (bf16[272,128]{1,0:T(8,128)(2,1)S(1)}, bf16[272,128]{1,0:T(8,128)(2,1)S(1)}, u32[]{:S(2)}, u32[]{:S(2)}) collective-permute-start(bf16[272,128]{1,0:T(8,128)(2,1)S(1)} %get-tuple-element.36), channel_id=1, source_target_pairs={{0,16},{16,32},{32,48},{48,0},{1,17},{17,33},{33,49},{49,1},{2,18}... | collective-permute-start | bytes 208904 | tf_op jit(solution)/shard_map/attention/ppermute | solution.py:41
  73.0 7.8 %collective-permute-start.17 = (bf16[272,128]{1,0:T(8,128)(2,1)S(1)}, bf16[272,128]{1,0:T(8,128)(2,1)S(1)}, u32[]{:S(2)}, u32[]{:S(2)}) collective-permute-start(bf16[272,128]{1,0:T(8,128)(2,1)S(1)} %get-tuple-element.37), channel_id=1, source_target_pairs={{0,32},{16,48},{32,0},{48,16},{1,33},{17,49},{33,1},{49,17},{2,34}... | collective-permute-start | bytes 208904 | tf_op jit(solution)/shard_map/attention/ppermute | solution.py:41
  76.0 4.8 %collective-permute-start.16 = (bf16[272,128]{1,0:T(8,128)(2,1)S(1)}, bf16[272,128]{1,0:T(8,128)(2,1)S(1)}, u32[]{:S(2)}, u32[]{:S(2)}) collective-permute-start(bf16[272,128]{1,0:T(8,128)(2,1)S(1)} %get-tuple-element.38), channel_id=1, source_target_pairs={{0,48},{16,0},{32,16},{48,32},{1,49},{17,1},{33,17},{49,33},{2,50}... | collective-permute-start | bytes 208904 | tf_op jit(solution)/shard_map/attention/ppermute | solution.py:41
  77.0 5.1 %collective-permute-start.21 = (bf16[1,1024]{1,0:T(2,128)(2,1)S(1)}, bf16[1,1024]{1,0:T(2,128)(2,1)S(1)}, u32[]{:S(2)}, u32[]{:S(2)}) collective-permute-start(bf16[1,1024]{1,0:T(2,128)(2,1)S(1)} %slice.48), channel_id=1, source_target_pairs={{8,0},{16,8},{24,16},{32,24},{40,32},{48,40},{56,48},{64,56},{72,6... | collective-permute-start | bytes 6152 | tf_op jit(solution)/shard_map/targets/ppermute | solution.py:591
  81.1 1.3 collective-permute-start.19
  82.4 27.0 %copy-start.15 = (bf16[128,512]{1,0:T(8,128)(2,1)S(1)}, bf16[128,512]{1,0:T(8,128)(2,1)}, u32[]{:S(2)}) copy-start(bf16[128,512]{1,0:T(8,128)(2,1)} %copy-done.14) | copy-start | bytes 393220
  83.3 42.0 %copy-start.18 = (s32[128]{0:T(128)S(1)}, s32[128]{0:T(128)}, u32[]{:S(2)}) copy-start(s32[128]{0:T(128)} %param.14) | copy-start | bytes 1540
  126.4 2.1 %collective-permute-start.22 = (bf16[128,128]{1,0:T(8,128)(2,1)S(1)}, bf16[128,128]{1,0:T(8,128)(2,1)S(1)}, u32[]{:S(2)}, u32[]{:S(2)}) collective-permute-start(bf16[128,128]{1,0:T(8,128)(2,1)S(1)} %get-tuple-element.31), channel_id=1, source_target_pairs={{0,8},{8,0},{1,9},{9,1},{2,10},{10,2},{3,11},{11,3},{4,12},{12,4},... | collective-permute-start | bytes 98312 | tf_op jit(solution)/shard_map/sent_grads/ppermute | solution.py:68
  128.7 30.2 %copy-start.2 = (bf16[4096,256]{1,0:T(8,128)(2,1)S(1)}, bf16[4096,256]{1,0:T(8,128)(2,1)}, u32[]{:S(2)}) copy-start(bf16[4096,256]{1,0:T(8,128)(2,1)} %key_ref.3) | copy-start | bytes 6291460
  128.7 6.3 %collective-permute-start.25 = (bf16[272,128]{1,0:T(8,128)(2,1)S(1)}, bf16[272,128]{1,0:T(8,128)(2,1)S(1)}, u32[]{:S(2)}, u32[]{:S(2)}) collective-permute-start(bf16[272,128]{1,0:T(8,128)(2,1)S(1)} %sent_grads.1.refs_0_), channel_id=1, source_target_pairs={{0,48},{16,0},{32,16},{48,32},{1,49},{17,1},{33,17},{49,33},{2,50}... | collective-permute-start | bytes 208904 | tf_op jit(solution)/shard_map/sent_grads/ppermute | solution.py:35
  132.1 4.8 %collective-permute-start.24 = (bf16[272,128]{1,0:T(8,128)(2,1)S(1)}, bf16[272,128]{1,0:T(8,128)(2,1)S(1)}, u32[]{:S(2)}, u32[]{:S(2)}) collective-permute-start(bf16[272,128]{1,0:T(8,128)(2,1)S(1)} %sent_grads.1.refs_0_), channel_id=1, source_target_pairs={{0,32},{16,48},{32,0},{48,16},{1,33},{17,49},{33,1},{49,17},{2,34}... | collective-permute-start | bytes 208904 | tf_op jit(solution)/shard_map/sent_grads/ppermute | solution.py:35
  132.1 5.9 %collective-permute-start.23 = (bf16[272,128]{1,0:T(8,128)(2,1)S(1)}, bf16[272,128]{1,0:T(8,128)(2,1)S(1)}, u32[]{:S(2)}, u32[]{:S(2)}) collective-permute-start(bf16[272,128]{1,0:T(8,128)(2,1)S(1)} %sent_grads.1.refs_0_), channel_id=1, source_target_pairs={{0,16},{16,32},{32,48},{48,0},{1,17},{17,33},{33,49},{49,1},{2,18}... | collective-permute-start | bytes 208904 | tf_op jit(solution)/shard_map/sent_grads/ppermute | solution.py:35
  154.2 4.7 %collective-permute-start.26 = (bf16[128,256]{1,0:T(8,128)(2,1)S(1)}, bf16[128,256]{1,0:T(8,128)(2,1)S(1)}, u32[]{:S(2)}, u32[]{:S(2)}) collective-permute-start(bf16[128,256]{1,0:T(8,128)(2,1)S(1)} %broadcast_select_fusion.2), channel_id=1, source_target_pairs={{0,8},{8,0},{1,9},{9,1},{2,10},{10,2},{3,11},{11,3},{4,12},{12,4},... | collective-permute-start | bytes 196616 | tf_op jit(solution)/shard_map/attention_grad/ppermute | solution.py:68
  157.0 1.1 collective-permute-start.27
  158.9 1.6 copy-start.4

commit v6 on v5

--- a/solution.py
+++ b/solution.py
@@ -138,7 +138,6 @@
 
 
 def send_kernel(
-    place_ref,
     steps_ref,
     time_ref,
     noised_ref,
@@ -154,37 +153,38 @@
 ):
     rows, features = noised.shape
     share = pre.shape[1]
-    slot = place_ref[2] * place_ref[3] + place_ref[1]
+    slot = lax.axis_index("core") * lax.axis_size(CHIPS)
+    slot = slot + lax.axis_index("y") * lax.axis_size("x") + lax.axis_index("x")
     lanes = pl.ds(pl.multiple_of(slot // (HDIM // FOLD_POST) * HDIM, HDIM), HDIM)
     lines = pl.ds(pl.multiple_of(slot // 2 * (2 * FOLD_OUT), 2 * FOLD_OUT), 2 * FOLD_OUT)
-    half = features // 2
-    copies = fetch(
-        (
-            (noised_ref, noised),
-            (pre_ref.at[:half], pre.at[:half]),
-            (pre_ref.at[half:], pre.at[half:]),
-            (post_ref.at[:, lanes], post_part),
-            (out_ref.at[lines], out_part),
-        ),
-        sems,
-    )
+    quarter = features // 4
+    pairs = [(post_ref.at[:, lanes], post_part), (out_ref.at[lines], out_part), (noised_ref, noised)]
+    pairs += [
+        (pre_ref.at[pl.ds(quarter * k, quarter)], pre.at[pl.ds(quarter * k, quarter)])
+        for k in range(4)
+    ]
+    copies = fetch(pairs, sems)
     angle = (0.5 * math.pi / TSTEPS) * steps_ref[...].astype(F32)
     noise = column(sine(angle)) * time_ref[...]
-    copies[3].wait()
+    copies[0].wait()
     post = post_part[...].astype(F32).T
-    quarter = lax.rem(slot, HDIM // FOLD_POST)
+    which = lax.rem(slot, HDIM // FOLD_POST)
     post_rows = post[:FOLD_POST]
     for k in range(1, HDIM // FOLD_POST):
-        post_rows = jnp.where(quarter == k, post[FOLD_POST * k : FOLD_POST * (k + 1)], post_rows)
-    copies[4].wait()
+        post_rows = jnp.where(which == k, post[FOLD_POST * k : FOLD_POST * (k + 1)], post_rows)
+    copies[1].wait()
     out_rows = out_part[...].astype(F32)
     out_rows = jnp.where(lax.rem(slot, 2) == 0, out_rows[:FOLD_OUT], out_rows[FOLD_OUT:])
     parts = out_rows.shape[1] // share
     out_rows = [out_rows[:, share * k : share * (k + 1)] for k in range(parts)]
     sent_ref[rows:, :] = jnp.concatenate([post_rows] + out_rows, axis=0).astype(BF16)
-    for k in range(3):
-        copies[k].wait()
-    sent_ref[:rows, :] = (dot(noised[...], pre[...]) + noise).astype(BF16)
+    copies[2].wait()
+    total = noise
+    for k in range(4):
+        at = slice(quarter * k, quarter * (k + 1))
+        copies[3 + k].wait()
+        total = total + dot(noised[:, at], pre[at])
+    sent_ref[:rows, :] = total.astype(BF16)
 
 
 def project_kernel(
@@ -214,48 +214,71 @@
     theirs_ref[...] = jnp.where(first, right, left).astype(BF16)
 
 
-def gathered_kernel(place_ref, w_query_ref, w_out_ref, post_ref, hold_ref, *refs):
-    block_refs, refs = refs[:-6], refs[-6:]
-    mine_ref, theirs_ref, cross_ref, post_out_ref, input_ref, folded_ref = refs
+def gathered_kernel(place_ref, w_query_ref, w_out_ref, hold_ref, *refs):
+    *block_refs, mine_ref, theirs_ref, cross_ref, folded_ref, near, sems = refs
     rows = mine_ref.shape[0]
     heads, width = w_out_ref.shape
-    blocks = gathered_blocks(block_refs)
-    squares = jnp.zeros((rows, 1), F32)
-    for block in blocks:
-        wide = block[:rows].astype(F32)
-        squares = squares + jnp.sum(wide * wide, axis=1, keepdims=True)
-    query = jnp.zeros((rows, heads), F32)
-    parts = len(blocks)
-    share = blocks[0].shape[1]
-    for distance, block in enumerate(blocks):
+    near_refs = (block_refs[1], block_refs[-1])
+    near_copies = fetch([(ref, near.at[k]) for k, ref in enumerate(near_refs)], sems)
+    half = (len(block_refs) - 1) // 2
+    parts = len(block_refs) - 1
+    far = jnp.concatenate((block_refs[half][...], block_refs[half + 1][...]), axis=0)
+    blocks = {0: block_refs[0][...], half: far}
+    for k in range(2, half):
+        blocks[k] = block_refs[k][...]
+    for k in range(half + 1, parts - 1):
+        blocks[k] = block_refs[k + 1][...]
+    share = far.shape[1]
+    top = rows + FOLD_POST
+
+    def against(total, weight_of, distance, count):
         owner = owner_of(place_ref, distance, parts)
         at = pl.ds(pl.multiple_of(owner * share, share), share)
-        query = query + dot(block[:rows], w_query_ref[at, :])
-    query = (query * lax.rsqrt(squares / width + EPSILON)).astype(BF16)
-    first = place_ref[2] == 0
-    mine_ref[...] = jnp.where(first, query[:, :HDIM], query[:, HDIM:])
-    theirs_ref[...] = jnp.where(first, query[:, HDIM:], query[:, :HDIM])
-
-    top = rows + FOLD_POST
+        return total + weight_of(blocks[distance][:count], at)
+
+    def by_out(block, at):
+        return dot(block, w_out_ref[:, at], ((1,), (1,)))
+
+    def by_query(block, at):
+        return dot(block, w_query_ref[at, :])
+
     both = jnp.zeros((top, heads), F32)
-    for distance, block in enumerate(blocks):
-        owner = owner_of(place_ref, distance, parts)
-        at = pl.ds(pl.multiple_of(owner * share, share), share)
-        both = both + dot(block[:top], w_out_ref[:, at], ((1,), (1,)))
+    for distance in list(blocks):
+        both = against(both, by_out, distance, top)
+    for copy in near_copies:
+        copy.wait()
+    for k, distance in enumerate((1, parts - 1)):
+        blocks[distance] = near[k]
+        both = against(both, by_out, distance, top)
     cross_ref[...] = both[:rows]
     span = FOLD_OUT * parts
-    slices = jnp.concatenate([block[top:] for block in blocks], axis=0)
+    slices = jnp.concatenate([blocks[k][top:] for k in range(parts)], axis=0)
     gram = [jnp.zeros((FOLD_OUT, heads), F32)] * parts
     for k in range(parts):
-        product = dot(slices, w_out_ref[:, share * k : share * (k + 1)], ((1,), (1,)))
+        product = by_out(slices, slice(share * k, share * (k + 1)))
         for b in range(parts):
             at = span * b + FOLD_OUT * k
             gram[b] = gram[b] + product[at : at + FOLD_OUT]
     folded = jnp.concatenate([both[rows:]] + gram, axis=0).astype(BF16)
     for k in range(folded_ref.shape[0]):
         folded_ref[k] = folded
-    post_out_ref[...] = dot(blocks[0][:rows], post_ref[...])
-    input_ref[...] = blocks[0][:rows]
+
+    squares = jnp.zeros((rows, 1), F32)
+    query = jnp.zeros((rows, heads), F32)
+    for distance in range(parts):
+        wide = blocks[distance][:rows].astype(F32)
+        squares = squares + jnp.sum(wide * wide, axis=1, keepdims=True)
+        query = against(query, by_query, distance, rows)
+    query = (query * lax.rsqrt(squares / width + EPSILON)).astype(BF16)
+    first = place_ref[2] == 0
+    mine_ref[...] = jnp.where(first, query[:, :HDIM], query[:, HDIM:])
+    theirs_ref[...] = jnp.where(first, query[:, HDIM:], query[:, :HDIM])
+
+
+def post_kernel(sent_ref, post_ref, hold_ref, input_ref, input_post_ref):
+    features = sent_ref[: input_ref.shape[0], :]
+    input_ref[...] = features
+    input_post_ref[...] = dot(features, post_ref[...])
 
 
 def line_positions(place_ref):
@@ -281,7 +304,7 @@
     return (key_pos >= query_start) & (key_pos <= query_pos)
 
 
-def forward_kernel(lengths_ref, place_ref, q_ref, kv_ref, out_ref):
+def forward_kernel(lengths_ref, place_ref, q_ref, kv_ref, hold_ref, out_ref):
     ends = ends_of(lengths_ref)
     width = GROUP * PAIR
     query_pos = line_positions(place_ref)
@@ -558,17 +581,17 @@
         sent = pl.pallas_call(
             send_kernel,
             out_shape=jax.ShapeDtypeStruct((rows + fold_rows, share), BF16),
-            in_specs=[SMEM, VMEM, VMEM, HBM, HBM, HBM, HBM],
+            in_specs=[VMEM, VMEM, HBM, HBM, HBM, HBM],
             out_specs=VMEM,
             scratch_shapes=[
                 pltpu.VMEM((rows, features), BF16),
                 pltpu.VMEM((features, share), BF16),
                 pltpu.VMEM((share, HDIM), BF16),
                 pltpu.VMEM((2 * FOLD_OUT, width), BF16),
-                pltpu.SemaphoreType.DMA((5,)),
+                pltpu.SemaphoreType.DMA((7,)),
             ],
             compiler_params=WHOLE,
-        )(place, steps, time_vec.reshape(1, share), noised, w_pre, w_post, w_out)
+        )(steps, time_vec.reshape(1, share), noised, w_pre, w_post, w_out)
         blocks = around(sent, "tp")
     with jax.named_scope("keys_values"):
         kv_shape = jax.ShapeDtypeStruct((rows, 2 * HDIM), BF16)
@@ -592,32 +615,44 @@
         targets = jnp.concatenate((concepts[1:], following), axis=0)
     with jax.named_scope("gathered"):
         query_shape = jax.ShapeDtypeStruct((rows, HDIM), BF16)
-        mine, theirs, cross, input_post, input_part, folded = pl.pallas_call(
+        mine, theirs, cross, folded = pl.pallas_call(
             gathered_kernel,
             out_shape=(
                 query_shape,
                 query_shape,
                 jax.ShapeDtypeStruct((rows, head_width), F32),
-                jax.ShapeDtypeStruct((rows, features), F32),
-                jax.ShapeDtypeStruct((rows, share), BF16),
                 jax.ShapeDtypeStruct((chips, fold_rows, head_width), BF16),
             ),
-            in_specs=[SMEM, VMEM, VMEM, VMEM, ANY] + [VMEM] * len(blocks),
-            out_specs=(VMEM,) * 6,
-            compiler_params=PARAMS,
-        )(place, w_query, w_out, w_post, all_kv, *blocks)
+            in_specs=[SMEM, VMEM, VMEM, ANY, VMEM, ANY] + [VMEM] * (len(blocks) - 3) + [ANY],
+            out_specs=(VMEM,) * 4,
+            scratch_shapes=[
+                pltpu.VMEM((2,) + sent.shape, BF16),
+                pltpu.SemaphoreType.DMA((2,)),
+            ],
+            compiler_params=PARAMS,
+        )(place, w_query, w_out, all_kv, *blocks)
         query_head = to_head(mine, theirs, core)
         line_queries = jnp.stack(shifted(query_head, "x"))
+        input_part, input_post = pl.pallas_call(
+            post_kernel,
+            out_shape=(
+                jax.ShapeDtypeStruct((rows, share), BF16),
+                jax.ShapeDtypeStruct((rows, features), F32),
+            ),
+            in_specs=[VMEM, VMEM, ANY],
+            out_specs=(VMEM, VMEM),
+            compiler_params=PARAMS,
+        )(sent, w_post, query_head)
         own_fold = lax.all_to_all(folded, CHIPS, 0, 0, tiled=True)
         other_fold = swap(own_fold)
     with jax.named_scope("attention"):
         sent = pl.pallas_call(
             forward_kernel,
             out_shape=jax.ShapeDtypeStruct((GROUP, PAIR + STATS, HDIM), BF16),
-            in_specs=[SMEM, SMEM, VMEM, VMEM],
+            in_specs=[SMEM, SMEM, VMEM, VMEM, ANY],
             out_specs=VMEM,
             compiler_params=PARAMS,
-        )(doc_lengths, place, line_queries, all_kv)
+        )(doc_lengths, place, line_queries, all_kv, input_post)
         attended_head, log_total = pl.pallas_call(
             merge_kernel,
             out_shape=(

time: 197 us -> 194 us (0.985)
  starting transfers between devices: 55.6 us -> 51 us
  waiting for transfers between devices: 20.1 us -> 23.7 us
  local copies, waits for them, and re-layouts: 11.9 us -> 8.7 us
    unnamed x40 -> x24, local copies, waits for them, and re-layouts: 10.1 us -> 6.93 us
    ppermute x9, waiting for transfers between devices: 8.78 us -> 11.8 us  [shifted(): return [block] + [lax.ppermute(block, axis, route) for route in routes]]
    ppermute x9, starting transfers between devices: 15.6 us -> 13.2 us  [shifted(): return [block] + [lax.ppermute(block, axis, route) for route in routes]]
    ppermute x7, starting transfers between devices: 13 us -> 11 us  [swap(): return lax.ppermute(block, 'core', [(0, 1), (1, 0)])]
  transfers between devices with their start and end apart: 29 -> 29, of which waited for: 13 -> 15; matrix products, arithmetic and copies ran while one was open for 1% -> 1% of each run, Pallas kernels for 2% -> 2%
where the time goes in v6:
time: 194 us; the launch traced here: 192 us
  blocking collectives  87.4 us (45%)
  starting transfers between devices  51 us (26%)
  waiting for transfers between devices  23.7 us (12%)
  Pallas kernels  18.6 us (10%)
  local copies, waits for them, and re-layouts  8.7 us (4%)
  between operations  2.83 us (1%)
    all_to_all x2, blocking collectives, local(): arrived = lax.all_to_all(sent, 'tp', 0, 0, tiled=True)  41.2 us
    all_to_all x1, blocking collectives, local(): lax.all_to_all(terms, 'tp', 0, 0, tiled=True)  31.6 us
    all_to_all x1, blocking collectives, local(): lax.all_to_all(sent, 'y', 0, 0, tiled=True)  14.5 us
    ppermute x9, starting transfers between devices, shifted(): return [block] + [lax.ppermute(block, axis, route) for route in routes]  13.2 us
    ppermute x3, starting transfers between devices, around(): ahead.append(lax.ppermute(ahead[-1], axis, down))  12.8 us
    ppermute x9, waiting for transfers between devices, shifted(): return [block] + [lax.ppermute(block, axis, route) for route in routes]  11.8 us
    ppermute x7, starting transfers between devices, swap(): return lax.ppermute(block, 'core', [(0, 1), (1, 0)])  11 us
    unnamed x24, local copies, waits for them, and re-layouts  6.93 us
  transfers between devices with their start and end apart: 29, of which 15 were waited for; matrix products, arithmetic and copies ran while one was open for 1% of the time, Pallas kernels for 2%

profile of v6, /device:TPU:1, one launch (start us, length us, event | category | flops | bytes accessed | tf_op | source)
XLA Modules:
  0.0 192.5 jit_solution(17995361751117418528)
XLA Ops:
  0.6 3.2 %inputs.1.refs_0_.sent_ref = bf16[224,512]{1,0:T(8,128)(2,1)} custom-call(s32[1,128]{1,0:T(1,128)} %bitcast.26, f32[1,512]{1,0:T(1,128)} %bitcast.36, bf16[128,1024]{1,0:T(8,128)(2,1)} %noised_ref.1, bf16[1024,512]{1,0:T(8,128)(2,1)} %pre_ref.1, bf16[512,1024]{1,0:T(8,128)(2,1)} %post_ref.3, bf16[256,4096]{1,0:T(8,128)(2,1)} %w_out_ref.1), custom_call_target="tpu_custom_call" | custom-call | tf_op jit(solution)/shard_map/inputs/pallas_call | solution.py:581
  3.9 6.5 %collective-permute-start.8 = (bf16[224,512]{1,0:T(8,128)(2,1)}, bf16[224,512]{1,0:T(8,128)(2,1)S(1)}, u32[]{:S(2)}, u32[]{:S(2)}) collective-permute-start(bf16[224,512]{1,0:T(8,128)(2,1)} %inputs.1.refs_0_.sent_ref), channel_id=1, source_target_pairs={{0,7},{1,0},{2,1},{3,2},{4,3},{5,4},{6,5},{7,6},{8,15},{9,8},{10,9... | collective-permute-start | bytes 688136 | tf_op jit(solution)/shard_map/inputs/ppermute | solution.py:51
  10.4 1.6 copy-done.3
  12.0 1.2 copy-done.8
  13.3 1.9 %keys_values.1 = (bf16[128,256]{1,0:T(8,128)(2,1)S(1)}, bf16[128,256]{1,0:T(8,128)(2,1)S(1)}) custom-call(s32[4]{0:T(128)S(1)} %pad_add_fusion.place_ref, bf16[128,4096]{1,0:T(8,128)(2,1)S(1)} %copy-done.8, bf16[4096,256]{1,0:T(8,128)(2,1)S(1)} %copy-done.1, bf16[4096,256]{1,0:T(8,128)(2,1)S(1)} %copy-done.3), custom_call_target="tpu_custom_call" | custom-call | tf_op jit(solution)/shard_map/keys_values/pallas_call | solution.py:598
  15.2 1.0 collective-permute-start
  16.3 3.0 %collective-permute-start.9 = (bf16[224,512]{1,0:T(8,128)(2,1)S(1)}, bf16[224,512]{1,0:T(8,128)(2,1)S(1)}, u32[]{:S(2)}, u32[]{:S(2)}) collective-permute-start(bf16[224,512]{1,0:T(8,128)(2,1)S(1)} %collective-permute-done.8.refs_8_), channel_id=1, source_target_pairs={{0,7},{1,0},{2,1},{3,2},{4,3},{5,4},{6,5},{7,6},{8,15},{9,8},{10,9... | collective-permute-start | bytes 688136 | tf_op jit(solution)/shard_map/inputs/ppermute | solution.py:51
  19.3 4.4 %collective-permute-done.9.refs_7_ = bf16[224,512]{1,0:T(8,128)(2,1)S(1)} collective-permute-done((bf16[224,512]{1,0:T(8,128)(2,1)S(1)}, bf16[224,512]{1,0:T(8,128)(2,1)S(1)}, u32[]{:S(2)}, u32[]{:S(2)}) %collective-permute-start.9) | collective-permute-done | bytes 229408 | tf_op jit(solution)/shard_map/inputs/ppermute | solution.py:51
  23.6 3.4 %collective-permute-start.10 = (bf16[224,512]{1,0:T(8,128)(2,1)S(1)}, bf16[224,512]{1,0:T(8,128)(2,1)S(1)}, u32[]{:S(2)}, u32[]{:S(2)}) collective-permute-start(bf16[224,512]{1,0:T(8,128)(2,1)S(1)} %collective-permute-done.9.refs_7_), channel_id=1, source_target_pairs={{0,7},{1,0},{2,1},{3,2},{4,3},{5,4},{6,5},{7,6},{8,15},{9,8},{10,9... | collective-permute-start | bytes 688136 | tf_op jit(solution)/shard_map/inputs/ppermute | solution.py:51
  27.0 3.0 %collective-permute-start.2 = (bf16[256,256]{1,0:T(8,128)(2,1)S(1)}, bf16[256,256]{1,0:T(8,128)(2,1)S(1)}, u32[]{:S(2)}, u32[]{:S(2)}) collective-permute-start(bf16[256,256]{1,0:T(8,128)(2,1)S(1)} %get-tuple-element.43), channel_id=1, source_target_pairs={{0,128},{64,192},{128,0},{192,64},{1,129},{65,193},{129,1},{193,65... | collective-permute-start | bytes 393224 | tf_op jit(solution)/shard_map/keys_values/ppermute | solution.py:35
  30.0 0.4 collective-permute-start.1
  30.4 2.3 %collective-permute-start.3 = (bf16[256,256]{1,0:T(8,128)(2,1)S(1)}, bf16[256,256]{1,0:T(8,128)(2,1)S(1)}, u32[]{:S(2)}, u32[]{:S(2)}) collective-permute-start(bf16[256,256]{1,0:T(8,128)(2,1)S(1)} %get-tuple-element.43), channel_id=1, source_target_pairs={{0,192},{64,0},{128,64},{192,128},{1,193},{65,1},{129,65},{193,129... | collective-permute-start | bytes 393224 | tf_op jit(solution)/shard_map/keys_values/ppermute | solution.py:35
  32.7 2.7 %collective-permute-start.11 = (bf16[112,512]{1,0:T(8,128)(2,1)S(1)}, bf16[112,512]{1,0:T(8,128)(2,1)S(1)}, u32[]{:S(2)}, u32[]{:S(2)}) collective-permute-start(bf16[112,512]{1,0:T(8,128)(2,1)S(1)} %slice.53), channel_id=1, source_target_pairs={{0,7},{1,0},{2,1},{3,2},{4,3},{5,4},{6,5},{7,6},{8,15},{9,8},{10,9... | collective-permute-start | bytes 344072 | tf_op jit(solution)/shard_map/inputs/ppermute | solution.py:53
  35.5 0.3 collective-permute-start.7
  35.8 0.8 collective-permute-done.1
  36.7 0.6 collective-permute-done.11.refs_5_
  37.3 3.3 %collective-permute-done.7.refs_4_ = bf16[112,512]{1,0:T(8,128)(2,1)S(1)} collective-permute-done((bf16[112,512]{1,0:T(8,128)(2,1)S(1)}, bf16[112,512]{1,0:T(8,128)(2,1)S(1)}, u32[]{:S(2)}, u32[]{:S(2)}) %collective-permute-start.7) | collective-permute-done | bytes 114720 | tf_op jit(solution)/shard_map/inputs/ppermute | solution.py:53
  40.6 1.6 copy-done.6
  42.2 4.2 %gathered.2 = (bf16[128,128]{1,0:T(8,128)(2,1)S(1)}, bf16[128,128]{1,0:T(8,128)(2,1)S(1)}, f32[128,256]{1,0:T(8,128)S(1)}, bf16[16,96,256]{2,1,0:T(8,128)(2,1)S(1)}) custom-call(s32[4]{0:T(128)S(1)} %pad_add_fusion.place_ref, bf16[4096,256]{1,0:T(8,128)(2,1)S(1)} %copy-done.6, bf16[256,4096]{1,0:T(8,128)(2,1)S(1)} %copy-done, ...), custom_call_target="tpu_custom_call" | custom-call | tf_op jit(solution)/shard_map/gathered/pallas_call | solution.py:618
  46.5 0.9 copy-done.9
  47.3 5.4 %all-to-all-start = ((bf16[16,96,256]{2,1,0:T(8,128)(2,1)}), bf16[16,96,256]{2,1,0:T(8,128)(2,1)S(1)}, u32[]{:S(2)}, u32[]{:S(2)}) async-start(bf16[16,96,256]{2,1,0:T(8,128)(2,1)} %copy-done.9), calls=%async_computation | async-start | bytes 1572864 | tf_op jit(solution)/shard_map/gathered/all_to_all | solution.py:646
  52.7 4.2 %collective-permute-start.12 = (bf16[128,128]{1,0:T(8,128)(2,1)S(1)}, bf16[128,128]{1,0:T(8,128)(2,1)S(1)}, u32[]{:S(2)}, u32[]{:S(2)}) collective-permute-start(bf16[128,128]{1,0:T(8,128)(2,1)S(1)} %get-tuple-element.22), channel_id=1, source_target_pairs={{0,8},{8,0},{1,9},{9,1},{2,10},{10,2},{3,11},{11,3},{4,12},{12,4},... | collective-permute-start | bytes 98312 | tf_op jit(solution)/shard_map/gathered/ppermute | solution.py:68
  56.9 0.9 collective-permute-done.12
  57.8 2.8 %collective-permute-start.15 = (bf16[256,128]{1,0:T(8,128)(2,1)S(1)}, bf16[256,128]{1,0:T(8,128)(2,1)S(1)}, u32[]{:S(2)}, u32[]{:S(2)}) collective-permute-start(bf16[256,128]{1,0:T(8,128)(2,1)S(1)} %get-tuple-element.51.hold_ref), channel_id=1, source_target_pairs={{0,48},{16,0},{32,16},{48,32},{1,49},{17,1},{33,17},{49,33},{2,50}... | collective-permute-start | bytes 196616 | tf_op jit(solution)/shard_map/gathered/ppermute | solution.py:35
  60.6 0.6 collective-permute-start.14
  61.2 0.6 collective-permute-start.13
  61.8 0.3 gathered.3
  62.1 0.9 collective-permute-done.15
  63.0 3.3 %collective-permute-done.14 = bf16[256,128]{1,0:T(8,128)(2,1)S(1)} collective-permute-done((bf16[256,128]{1,0:T(8,128)(2,1)S(1)}, bf16[256,128]{1,0:T(8,128)(2,1)S(1)}, u32[]{:S(2)}, u32[]{:S(2)}) %collective-permute-start.14) | collective-permute-done | bytes 65568 | tf_op jit(solution)/shard_map/gathered/ppermute | solution.py:35
  66.3 1.4 collective-permute-done.13
  67.7 1.6 attention.2
  69.4 1.2 collective-permute-start.20
  70.6 0.6 collective-permute-start.18
  71.2 1.8 collective-permute-start.17
  73.0 0.7 collective-permute-start.16
  73.7 0.7 slice.48
  74.4 2.5 %collective-permute-start.21 = (bf16[1,1024]{1,0:T(2,128)(2,1)S(1)}, bf16[1,1024]{1,0:T(2,128)(2,1)S(1)}, u32[]{:S(2)}, u32[]{:S(2)}) collective-permute-start(bf16[1,1024]{1,0:T(2,128)(2,1)S(1)} %slice.48), channel_id=1, source_target_pairs={{8,0},{16,8},{24,16},{32,24},{40,32},{48,40},{56,48},{64,56},{72,6... | collective-permute-start | bytes 6152 | tf_op jit(solution)/shard_map/targets/ppermute | solution.py:614
  76.9 1.0 slice.47
  77.9 0.2 attention.3
  78.2 0.7 collective-permute-start.19
  78.9 0.4 collective-permute-done.21
  79.3 0.4 collective-permute-done.19
  79.8 0.9 raw.1
  80.7 26.0 %all_to_all.25.arrived_ref = bf16[8,16,3072]{2,1,0:T(8,128)(2,1)S(1)} all-to-all(bf16[8,16,3072]{2,1,0:T(8,128)(2,1)S(1)} %raw.1), channel_id=1, replica_groups=mesh['y'=4,'x'=4,'core'=2,'tp'=8] {'tp'}, dimensions={0} | all-to-all | bytes 1572864 | tf_op jit(solution)/shard_map/raw/all_to_all | solution.py:675
  106.7 1.1 norm.1
  107.8 15.2 %all_to_all.26.arrived_ref = bf16[8,16,1152]{2,1,0:T(8,128)(2,1)S(1)} all-to-all(bf16[8,16,1152]{2,1,0:T(8,128)(2,1)S(1)} %get-tuple-element.28), channel_id=1, replica_groups=mesh['y'=4,'x'=4,'core'=2,'tp'=8] {'tp'}, dimensions={0} | all-to-all | bytes 589824 | tf_op jit(solution)/shard_map/norm/all_to_all | solution.py:687
  123.0 1.0 loss.1
  124.0 1.0 collective-permute-start.22
  125.1 0.9 collective-permute-done.22
  126.0 0.1 sent_grads.1.refs_0_
  126.1 2.9 %collective-permute-start.25 = (bf16[272,128]{1,0:T(8,128)(2,1)S(1)}, bf16[272,128]{1,0:T(8,128)(2,1)S(1)}, u32[]{:S(2)}, u32[]{:S(2)}) collective-permute-start(bf16[272,128]{1,0:T(8,128)(2,1)S(1)} %sent_grads.1.refs_0_), channel_id=1, source_target_pairs={{0,48},{16,0},{32,16},{48,32},{1,49},{17,1},{33,17},{49,33},{2,50}... | collective-permute-start | bytes 208904 | tf_op jit(solution)/shard_map/sent_grads/ppermute | solution.py:35
  129.0 0.7 collective-permute-start.23
  129.6 2.2 %collective-permute-done.25.refs_3_ = bf16[272,128]{1,0:T(8,128)(2,1)S(1)} collective-permute-done((bf16[272,128]{1,0:T(8,128)(2,1)S(1)}, bf16[272,128]{1,0:T(8,128)(2,1)S(1)}, u32[]{:S(2)}, u32[]{:S(2)}) %collective-permute-start.25) | collective-permute-done | bytes 69664 | tf_op jit(solution)/shard_map/sent_grads/ppermute | solution.py:35
  131.8 1.9 collective-permute-done.24.refs_2_
  133.7 1.3 collective-permute-done.23.refs_1_
  135.0 1.6 attention_grad.2
  136.6 14.5 %all_to_all.27.refs_0_ = bf16[4,272,256]{2,1,0:T(8,128)(2,1)S(1)} all-to-all(bf16[4,272,256]{2,1,0:T(8,128)(2,1)S(1)} %attention_grad.2), channel_id=1, replica_groups=mesh['y'=4,'x'=4,'core'=2,'tp'=8] {'y'}, dimensions={0} | all-to-all | bytes 1114112 | tf_op jit(solution)/shard_map/attention_grad/all_to_all | solution.py:727
  151.2 2.8 %collective-permute-start.26 = (bf16[128,256]{1,0:T(8,128)(2,1)S(1)}, bf16[128,256]{1,0:T(8,128)(2,1)S(1)}, u32[]{:S(2)}, u32[]{:S(2)}) collective-permute-start(bf16[128,256]{1,0:T(8,128)(2,1)S(1)} %broadcast_select_fusion.2), channel_id=1, source_target_pairs={{0,8},{8,0},{1,9},{9,1},{2,10},{10,2},{3,11},{11,3},{4,12},{12,4},... | collective-permute-start | bytes 196616 | tf_op jit(solution)/shard_map/attention_grad/ppermute | solution.py:68
  154.0 0.1 collective-permute-start.27
  154.1 1.0 collective-permute-done.27
  155.9 1.6 copy-done.4
  157.5 1.3 d_context.2
  158.9 31.6 %all_to_all.28.arrived_ref = bf16[8,512,128]{2,1,0:T(8,128)(2,1)S(1)} all-to-all(bf16[8,512,128]{2,1,0:T(8,128)(2,1)S(1)} %d_context.2), channel_id=1, replica_groups=mesh['y'=4,'x'=4,'core'=2,'tp'=8] {'tp'}, dimensions={0} | all-to-all | bytes 2097152 | tf_op jit(solution)/shard_map/d_context/all_to_all | solution.py:745
  190.5 0.9 d_context.3
  (57 shorter events, 0.5 us)
Async XLA Ops:
  0.6 9.8 %copy-start.1 = (bf16[4096,256]{1,0:T(8,128)(2,1)S(1)}, bf16[4096,256]{1,0:T(8,128)(2,1)}, u32[]{:S(2)}) copy-start(bf16[4096,256]{1,0:T(8,128)(2,1)} %key_ref.3) | copy-start | bytes 6291460
  3.9 12.4 %collective-permute-start.8 = (bf16[224,512]{1,0:T(8,128)(2,1)}, bf16[224,512]{1,0:T(8,128)(2,1)S(1)}, u32[]{:S(2)}, u32[]{:S(2)}) collective-permute-start(bf16[224,512]{1,0:T(8,128)(2,1)} %inputs.1.refs_0_.sent_ref), channel_id=1, source_target_pairs={{0,7},{1,0},{2,1},{3,2},{4,3},{5,4},{6,5},{7,6},{8,15},{9,8},{10,9... | collective-permute-start | bytes 688136 | tf_op jit(solution)/shard_map/inputs/ppermute | solution.py:51
  10.4 8.9 %collective-permute-start.4 = (bf16[224,512]{1,0:T(8,128)(2,1)}, bf16[224,512]{1,0:T(8,128)(2,1)S(1)}, u32[]{:S(2)}, u32[]{:S(2)}) collective-permute-start(bf16[224,512]{1,0:T(8,128)(2,1)} %inputs.1.refs_0_.sent_ref), channel_id=1, source_target_pairs={{0,1},{1,2},{2,3},{3,4},{4,5},{5,6},{6,7},{7,0},{8,9},{9,10},{10,1... | collective-permute-start | bytes 688136 | tf_op jit(solution)/shard_map/inputs/ppermute | solution.py:50
  10.4 1.6 copy-start.3
  12.0 1.2 copy-start.8
  13.3 27.4 %copy-start.7 = (bf16[224,512]{1,0:T(8,128)(2,1)S(1)}, bf16[224,512]{1,0:T(8,128)(2,1)}, u32[]{:S(2)}) copy-start(bf16[224,512]{1,0:T(8,128)(2,1)} %inputs.1.refs_0_.sent_ref) | copy-start | bytes 688132
  15.2 25.4 %copy-start = (bf16[256,4096]{1,0:T(8,128)(2,1)S(1)}, bf16[256,4096]{1,0:T(8,128)(2,1)}, u32[]{:S(2)}) copy-start(bf16[256,4096]{1,0:T(8,128)(2,1)} %w_out_ref.1) | copy-start | bytes 6291460
  15.2 4.0 %collective-permute-start = (bf16[128,256]{1,0:T(8,128)(2,1)S(1)}, bf16[128,256]{1,0:T(8,128)(2,1)S(1)}, u32[]{:S(2)}, u32[]{:S(2)}) collective-permute-start(bf16[128,256]{1,0:T(8,128)(2,1)S(1)} %get-tuple-element.20), channel_id=1, source_target_pairs={{0,8},{8,0},{1,9},{9,1},{2,10},{10,2},{3,11},{11,3},{4,12},{12,4},... | collective-permute-start | bytes 196616 | tf_op jit(solution)/shard_map/keys_values/ppermute | solution.py:68
  16.3 7.3 %collective-permute-start.9 = (bf16[224,512]{1,0:T(8,128)(2,1)S(1)}, bf16[224,512]{1,0:T(8,128)(2,1)S(1)}, u32[]{:S(2)}, u32[]{:S(2)}) collective-permute-start(bf16[224,512]{1,0:T(8,128)(2,1)S(1)} %collective-permute-done.8.refs_8_), channel_id=1, source_target_pairs={{0,7},{1,0},{2,1},{3,2},{4,3},{5,4},{6,5},{7,6},{8,15},{9,8},{10,9... | collective-permute-start | bytes 688136 | tf_op jit(solution)/shard_map/inputs/ppermute | solution.py:51
  19.2 7.8 %collective-permute-start.5 = (bf16[224,512]{1,0:T(8,128)(2,1)S(1)}, bf16[224,512]{1,0:T(8,128)(2,1)S(1)}, u32[]{:S(2)}, u32[]{:S(2)}) collective-permute-start(bf16[224,512]{1,0:T(8,128)(2,1)S(1)} %collective-permute-done.4.refs_1_), channel_id=1, source_target_pairs={{0,1},{1,2},{2,3},{3,4},{4,5},{5,6},{6,7},{7,0},{8,9},{9,10},{10,1... | collective-permute-start | bytes 688136 | tf_op jit(solution)/shard_map/inputs/ppermute | solution.py:50
  23.6 9.1 %collective-permute-start.10 = (bf16[224,512]{1,0:T(8,128)(2,1)S(1)}, bf16[224,512]{1,0:T(8,128)(2,1)S(1)}, u32[]{:S(2)}, u32[]{:S(2)}) collective-permute-start(bf16[224,512]{1,0:T(8,128)(2,1)S(1)} %collective-permute-done.9.refs_7_), channel_id=1, source_target_pairs={{0,7},{1,0},{2,1},{3,2},{4,3},{5,4},{6,5},{7,6},{8,15},{9,8},{10,9... | collective-permute-start | bytes 688136 | tf_op jit(solution)/shard_map/inputs/ppermute | solution.py:51
  27.0 8.5 %collective-permute-start.6 = (bf16[224,512]{1,0:T(8,128)(2,1)S(1)}, bf16[224,512]{1,0:T(8,128)(2,1)S(1)}, u32[]{:S(2)}, u32[]{:S(2)}) collective-permute-start(bf16[224,512]{1,0:T(8,128)(2,1)S(1)} %collective-permute-done.5.refs_2_), channel_id=1, source_target_pairs={{0,1},{1,2},{2,3},{3,4},{4,5},{5,6},{6,7},{7,0},{8,9},{9,10},{10,1... | collective-permute-start | bytes 688136 | tf_op jit(solution)/shard_map/inputs/ppermute | solution.py:50
  27.0 8.7 %collective-permute-start.2 = (bf16[256,256]{1,0:T(8,128)(2,1)S(1)}, bf16[256,256]{1,0:T(8,128)(2,1)S(1)}, u32[]{:S(2)}, u32[]{:S(2)}) collective-permute-start(bf16[256,256]{1,0:T(8,128)(2,1)S(1)} %get-tuple-element.43), channel_id=1, source_target_pairs={{0,128},{64,192},{128,0},{192,64},{1,129},{65,193},{129,1},{193,65... | collective-permute-start | bytes 393224 | tf_op jit(solution)/shard_map/keys_values/ppermute | solution.py:35
  30.0 6.6 %collective-permute-start.1 = (bf16[256,256]{1,0:T(8,128)(2,1)S(1)}, bf16[256,256]{1,0:T(8,128)(2,1)S(1)}, u32[]{:S(2)}, u32[]{:S(2)}) collective-permute-start(bf16[256,256]{1,0:T(8,128)(2,1)S(1)} %get-tuple-element.43), channel_id=1, source_target_pairs={{0,64},{64,128},{128,192},{192,0},{1,65},{65,129},{129,193},{193,1... | collective-permute-start | bytes 393224 | tf_op jit(solution)/shard_map/keys_values/ppermute | solution.py:35
  30.4 6.2 %collective-permute-start.3 = (bf16[256,256]{1,0:T(8,128)(2,1)S(1)}, bf16[256,256]{1,0:T(8,128)(2,1)S(1)}, u32[]{:S(2)}, u32[]{:S(2)}) collective-permute-start(bf16[256,256]{1,0:T(8,128)(2,1)S(1)} %get-tuple-element.43), channel_id=1, source_target_pairs={{0,192},{64,0},{128,64},{192,128},{1,193},{65,1},{129,65},{193,129... | collective-permute-start | bytes 393224 | tf_op jit(solution)/shard_map/keys_values/ppermute | solution.py:35
  32.7 4.5 %collective-permute-start.11 = (bf16[112,512]{1,0:T(8,128)(2,1)S(1)}, bf16[112,512]{1,0:T(8,128)(2,1)S(1)}, u32[]{:S(2)}, u32[]{:S(2)}) collective-permute-start(bf16[112,512]{1,0:T(8,128)(2,1)S(1)} %slice.53), channel_id=1, source_target_pairs={{0,7},{1,0},{2,1},{3,2},{4,3},{5,4},{6,5},{7,6},{8,15},{9,8},{10,9... | collective-permute-start | bytes 344072 | tf_op jit(solution)/shard_map/inputs/ppermute | solution.py:53
  35.5 5.1 %collective-permute-start.7 = (bf16[112,512]{1,0:T(8,128)(2,1)S(1)}, bf16[112,512]{1,0:T(8,128)(2,1)S(1)}, u32[]{:S(2)}, u32[]{:S(2)}) collective-permute-start(bf16[112,512]{1,0:T(8,128)(2,1)S(1)} %slice.52), channel_id=1, source_target_pairs={{0,1},{1,2},{2,3},{3,4},{4,5},{5,6},{6,7},{7,0},{8,9},{9,10},{10,1... | collective-permute-start | bytes 344072 | tf_op jit(solution)/shard_map/inputs/ppermute | solution.py:53
  40.6 1.6 copy-start.6
  46.4 0.9 copy-start.9
  47.3 14.4 %copy-start.5 = (bf16[512,1024]{1,0:T(8,128)(2,1)S(1)}, bf16[512,1024]{1,0:T(8,128)(2,1)}, u32[]{:S(2)}) copy-start(bf16[512,1024]{1,0:T(8,128)(2,1)} %post_ref.3) | copy-start | bytes 3145732
  47.3 20.4 %copy-start.10 = (s32[4]{0:T(128)S(1)}, s32[4]{0:T(128)}, u32[]{:S(2)}) copy-start(s32[4]{0:T(128)} %lengths_ref.5) | copy-start | bytes 52
  47.3 22.0 %all-to-all-start = ((bf16[16,96,256]{2,1,0:T(8,128)(2,1)}), bf16[16,96,256]{2,1,0:T(8,128)(2,1)S(1)}, u32[]{:S(2)}, u32[]{:S(2)}) async-start(bf16[16,96,256]{2,1,0:T(8,128)(2,1)} %copy-done.9), calls=%async_computation | async-start | bytes 1572864 | tf_op jit(solution)/shard_map/gathered/all_to_all | solution.py:646
  52.7 5.0 %collective-permute-start.12 = (bf16[128,128]{1,0:T(8,128)(2,1)S(1)}, bf16[128,128]{1,0:T(8,128)(2,1)S(1)}, u32[]{:S(2)}, u32[]{:S(2)}) collective-permute-start(bf16[128,128]{1,0:T(8,128)(2,1)S(1)} %get-tuple-element.22), channel_id=1, source_target_pairs={{0,8},{8,0},{1,9},{9,1},{2,10},{10,2},{3,11},{11,3},{4,12},{12,4},... | collective-permute-start | bytes 98312 | tf_op jit(solution)/shard_map/gathered/ppermute | solution.py:68
  57.8 5.3 %collective-permute-start.15 = (bf16[256,128]{1,0:T(8,128)(2,1)S(1)}, bf16[256,128]{1,0:T(8,128)(2,1)S(1)}, u32[]{:S(2)}, u32[]{:S(2)}) collective-permute-start(bf16[256,128]{1,0:T(8,128)(2,1)S(1)} %get-tuple-element.51.hold_ref), channel_id=1, source_target_pairs={{0,48},{16,0},{32,16},{48,32},{1,49},{17,1},{33,17},{49,33},{2,50}... | collective-permute-start | bytes 196616 | tf_op jit(solution)/shard_map/gathered/ppermute | solution.py:35
  60.6 5.7 %collective-permute-start.14 = (bf16[256,128]{1,0:T(8,128)(2,1)S(1)}, bf16[256,128]{1,0:T(8,128)(2,1)S(1)}, u32[]{:S(2)}, u32[]{:S(2)}) collective-permute-start(bf16[256,128]{1,0:T(8,128)(2,1)S(1)} %get-tuple-element.51.hold_ref), channel_id=1, source_target_pairs={{0,32},{16,48},{32,0},{48,16},{1,33},{17,49},{33,1},{49,17},{2,34}... | collective-permute-start | bytes 196616 | tf_op jit(solution)/shard_map/gathered/ppermute | solution.py:35
  61.2 6.5 %collective-permute-start.13 = (bf16[256,128]{1,0:T(8,128)(2,1)S(1)}, bf16[256,128]{1,0:T(8,128)(2,1)S(1)}, u32[]{:S(2)}, u32[]{:S(2)}) collective-permute-start(bf16[256,128]{1,0:T(8,128)(2,1)S(1)} %get-tuple-element.51.hold_ref), channel_id=1, source_target_pairs={{0,16},{16,32},{32,48},{48,0},{1,17},{17,33},{33,49},{49,1},{2,18}... | collective-permute-start | bytes 196616 | tf_op jit(solution)/shard_map/gathered/ppermute | solution.py:35
  69.4 10.4 %collective-permute-start.20 = (bf16[16,96,256]{2,1,0:T(8,128)(2,1)S(1)}, bf16[16,96,256]{2,1,0:T(8,128)(2,1)S(1)}, u32[]{:S(2)}, u32[]{:S(2)}) collective-permute-start(bf16[16,96,256]{2,1,0:T(8,128)(2,1)S(1)} %all-to-all-done.own_ref), channel_id=1, source_target_pairs={{0,8},{8,0},{1,9},{9,1},{2,10},{10,2},{3,11},{11,3},{4,12},{12,4},... | collective-permute-start | bytes 2359304 | tf_op jit(solution)/shard_map/gathered/ppermute | solution.py:68
  70.6 7.3 %collective-permute-start.18 = (bf16[272,128]{1,0:T(8,128)(2,1)S(1)}, bf16[272,128]{1,0:T(8,128)(2,1)S(1)}, u32[]{:S(2)}, u32[]{:S(2)}) collective-permute-start(bf16[272,128]{1,0:T(8,128)(2,1)S(1)} %get-tuple-element.36), channel_id=1, source_target_pairs={{0,16},{16,32},{32,48},{48,0},{1,17},{17,33},{33,49},{49,1},{2,18}... | collective-permute-start | bytes 208904 | tf_op jit(solution)/shard_map/attention/ppermute | solution.py:41
  71.2 6.7 %collective-permute-start.17 = (bf16[272,128]{1,0:T(8,128)(2,1)S(1)}, bf16[272,128]{1,0:T(8,128)(2,1)S(1)}, u32[]{:S(2)}, u32[]{:S(2)}) collective-permute-start(bf16[272,128]{1,0:T(8,128)(2,1)S(1)} %get-tuple-element.37), channel_id=1, source_target_pairs={{0,32},{16,48},{32,0},{48,16},{1,33},{17,49},{33,1},{49,17},{2,34}... | collective-permute-start | bytes 208904 | tf_op jit(solution)/shard_map/attention/ppermute | solution.py:41
  73.0 5.0 %collective-permute-start.16 = (bf16[272,128]{1,0:T(8,128)(2,1)S(1)}, bf16[272,128]{1,0:T(8,128)(2,1)S(1)}, u32[]{:S(2)}, u32[]{:S(2)}) collective-permute-start(bf16[272,128]{1,0:T(8,128)(2,1)S(1)} %get-tuple-element.38), channel_id=1, source_target_pairs={{0,48},{16,0},{32,16},{48,32},{1,49},{17,1},{33,17},{49,33},{2,50}... | collective-permute-start | bytes 208904 | tf_op jit(solution)/shard_map/attention/ppermute | solution.py:41
  74.4 4.9 %collective-permute-start.21 = (bf16[1,1024]{1,0:T(2,128)(2,1)S(1)}, bf16[1,1024]{1,0:T(2,128)(2,1)S(1)}, u32[]{:S(2)}, u32[]{:S(2)}) collective-permute-start(bf16[1,1024]{1,0:T(2,128)(2,1)S(1)} %slice.48), channel_id=1, source_target_pairs={{8,0},{16,8},{24,16},{32,24},{40,32},{48,40},{56,48},{64,56},{72,6... | collective-permute-start | bytes 6152 | tf_op jit(solution)/shard_map/targets/ppermute | solution.py:614
  78.2 1.5 collective-permute-start.19
  80.7 42.3 %copy-start.11 = (s32[128]{0:T(128)S(1)}, s32[128]{0:T(128)}, u32[]{:S(2)}) copy-start(s32[128]{0:T(128)} %param.14) | copy-start | bytes 1540
  124.0 1.9 collective-permute-start.22
  126.1 29.8 %copy-start.2 = (bf16[4096,256]{1,0:T(8,128)(2,1)S(1)}, bf16[4096,256]{1,0:T(8,128)(2,1)}, u32[]{:S(2)}) copy-start(bf16[4096,256]{1,0:T(8,128)(2,1)} %key_ref.3) | copy-start | bytes 6291460
  126.1 5.7 %collective-permute-start.25 = (bf16[272,128]{1,0:T(8,128)(2,1)S(1)}, bf16[272,128]{1,0:T(8,128)(2,1)S(1)}, u32[]{:S(2)}, u32[]{:S(2)}) collective-permute-start(bf16[272,128]{1,0:T(8,128)(2,1)S(1)} %sent_grads.1.refs_0_), channel_id=1, source_target_pairs={{0,48},{16,0},{32,16},{48,32},{1,49},{17,1},{33,17},{49,33},{2,50}... | collective-permute-start | bytes 208904 | tf_op jit(solution)/shard_map/sent_grads/ppermute | solution.py:35
  129.0 4.8 %collective-permute-start.24 = (bf16[272,128]{1,0:T(8,128)(2,1)S(1)}, bf16[272,128]{1,0:T(8,128)(2,1)S(1)}, u32[]{:S(2)}, u32[]{:S(2)}) collective-permute-start(bf16[272,128]{1,0:T(8,128)(2,1)S(1)} %sent_grads.1.refs_0_), channel_id=1, source_target_pairs={{0,32},{16,48},{32,0},{48,16},{1,33},{17,49},{33,1},{49,17},{2,34}... | collective-permute-start | bytes 208904 | tf_op jit(solution)/shard_map/sent_grads/ppermute | solution.py:35
  129.0 6.1 %collective-permute-start.23 = (bf16[272,128]{1,0:T(8,128)(2,1)S(1)}, bf16[272,128]{1,0:T(8,128)(2,1)S(1)}, u32[]{:S(2)}, u32[]{:S(2)}) collective-permute-start(bf16[272,128]{1,0:T(8,128)(2,1)S(1)} %sent_grads.1.refs_0_), channel_id=1, source_target_pairs={{0,16},{16,32},{32,48},{48,0},{1,17},{17,33},{33,49},{49,1},{2,18}... | collective-permute-start | bytes 208904 | tf_op jit(solution)/shard_map/sent_grads/ppermute | solution.py:35
  151.2 4.6 %collective-permute-start.26 = (bf16[128,256]{1,0:T(8,128)(2,1)S(1)}, bf16[128,256]{1,0:T(8,128)(2,1)S(1)}, u32[]{:S(2)}, u32[]{:S(2)}) collective-permute-start(bf16[128,256]{1,0:T(8,128)(2,1)S(1)} %broadcast_select_fusion.2), channel_id=1, source_target_pairs={{0,8},{8,0},{1,9},{9,1},{2,10},{10,2},{3,11},{11,3},{4,12},{12,4},... | collective-permute-start | bytes 196616 | tf_op jit(solution)/shard_map/attention_grad/ppermute | solution.py:68
  154.0 1.1 collective-permute-start.27
  155.9 1.6 copy-start.4

commit v7 on v6

--- a/solution.py
+++ b/solution.py
@@ -16,6 +16,7 @@
 ROWS = ("y", "x", "core")
 CHIPS = ("y", "x")
 SCALE = 1.0 / math.sqrt(HDIM)
+LOG2E = math.log2(math.e)
 PAIR = 256
 GROUP = 4
 FOLD_POST = 32
@@ -243,32 +244,28 @@
         return dot(block, w_query_ref[at, :])
 
     both = jnp.zeros((top, heads), F32)
-    for distance in list(blocks):
+    squares = jnp.zeros((rows, 1), F32)
+    query = jnp.zeros((rows, heads), F32)
+    for step, distance in enumerate(list(blocks) + [1, parts - 1]):
+        if step >= parts - 2:
+            near_copies[step - parts + 2].wait()
+            blocks[distance] = near[step - parts + 2]
+        wide = blocks[distance][:rows].astype(F32)
+        squares = squares + jnp.sum(wide * wide, axis=1, keepdims=True)
         both = against(both, by_out, distance, top)
-    for copy in near_copies:
-        copy.wait()
-    for k, distance in enumerate((1, parts - 1)):
-        blocks[distance] = near[k]
-        both = against(both, by_out, distance, top)
+        query = against(query, by_query, distance, rows)
     cross_ref[...] = both[:rows]
     span = FOLD_OUT * parts
-    slices = jnp.concatenate([blocks[k][top:] for k in range(parts)], axis=0)
-    gram = [jnp.zeros((FOLD_OUT, heads), F32)] * parts
+    slices = [blocks[k][top:].astype(F32) for k in range(parts)]
+    gram = jnp.zeros((span, heads), F32)
     for k in range(parts):
-        product = by_out(slices, slice(share * k, share * (k + 1)))
-        for b in range(parts):
-            at = span * b + FOLD_OUT * k
-            gram[b] = gram[b] + product[at : at + FOLD_OUT]
-    folded = jnp.concatenate([both[rows:]] + gram, axis=0).astype(BF16)
+        at = slice(FOLD_OUT * k, FOLD_OUT * (k + 1))
+        chunk = jnp.concatenate([block[at] for block in slices], axis=0).astype(BF16)
+        gram = gram + by_out(chunk, slice(share * k, share * (k + 1)))
+    folded = jnp.concatenate((both[rows:], gram), axis=0).astype(BF16)
     for k in range(folded_ref.shape[0]):
         folded_ref[k] = folded
 
-    squares = jnp.zeros((rows, 1), F32)
-    query = jnp.zeros((rows, heads), F32)
-    for distance in range(parts):
-        wide = blocks[distance][:rows].astype(F32)
-        squares = squares + jnp.sum(wide * wide, axis=1, keepdims=True)
-        query = against(query, by_query, distance, rows)
     query = (query * lax.rsqrt(squares / width + EPSILON)).astype(BF16)
     first = place_ref[2] == 0
     mine_ref[...] = jnp.where(first, query[:, :HDIM], query[:, HDIM:])
@@ -304,36 +301,52 @@
     return (key_pos >= query_start) & (key_pos <= query_pos)
 
 
-def forward_kernel(lengths_ref, place_ref, q_ref, kv_ref, hold_ref, out_ref):
+def unmasked(place_ref, ends, step):
+    row = place_ref[1] // GROUP
+    first_key = (place_ref[1] - step * GROUP) * PAIR
+    return (step > 0) & (start_of(ends, (row + 1) * (GROUP * PAIR) - 1) <= first_key)
+
+
+def forward_kernel(lengths_ref, place_ref, q_ref, kv_ref, hold_ref, out_ref, max_ref, sum_ref, acc_ref):
     ends = ends_of(lengths_ref)
     width = GROUP * PAIR
     query_pos = line_positions(place_ref)
     query_start = start_of(ends, query_pos)
     q = q_ref[...].reshape(width, HDIM)
-
-    def body(step, carry):
-        row_max, row_total, weighted = carry
-        scores = dot(kv_ref[step, :, :HDIM], q, ((1,), (1,))) * SCALE
-        scores = jnp.where(allowed_pairs(place_ref, step, query_start, query_pos), scores, MASKED)
+    max_ref[...] = jnp.full((1, width), MASKED, F32)
+    sum_ref[...] = jnp.zeros((1, width), F32)
+    acc_ref[...] = jnp.zeros((HDIM, width), F32)
+
+    def add(step, scores):
+        row_max = max_ref[...]
         new_max = jnp.maximum(row_max, jnp.max(scores, axis=0, keepdims=True))
-        probs = jnp.exp(scores - new_max)
-        fading = jnp.exp(row_max - new_max)
-        row_total = row_total * fading + jnp.sum(probs, axis=0, keepdims=True)
-        weighted = weighted * fading + dot(kv_ref[step, :, HDIM:], probs.astype(BF16), ((0,), (0,)))
-        return new_max, row_total, weighted
-
-    row_max, row_total, weighted = lax.fori_loop(
-        0,
-        key_steps(place_ref, ends),
-        body,
-        (
-            jnp.full((1, width), MASKED, F32),
-            jnp.zeros((1, width), F32),
-            jnp.zeros((HDIM, width), F32),
-        ),
-    )
-    out = (weighted / row_total).T.astype(BF16)
-    log_total = row_max + jnp.log(row_total)
+        probs = jnp.exp2(scores - new_max)
+        fading = jnp.exp2(row_max - new_max)
+        max_ref[...] = new_max
+        sum_ref[...] = sum_ref[...] * fading + jnp.sum(probs, axis=0, keepdims=True)
+        acc_ref[...] = acc_ref[...] * fading + dot(
+            kv_ref[step, :, HDIM:], probs.astype(BF16), ((0,), (0,))
+        )
+
+    steps = key_steps(place_ref, ends)
+    for step in range(kv_ref.shape[0]):
+        whole = unmasked(place_ref, ends, step)
+
+        def scores_of():
+            return dot(kv_ref[step, :, :HDIM], q, ((1,), (1,))) * (SCALE * LOG2E)
+
+        @pl.when((step < steps) & whole)
+        def _():
+            add(step, scores_of())
+
+        @pl.when((step < steps) & jnp.logical_not(whole))
+        def _():
+            allowed = allowed_pairs(place_ref, step, query_start, query_pos)
+            add(step, jnp.where(allowed, scores_of(), MASKED))
+
+    row_total = sum_ref[...]
+    out = (acc_ref[...] / row_total).T.astype(BF16)
+    log_total = max_ref[...] * (1.0 / LOG2E) + jnp.log(row_total)
     for k in range(GROUP):
         at = slice(PAIR * k, PAIR * (k + 1))
         out_ref[k, :PAIR, :] = out[at]
@@ -488,7 +501,7 @@
     q = q_ref[...].reshape(width, HDIM)
     grad = jnp.concatenate([ref[:PAIR, :] for ref in sent_refs], axis=0)
     stats = [ref[PAIR:, :].astype(F32) for ref in sent_refs]
-    log_total = jnp.concatenate([stat_row(x, 0) for x in stats], axis=1)
+    log_total = jnp.concatenate([stat_row(x, 0) for x in stats], axis=1) * LOG2E
     output_dot = jnp.concatenate([stat_row(x, 6) for x in stats], axis=1)
     loss = functools.reduce(jnp.add, [x[12:13] + x[13:14] + x[14:15] for x in stats])
     tail = jnp.concatenate(
@@ -500,15 +513,20 @@
         row = lax.rem(place_ref[1] // GROUP + (out_ref.shape[0] - step), out_ref.shape[0])
         out_ref[row, PAIR:, :] = tail
 
-        @pl.when(step < steps)
-        def _():
-            allowed = allowed_pairs(place_ref, step, query_start, query_pos)
-            scores = dot(kv_ref[step, :, :HDIM], q, ((1,), (1,))) * SCALE
-            probs = jnp.where(allowed, jnp.exp(scores - log_total), 0.0)
+        def grads(masked):
+            scores = dot(kv_ref[step, :, :HDIM], q, ((1,), (1,))) * (SCALE * LOG2E)
+            probs = jnp.exp2(scores - log_total)
+            if masked:
+                allowed = allowed_pairs(place_ref, step, query_start, query_pos)
+                probs = jnp.where(allowed, probs, 0.0)
             out_ref[row, :PAIR, HDIM:] = dot(probs.astype(BF16), grad).astype(BF16)
             prob_grad = dot(kv_ref[step, :, HDIM:], grad, ((1,), (1,)))
-            score_grad = (probs * (prob_grad - output_dot) * SCALE).astype(BF16)
-            out_ref[row, :PAIR, :HDIM] = dot(score_grad, q).astype(BF16)
+            score_grad = (probs * (prob_grad - output_dot)).astype(BF16)
+            out_ref[row, :PAIR, :HDIM] = (dot(score_grad, q) * SCALE).astype(BF16)
+
+        whole = unmasked(place_ref, ends, step)
+        pl.when((step < steps) & whole)(functools.partial(grads, False))
+        pl.when((step < steps) & jnp.logical_not(whole))(functools.partial(grads, True))
 
         @pl.when(step >= steps)
         def _():
@@ -524,15 +542,15 @@
     loss_ref[...] = jnp.sum(rows, axis=0, keepdims=True)
 
 
-def context_kernel(grad_ref, hold_ref, key_ref, value_ref, out_ref):
-    grad = grad_ref[...].astype(F32).T.astype(BF16)
-    key_grad = jnp.concatenate((grad[:HDIM], grad[2 * HDIM : 3 * HDIM]), axis=0)
-    value_grad = jnp.concatenate((grad[HDIM : 2 * HDIM], grad[3 * HDIM :]), axis=0)
+def context_kernel(lanes, grad_ref, start_ref, weight_ref, out_ref):
+    grad = jnp.concatenate([grad_ref[:, HDIM * k : HDIM * (k + 1)] for k in lanes], axis=1)
+    grad = grad.astype(F32).T.astype(BF16)
     parts, share, _ = out_ref.shape
     for k in range(parts):
-        at = slice(share * k, share * (k + 1))
-        total = dot(key_ref[at], key_grad) + dot(value_ref[at], value_grad)
-        out_ref[k] = total.astype(BF16)
+        total = dot(weight_ref[share * k : share * (k + 1)], grad)
+        if out_ref.dtype == BF16:
+            total = total + start_ref[k]
+        out_ref[k] = total.astype(out_ref.dtype)
 
 
 def total_kernel(arrived_ref, out_ref):
@@ -651,6 +669,11 @@
             out_shape=jax.ShapeDtypeStruct((GROUP, PAIR + STATS, HDIM), BF16),
             in_specs=[SMEM, SMEM, VMEM, VMEM, ANY],
             out_specs=VMEM,
+            scratch_shapes=[
+                pltpu.VMEM((1, GROUP * PAIR), F32),
+                pltpu.VMEM((1, GROUP * PAIR), F32),
+                pltpu.VMEM((HDIM, GROUP * PAIR), F32),
+            ],
             compiler_params=PARAMS,
         )(doc_lengths, place, line_queries, all_kv, input_post)
         attended_head, log_total = pl.pallas_call(
@@ -729,13 +752,20 @@
         loss_part = loss_part[0, 0]
         loss = (loss_part + swap(loss_part)) / (seq_total * features)
     with jax.named_scope("d_context"):
+        key_terms = pl.pallas_call(
+            functools.partial(context_kernel, (0, 2)),
+            out_shape=jax.ShapeDtypeStruct((parts, share, rows), F32),
+            in_specs=[VMEM, ANY, VMEM],
+            out_specs=VMEM,
+            compiler_params=PARAMS,
+        )(kv_grad, loss.reshape(1, 1), w_key)
         terms = pl.pallas_call(
-            context_kernel,
+            functools.partial(context_kernel, (1, 3)),
             out_shape=jax.ShapeDtypeStruct((parts, share, rows), BF16),
-            in_specs=[VMEM, ANY, VMEM, VMEM],
+            in_specs=[VMEM, VMEM, VMEM],
             out_specs=VMEM,
             compiler_params=PARAMS,
-        )(kv_grad, loss.reshape(1, 1), w_key, w_value)
+        )(kv_grad, key_terms, w_value)
         d_context = pl.pallas_call(
             total_kernel,
             out_shape=jax.ShapeDtypeStruct((rows, share), BF16),

time: 194 us -> 192 us (0.990)
  no operation moved by 1% of the time
where the time goes in v7:
time: 192 us; the launch traced here: 190 us
  blocking collectives  86.6 us (45%)
  starting transfers between devices  51 us (27%)
  waiting for transfers between devices  23.5 us (12%)
  Pallas kernels  18 us (9%)
  local copies, waits for them, and re-layouts  7.91 us (4%)
  between operations  2.84 us (1%)
    all_to_all x2, blocking collectives, local(): arrived = lax.all_to_all(sent, 'tp', 0, 0, tiled=True)  40.7 us
    all_to_all x1, blocking collectives, local(): lax.all_to_all(terms, 'tp', 0, 0, tiled=True)  31.6 us
    all_to_all x1, blocking collectives, local(): lax.all_to_all(sent, 'y', 0, 0, tiled=True)  14.3 us
    ppermute x9, starting transfers between devices, shifted(): return [block] + [lax.ppermute(block, axis, route) for route in routes]  13 us
    ppermute x3, starting transfers between devices, around(): ahead.append(lax.ppermute(ahead[-1], axis, down))  12.8 us
    ppermute x9, waiting for transfers between devices, shifted(): return [block] + [lax.ppermute(block, axis, route) for route in routes]  11.8 us
    ppermute x7, starting transfers between devices, swap(): return lax.ppermute(block, 'core', [(0, 1), (1, 0)])  11.4 us
    unnamed x24, local copies, waits for them, and re-layouts  6.13 us
  transfers between devices with their start and end apart: 29, of which 15 were waited for; matrix products, arithmetic and copies ran while one was open for 1% of the time, Pallas kernels for 2%

profile of v7, /device:TPU:1, one launch (start us, length us, event | category | flops | bytes accessed | tf_op | source)
XLA Modules:
  0.0 190.2 jit_solution(15289390636898984572)
XLA Ops:
  0.6 3.2 %inputs.1.refs_0_.sent_ref = bf16[224,512]{1,0:T(8,128)(2,1)} custom-call(s32[1,128]{1,0:T(1,128)} %bitcast.26, f32[1,512]{1,0:T(1,128)} %bitcast.36, bf16[128,1024]{1,0:T(8,128)(2,1)} %noised_ref.1, bf16[1024,512]{1,0:T(8,128)(2,1)} %pre_ref.1, bf16[512,1024]{1,0:T(8,128)(2,1)} %post_ref.3, bf16[256,4096]{1,0:T(8,128)(2,1)} %w_out_ref.1), custom_call_target="tpu_custom_call" | custom-call | tf_op jit(solution)/shard_map/inputs/pallas_call | solution.py:599
  3.9 6.5 %collective-permute-start.8 = (bf16[224,512]{1,0:T(8,128)(2,1)}, bf16[224,512]{1,0:T(8,128)(2,1)S(1)}, u32[]{:S(2)}, u32[]{:S(2)}) collective-permute-start(bf16[224,512]{1,0:T(8,128)(2,1)} %inputs.1.refs_0_.sent_ref), channel_id=1, source_target_pairs={{0,7},{1,0},{2,1},{3,2},{4,3},{5,4},{6,5},{7,6},{8,15},{9,8},{10,9... | collective-permute-start | bytes 688136 | tf_op jit(solution)/shard_map/inputs/ppermute | solution.py:52
  10.4 1.6 copy-done.3
  12.0 1.2 copy-done.8
  13.3 1.9 %keys_values.1 = (bf16[128,256]{1,0:T(8,128)(2,1)S(1)}, bf16[128,256]{1,0:T(8,128)(2,1)S(1)}) custom-call(s32[4]{0:T(128)S(1)} %pad_add_fusion.place_ref, bf16[128,4096]{1,0:T(8,128)(2,1)S(1)} %copy-done.8, bf16[4096,256]{1,0:T(8,128)(2,1)S(1)} %copy-done.1, bf16[4096,256]{1,0:T(8,128)(2,1)S(1)} %copy-done.3), custom_call_target="tpu_custom_call" | custom-call | tf_op jit(solution)/shard_map/keys_values/pallas_call | solution.py:616
  15.2 1.0 collective-permute-start
  16.3 3.0 %collective-permute-start.9 = (bf16[224,512]{1,0:T(8,128)(2,1)S(1)}, bf16[224,512]{1,0:T(8,128)(2,1)S(1)}, u32[]{:S(2)}, u32[]{:S(2)}) collective-permute-start(bf16[224,512]{1,0:T(8,128)(2,1)S(1)} %collective-permute-done.8.refs_8_), channel_id=1, source_target_pairs={{0,7},{1,0},{2,1},{3,2},{4,3},{5,4},{6,5},{7,6},{8,15},{9,8},{10,9... | collective-permute-start | bytes 688136 | tf_op jit(solution)/shard_map/inputs/ppermute | solution.py:52
  19.3 4.4 %collective-permute-done.9.refs_7_ = bf16[224,512]{1,0:T(8,128)(2,1)S(1)} collective-permute-done((bf16[224,512]{1,0:T(8,128)(2,1)S(1)}, bf16[224,512]{1,0:T(8,128)(2,1)S(1)}, u32[]{:S(2)}, u32[]{:S(2)}) %collective-permute-start.9) | collective-permute-done | bytes 229408 | tf_op jit(solution)/shard_map/inputs/ppermute | solution.py:52
  23.6 3.4 %collective-permute-start.10 = (bf16[224,512]{1,0:T(8,128)(2,1)S(1)}, bf16[224,512]{1,0:T(8,128)(2,1)S(1)}, u32[]{:S(2)}, u32[]{:S(2)}) collective-permute-start(bf16[224,512]{1,0:T(8,128)(2,1)S(1)} %collective-permute-done.9.refs_7_), channel_id=1, source_target_pairs={{0,7},{1,0},{2,1},{3,2},{4,3},{5,4},{6,5},{7,6},{8,15},{9,8},{10,9... | collective-permute-start | bytes 688136 | tf_op jit(solution)/shard_map/inputs/ppermute | solution.py:52
  27.0 3.0 %collective-permute-start.2 = (bf16[256,256]{1,0:T(8,128)(2,1)S(1)}, bf16[256,256]{1,0:T(8,128)(2,1)S(1)}, u32[]{:S(2)}, u32[]{:S(2)}) collective-permute-start(bf16[256,256]{1,0:T(8,128)(2,1)S(1)} %get-tuple-element.43), channel_id=1, source_target_pairs={{0,128},{64,192},{128,0},{192,64},{1,129},{65,193},{129,1},{193,65... | collective-permute-start | bytes 393224 | tf_op jit(solution)/shard_map/keys_values/ppermute | solution.py:36
  30.0 0.4 collective-permute-start.1
  30.4 2.3 %collective-permute-start.3 = (bf16[256,256]{1,0:T(8,128)(2,1)S(1)}, bf16[256,256]{1,0:T(8,128)(2,1)S(1)}, u32[]{:S(2)}, u32[]{:S(2)}) collective-permute-start(bf16[256,256]{1,0:T(8,128)(2,1)S(1)} %get-tuple-element.43), channel_id=1, source_target_pairs={{0,192},{64,0},{128,64},{192,128},{1,193},{65,1},{129,65},{193,129... | collective-permute-start | bytes 393224 | tf_op jit(solution)/shard_map/keys_values/ppermute | solution.py:36
  32.7 2.7 %collective-permute-start.11 = (bf16[112,512]{1,0:T(8,128)(2,1)S(1)}, bf16[112,512]{1,0:T(8,128)(2,1)S(1)}, u32[]{:S(2)}, u32[]{:S(2)}) collective-permute-start(bf16[112,512]{1,0:T(8,128)(2,1)S(1)} %slice.53), channel_id=1, source_target_pairs={{0,7},{1,0},{2,1},{3,2},{4,3},{5,4},{6,5},{7,6},{8,15},{9,8},{10,9... | collective-permute-start | bytes 344072 | tf_op jit(solution)/shard_map/inputs/ppermute | solution.py:54
  35.6 1.0 collective-permute-done.1
  36.7 0.6 collective-permute-done.11.refs_5_
  37.3 3.2 %collective-permute-done.7.refs_4_ = bf16[112,512]{1,0:T(8,128)(2,1)S(1)} collective-permute-done((bf16[112,512]{1,0:T(8,128)(2,1)S(1)}, bf16[112,512]{1,0:T(8,128)(2,1)S(1)}, u32[]{:S(2)}, u32[]{:S(2)}) %collective-permute-start.7) | collective-permute-done | bytes 114720 | tf_op jit(solution)/shard_map/inputs/ppermute | solution.py:54
  40.4 1.6 copy-done.6
  42.0 3.4 %gathered.2 = (bf16[128,128]{1,0:T(8,128)(2,1)S(1)}, bf16[128,128]{1,0:T(8,128)(2,1)S(1)}, f32[128,256]{1,0:T(8,128)S(1)}, bf16[16,96,256]{2,1,0:T(8,128)(2,1)S(1)}) custom-call(s32[4]{0:T(128)S(1)} %pad_add_fusion.place_ref, bf16[4096,256]{1,0:T(8,128)(2,1)S(1)} %copy-done.6, bf16[256,4096]{1,0:T(8,128)(2,1)S(1)} %copy-done, ...), custom_call_target="tpu_custom_call" | custom-call | tf_op jit(solution)/shard_map/gathered/pallas_call | solution.py:636
  45.5 0.9 copy-done.9
  46.4 5.4 %all-to-all-start = ((bf16[16,96,256]{2,1,0:T(8,128)(2,1)}), bf16[16,96,256]{2,1,0:T(8,128)(2,1)S(1)}, u32[]{:S(2)}, u32[]{:S(2)}) async-start(bf16[16,96,256]{2,1,0:T(8,128)(2,1)} %copy-done.9), calls=%async_computation | async-start | bytes 1572864 | tf_op jit(solution)/shard_map/gathered/all_to_all | solution.py:664
  51.7 4.3 %collective-permute-start.12 = (bf16[128,128]{1,0:T(8,128)(2,1)S(1)}, bf16[128,128]{1,0:T(8,128)(2,1)S(1)}, u32[]{:S(2)}, u32[]{:S(2)}) collective-permute-start(bf16[128,128]{1,0:T(8,128)(2,1)S(1)} %get-tuple-element.22), channel_id=1, source_target_pairs={{0,8},{8,0},{1,9},{9,1},{2,10},{10,2},{3,11},{11,3},{4,12},{12,4},... | collective-permute-start | bytes 98312 | tf_op jit(solution)/shard_map/gathered/ppermute | solution.py:69
  56.1 0.9 collective-permute-done.12
  57.0 2.7 %collective-permute-start.15 = (bf16[256,128]{1,0:T(8,128)(2,1)S(1)}, bf16[256,128]{1,0:T(8,128)(2,1)S(1)}, u32[]{:S(2)}, u32[]{:S(2)}) collective-permute-start(bf16[256,128]{1,0:T(8,128)(2,1)S(1)} %get-tuple-element.51.hold_ref), channel_id=1, source_target_pairs={{0,48},{16,0},{32,16},{48,32},{1,49},{17,1},{33,17},{49,33},{2,50}... | collective-permute-start | bytes 196616 | tf_op jit(solution)/shard_map/gathered/ppermute | solution.py:36
  59.7 0.6 collective-permute-start.14
  60.2 0.6 collective-permute-start.13
  60.8 0.3 gathered.3
  61.1 0.9 collective-permute-done.15
  62.1 3.3 %collective-permute-done.14 = bf16[256,128]{1,0:T(8,128)(2,1)S(1)} collective-permute-done((bf16[256,128]{1,0:T(8,128)(2,1)S(1)}, bf16[256,128]{1,0:T(8,128)(2,1)S(1)}, u32[]{:S(2)}, u32[]{:S(2)}) %collective-permute-start.14) | collective-permute-done | bytes 65568 | tf_op jit(solution)/shard_map/gathered/ppermute | solution.py:36
  65.3 1.3 collective-permute-done.13
  66.7 1.6 attention.2
  68.3 1.2 collective-permute-start.20
  69.5 0.6 collective-permute-start.18
  70.2 1.8 collective-permute-start.17
  72.0 0.7 collective-permute-start.16
  72.7 0.7 slice.48
  73.4 2.5 %collective-permute-start.21 = (bf16[1,1024]{1,0:T(2,128)(2,1)S(1)}, bf16[1,1024]{1,0:T(2,128)(2,1)S(1)}, u32[]{:S(2)}, u32[]{:S(2)}) collective-permute-start(bf16[1,1024]{1,0:T(2,128)(2,1)S(1)} %slice.48), channel_id=1, source_target_pairs={{8,0},{16,8},{24,16},{32,24},{40,32},{48,40},{56,48},{64,56},{72,6... | collective-permute-start | bytes 6152 | tf_op jit(solution)/shard_map/targets/ppermute | solution.py:632
  75.9 1.0 slice.47
  76.9 0.2 attention.3
  77.2 0.7 collective-permute-start.19
  77.8 0.4 collective-permute-done.21
  78.3 0.4 collective-permute-done.19
  78.8 0.9 raw.1
  79.7 26.0 %all_to_all.25.arrived_ref = bf16[8,16,3072]{2,1,0:T(8,128)(2,1)S(1)} all-to-all(bf16[8,16,3072]{2,1,0:T(8,128)(2,1)S(1)} %raw.1), channel_id=1, replica_groups=mesh['y'=4,'x'=4,'core'=2,'tp'=8] {'tp'}, dimensions={0} | all-to-all | bytes 1572864 | tf_op jit(solution)/shard_map/raw/all_to_all | solution.py:698
  105.7 1.1 norm.1
  106.8 14.7 %all_to_all.26.arrived_ref = bf16[8,16,1152]{2,1,0:T(8,128)(2,1)S(1)} all-to-all(bf16[8,16,1152]{2,1,0:T(8,128)(2,1)S(1)} %get-tuple-element.28), channel_id=1, replica_groups=mesh['y'=4,'x'=4,'core'=2,'tp'=8] {'tp'}, dimensions={0} | all-to-all | bytes 589824 | tf_op jit(solution)/shard_map/norm/all_to_all | solution.py:710
  121.5 1.1 loss.1
  122.5 1.3 collective-permute-start.22
  123.8 0.9 collective-permute-done.22
  124.7 0.1 sent_grads.1.refs_0_
  124.9 2.8 %collective-permute-start.25 = (bf16[272,128]{1,0:T(8,128)(2,1)S(1)}, bf16[272,128]{1,0:T(8,128)(2,1)S(1)}, u32[]{:S(2)}, u32[]{:S(2)}) collective-permute-start(bf16[272,128]{1,0:T(8,128)(2,1)S(1)} %sent_grads.1.refs_0_), channel_id=1, source_target_pairs={{0,48},{16,0},{32,16},{48,32},{1,49},{17,1},{33,17},{49,33},{2,50}... | collective-permute-start | bytes 208904 | tf_op jit(solution)/shard_map/sent_grads/ppermute | solution.py:36
  127.7 0.7 collective-permute-start.23
  128.3 2.2 %collective-permute-done.25.refs_3_ = bf16[272,128]{1,0:T(8,128)(2,1)S(1)} collective-permute-done((bf16[272,128]{1,0:T(8,128)(2,1)S(1)}, bf16[272,128]{1,0:T(8,128)(2,1)S(1)}, u32[]{:S(2)}, u32[]{:S(2)}) %collective-permute-start.25) | collective-permute-done | bytes 69664 | tf_op jit(solution)/shard_map/sent_grads/ppermute | solution.py:36
  130.5 1.9 collective-permute-done.24.refs_2_
  132.4 1.2 collective-permute-done.23.refs_1_
  133.6 1.5 attention_grad.2
  135.1 14.3 %all_to_all.27.refs_0_ = bf16[4,272,256]{2,1,0:T(8,128)(2,1)S(1)} all-to-all(bf16[4,272,256]{2,1,0:T(8,128)(2,1)S(1)} %attention_grad.2), channel_id=1, replica_groups=mesh['y'=4,'x'=4,'core'=2,'tp'=8] {'y'}, dimensions={0} | all-to-all | bytes 1114112 | tf_op jit(solution)/shard_map/attention_grad/all_to_all | solution.py:750
  149.5 2.8 %collective-permute-start.26 = (bf16[128,256]{1,0:T(8,128)(2,1)S(1)}, bf16[128,256]{1,0:T(8,128)(2,1)S(1)}, u32[]{:S(2)}, u32[]{:S(2)}) collective-permute-start(bf16[128,256]{1,0:T(8,128)(2,1)S(1)} %broadcast_select_fusion.2), channel_id=1, source_target_pairs={{0,8},{8,0},{1,9},{9,1},{2,10},{10,2},{3,11},{11,3},{4,12},{12,4},... | collective-permute-start | bytes 196616 | tf_op jit(solution)/shard_map/attention_grad/ppermute | solution.py:69
  152.3 0.1 collective-permute-start.27
  152.4 1.0 collective-permute-done.27
  154.2 0.8 d_context.3.start_ref
  155.0 0.8 copy-done.4
  155.7 0.8 d_context.4
  156.5 31.6 %all_to_all.28.arrived_ref = bf16[8,512,128]{2,1,0:T(8,128)(2,1)S(1)} all-to-all(bf16[8,512,128]{2,1,0:T(8,128)(2,1)S(1)} %d_context.4), channel_id=1, replica_groups=mesh['y'=4,'x'=4,'core'=2,'tp'=8] {'tp'}, dimensions={0} | all-to-all | bytes 2097152 | tf_op jit(solution)/shard_map/d_context/all_to_all | solution.py:775
  188.2 0.9 d_context.5
  (58 shorter events, 0.6 us)
Async XLA Ops:
  0.6 9.8 %copy-start.1 = (bf16[4096,256]{1,0:T(8,128)(2,1)S(1)}, bf16[4096,256]{1,0:T(8,128)(2,1)}, u32[]{:S(2)}) copy-start(bf16[4096,256]{1,0:T(8,128)(2,1)} %weight_ref.2) | copy-start | bytes 6291460
  3.9 12.4 %collective-permute-start.8 = (bf16[224,512]{1,0:T(8,128)(2,1)}, bf16[224,512]{1,0:T(8,128)(2,1)S(1)}, u32[]{:S(2)}, u32[]{:S(2)}) collective-permute-start(bf16[224,512]{1,0:T(8,128)(2,1)} %inputs.1.refs_0_.sent_ref), channel_id=1, source_target_pairs={{0,7},{1,0},{2,1},{3,2},{4,3},{5,4},{6,5},{7,6},{8,15},{9,8},{10,9... | collective-permute-start | bytes 688136 | tf_op jit(solution)/shard_map/inputs/ppermute | solution.py:52
  10.4 8.9 %collective-permute-start.4 = (bf16[224,512]{1,0:T(8,128)(2,1)}, bf16[224,512]{1,0:T(8,128)(2,1)S(1)}, u32[]{:S(2)}, u32[]{:S(2)}) collective-permute-start(bf16[224,512]{1,0:T(8,128)(2,1)} %inputs.1.refs_0_.sent_ref), channel_id=1, source_target_pairs={{0,1},{1,2},{2,3},{3,4},{4,5},{5,6},{6,7},{7,0},{8,9},{9,10},{10,1... | collective-permute-start | bytes 688136 | tf_op jit(solution)/shard_map/inputs/ppermute | solution.py:51
  10.4 1.6 copy-start.3
  12.0 1.2 copy-start.8
  13.3 27.2 %copy-start.7 = (bf16[224,512]{1,0:T(8,128)(2,1)S(1)}, bf16[224,512]{1,0:T(8,128)(2,1)}, u32[]{:S(2)}) copy-start(bf16[224,512]{1,0:T(8,128)(2,1)} %inputs.1.refs_0_.sent_ref) | copy-start | bytes 688132
  15.2 25.2 %copy-start = (bf16[256,4096]{1,0:T(8,128)(2,1)S(1)}, bf16[256,4096]{1,0:T(8,128)(2,1)}, u32[]{:S(2)}) copy-start(bf16[256,4096]{1,0:T(8,128)(2,1)} %w_out_ref.1) | copy-start | bytes 6291460
  15.2 4.0 %collective-permute-start = (bf16[128,256]{1,0:T(8,128)(2,1)S(1)}, bf16[128,256]{1,0:T(8,128)(2,1)S(1)}, u32[]{:S(2)}, u32[]{:S(2)}) collective-permute-start(bf16[128,256]{1,0:T(8,128)(2,1)S(1)} %get-tuple-element.20), channel_id=1, source_target_pairs={{0,8},{8,0},{1,9},{9,1},{2,10},{10,2},{3,11},{11,3},{4,12},{12,4},... | collective-permute-start | bytes 196616 | tf_op jit(solution)/shard_map/keys_values/ppermute | solution.py:69
  16.3 7.3 %collective-permute-start.9 = (bf16[224,512]{1,0:T(8,128)(2,1)S(1)}, bf16[224,512]{1,0:T(8,128)(2,1)S(1)}, u32[]{:S(2)}, u32[]{:S(2)}) collective-permute-start(bf16[224,512]{1,0:T(8,128)(2,1)S(1)} %collective-permute-done.8.refs_8_), channel_id=1, source_target_pairs={{0,7},{1,0},{2,1},{3,2},{4,3},{5,4},{6,5},{7,6},{8,15},{9,8},{10,9... | collective-permute-start | bytes 688136 | tf_op jit(solution)/shard_map/inputs/ppermute | solution.py:52
  19.2 7.8 %collective-permute-start.5 = (bf16[224,512]{1,0:T(8,128)(2,1)S(1)}, bf16[224,512]{1,0:T(8,128)(2,1)S(1)}, u32[]{:S(2)}, u32[]{:S(2)}) collective-permute-start(bf16[224,512]{1,0:T(8,128)(2,1)S(1)} %collective-permute-done.4.refs_1_), channel_id=1, source_target_pairs={{0,1},{1,2},{2,3},{3,4},{4,5},{5,6},{6,7},{7,0},{8,9},{9,10},{10,1... | collective-permute-start | bytes 688136 | tf_op jit(solution)/shard_map/inputs/ppermute | solution.py:51
  23.6 9.1 %collective-permute-start.10 = (bf16[224,512]{1,0:T(8,128)(2,1)S(1)}, bf16[224,512]{1,0:T(8,128)(2,1)S(1)}, u32[]{:S(2)}, u32[]{:S(2)}) collective-permute-start(bf16[224,512]{1,0:T(8,128)(2,1)S(1)} %collective-permute-done.9.refs_7_), channel_id=1, source_target_pairs={{0,7},{1,0},{2,1},{3,2},{4,3},{5,4},{6,5},{7,6},{8,15},{9,8},{10,9... | collective-permute-start | bytes 688136 | tf_op jit(solution)/shard_map/inputs/ppermute | solution.py:52
  27.0 8.5 %collective-permute-start.6 = (bf16[224,512]{1,0:T(8,128)(2,1)S(1)}, bf16[224,512]{1,0:T(8,128)(2,1)S(1)}, u32[]{:S(2)}, u32[]{:S(2)}) collective-permute-start(bf16[224,512]{1,0:T(8,128)(2,1)S(1)} %collective-permute-done.5.refs_2_), channel_id=1, source_target_pairs={{0,1},{1,2},{2,3},{3,4},{4,5},{5,6},{6,7},{7,0},{8,9},{9,10},{10,1... | collective-permute-start | bytes 688136 | tf_op jit(solution)/shard_map/inputs/ppermute | solution.py:51
  27.0 8.5 %collective-permute-start.2 = (bf16[256,256]{1,0:T(8,128)(2,1)S(1)}, bf16[256,256]{1,0:T(8,128)(2,1)S(1)}, u32[]{:S(2)}, u32[]{:S(2)}) collective-permute-start(bf16[256,256]{1,0:T(8,128)(2,1)S(1)} %get-tuple-element.43), channel_id=1, source_target_pairs={{0,128},{64,192},{128,0},{192,64},{1,129},{65,193},{129,1},{193,65... | collective-permute-start | bytes 393224 | tf_op jit(solution)/shard_map/keys_values/ppermute | solution.py:36
  30.0 6.6 %collective-permute-start.1 = (bf16[256,256]{1,0:T(8,128)(2,1)S(1)}, bf16[256,256]{1,0:T(8,128)(2,1)S(1)}, u32[]{:S(2)}, u32[]{:S(2)}) collective-permute-start(bf16[256,256]{1,0:T(8,128)(2,1)S(1)} %get-tuple-element.43), channel_id=1, source_target_pairs={{0,64},{64,128},{128,192},{192,0},{1,65},{65,129},{129,193},{193,1... | collective-permute-start | bytes 393224 | tf_op jit(solution)/shard_map/keys_values/ppermute | solution.py:36
  30.4 6.2 %collective-permute-start.3 = (bf16[256,256]{1,0:T(8,128)(2,1)S(1)}, bf16[256,256]{1,0:T(8,128)(2,1)S(1)}, u32[]{:S(2)}, u32[]{:S(2)}) collective-permute-start(bf16[256,256]{1,0:T(8,128)(2,1)S(1)} %get-tuple-element.43), channel_id=1, source_target_pairs={{0,192},{64,0},{128,64},{192,128},{1,193},{65,1},{129,65},{193,129... | collective-permute-start | bytes 393224 | tf_op jit(solution)/shard_map/keys_values/ppermute | solution.py:36
  32.7 4.5 %collective-permute-start.11 = (bf16[112,512]{1,0:T(8,128)(2,1)S(1)}, bf16[112,512]{1,0:T(8,128)(2,1)S(1)}, u32[]{:S(2)}, u32[]{:S(2)}) collective-permute-start(bf16[112,512]{1,0:T(8,128)(2,1)S(1)} %slice.53), channel_id=1, source_target_pairs={{0,7},{1,0},{2,1},{3,2},{4,3},{5,4},{6,5},{7,6},{8,15},{9,8},{10,9... | collective-permute-start | bytes 344072 | tf_op jit(solution)/shard_map/inputs/ppermute | solution.py:54
  35.5 4.9 %collective-permute-start.7 = (bf16[112,512]{1,0:T(8,128)(2,1)S(1)}, bf16[112,512]{1,0:T(8,128)(2,1)S(1)}, u32[]{:S(2)}, u32[]{:S(2)}) collective-permute-start(bf16[112,512]{1,0:T(8,128)(2,1)S(1)} %slice.52), channel_id=1, source_target_pairs={{0,1},{1,2},{2,3},{3,4},{4,5},{5,6},{6,7},{7,0},{8,9},{9,10},{10,1... | collective-permute-start | bytes 344072 | tf_op jit(solution)/shard_map/inputs/ppermute | solution.py:54
  40.4 1.6 copy-start.6
  45.5 0.9 copy-start.9
  46.4 14.4 %copy-start.5 = (bf16[512,1024]{1,0:T(8,128)(2,1)S(1)}, bf16[512,1024]{1,0:T(8,128)(2,1)}, u32[]{:S(2)}) copy-start(bf16[512,1024]{1,0:T(8,128)(2,1)} %post_ref.3) | copy-start | bytes 3145732
  46.4 20.4 %copy-start.10 = (s32[4]{0:T(128)S(1)}, s32[4]{0:T(128)}, u32[]{:S(2)}) copy-start(s32[4]{0:T(128)} %lengths_ref.5) | copy-start | bytes 52
  46.4 22.0 %all-to-all-start = ((bf16[16,96,256]{2,1,0:T(8,128)(2,1)}), bf16[16,96,256]{2,1,0:T(8,128)(2,1)S(1)}, u32[]{:S(2)}, u32[]{:S(2)}) async-start(bf16[16,96,256]{2,1,0:T(8,128)(2,1)} %copy-done.9), calls=%async_computation | async-start | bytes 1572864 | tf_op jit(solution)/shard_map/gathered/all_to_all | solution.py:664
  51.7 5.2 %collective-permute-start.12 = (bf16[128,128]{1,0:T(8,128)(2,1)S(1)}, bf16[128,128]{1,0:T(8,128)(2,1)S(1)}, u32[]{:S(2)}, u32[]{:S(2)}) collective-permute-start(bf16[128,128]{1,0:T(8,128)(2,1)S(1)} %get-tuple-element.22), channel_id=1, source_target_pairs={{0,8},{8,0},{1,9},{9,1},{2,10},{10,2},{3,11},{11,3},{4,12},{12,4},... | collective-permute-start | bytes 98312 | tf_op jit(solution)/shard_map/gathered/ppermute | solution.py:69
  57.0 5.1 %collective-permute-start.15 = (bf16[256,128]{1,0:T(8,128)(2,1)S(1)}, bf16[256,128]{1,0:T(8,128)(2,1)S(1)}, u32[]{:S(2)}, u32[]{:S(2)}) collective-permute-start(bf16[256,128]{1,0:T(8,128)(2,1)S(1)} %get-tuple-element.51.hold_ref), channel_id=1, source_target_pairs={{0,48},{16,0},{32,16},{48,32},{1,49},{17,1},{33,17},{49,33},{2,50}... | collective-permute-start | bytes 196616 | tf_op jit(solution)/shard_map/gathered/ppermute | solution.py:36
  59.7 5.7 %collective-permute-start.14 = (bf16[256,128]{1,0:T(8,128)(2,1)S(1)}, bf16[256,128]{1,0:T(8,128)(2,1)S(1)}, u32[]{:S(2)}, u32[]{:S(2)}) collective-permute-start(bf16[256,128]{1,0:T(8,128)(2,1)S(1)} %get-tuple-element.51.hold_ref), channel_id=1, source_target_pairs={{0,32},{16,48},{32,0},{48,16},{1,33},{17,49},{33,1},{49,17},{2,34}... | collective-permute-start | bytes 196616 | tf_op jit(solution)/shard_map/gathered/ppermute | solution.py:36
  60.2 6.4 %collective-permute-start.13 = (bf16[256,128]{1,0:T(8,128)(2,1)S(1)}, bf16[256,128]{1,0:T(8,128)(2,1)S(1)}, u32[]{:S(2)}, u32[]{:S(2)}) collective-permute-start(bf16[256,128]{1,0:T(8,128)(2,1)S(1)} %get-tuple-element.51.hold_ref), channel_id=1, source_target_pairs={{0,16},{16,32},{32,48},{48,0},{1,17},{17,33},{33,49},{49,1},{2,18}... | collective-permute-start | bytes 196616 | tf_op jit(solution)/shard_map/gathered/ppermute | solution.py:36
  68.3 10.4 %collective-permute-start.20 = (bf16[16,96,256]{2,1,0:T(8,128)(2,1)S(1)}, bf16[16,96,256]{2,1,0:T(8,128)(2,1)S(1)}, u32[]{:S(2)}, u32[]{:S(2)}) collective-permute-start(bf16[16,96,256]{2,1,0:T(8,128)(2,1)S(1)} %all-to-all-done.own_ref), channel_id=1, source_target_pairs={{0,8},{8,0},{1,9},{9,1},{2,10},{10,2},{3,11},{11,3},{4,12},{12,4},... | collective-permute-start | bytes 2359304 | tf_op jit(solution)/shard_map/gathered/ppermute | solution.py:69
  69.5 7.3 %collective-permute-start.18 = (bf16[272,128]{1,0:T(8,128)(2,1)S(1)}, bf16[272,128]{1,0:T(8,128)(2,1)S(1)}, u32[]{:S(2)}, u32[]{:S(2)}) collective-permute-start(bf16[272,128]{1,0:T(8,128)(2,1)S(1)} %get-tuple-element.36), channel_id=1, source_target_pairs={{0,16},{16,32},{32,48},{48,0},{1,17},{17,33},{33,49},{49,1},{2,18}... | collective-permute-start | bytes 208904 | tf_op jit(solution)/shard_map/attention/ppermute | solution.py:42
  70.2 6.7 %collective-permute-start.17 = (bf16[272,128]{1,0:T(8,128)(2,1)S(1)}, bf16[272,128]{1,0:T(8,128)(2,1)S(1)}, u32[]{:S(2)}, u32[]{:S(2)}) collective-permute-start(bf16[272,128]{1,0:T(8,128)(2,1)S(1)} %get-tuple-element.37), channel_id=1, source_target_pairs={{0,32},{16,48},{32,0},{48,16},{1,33},{17,49},{33,1},{49,17},{2,34}... | collective-permute-start | bytes 208904 | tf_op jit(solution)/shard_map/attention/ppermute | solution.py:42
  72.0 5.0 %collective-permute-start.16 = (bf16[272,128]{1,0:T(8,128)(2,1)S(1)}, bf16[272,128]{1,0:T(8,128)(2,1)S(1)}, u32[]{:S(2)}, u32[]{:S(2)}) collective-permute-start(bf16[272,128]{1,0:T(8,128)(2,1)S(1)} %get-tuple-element.38), channel_id=1, source_target_pairs={{0,48},{16,0},{32,16},{48,32},{1,49},{17,1},{33,17},{49,33},{2,50}... | collective-permute-start | bytes 208904 | tf_op jit(solution)/shard_map/attention/ppermute | solution.py:42
  73.4 4.9 %collective-permute-start.21 = (bf16[1,1024]{1,0:T(2,128)(2,1)S(1)}, bf16[1,1024]{1,0:T(2,128)(2,1)S(1)}, u32[]{:S(2)}, u32[]{:S(2)}) collective-permute-start(bf16[1,1024]{1,0:T(2,128)(2,1)S(1)} %slice.48), channel_id=1, source_target_pairs={{8,0},{16,8},{24,16},{32,24},{40,32},{48,40},{56,48},{64,56},{72,6... | collective-permute-start | bytes 6152 | tf_op jit(solution)/shard_map/targets/ppermute | solution.py:632
  77.2 1.5 collective-permute-start.19
  79.6 41.8 %copy-start.11 = (s32[128]{0:T(128)S(1)}, s32[128]{0:T(128)}, u32[]{:S(2)}) copy-start(s32[128]{0:T(128)} %param.14) | copy-start | bytes 1540
  122.5 2.2 %collective-permute-start.22 = (bf16[128,128]{1,0:T(8,128)(2,1)S(1)}, bf16[128,128]{1,0:T(8,128)(2,1)S(1)}, u32[]{:S(2)}, u32[]{:S(2)}) collective-permute-start(bf16[128,128]{1,0:T(8,128)(2,1)S(1)} %get-tuple-element.31), channel_id=1, source_target_pairs={{0,8},{8,0},{1,9},{9,1},{2,10},{10,2},{3,11},{11,3},{4,12},{12,4},... | collective-permute-start | bytes 98312 | tf_op jit(solution)/shard_map/sent_grads/ppermute | solution.py:69
  124.8 29.3 %copy-start.2 = (bf16[4096,256]{1,0:T(8,128)(2,1)S(1)}, bf16[4096,256]{1,0:T(8,128)(2,1)}, u32[]{:S(2)}) copy-start(bf16[4096,256]{1,0:T(8,128)(2,1)} %weight_ref.2) | copy-start | bytes 6291460
  124.9 5.7 %collective-permute-start.25 = (bf16[272,128]{1,0:T(8,128)(2,1)S(1)}, bf16[272,128]{1,0:T(8,128)(2,1)S(1)}, u32[]{:S(2)}, u32[]{:S(2)}) collective-permute-start(bf16[272,128]{1,0:T(8,128)(2,1)S(1)} %sent_grads.1.refs_0_), channel_id=1, source_target_pairs={{0,48},{16,0},{32,16},{48,32},{1,49},{17,1},{33,17},{49,33},{2,50}... | collective-permute-start | bytes 208904 | tf_op jit(solution)/shard_map/sent_grads/ppermute | solution.py:36
  127.7 4.8 %collective-permute-start.24 = (bf16[272,128]{1,0:T(8,128)(2,1)S(1)}, bf16[272,128]{1,0:T(8,128)(2,1)S(1)}, u32[]{:S(2)}, u32[]{:S(2)}) collective-permute-start(bf16[272,128]{1,0:T(8,128)(2,1)S(1)} %sent_grads.1.refs_0_), channel_id=1, source_target_pairs={{0,32},{16,48},{32,0},{48,16},{1,33},{17,49},{33,1},{49,17},{2,34}... | collective-permute-start | bytes 208904 | tf_op jit(solution)/shard_map/sent_grads/ppermute | solution.py:36
  127.7 5.9 %collective-permute-start.23 = (bf16[272,128]{1,0:T(8,128)(2,1)S(1)}, bf16[272,128]{1,0:T(8,128)(2,1)S(1)}, u32[]{:S(2)}, u32[]{:S(2)}) collective-permute-start(bf16[272,128]{1,0:T(8,128)(2,1)S(1)} %sent_grads.1.refs_0_), channel_id=1, source_target_pairs={{0,16},{16,32},{32,48},{48,0},{1,17},{17,33},{33,49},{49,1},{2,18}... | collective-permute-start | bytes 208904 | tf_op jit(solution)/shard_map/sent_grads/ppermute | solution.py:36
  149.5 4.6 %collective-permute-start.26 = (bf16[128,256]{1,0:T(8,128)(2,1)S(1)}, bf16[128,256]{1,0:T(8,128)(2,1)S(1)}, u32[]{:S(2)}, u32[]{:S(2)}) collective-permute-start(bf16[128,256]{1,0:T(8,128)(2,1)S(1)} %broadcast_select_fusion.2), channel_id=1, source_target_pairs={{0,8},{8,0},{1,9},{9,1},{2,10},{10,2},{3,11},{11,3},{4,12},{12,4},... | collective-permute-start | bytes 196616 | tf_op jit(solution)/shard_map/attention_grad/ppermute | solution.py:69
  152.3 1.1 collective-permute-start.27
  154.2 1.6 copy-start.4

commit v8 on v7

--- a/solution.py
+++ b/solution.py
@@ -188,26 +188,9 @@
     sent_ref[:rows, :] = total.astype(BF16)
 
 
-def project_kernel(
-    place_ref, context_ref, key_ref, value_ref, mine_ref, theirs_ref, context, weight, sems
-):
-    parts = 4
-    share = context.shape[1] // parts
-    pairs = []
-    for k in range(parts):
-        at = pl.ds(share * k, share)
-        pairs.append((context_ref.at[:, at], context.at[:, at]))
-        pairs.append((key_ref.at[at], weight.at[0, at]))
-        pairs.append((value_ref.at[at], weight.at[1, at]))
-    copies = fetch(pairs, sems)
-    keys = jnp.zeros((context.shape[0], 2 * HDIM), F32)
-    values = keys
-    for k in range(parts):
-        at = slice(share * k, share * (k + 1))
-        for copy in copies[3 * k : 3 * k + 3]:
-            copy.wait()
-        keys = keys + dot(context[:, at], weight[0, at])
-        values = values + dot(context[:, at], weight[1, at])
+def project_kernel(place_ref, context_ref, key_ref, value_ref, mine_ref, theirs_ref):
+    keys = dot(context_ref[...], key_ref[...])
+    values = dot(context_ref[...], value_ref[...])
     left = jnp.concatenate((keys[:, :HDIM], values[:, :HDIM]), axis=1)
     right = jnp.concatenate((keys[:, HDIM:], values[:, HDIM:]), axis=1)
     first = place_ref[2] == 0
@@ -616,13 +599,8 @@
         mine, theirs = pl.pallas_call(
             project_kernel,
             out_shape=(kv_shape, kv_shape),
-            in_specs=[SMEM, HBM, HBM, HBM],
+            in_specs=[SMEM, VMEM, VMEM, VMEM],
             out_specs=(VMEM, VMEM),
-            scratch_shapes=[
-                pltpu.VMEM(context.shape, BF16),
-                pltpu.VMEM((2,) + w_key.shape, BF16),
-                pltpu.SemaphoreType.DMA((12,)),
-            ],
             compiler_params=PARAMS,
         )(place, context, w_key, w_value)
         own_kv = to_head(mine, theirs, core)

time: 192 us -> 190 us (0.990)
  starting transfers between devices: 51 us -> 53.4 us
  blocking collectives: 86.6 us -> 84.4 us
    ppermute x7, starting transfers between devices: 11.4 us -> 13.9 us  [swap(): return lax.ppermute(block, 'core', [(0, 1), (1, 0)])]
    all_to_all x2, blocking collectives: 40.7 us -> 38.6 us  [local(): arrived = lax.all_to_all(sent, 'tp', 0, 0, tiled=True)]
where the time goes in v8:
time: 190 us; the launch traced here: 189 us
  blocking collectives  84.4 us (44%)
  starting transfers between devices  53.4 us (28%)
  waiting for transfers between devices  23 us (12%)
  Pallas kernels  17.3 us (9%)
  local copies, waits for them, and re-layouts  7.91 us (4%)
  between operations  2.84 us (1%)
    all_to_all x2, blocking collectives, local(): arrived = lax.all_to_all(sent, 'tp', 0, 0, tiled=True)  38.6 us
    all_to_all x1, blocking collectives, local(): lax.all_to_all(terms, 'tp', 0, 0, tiled=True)  31.6 us
    all_to_all x1, blocking collectives, local(): lax.all_to_all(sent, 'y', 0, 0, tiled=True)  14.1 us
    ppermute x7, starting transfers between devices, swap(): return lax.ppermute(block, 'core', [(0, 1), (1, 0)])  13.9 us
    ppermute x9, starting transfers between devices, shifted(): return [block] + [lax.ppermute(block, axis, route) for route in routes]  13.5 us
    ppermute x3, starting transfers between devices, around(): ahead.append(lax.ppermute(ahead[-1], axis, down))  12.8 us
    ppermute x9, waiting for transfers between devices, shifted(): return [block] + [lax.ppermute(block, axis, route) for route in routes]  12 us
    unnamed x24, local copies, waits for them, and re-layouts  6.13 us
  transfers between devices with their start and end apart: 29, of which 15 were waited for; matrix products, arithmetic and copies ran while one was open for 1% of the time, Pallas kernels for 2%

profile of v8, /device:TPU:1, one launch (start us, length us, event | category | flops | bytes accessed | tf_op | source)
XLA Modules:
  0.0 189.2 jit_solution(3757591642549748166)
XLA Ops:
  0.6 3.2 %inputs.1.refs_0_.sent_ref = bf16[224,512]{1,0:T(8,128)(2,1)} custom-call(s32[1,128]{1,0:T(1,128)} %bitcast.26, f32[1,512]{1,0:T(1,128)} %bitcast.36, bf16[128,1024]{1,0:T(8,128)(2,1)} %noised_ref.1, bf16[1024,512]{1,0:T(8,128)(2,1)} %pre_ref.1, bf16[512,1024]{1,0:T(8,128)(2,1)} %post_ref.3, bf16[256,4096]{1,0:T(8,128)(2,1)} %w_out_ref.1), custom_call_target="tpu_custom_call" | custom-call | tf_op jit(solution)/shard_map/inputs/pallas_call | solution.py:582
  3.9 6.5 %collective-permute-start.8 = (bf16[224,512]{1,0:T(8,128)(2,1)}, bf16[224,512]{1,0:T(8,128)(2,1)S(1)}, u32[]{:S(2)}, u32[]{:S(2)}) collective-permute-start(bf16[224,512]{1,0:T(8,128)(2,1)} %inputs.1.refs_0_.sent_ref), channel_id=1, source_target_pairs={{0,7},{1,0},{2,1},{3,2},{4,3},{5,4},{6,5},{7,6},{8,15},{9,8},{10,9... | collective-permute-start | bytes 688136 | tf_op jit(solution)/shard_map/inputs/ppermute | solution.py:52
  10.4 1.6 copy-done.3
  12.0 1.2 copy-done.8
  13.3 1.3 keys_values.1
  14.6 1.0 collective-permute-start
  15.6 2.9 %collective-permute-start.9 = (bf16[224,512]{1,0:T(8,128)(2,1)S(1)}, bf16[224,512]{1,0:T(8,128)(2,1)S(1)}, u32[]{:S(2)}, u32[]{:S(2)}) collective-permute-start(bf16[224,512]{1,0:T(8,128)(2,1)S(1)} %collective-permute-done.8.refs_8_), channel_id=1, source_target_pairs={{0,7},{1,0},{2,1},{3,2},{4,3},{5,4},{6,5},{7,6},{8,15},{9,8},{10,9... | collective-permute-start | bytes 688136 | tf_op jit(solution)/shard_map/inputs/ppermute | solution.py:52
  18.6 3.6 %collective-permute-done.9.refs_7_ = bf16[224,512]{1,0:T(8,128)(2,1)S(1)} collective-permute-done((bf16[224,512]{1,0:T(8,128)(2,1)S(1)}, bf16[224,512]{1,0:T(8,128)(2,1)S(1)}, u32[]{:S(2)}, u32[]{:S(2)}) %collective-permute-start.9) | collective-permute-done | bytes 229408 | tf_op jit(solution)/shard_map/inputs/ppermute | solution.py:52
  22.2 3.4 %collective-permute-start.10 = (bf16[224,512]{1,0:T(8,128)(2,1)S(1)}, bf16[224,512]{1,0:T(8,128)(2,1)S(1)}, u32[]{:S(2)}, u32[]{:S(2)}) collective-permute-start(bf16[224,512]{1,0:T(8,128)(2,1)S(1)} %collective-permute-done.9.refs_7_), channel_id=1, source_target_pairs={{0,7},{1,0},{2,1},{3,2},{4,3},{5,4},{6,5},{7,6},{8,15},{9,8},{10,9... | collective-permute-start | bytes 688136 | tf_op jit(solution)/shard_map/inputs/ppermute | solution.py:52
  25.6 3.0 %collective-permute-start.2 = (bf16[256,256]{1,0:T(8,128)(2,1)S(1)}, bf16[256,256]{1,0:T(8,128)(2,1)S(1)}, u32[]{:S(2)}, u32[]{:S(2)}) collective-permute-start(bf16[256,256]{1,0:T(8,128)(2,1)S(1)} %get-tuple-element.43), channel_id=1, source_target_pairs={{0,128},{64,192},{128,0},{192,64},{1,129},{65,193},{129,1},{193,65... | collective-permute-start | bytes 393224 | tf_op jit(solution)/shard_map/keys_values/ppermute | solution.py:36
  28.7 0.4 collective-permute-start.1
  29.1 2.3 %collective-permute-start.3 = (bf16[256,256]{1,0:T(8,128)(2,1)S(1)}, bf16[256,256]{1,0:T(8,128)(2,1)S(1)}, u32[]{:S(2)}, u32[]{:S(2)}) collective-permute-start(bf16[256,256]{1,0:T(8,128)(2,1)S(1)} %get-tuple-element.43), channel_id=1, source_target_pairs={{0,192},{64,0},{128,64},{192,128},{1,193},{65,1},{129,65},{193,129... | collective-permute-start | bytes 393224 | tf_op jit(solution)/shard_map/keys_values/ppermute | solution.py:36
  31.3 2.7 %collective-permute-start.11 = (bf16[112,512]{1,0:T(8,128)(2,1)S(1)}, bf16[112,512]{1,0:T(8,128)(2,1)S(1)}, u32[]{:S(2)}, u32[]{:S(2)}) collective-permute-start(bf16[112,512]{1,0:T(8,128)(2,1)S(1)} %slice.53), channel_id=1, source_target_pairs={{0,7},{1,0},{2,1},{3,2},{4,3},{5,4},{6,5},{7,6},{8,15},{9,8},{10,9... | collective-permute-start | bytes 344072 | tf_op jit(solution)/shard_map/inputs/ppermute | solution.py:54
  34.2 0.9 collective-permute-done.1
  35.2 0.7 collective-permute-done.11.refs_5_
  35.9 3.2 %collective-permute-done.7.refs_4_ = bf16[112,512]{1,0:T(8,128)(2,1)S(1)} collective-permute-done((bf16[112,512]{1,0:T(8,128)(2,1)S(1)}, bf16[112,512]{1,0:T(8,128)(2,1)S(1)}, u32[]{:S(2)}, u32[]{:S(2)}) %collective-permute-start.7) | collective-permute-done | bytes 114720 | tf_op jit(solution)/shard_map/inputs/ppermute | solution.py:54
  39.1 1.6 copy-done.6
  40.6 3.4 %gathered.2 = (bf16[128,128]{1,0:T(8,128)(2,1)S(1)}, bf16[128,128]{1,0:T(8,128)(2,1)S(1)}, f32[128,256]{1,0:T(8,128)S(1)}, bf16[16,96,256]{2,1,0:T(8,128)(2,1)S(1)}) custom-call(s32[4]{0:T(128)S(1)} %pad_add_fusion.place_ref, bf16[4096,256]{1,0:T(8,128)(2,1)S(1)} %copy-done.6, bf16[256,4096]{1,0:T(8,128)(2,1)S(1)} %copy-done, ...), custom_call_target="tpu_custom_call" | custom-call | tf_op jit(solution)/shard_map/gathered/pallas_call | solution.py:614
  44.1 0.9 copy-done.9
  45.0 4.7 %all-to-all-start = ((bf16[16,96,256]{2,1,0:T(8,128)(2,1)}), bf16[16,96,256]{2,1,0:T(8,128)(2,1)S(1)}, u32[]{:S(2)}, u32[]{:S(2)}) async-start(bf16[16,96,256]{2,1,0:T(8,128)(2,1)} %copy-done.9), calls=%async_computation | async-start | bytes 1572864 | tf_op jit(solution)/shard_map/gathered/all_to_all | solution.py:642
  49.7 5.2 %collective-permute-start.12 = (bf16[128,128]{1,0:T(8,128)(2,1)S(1)}, bf16[128,128]{1,0:T(8,128)(2,1)S(1)}, u32[]{:S(2)}, u32[]{:S(2)}) collective-permute-start(bf16[128,128]{1,0:T(8,128)(2,1)S(1)} %get-tuple-element.22), channel_id=1, source_target_pairs={{0,8},{8,0},{1,9},{9,1},{2,10},{10,2},{3,11},{11,3},{4,12},{12,4},... | collective-permute-start | bytes 98312 | tf_op jit(solution)/shard_map/gathered/ppermute | solution.py:69
  54.9 0.9 collective-permute-done.12
  55.8 2.7 %collective-permute-start.15 = (bf16[256,128]{1,0:T(8,128)(2,1)S(1)}, bf16[256,128]{1,0:T(8,128)(2,1)S(1)}, u32[]{:S(2)}, u32[]{:S(2)}) collective-permute-start(bf16[256,128]{1,0:T(8,128)(2,1)S(1)} %get-tuple-element.51.hold_ref), channel_id=1, source_target_pairs={{0,48},{16,0},{32,16},{48,32},{1,49},{17,1},{33,17},{49,33},{2,50}... | collective-permute-start | bytes 196616 | tf_op jit(solution)/shard_map/gathered/ppermute | solution.py:36
  58.4 0.6 collective-permute-start.14
  59.0 0.6 collective-permute-start.13
  59.6 0.3 gathered.3
  59.9 0.9 collective-permute-done.15
  60.8 3.3 %collective-permute-done.14 = bf16[256,128]{1,0:T(8,128)(2,1)S(1)} collective-permute-done((bf16[256,128]{1,0:T(8,128)(2,1)S(1)}, bf16[256,128]{1,0:T(8,128)(2,1)S(1)}, u32[]{:S(2)}, u32[]{:S(2)}) %collective-permute-start.14) | collective-permute-done | bytes 65568 | tf_op jit(solution)/shard_map/gathered/ppermute | solution.py:36
  64.1 1.1 collective-permute-done.13
  65.2 1.6 attention.2
  66.8 1.5 collective-permute-start.20
  68.3 0.7 collective-permute-start.18
  69.0 1.7 collective-permute-start.17
  70.7 0.8 collective-permute-start.16
  71.5 0.7 slice.48
  72.2 2.5 %collective-permute-start.21 = (bf16[1,1024]{1,0:T(2,128)(2,1)S(1)}, bf16[1,1024]{1,0:T(2,128)(2,1)S(1)}, u32[]{:S(2)}, u32[]{:S(2)}) collective-permute-start(bf16[1,1024]{1,0:T(2,128)(2,1)S(1)} %slice.48), channel_id=1, source_target_pairs={{8,0},{16,8},{24,16},{32,24},{40,32},{48,40},{56,48},{64,56},{72,6... | collective-permute-start | bytes 6152 | tf_op jit(solution)/shard_map/targets/ppermute | solution.py:610
  74.7 1.0 slice.47
  75.7 0.2 attention.3
  76.0 0.6 collective-permute-start.19
  76.6 0.5 collective-permute-done.21
  77.1 0.3 collective-permute-done.19
  77.5 0.9 raw.1
  78.4 25.5 %all_to_all.25.arrived_ref = bf16[8,16,3072]{2,1,0:T(8,128)(2,1)S(1)} all-to-all(bf16[8,16,3072]{2,1,0:T(8,128)(2,1)S(1)} %raw.1), channel_id=1, replica_groups=mesh['y'=4,'x'=4,'core'=2,'tp'=8] {'tp'}, dimensions={0} | all-to-all | bytes 1572864 | tf_op jit(solution)/shard_map/raw/all_to_all | solution.py:676
  103.9 1.1 norm.1
  105.0 13.1 %all_to_all.26.arrived_ref = bf16[8,16,1152]{2,1,0:T(8,128)(2,1)S(1)} all-to-all(bf16[8,16,1152]{2,1,0:T(8,128)(2,1)S(1)} %get-tuple-element.28), channel_id=1, replica_groups=mesh['y'=4,'x'=4,'core'=2,'tp'=8] {'tp'}, dimensions={0} | all-to-all | bytes 589824 | tf_op jit(solution)/shard_map/norm/all_to_all | solution.py:688
  118.2 1.0 loss.1
  119.2 3.1 %collective-permute-start.22 = (bf16[128,128]{1,0:T(8,128)(2,1)S(1)}, bf16[128,128]{1,0:T(8,128)(2,1)S(1)}, u32[]{:S(2)}, u32[]{:S(2)}) collective-permute-start(bf16[128,128]{1,0:T(8,128)(2,1)S(1)} %get-tuple-element.31), channel_id=1, source_target_pairs={{0,8},{8,0},{1,9},{9,1},{2,10},{10,2},{3,11},{11,3},{4,12},{12,4},... | collective-permute-start | bytes 98312 | tf_op jit(solution)/shard_map/sent_grads/ppermute | solution.py:69
  122.3 0.9 collective-permute-done.22
  123.2 0.1 sent_grads.1.refs_0_
  123.3 3.3 %collective-permute-start.25 = (bf16[272,128]{1,0:T(8,128)(2,1)S(1)}, bf16[272,128]{1,0:T(8,128)(2,1)S(1)}, u32[]{:S(2)}, u32[]{:S(2)}) collective-permute-start(bf16[272,128]{1,0:T(8,128)(2,1)S(1)} %sent_grads.1.refs_0_), channel_id=1, source_target_pairs={{0,48},{16,0},{32,16},{48,32},{1,49},{17,1},{33,17},{49,33},{2,50}... | collective-permute-start | bytes 208904 | tf_op jit(solution)/shard_map/sent_grads/ppermute | solution.py:36
  126.7 0.7 collective-permute-start.23
  127.3 2.2 %collective-permute-done.25.refs_3_ = bf16[272,128]{1,0:T(8,128)(2,1)S(1)} collective-permute-done((bf16[272,128]{1,0:T(8,128)(2,1)S(1)}, bf16[272,128]{1,0:T(8,128)(2,1)S(1)}, u32[]{:S(2)}, u32[]{:S(2)}) %collective-permute-start.25) | collective-permute-done | bytes 69664 | tf_op jit(solution)/shard_map/sent_grads/ppermute | solution.py:36
  129.5 1.9 collective-permute-done.24.refs_2_
  131.4 1.7 collective-permute-done.23.refs_1_
  133.2 1.5 attention_grad.2
  134.7 14.1 %all_to_all.27.refs_0_ = bf16[4,272,256]{2,1,0:T(8,128)(2,1)S(1)} all-to-all(bf16[4,272,256]{2,1,0:T(8,128)(2,1)S(1)} %attention_grad.2), channel_id=1, replica_groups=mesh['y'=4,'x'=4,'core'=2,'tp'=8] {'y'}, dimensions={0} | all-to-all | bytes 1114112 | tf_op jit(solution)/shard_map/attention_grad/all_to_all | solution.py:728
  148.9 2.4 %collective-permute-start.26 = (bf16[128,256]{1,0:T(8,128)(2,1)S(1)}, bf16[128,256]{1,0:T(8,128)(2,1)S(1)}, u32[]{:S(2)}, u32[]{:S(2)}) collective-permute-start(bf16[128,256]{1,0:T(8,128)(2,1)S(1)} %broadcast_select_fusion.2), channel_id=1, source_target_pairs={{0,8},{8,0},{1,9},{9,1},{2,10},{10,2},{3,11},{11,3},{4,12},{12,4},... | collective-permute-start | bytes 196616 | tf_op jit(solution)/shard_map/attention_grad/ppermute | solution.py:69
  151.3 0.1 collective-permute-start.27
  151.4 1.0 collective-permute-done.27
  153.2 0.8 d_context.3.start_ref
  154.0 0.8 copy-done.4
  154.8 0.8 d_context.4
  155.6 31.6 %all_to_all.28.arrived_ref = bf16[8,512,128]{2,1,0:T(8,128)(2,1)S(1)} all-to-all(bf16[8,512,128]{2,1,0:T(8,128)(2,1)S(1)} %d_context.4), channel_id=1, replica_groups=mesh['y'=4,'x'=4,'core'=2,'tp'=8] {'tp'}, dimensions={0} | all-to-all | bytes 2097152 | tf_op jit(solution)/shard_map/d_context/all_to_all | solution.py:753
  187.2 0.9 d_context.5
  (58 shorter events, 0.6 us)
Async XLA Ops:
  0.6 9.8 %copy-start.1 = (bf16[4096,256]{1,0:T(8,128)(2,1)S(1)}, bf16[4096,256]{1,0:T(8,128)(2,1)}, u32[]{:S(2)}) copy-start(bf16[4096,256]{1,0:T(8,128)(2,1)} %weight_ref.2) | copy-start | bytes 6291460
  3.9 11.7 %collective-permute-start.8 = (bf16[224,512]{1,0:T(8,128)(2,1)}, bf16[224,512]{1,0:T(8,128)(2,1)S(1)}, u32[]{:S(2)}, u32[]{:S(2)}) collective-permute-start(bf16[224,512]{1,0:T(8,128)(2,1)} %inputs.1.refs_0_.sent_ref), channel_id=1, source_target_pairs={{0,7},{1,0},{2,1},{3,2},{4,3},{5,4},{6,5},{7,6},{8,15},{9,8},{10,9... | collective-permute-start | bytes 688136 | tf_op jit(solution)/shard_map/inputs/ppermute | solution.py:52
  10.4 8.2 %collective-permute-start.4 = (bf16[224,512]{1,0:T(8,128)(2,1)}, bf16[224,512]{1,0:T(8,128)(2,1)S(1)}, u32[]{:S(2)}, u32[]{:S(2)}) collective-permute-start(bf16[224,512]{1,0:T(8,128)(2,1)} %inputs.1.refs_0_.sent_ref), channel_id=1, source_target_pairs={{0,1},{1,2},{2,3},{3,4},{4,5},{5,6},{6,7},{7,0},{8,9},{9,10},{10,1... | collective-permute-start | bytes 688136 | tf_op jit(solution)/shard_map/inputs/ppermute | solution.py:51
  10.4 1.6 copy-start.3
  12.0 1.2 copy-start.8
  13.3 25.8 %copy-start.7 = (bf16[224,512]{1,0:T(8,128)(2,1)S(1)}, bf16[224,512]{1,0:T(8,128)(2,1)}, u32[]{:S(2)}) copy-start(bf16[224,512]{1,0:T(8,128)(2,1)} %inputs.1.refs_0_.sent_ref) | copy-start | bytes 688132
  14.5 24.5 %copy-start = (bf16[256,4096]{1,0:T(8,128)(2,1)S(1)}, bf16[256,4096]{1,0:T(8,128)(2,1)}, u32[]{:S(2)}) copy-start(bf16[256,4096]{1,0:T(8,128)(2,1)} %w_out_ref.1) | copy-start | bytes 6291460
  14.6 4.0 %collective-permute-start = (bf16[128,256]{1,0:T(8,128)(2,1)S(1)}, bf16[128,256]{1,0:T(8,128)(2,1)S(1)}, u32[]{:S(2)}, u32[]{:S(2)}) collective-permute-start(bf16[128,256]{1,0:T(8,128)(2,1)S(1)} %get-tuple-element.20), channel_id=1, source_target_pairs={{0,8},{8,0},{1,9},{9,1},{2,10},{10,2},{3,11},{11,3},{4,12},{12,4},... | collective-permute-start | bytes 196616 | tf_op jit(solution)/shard_map/keys_values/ppermute | solution.py:69
  15.6 6.6 %collective-permute-start.9 = (bf16[224,512]{1,0:T(8,128)(2,1)S(1)}, bf16[224,512]{1,0:T(8,128)(2,1)S(1)}, u32[]{:S(2)}, u32[]{:S(2)}) collective-permute-start(bf16[224,512]{1,0:T(8,128)(2,1)S(1)} %collective-permute-done.8.refs_8_), channel_id=1, source_target_pairs={{0,7},{1,0},{2,1},{3,2},{4,3},{5,4},{6,5},{7,6},{8,15},{9,8},{10,9... | collective-permute-start | bytes 688136 | tf_op jit(solution)/shard_map/inputs/ppermute | solution.py:52
  18.6 7.1 %collective-permute-start.5 = (bf16[224,512]{1,0:T(8,128)(2,1)S(1)}, bf16[224,512]{1,0:T(8,128)(2,1)S(1)}, u32[]{:S(2)}, u32[]{:S(2)}) collective-permute-start(bf16[224,512]{1,0:T(8,128)(2,1)S(1)} %collective-permute-done.4.refs_1_), channel_id=1, source_target_pairs={{0,1},{1,2},{2,3},{3,4},{4,5},{5,6},{6,7},{7,0},{8,9},{9,10},{10,1... | collective-permute-start | bytes 688136 | tf_op jit(solution)/shard_map/inputs/ppermute | solution.py:51
  22.2 9.1 %collective-permute-start.10 = (bf16[224,512]{1,0:T(8,128)(2,1)S(1)}, bf16[224,512]{1,0:T(8,128)(2,1)S(1)}, u32[]{:S(2)}, u32[]{:S(2)}) collective-permute-start(bf16[224,512]{1,0:T(8,128)(2,1)S(1)} %collective-permute-done.9.refs_7_), channel_id=1, source_target_pairs={{0,7},{1,0},{2,1},{3,2},{4,3},{5,4},{6,5},{7,6},{8,15},{9,8},{10,9... | collective-permute-start | bytes 688136 | tf_op jit(solution)/shard_map/inputs/ppermute | solution.py:52
  25.6 8.5 %collective-permute-start.6 = (bf16[224,512]{1,0:T(8,128)(2,1)S(1)}, bf16[224,512]{1,0:T(8,128)(2,1)S(1)}, u32[]{:S(2)}, u32[]{:S(2)}) collective-permute-start(bf16[224,512]{1,0:T(8,128)(2,1)S(1)} %collective-permute-done.5.refs_2_), channel_id=1, source_target_pairs={{0,1},{1,2},{2,3},{3,4},{4,5},{5,6},{6,7},{7,0},{8,9},{9,10},{10,1... | collective-permute-start | bytes 688136 | tf_op jit(solution)/shard_map/inputs/ppermute | solution.py:51
  25.6 8.6 %collective-permute-start.2 = (bf16[256,256]{1,0:T(8,128)(2,1)S(1)}, bf16[256,256]{1,0:T(8,128)(2,1)S(1)}, u32[]{:S(2)}, u32[]{:S(2)}) collective-permute-start(bf16[256,256]{1,0:T(8,128)(2,1)S(1)} %get-tuple-element.43), channel_id=1, source_target_pairs={{0,128},{64,192},{128,0},{192,64},{1,129},{65,193},{129,1},{193,65... | collective-permute-start | bytes 393224 | tf_op jit(solution)/shard_map/keys_values/ppermute | solution.py:36
  28.7 6.4 %collective-permute-start.1 = (bf16[256,256]{1,0:T(8,128)(2,1)S(1)}, bf16[256,256]{1,0:T(8,128)(2,1)S(1)}, u32[]{:S(2)}, u32[]{:S(2)}) collective-permute-start(bf16[256,256]{1,0:T(8,128)(2,1)S(1)} %get-tuple-element.43), channel_id=1, source_target_pairs={{0,64},{64,128},{128,192},{192,0},{1,65},{65,129},{129,193},{193,1... | collective-permute-start | bytes 393224 | tf_op jit(solution)/shard_map/keys_values/ppermute | solution.py:36
  29.1 6.0 %collective-permute-start.3 = (bf16[256,256]{1,0:T(8,128)(2,1)S(1)}, bf16[256,256]{1,0:T(8,128)(2,1)S(1)}, u32[]{:S(2)}, u32[]{:S(2)}) collective-permute-start(bf16[256,256]{1,0:T(8,128)(2,1)S(1)} %get-tuple-element.43), channel_id=1, source_target_pairs={{0,192},{64,0},{128,64},{192,128},{1,193},{65,1},{129,65},{193,129... | collective-permute-start | bytes 393224 | tf_op jit(solution)/shard_map/keys_values/ppermute | solution.py:36
  31.3 4.5 %collective-permute-start.11 = (bf16[112,512]{1,0:T(8,128)(2,1)S(1)}, bf16[112,512]{1,0:T(8,128)(2,1)S(1)}, u32[]{:S(2)}, u32[]{:S(2)}) collective-permute-start(bf16[112,512]{1,0:T(8,128)(2,1)S(1)} %slice.53), channel_id=1, source_target_pairs={{0,7},{1,0},{2,1},{3,2},{4,3},{5,4},{6,5},{7,6},{8,15},{9,8},{10,9... | collective-permute-start | bytes 344072 | tf_op jit(solution)/shard_map/inputs/ppermute | solution.py:54
  34.1 4.9 %collective-permute-start.7 = (bf16[112,512]{1,0:T(8,128)(2,1)S(1)}, bf16[112,512]{1,0:T(8,128)(2,1)S(1)}, u32[]{:S(2)}, u32[]{:S(2)}) collective-permute-start(bf16[112,512]{1,0:T(8,128)(2,1)S(1)} %slice.52), channel_id=1, source_target_pairs={{0,1},{1,2},{2,3},{3,4},{4,5},{5,6},{6,7},{7,0},{8,9},{9,10},{10,1... | collective-permute-start | bytes 344072 | tf_op jit(solution)/shard_map/inputs/ppermute | solution.py:54
  39.0 1.6 copy-start.6
  44.1 0.9 copy-start.9
  45.0 14.6 %copy-start.5 = (bf16[512,1024]{1,0:T(8,128)(2,1)S(1)}, bf16[512,1024]{1,0:T(8,128)(2,1)}, u32[]{:S(2)}) copy-start(bf16[512,1024]{1,0:T(8,128)(2,1)} %post_ref.3) | copy-start | bytes 3145732
  45.0 20.2 %copy-start.10 = (s32[4]{0:T(128)S(1)}, s32[4]{0:T(128)}, u32[]{:S(2)}) copy-start(s32[4]{0:T(128)} %lengths_ref.5) | copy-start | bytes 52
  45.0 21.8 %all-to-all-start = ((bf16[16,96,256]{2,1,0:T(8,128)(2,1)}), bf16[16,96,256]{2,1,0:T(8,128)(2,1)S(1)}, u32[]{:S(2)}, u32[]{:S(2)}) async-start(bf16[16,96,256]{2,1,0:T(8,128)(2,1)} %copy-done.9), calls=%async_computation | async-start | bytes 1572864 | tf_op jit(solution)/shard_map/gathered/all_to_all | solution.py:642
  49.7 6.0 %collective-permute-start.12 = (bf16[128,128]{1,0:T(8,128)(2,1)S(1)}, bf16[128,128]{1,0:T(8,128)(2,1)S(1)}, u32[]{:S(2)}, u32[]{:S(2)}) collective-permute-start(bf16[128,128]{1,0:T(8,128)(2,1)S(1)} %get-tuple-element.22), channel_id=1, source_target_pairs={{0,8},{8,0},{1,9},{9,1},{2,10},{10,2},{3,11},{11,3},{4,12},{12,4},... | collective-permute-start | bytes 98312 | tf_op jit(solution)/shard_map/gathered/ppermute | solution.py:69
  55.8 5.1 %collective-permute-start.15 = (bf16[256,128]{1,0:T(8,128)(2,1)S(1)}, bf16[256,128]{1,0:T(8,128)(2,1)S(1)}, u32[]{:S(2)}, u32[]{:S(2)}) collective-permute-start(bf16[256,128]{1,0:T(8,128)(2,1)S(1)} %get-tuple-element.51.hold_ref), channel_id=1, source_target_pairs={{0,48},{16,0},{32,16},{48,32},{1,49},{17,1},{33,17},{49,33},{2,50}... | collective-permute-start | bytes 196616 | tf_op jit(solution)/shard_map/gathered/ppermute | solution.py:36
  58.4 5.7 %collective-permute-start.14 = (bf16[256,128]{1,0:T(8,128)(2,1)S(1)}, bf16[256,128]{1,0:T(8,128)(2,1)S(1)}, u32[]{:S(2)}, u32[]{:S(2)}) collective-permute-start(bf16[256,128]{1,0:T(8,128)(2,1)S(1)} %get-tuple-element.51.hold_ref), channel_id=1, source_target_pairs={{0,32},{16,48},{32,0},{48,16},{1,33},{17,49},{33,1},{49,17},{2,34}... | collective-permute-start | bytes 196616 | tf_op jit(solution)/shard_map/gathered/ppermute | solution.py:36
  59.0 6.2 %collective-permute-start.13 = (bf16[256,128]{1,0:T(8,128)(2,1)S(1)}, bf16[256,128]{1,0:T(8,128)(2,1)S(1)}, u32[]{:S(2)}, u32[]{:S(2)}) collective-permute-start(bf16[256,128]{1,0:T(8,128)(2,1)S(1)} %get-tuple-element.51.hold_ref), channel_id=1, source_target_pairs={{0,16},{16,32},{32,48},{48,0},{1,17},{17,33},{33,49},{49,1},{2,18}... | collective-permute-start | bytes 196616 | tf_op jit(solution)/shard_map/gathered/ppermute | solution.py:36
  66.8 10.7 %collective-permute-start.20 = (bf16[16,96,256]{2,1,0:T(8,128)(2,1)S(1)}, bf16[16,96,256]{2,1,0:T(8,128)(2,1)S(1)}, u32[]{:S(2)}, u32[]{:S(2)}) collective-permute-start(bf16[16,96,256]{2,1,0:T(8,128)(2,1)S(1)} %all-to-all-done.own_ref), channel_id=1, source_target_pairs={{0,8},{8,0},{1,9},{9,1},{2,10},{10,2},{3,11},{11,3},{4,12},{12,4},... | collective-permute-start | bytes 2359304 | tf_op jit(solution)/shard_map/gathered/ppermute | solution.py:69
  68.3 7.4 %collective-permute-start.18 = (bf16[272,128]{1,0:T(8,128)(2,1)S(1)}, bf16[272,128]{1,0:T(8,128)(2,1)S(1)}, u32[]{:S(2)}, u32[]{:S(2)}) collective-permute-start(bf16[272,128]{1,0:T(8,128)(2,1)S(1)} %get-tuple-element.36), channel_id=1, source_target_pairs={{0,16},{16,32},{32,48},{48,0},{1,17},{17,33},{33,49},{49,1},{2,18}... | collective-permute-start | bytes 208904 | tf_op jit(solution)/shard_map/attention/ppermute | solution.py:42
  69.0 6.7 %collective-permute-start.17 = (bf16[272,128]{1,0:T(8,128)(2,1)S(1)}, bf16[272,128]{1,0:T(8,128)(2,1)S(1)}, u32[]{:S(2)}, u32[]{:S(2)}) collective-permute-start(bf16[272,128]{1,0:T(8,128)(2,1)S(1)} %get-tuple-element.37), channel_id=1, source_target_pairs={{0,32},{16,48},{32,0},{48,16},{1,33},{17,49},{33,1},{49,17},{2,34}... | collective-permute-start | bytes 208904 | tf_op jit(solution)/shard_map/attention/ppermute | solution.py:42
  70.7 5.0 %collective-permute-start.16 = (bf16[272,128]{1,0:T(8,128)(2,1)S(1)}, bf16[272,128]{1,0:T(8,128)(2,1)S(1)}, u32[]{:S(2)}, u32[]{:S(2)}) collective-permute-start(bf16[272,128]{1,0:T(8,128)(2,1)S(1)} %get-tuple-element.38), channel_id=1, source_target_pairs={{0,48},{16,0},{32,16},{48,32},{1,49},{17,1},{33,17},{49,33},{2,50}... | collective-permute-start | bytes 208904 | tf_op jit(solution)/shard_map/attention/ppermute | solution.py:42
  72.2 4.9 %collective-permute-start.21 = (bf16[1,1024]{1,0:T(2,128)(2,1)S(1)}, bf16[1,1024]{1,0:T(2,128)(2,1)S(1)}, u32[]{:S(2)}, u32[]{:S(2)}) collective-permute-start(bf16[1,1024]{1,0:T(2,128)(2,1)S(1)} %slice.48), channel_id=1, source_target_pairs={{8,0},{16,8},{24,16},{32,24},{40,32},{48,40},{56,48},{64,56},{72,6... | collective-permute-start | bytes 6152 | tf_op jit(solution)/shard_map/targets/ppermute | solution.py:610
  76.0 1.5 collective-permute-start.19
  78.4 39.8 %copy-start.11 = (s32[128]{0:T(128)S(1)}, s32[128]{0:T(128)}, u32[]{:S(2)}) copy-start(s32[128]{0:T(128)} %param.14) | copy-start | bytes 1540
  119.2 3.9 %collective-permute-start.22 = (bf16[128,128]{1,0:T(8,128)(2,1)S(1)}, bf16[128,128]{1,0:T(8,128)(2,1)S(1)}, u32[]{:S(2)}, u32[]{:S(2)}) collective-permute-start(bf16[128,128]{1,0:T(8,128)(2,1)S(1)} %get-tuple-element.31), channel_id=1, source_target_pairs={{0,8},{8,0},{1,9},{9,1},{2,10},{10,2},{3,11},{11,3},{4,12},{12,4},... | collective-permute-start | bytes 98312 | tf_op jit(solution)/shard_map/sent_grads/ppermute | solution.py:69
  123.3 29.9 %copy-start.2 = (bf16[4096,256]{1,0:T(8,128)(2,1)S(1)}, bf16[4096,256]{1,0:T(8,128)(2,1)}, u32[]{:S(2)}) copy-start(bf16[4096,256]{1,0:T(8,128)(2,1)} %weight_ref.2) | copy-start | bytes 6291460
  123.3 6.2 %collective-permute-start.25 = (bf16[272,128]{1,0:T(8,128)(2,1)S(1)}, bf16[272,128]{1,0:T(8,128)(2,1)S(1)}, u32[]{:S(2)}, u32[]{:S(2)}) collective-permute-start(bf16[272,128]{1,0:T(8,128)(2,1)S(1)} %sent_grads.1.refs_0_), channel_id=1, source_target_pairs={{0,48},{16,0},{32,16},{48,32},{1,49},{17,1},{33,17},{49,33},{2,50}... | collective-permute-start | bytes 208904 | tf_op jit(solution)/shard_map/sent_grads/ppermute | solution.py:36
  126.7 4.8 %collective-permute-start.24 = (bf16[272,128]{1,0:T(8,128)(2,1)S(1)}, bf16[272,128]{1,0:T(8,128)(2,1)S(1)}, u32[]{:S(2)}, u32[]{:S(2)}) collective-permute-start(bf16[272,128]{1,0:T(8,128)(2,1)S(1)} %sent_grads.1.refs_0_), channel_id=1, source_target_pairs={{0,32},{16,48},{32,0},{48,16},{1,33},{17,49},{33,1},{49,17},{2,34}... | collective-permute-start | bytes 208904 | tf_op jit(solution)/shard_map/sent_grads/ppermute | solution.py:36
  126.7 6.5 %collective-permute-start.23 = (bf16[272,128]{1,0:T(8,128)(2,1)S(1)}, bf16[272,128]{1,0:T(8,128)(2,1)S(1)}, u32[]{:S(2)}, u32[]{:S(2)}) collective-permute-start(bf16[272,128]{1,0:T(8,128)(2,1)S(1)} %sent_grads.1.refs_0_), channel_id=1, source_target_pairs={{0,16},{16,32},{32,48},{48,0},{1,17},{17,33},{33,49},{49,1},{2,18}... | collective-permute-start | bytes 208904 | tf_op jit(solution)/shard_map/sent_grads/ppermute | solution.py:36
  148.9 4.2 %collective-permute-start.26 = (bf16[128,256]{1,0:T(8,128)(2,1)S(1)}, bf16[128,256]{1,0:T(8,128)(2,1)S(1)}, u32[]{:S(2)}, u32[]{:S(2)}) collective-permute-start(bf16[128,256]{1,0:T(8,128)(2,1)S(1)} %broadcast_select_fusion.2), channel_id=1, source_target_pairs={{0,8},{8,0},{1,9},{9,1},{2,10},{10,2},{3,11},{11,3},{4,12},{12,4},... | collective-permute-start | bytes 196616 | tf_op jit(solution)/shard_map/attention_grad/ppermute | solution.py:69
  151.3 1.1 collective-permute-start.27
  153.2 1.6 copy-start.4
